TPU v7x, 512 devices: a whole 4x4x16 slice. The times are simulated.
512 devices in a mesh: tile: 256 (over x_lo, y, z, core), cores: 2 (over x_hi).
Axes of the slice: x: 4 (x_hi: 2, x_lo: 2; x = x_hi * 2 + x_lo), y: 4, z: 16, core: 2. Of those that a mesh axis runs over, the one named last changes fastest.
Arguments:
- state: float32 [256, 256, 256], P('tile', 'cores'), may hold values from -6 to 6
- increment: float32 [256, 256, 256], P('tile', 'cores'), may hold values from -4 to 4
- diffusivity: float32 [256, 256, 256], P('tile', 'cores'), may hold values from 0.03 to 0.24
- land_sea: int32 [256, 256], P('tile', 'cores'), may hold values 0 or 1
- w_in: float32 [1024, 256], P('tile'), may hold values from -0.375 to 0.375
- w_mid: bfloat16 [1024, 1024], P('tile'), may hold values from -0.2625 to 0.2625
- w_out: float32 [1024, 256], P('tile'), may hold values from -0.1875 to 0.1875
- obs_col: int32 [32768], P(('tile', 'cores')), may hold values from 0 to 127
- obs_lev: int32 [32768], P(('tile', 'cores')), may hold values from 0 to 255
- obs_val: float32 [32768], P(('tile', 'cores')), may hold values from -6 to 6
- obs_prec: float32 [32768], P(('tile', 'cores')), may hold values from 0.5 to 6
Outputs:
- adjoint: float32 [256, 256, 256], P('tile', 'cores')
- w_in_new: float32 [1024, 256], P('tile')
- w_out_new: float32 [1024, 256], P('tile')
All inputs are finite; a program needn't handle non-finite values. No bound on the sum of `land_sea` on one device may be relied on, other than what follows from the above.
Results may differ from a plain program's by a relative error of at most 0.015.
Values may be sent and summed in bfloat16 or wider, within the bound.
No kernel may reach another device: no remote copies, remote signals or barrier semaphores. Data moves between devices by JAX's collectives and lax.ppermute only.
A program may use at most 64 MiB of HBM per device.

v0:
```python
import jax
import jax.numpy as jnp
from jax import lax
from jax.sharding import PartitionSpec as P

LEARN_RATE = 0.02
EPSILON = 1e-06
CONTRACT_LAST = (((1,), (1,)), ((), ()))
CONTRACT_FIRST = (((0,), (0,)), ((), ()))


def extended(block, sides, width, periodic):
    for axis, dim in sides:
        count = lax.axis_size(axis)
        forward = [(i, i + 1) for i in range(count - 1)]
        if periodic:
            forward.append((count - 1, 0))
        backward = [(target, source) for source, target in forward]
        low = lax.ppermute(
            lax.slice_in_dim(block, block.shape[dim] - width, None, axis=dim), axis, forward
        )
        high = lax.ppermute(lax.slice_in_dim(block, 0, width, axis=dim), axis, backward)
        block = jnp.concatenate([low, block, high], axis=dim)
    return block


def laplace_tiles(fields):
    lat_padded = extended(fields, (("tile", 1),), 1, False)
    lon_padded = extended(fields, (("cores", 2),), 1, True)
    return (
        lat_padded[:, 2:]
        + lat_padded[:, :-2]
        + lon_padded[:, :, 2:]
        + lon_padded[:, :, :-2]
        - 4.0 * fields
    )


def local(
    state, increment, diffusivity, land_sea, w_in, w_mid, w_out, obs_col, obs_lev, obs_val, obs_prec
):
    lat_dev, lon_dev, features = state.shape
    cell_count = lat_dev * lon_dev
    w_in_b, w_mid_all, w_out_b = (
        lax.all_gather(w_in.astype(jnp.bfloat16), "tile", axis=0, tiled=True),
        lax.all_gather(w_mid, "tile", axis=0, tiled=True),
        lax.all_gather(w_out.astype(jnp.bfloat16), "tile", axis=0, tiled=True),
    )
    hidden_units = w_in_b.shape[0]
    gating = (0.5 + land_sea.astype(jnp.float32)).reshape(cell_count, 1)
    current = state
    increment_now = increment
    saved = []
    for section_index in range(2):
        states_b = current.reshape(cell_count, features).astype(jnp.bfloat16)
        hidden_one = jnp.tanh(
            lax.dot_general(states_b, w_in_b, CONTRACT_LAST, preferred_element_type=jnp.float32)
        ).astype(jnp.bfloat16)
        hidden_two = jnp.tanh(
            jnp.dot(hidden_one, w_mid_all, preferred_element_type=jnp.float32)
        ).astype(jnp.bfloat16)
        output = jnp.dot(hidden_two, w_out_b, preferred_element_type=jnp.float32)
        slope_one = 1.0 - jnp.square(hidden_one.astype(jnp.float32))
        slope_two = 1.0 - jnp.square(hidden_two.astype(jnp.float32))
        tangent_b = increment_now.reshape(cell_count, features).astype(jnp.bfloat16)
        tangent_one = (
            slope_one
            * lax.dot_general(tangent_b, w_in_b, CONTRACT_LAST, preferred_element_type=jnp.float32)
        ).astype(jnp.bfloat16)
        tangent_two = (
            slope_two * jnp.dot(tangent_one, w_mid_all, preferred_element_type=jnp.float32)
        ).astype(jnp.bfloat16)
        tangent_out = jnp.dot(tangent_two, w_out_b, preferred_element_type=jnp.float32)
        paired = laplace_tiles(jnp.stack([current, increment_now]))
        current_next = current + diffusivity * paired[0] + (gating * output).reshape(state.shape)
        increment_now = (
            increment_now + diffusivity * paired[1] + (gating * tangent_out).reshape(state.shape)
        )
        saved.append((states_b, hidden_two, slope_one, slope_two))
        current = current_next
    cells = jnp.arange(cell_count, dtype=jnp.int32)
    levels = jnp.arange(features, dtype=jnp.int32)
    pick_cell = (obs_col[:, None] == cells[None, :]).astype(jnp.float32)
    pick_level = (obs_lev[:, None] == levels[None, :]).astype(jnp.float32)
    final_rows = (current + increment_now).reshape(cell_count, features)
    modelled = jnp.sum(
        jnp.dot(pick_cell, final_rows, precision=lax.Precision.HIGHEST) * pick_level, axis=1
    )
    weighted = obs_prec * (modelled - obs_val)
    adjoint = lax.dot_general(
        pick_cell, weighted[:, None] * pick_level, CONTRACT_FIRST, precision=lax.Precision.HIGHEST
    ).reshape(state.shape)
    grad_in = jnp.zeros((hidden_units, features), jnp.float32)
    grad_out = jnp.zeros((hidden_units, features), jnp.float32)
    for section_index in (1, 0):
        states_b, hidden_two, slope_one, slope_two = saved[section_index]
        source = (gating * adjoint.reshape(cell_count, features)).astype(jnp.bfloat16)
        back_two = (
            slope_two
            * lax.dot_general(source, w_out_b, CONTRACT_LAST, preferred_element_type=jnp.float32)
        ).astype(jnp.bfloat16)
        back_one = (
            slope_one
            * lax.dot_general(
                back_two, w_mid_all, CONTRACT_LAST, preferred_element_type=jnp.float32
            )
        ).astype(jnp.bfloat16)
        grad_out = grad_out + lax.dot_general(
            hidden_two, source, CONTRACT_FIRST, preferred_element_type=jnp.float32
        )
        grad_in = grad_in + lax.dot_general(
            back_one, states_b, CONTRACT_FIRST, preferred_element_type=jnp.float32
        )
        spread_term = laplace_tiles((diffusivity * adjoint)[None])[0]
        adjoint = (
            adjoint
            + spread_term
            + jnp.dot(back_one, w_in_b, preferred_element_type=jnp.float32).reshape(state.shape)
        )
    shard_rows = w_in.shape[0]
    total_in, total_out = lax.psum((grad_in, grad_out), ("tile", "cores"))
    square_sum = jnp.sum(total_in * total_in) + jnp.sum(total_out * total_out)
    start = lax.axis_index("tile") * shard_rows
    share_in = lax.dynamic_slice_in_dim(total_in, start, shard_rows, 0)
    share_out = lax.dynamic_slice_in_dim(total_out, start, shard_rows, 0)
    scale = LEARN_RATE / jnp.sqrt(square_sum / (2.0 * hidden_units * features) + EPSILON)
    return (adjoint, w_in - scale * share_in, w_out - scale * share_out)


def solution(mesh):
    return jax.shard_map(
        local,
        mesh=mesh,
        in_specs=(
            P("tile", "cores", None),
            P("tile", "cores", None),
            P("tile", "cores", None),
            P("tile", "cores"),
            P("tile", None),
            P("tile", None),
            P("tile", None),
            P(("tile", "cores")),
            P(("tile", "cores")),
            P(("tile", "cores")),
            P(("tile", "cores")),
        ),
        out_specs=(P("tile", "cores", None), P("tile", None), P("tile", None)),
        check_vma=False,
    )
```

profile of v0, /device:TPU:1, one launch (start us, length us, event | category | flops | bytes accessed | tf_op | source)
XLA Modules:
  0.0 1188.5 jit_solution(13728983786986541515)
XLA Ops:
  7.2 0.0 copy-start.12
  7.2 0.0 all-gather.5.cloned.1.call-start
  7.2 0.7 all-gather.5.cloned.1.call-update
  7.9 0.0 all-reduce.3.cloned.1.call-start
  8.0 1.0 pad_maximum_fusion
  9.0 8.8 collective-permute-start
  17.8 1.9 collective-permute-start.1
  19.7 0.8 fusion.80
  20.4 1.9 collective-permute-start.3
  22.4 4.9 collective-permute-start.2
  27.2 0.7 convert_bitcast_fusion.1
  27.9 309.8 %all-gather = bf16[256,4,256]{2,1,0:T(4,128)(2,1)S(1)} all-gather(bf16[1,4,256]{2,1,0:T(4,128)(2,1)S(1)} %convert_bitcast_fusion.1), channel_id=1, replica_groups=mesh['tile'=256,'cores'=2] {'tile'}, dimensions={0}, use_global_device_ids=true | all-gather | bytes 526336 | tf_op jit(solution)/shard_map/all_gather | solution.py:45
  337.7 0.1 reshape.150
  337.9 0.3 fusion
  338.2 301.8 %all-gather.2 = bf16[256,4,256]{2,1,0:T(4,128)(2,1)S(1)} all-gather(bf16[1,4,256]{2,1,0:T(4,128)(2,1)S(1)} %convert_bitcast_fusion), channel_id=1, replica_groups=mesh['tile'=256,'cores'=2] {'tile'}, dimensions={0}, use_global_device_ids=true | all-gather | bytes 526336 | tf_op jit(solution)/shard_map/all_gather | solution.py:47
  640.0 1.0 fusion.4
  641.0 0.1 reshape.154
  641.1 0.8 fusion.32
  641.9 2.5 reshape.152
  644.5 0.0 copy-start.2
  644.5 0.0 copy-start.6
  644.5 1.5 fusion.1
  646.0 0.2 fusion.25
  646.3 1.0 fusion.2
  647.3 2.4 fusion.24
  649.7 1.0 pad_maximum_fusion.1
  650.7 0.0 copy-start.3
  650.7 2.2 collective-permute-start.4
  653.0 3.5 collective-permute-start.5
  656.5 1.4 fusion.3
  657.9 4.4 collective-permute-start.7
  662.3 2.4 collective-permute-start.6
  664.7 1.0 fusion.6
  665.7 2.4 collective-permute-done.6
  668.1 0.1 fusion.29
  668.2 0.7 copy-done.17
  668.9 0.9 fusion.26
  669.8 2.5 fusion.23
  672.3 1.2 fusion.27
  673.5 0.7 subtract_multiply_fusion
  674.2 1.0 fusion.65
  675.2 2.7 fusion.9
  678.0 1.0 fusion.57
  679.0 2.3 collective-permute-start.8
  681.3 3.3 collective-permute-start.9
  684.6 2.2 fusion.87
  686.8 2.4 collective-permute-start.11
  689.2 4.6 collective-permute-start.10
  693.8 2.3 fusion.59
  696.1 0.2 convolution_add_fusion.3
  696.4 2.8 fusion.11
  699.2 2.7 convolution_add_fusion
  701.9 1.3 convolution_add_fusion.1
  703.2 0.0 all-reduce.3.cloned.1.call-update
  703.3 1.9 collective-permute-start.12
  705.2 3.6 collective-permute-start.13
  708.8 3.5 collective-permute-start.15
  712.4 3.3 collective-permute-start.14
  715.7 2.7 collective-permute-done.14
  718.4 0.9 fusion.14
  719.3 456.0 %all-reduce.3.cloned.1.call-done = (f32[1024,256]{1,0:T(8,128)}, f32[1024,256]{1,0:T(8,128)}) async-done(((f32[1024,256]{1,0:T(8,128)}, f32[1024,256]{1,0:T(8,128)}), (f32[1024,256]{1,0:T(8,128)}, f32[1024,256]{1,0:T(8,128)})) %all-reduce.3.cloned.1.call-update) | async-done | bytes 2097168 | tf_op jit(solution)/shard_map/psum | solution.py:121
  1175.3 2.4 multiply_reduce_fusion
  1179.1 1.3 multiply_subtract_fusion.9
  1180.4 1.3 multiply_subtract_fusion.8
  (62 shorter events, 0.2 us)
Async XLA Ops:
  7.2 330.7 %copy-start.5 = (f32[1,128,256]{2,1,0:T(8,128)S(1)}, f32[1,128,256]{2,1,0:T(8,128)}, u32[]{:S(2)}) copy-start(f32[1,128,256]{2,1,0:T(8,128)} %param.11) | copy-start | bytes 393220
  7.2 632.8 %copy-start.12 = (f32[1,128,256]{2,1,0:T(8,128)S(1)}, f32[1,128,256]{2,1,0:T(8,128)}, u32[]{:S(2)}) copy-start(f32[1,128,256]{2,1,0:T(8,128)} %param.12) | copy-start | bytes 393220
  7.2 330.6 %copy-start.19 = (f32[4,256]{1,0:T(4,128)S(1)}, f32[4,256]{1,0:T(4,128)}, u32[]{:S(2)}) copy-start(f32[4,256]{1,0:T(4,128)} %param.17) | copy-start | bytes 12292
  7.2 634.7 %all-gather.5.cloned.1.call-start = ((), (), s32[]{:S(2)}) async-start(), calls=%async_computation | async-start | bytes 2105344 | tf_op jit(solution)/shard_map/all_gather | solution.py:46
  7.9 1167.4 %all-reduce.3.cloned.1.call-start = ((), (), s32[]{:S(2)}) async-start(), calls=%async_computation.1 | async-start | bytes 4194304 | tf_op jit(solution)/shard_map/psum | solution.py:121
  9.0 632.2 %collective-permute-start = (f32[2,1,128,256]{3,2,1,0:T(8,128)S(1)}, f32[2,1,128,256]{3,2,1,0:T(8,128)S(1)}, u32[]{:S(2)}, u32[]{:S(2)}) collective-permute-start(f32[2,1,128,256]{3,2,1,0:T(8,128)S(1)} %pad_maximum_fusion), channel_id=1, source_target_pairs={{2,0},{4,2},{6,4},{8,6},{10,8},{12,10},{14,12},{16,14},{18,16},{20... | collective-permute-start | bytes 786440 | tf_op jit(solution)/shard_map/ppermute | solution.py:22
  17.8 623.4 %collective-permute-start.1 = (f32[2,1,128,256]{3,2,1,0:T(8,128)S(1)}, f32[2,1,128,256]{3,2,1,0:T(8,128)S(1)}, u32[]{:S(2)}, u32[]{:S(2)}) collective-permute-start(f32[2,1,128,256]{3,2,1,0:T(8,128)S(1)} %pad_maximum_fusion), channel_id=1, source_target_pairs={{0,2},{2,4},{4,6},{6,8},{8,10},{10,12},{12,14},{14,16},{16,18},{18... | collective-permute-start | bytes 786440 | tf_op jit(solution)/shard_map/ppermute | solution.py:19
  20.4 620.7 %collective-permute-start.3 = (f32[2,1,1,256]{3,2,1,0:T(1,128)S(1)}, f32[2,1,1,256]{3,2,1,0:T(1,128)S(1)}, u32[]{:S(2)}, u32[]{:S(2)}) collective-permute-start(f32[2,1,1,256]{3,2,1,0:T(1,128)S(1)} %get-tuple-element.8), channel_id=1, source_target_pairs={{0,1},{1,0},{2,3},{3,2},{4,5},{5,4},{6,7},{7,6},{8,9},{9,8},{10,11... | collective-permute-start | bytes 6152 | tf_op jit(solution)/shard_map/ppermute | solution.py:19
  22.4 618.8 %collective-permute-start.2 = (f32[2,1,1,256]{3,2,1,0:T(1,128)S(1)}, f32[2,1,1,256]{3,2,1,0:T(1,128)S(1)}, u32[]{:S(2)}, u32[]{:S(2)}) collective-permute-start(f32[2,1,1,256]{3,2,1,0:T(1,128)S(1)} %get-tuple-element.7), channel_id=1, source_target_pairs={{1,0},{0,1},{3,2},{2,3},{5,4},{4,5},{7,6},{6,7},{9,8},{8,9},{11,10... | collective-permute-start | bytes 6152 | tf_op jit(solution)/shard_map/ppermute | solution.py:22
  27.9 613.0 %copy-start.22 = (s32[1,128]{1,0:T(1,128)S(1)}, s32[1,128]{1,0:T(1,128)}, u32[]{:S(2)}) copy-start(s32[1,128]{1,0:T(1,128)} %param.14) | copy-start | bytes 1540
  338.2 302.8 %copy-start.10 = (bf16[128,1024]{1,0:T(8,128)(2,1)}, bf16[128,1024]{1,0:T(8,128)(2,1)S(1)}, u32[]{:S(2)}) copy-start(bf16[128,1024]{1,0:T(8,128)(2,1)S(1)} %fusion) | copy-start | bytes 786436
  644.5 1.5 copy-start.2
  644.5 1.5 copy-start.6
  644.5 1.5 copy-start.16
  646.0 3.7 copy-start
  649.7 8.1 copy-start.8
  649.7 15.0 %copy-start.11 = (bf16[128,1024]{1,0:T(8,128)(2,1)S(1)}, bf16[128,1024]{1,0:T(8,128)(2,1)}, u32[]{:S(2)}) copy-start(bf16[128,1024]{1,0:T(8,128)(2,1)} %fusion.2) | copy-start | bytes 786436
  650.7 18.2 %copy-start.3 = (f32[1,128,256]{2,1,0:T(8,128)S(1)}, f32[1,128,256]{2,1,0:T(8,128)}, u32[]{:S(2)}) copy-start(f32[1,128,256]{2,1,0:T(8,128)} %param.13) | copy-start | bytes 393220
  650.7 17.4 %collective-permute-start.4 = (f32[2,1,128,256]{3,2,1,0:T(8,128)S(1)}, f32[2,1,128,256]{3,2,1,0:T(8,128)S(1)}, u32[]{:S(2)}, u32[]{:S(2)}) collective-permute-start(f32[2,1,128,256]{3,2,1,0:T(8,128)S(1)} %pad_maximum_fusion.1), channel_id=1, source_target_pairs={{2,0},{4,2},{6,4},{8,6},{10,8},{12,10},{14,12},{16,14},{18,16},{20... | collective-permute-start | bytes 786440 | tf_op jit(solution)/shard_map/ppermute | solution.py:22
  653.0 15.1 %collective-permute-start.5 = (f32[2,1,128,256]{3,2,1,0:T(8,128)S(1)}, f32[2,1,128,256]{3,2,1,0:T(8,128)S(1)}, u32[]{:S(2)}, u32[]{:S(2)}) collective-permute-start(f32[2,1,128,256]{3,2,1,0:T(8,128)S(1)} %pad_maximum_fusion.1), channel_id=1, source_target_pairs={{0,2},{2,4},{4,6},{6,8},{8,10},{10,12},{12,14},{14,16},{16,18},{18... | collective-permute-start | bytes 786440 | tf_op jit(solution)/shard_map/ppermute | solution.py:19
  657.9 7.8 collective-permute-start.7
  662.3 5.8 collective-permute-start.6
  668.2 0.7 copy-start.17
  669.8 2.5 copy-start.20
  669.8 2.5 copy-start.21
  678.0 18.1 %copy-start.14 = (bf16[128,1024]{1,0:T(8,128)(2,1)S(1)}, bf16[128,1024]{1,0:T(8,128)(2,1)}, u32[]{:S(2)}) copy-start(bf16[128,1024]{1,0:T(8,128)(2,1)} %fusion.9) | copy-start | bytes 786436
  678.0 18.1 %copy-start.15 = (f32[128,256]{1,0:T(8,128)S(1)}, f32[128,256]{1,0:T(8,128)}, u32[]{:S(2)}) copy-start(f32[128,256]{1,0:T(8,128)} %fusion.65) | copy-start | bytes 393220
  679.0 17.0 %collective-permute-start.8 = (f32[1,1,128,256]{3,2,1,0:T(8,128)S(1)}, f32[1,1,128,256]{3,2,1,0:T(8,128)S(1)}, u32[]{:S(2)}, u32[]{:S(2)}) collective-permute-start(f32[1,1,128,256]{3,2,1,0:T(8,128)S(1)} %fusion.57), channel_id=1, source_target_pairs={{2,0},{4,2},{6,4},{8,6},{10,8},{12,10},{14,12},{16,14},{18,16},{20... | collective-permute-start | bytes 393224 | tf_op jit(solution)/shard_map/ppermute | solution.py:22
  681.3 14.8 %collective-permute-start.9 = (f32[1,1,128,256]{3,2,1,0:T(8,128)S(1)}, f32[1,1,128,256]{3,2,1,0:T(8,128)S(1)}, u32[]{:S(2)}, u32[]{:S(2)}) collective-permute-start(f32[1,1,128,256]{3,2,1,0:T(8,128)S(1)} %fusion.57), channel_id=1, source_target_pairs={{0,2},{2,4},{4,6},{6,8},{8,10},{10,12},{12,14},{14,16},{16,18},{18... | collective-permute-start | bytes 393224 | tf_op jit(solution)/shard_map/ppermute | solution.py:19
  686.8 9.2 collective-permute-start.11
  689.2 6.8 collective-permute-start.10
  696.3 2.8 copy-start.1
  699.2 2.7 copy-start.7
  699.2 2.7 copy-start.9
  699.2 2.7 copy-start.13
  701.8 1.4 copy-start.4
  703.2 475.9 %copy-start.18 = (f32[4,256]{1,0:T(4,128)S(1)}, f32[4,256]{1,0:T(4,128)}, u32[]{:S(2)}) copy-start(f32[4,256]{1,0:T(4,128)} %param.15) | copy-start | bytes 12292
  703.3 15.2 %collective-permute-start.12 = (f32[1,1,128,256]{3,2,1,0:T(8,128)S(1)}, f32[1,1,128,256]{3,2,1,0:T(8,128)S(1)}, u32[]{:S(2)}, u32[]{:S(2)}) collective-permute-start(f32[1,1,128,256]{3,2,1,0:T(8,128)S(1)} %fusion.56), channel_id=1, source_target_pairs={{2,0},{4,2},{6,4},{8,6},{10,8},{12,10},{14,12},{16,14},{18,16},{20... | collective-permute-start | bytes 393224 | tf_op jit(solution)/shard_map/ppermute | solution.py:22
  705.2 13.2 %collective-permute-start.13 = (f32[1,1,128,256]{3,2,1,0:T(8,128)S(1)}, f32[1,1,128,256]{3,2,1,0:T(8,128)S(1)}, u32[]{:S(2)}, u32[]{:S(2)}) collective-permute-start(f32[1,1,128,256]{3,2,1,0:T(8,128)S(1)} %fusion.56), channel_id=1, source_target_pairs={{0,2},{2,4},{4,6},{6,8},{8,10},{10,12},{12,14},{14,16},{16,18},{18... | collective-permute-start | bytes 393224 | tf_op jit(solution)/shard_map/ppermute | solution.py:19
  708.8 6.8 collective-permute-start.15
  712.4 6.0 collective-permute-start.14
Sparse Core Ops, SparseCore 0:
  10.2 418.2 all-gather.4
  703.3 471.9 all-reduce.2
where the time goes:
time: 1190 us
  blocking collectives  612 us (51%)
  waiting for transfers between devices  462 us (39%)
  starting transfers between devices  54.9 us (5%)
  matrix products  29.7 us (2%)
  between operations  15.9 us (1%)
    psum x1, waiting for transfers between devices, local(): total_in, total_out = lax.psum((grad_in, grad_out), ('tile', 'cores'))  456 us
    all_gather x1, blocking collectives, local(): lax.all_gather(w_in.astype(jnp.bfloat16), 'tile', axis=0, tiled=True)  310 us
    all_gather x1, blocking collectives, local(): lax.all_gather(w_out.astype(jnp.bfloat16), 'tile', axis=0, tiled=True)  302 us
    ppermute x8, starting transfers between devices, extended(): lax.ppermute(lax.slice_in_dim(block, 0, width, axis=dim), axis, backward)  30.3 us
    ppermute x8, starting transfers between devices, extended(): lax.ppermute(lax.slice_in_dim(block, block.shape[dim] - width, None, axis...  24.5 us
  transfers between devices with their start and end apart: 18, of which 3 were waited for; matrix products, arithmetic and copies ran while one was open for 1% of the time, Pallas kernels for 0%

commit v1 on v0

v1 whole, which is shorter than its diff:
```python
import jax
import jax.numpy as jnp
from jax import lax
from jax.sharding import Mesh
from jax.sharding import PartitionSpec as P

LEARN_RATE = 0.02
EPSILON = 1e-06
CONTRACT_LAST = (((1,), (1,)), ((), ()))
CONTRACT_FIRST = (((0,), (0,)), ((), ()))
FINE_AXES = ("x_lo", "y", "z", "core", "x_hi")
FINE_SIZES = (2, 4, 16, 2, 2)
TILE = ("x_lo", "y", "z", "core")


def spread(block, axis):
    count = lax.axis_size(axis)
    return lax.all_to_all(jnp.broadcast_to(block[None], (count,) + block.shape), axis, 0, 0)


def gather_weights(w_in, w_mid, w_out):
    rows = jnp.concatenate(
        [w_in.astype(jnp.bfloat16), w_mid, w_out.astype(jnp.bfloat16)], axis=1
    )
    rows = lax.all_gather(rows, "core", axis=0, tiled=True)
    width = rows.shape[1] // 2
    half = lax.dynamic_slice_in_dim(rows, lax.axis_index("core") * width, width, 1)
    half = spread(half, "z").reshape(-1, width)
    half = spread(half, ("x_lo", "y")).reshape(-1, width)
    both = spread(half, "core")
    features = w_in.shape[1]
    w_in_all = both[0, :, :features]
    w_mid_all = jnp.concatenate([both[0, :, features:], both[1, :, :-features]], axis=1)
    return w_in_all, w_mid_all, both[1, :, -features:]


def halo(field):
    count = 1
    for axis in TILE:
        count *= lax.axis_size(axis)
    pairs = []
    for row in range(1, count - 1, 2):
        pairs += [(row, row + 1), (row + 1, row)]
    far = lax.ppermute(field, TILE, pairs)
    edges = jnp.concatenate([field[:, :1], field[:, -1:]], axis=1)
    edges = lax.ppermute(edges, "x_hi", [(0, 1), (1, 0)])
    near = lax.ppermute(field, "core", [(0, 1), (1, 0)])
    east = jnp.concatenate([field[:, 1:], edges[:, :1]], axis=1)
    west = jnp.concatenate([edges[:, 1:], field[:, :-1]], axis=1)
    return far + near + east + west


def reduce_gradients(grad_in, grad_out):
    rows, features = grad_in.shape
    part = features // 2
    grads = jnp.stack([grad_in, grad_out]).reshape(2, rows, 2, part)
    me = lax.axis_index("core")
    mine = lax.dynamic_index_in_dim(grads, me, 2, keepdims=False)
    other = lax.dynamic_index_in_dim(grads, 1 - me, 2, keepdims=False)
    got = lax.ppermute(other.astype(jnp.bfloat16), "core", [(0, 1), (1, 0)])
    total = mine + got.astype(jnp.float32)
    peers = lax.axis_size(("x_hi", "x_lo", "y"))
    total = total.reshape(peers, rows * 2 // peers, part).astype(jnp.bfloat16)
    total = lax.all_to_all(total, ("x_hi", "x_lo", "y"), 0, 0)
    total = jnp.sum(total.astype(jnp.float32), axis=0)
    depth = lax.axis_size("z")
    total = total.reshape(depth, 1, -1, part)
    total = jnp.broadcast_to(total, (depth, 2) + total.shape[2:])
    total = lax.all_to_all(
        total.reshape((2 * depth,) + total.shape[2:]), ("z", "x_hi"), 0, 0
    ).reshape(total.shape)
    total = jnp.sum(total, axis=0)
    both = lax.all_gather(total, "core", axis=2, tiled=True)
    square = jnp.broadcast_to(jnp.sum(both * both), (1, 128))
    square = jnp.sum(spread(square, "z"), axis=0)
    square = jnp.sum(spread(square, ("x_lo", "y")), axis=0)[0, 0]
    shard = both.shape[1] // 2
    own = lax.dynamic_slice_in_dim(both, me * shard, shard, 1)
    return own[0], own[1], square


def local(
    state, increment, diffusivity, land_sea, w_in, w_mid, w_out, obs_col, obs_lev, obs_val, obs_prec
):
    _, cells, features = state.shape
    current, increment_now, diffusivity = state[0], increment[0], diffusivity[0]
    pair_sum = halo(jnp.stack([current, increment_now]))
    w_in_b, w_mid_all, w_out_b = gather_weights(w_in, w_mid, w_out)
    hidden_units = w_in_b.shape[0]
    gating = (0.5 + land_sea.astype(jnp.float32)).reshape(cells, 1)
    saved = []

    def network(current, increment_now):
        states_b = current.astype(jnp.bfloat16)
        stacked = jnp.concatenate([states_b, increment_now.astype(jnp.bfloat16)])
        one = lax.dot_general(stacked, w_in_b, CONTRACT_LAST, preferred_element_type=jnp.float32)
        hidden_one = jnp.tanh(one[:cells]).astype(jnp.bfloat16)
        slope_one = 1.0 - jnp.square(hidden_one.astype(jnp.float32))
        tangent_one = (slope_one * one[cells:]).astype(jnp.bfloat16)
        two = jnp.dot(
            jnp.concatenate([hidden_one, tangent_one]),
            w_mid_all,
            preferred_element_type=jnp.float32,
        )
        hidden_two = jnp.tanh(two[:cells]).astype(jnp.bfloat16)
        slope_two = 1.0 - jnp.square(hidden_two.astype(jnp.float32))
        tangent_two = (slope_two * two[cells:]).astype(jnp.bfloat16)
        out = jnp.dot(
            jnp.concatenate([hidden_two, tangent_two]),
            w_out_b,
            preferred_element_type=jnp.float32,
        )
        saved.append((states_b, hidden_two, slope_one, slope_two))
        return gating * out[:cells], gating * out[cells:]

    tend, tangent = network(current, increment_now)
    current = current + diffusivity * (pair_sum[0] - 4.0 * current) + tend
    increment_now = increment_now + diffusivity * (pair_sum[1] - 4.0 * increment_now) + tangent
    final = current + increment_now
    final_sum = halo(final[None])[0]
    tend, tangent = network(current, increment_now)
    final = final + diffusivity * (final_sum - 4.0 * final) + (tend + tangent)

    cell_ids = jnp.arange(cells, dtype=jnp.int32)
    level_ids = jnp.arange(features, dtype=jnp.int32)
    pick_cell = (obs_col[:, None] == cell_ids[None, :]).astype(jnp.float32)
    pick_level = (obs_lev[:, None] == level_ids[None, :]).astype(jnp.float32)
    modelled = jnp.sum(
        jnp.dot(pick_cell, final, precision=lax.Precision.HIGHEST) * pick_level, axis=1
    )
    weighted = obs_prec * (modelled - obs_val)
    adjoint = lax.dot_general(
        pick_cell, weighted[:, None] * pick_level, CONTRACT_FIRST, precision=lax.Precision.HIGHEST
    )
    grad_in = jnp.zeros((hidden_units, features), jnp.float32)
    grad_out = jnp.zeros((hidden_units, features), jnp.float32)
    for section_index in (1, 0):
        states_b, hidden_two, slope_one, slope_two = saved[section_index]
        spreading = diffusivity * adjoint
        spread_sum = halo(spreading[None])[0]
        source = (gating * adjoint).astype(jnp.bfloat16)
        back_two = (
            slope_two
            * lax.dot_general(source, w_out_b, CONTRACT_LAST, preferred_element_type=jnp.float32)
        ).astype(jnp.bfloat16)
        back_one = (
            slope_one
            * lax.dot_general(
                back_two, w_mid_all, CONTRACT_LAST, preferred_element_type=jnp.float32
            )
        ).astype(jnp.bfloat16)
        grad_out = grad_out + lax.dot_general(
            hidden_two, source, CONTRACT_FIRST, preferred_element_type=jnp.float32
        )
        grad_in = grad_in + lax.dot_general(
            back_one, states_b, CONTRACT_FIRST, preferred_element_type=jnp.float32
        )
        adjoint = (
            adjoint
            + (spread_sum - 4.0 * spreading)
            + jnp.dot(back_one, w_in_b, preferred_element_type=jnp.float32)
        )
    share_in, share_out, square_sum = reduce_gradients(grad_in, grad_out)
    scale = LEARN_RATE / jnp.sqrt(square_sum / (2.0 * hidden_units * features) + EPSILON)
    return (adjoint[None], w_in - scale * share_in, w_out - scale * share_out)


def solution(mesh):
    fine = Mesh(mesh.devices.reshape(FINE_SIZES), FINE_AXES)
    everywhere = TILE + ("x_hi",)
    return jax.shard_map(
        local,
        mesh=fine,
        in_specs=(
            P(TILE, "x_hi", None),
            P(TILE, "x_hi", None),
            P(TILE, "x_hi", None),
            P(TILE, "x_hi"),
            P(TILE, None),
            P(TILE, None),
            P(TILE, None),
            P(everywhere),
            P(everywhere),
            P(everywhere),
            P(everywhere),
        ),
        out_specs=(P(TILE, "x_hi", None), P(TILE, None), P(TILE, None)),
        check_vma=False,
    )
```

time: 1190 us -> 207 us (0.17)
  blocking collectives: 612 us -> 24.6 us
  waiting for transfers between devices: 462 us -> 45.5 us
  starting transfers between devices: 54.9 us -> 83.2 us
  between operations: 15.9 us -> 1.43 us
    all_gather x2, blocking collectives: 612 us -> 13.8 us  [the longest x1 8.36 us: gather_weights(): rows = lax.all_gather(rows, 'core', axis=0, tiled=True)]
    psum x1 -> x0, waiting for transfers between devices: 456 us -> none  [local(): total_in, total_out = lax.psum((grad_in, grad_out), ('tile', 'cores'))]
    all_to_all x0 -> x6, waiting for transfers between devices: none -> 39.1 us  [the longest x4 24.5 us: spread(): lax.all_to_all(jnp.broadcast_to(block[None], (count,) + block.shape), axi...]
    all_to_all x0 -> x6, starting transfers between devices: none -> 35.8 us  [the longest x4 22.7 us: spread(): lax.all_to_all(jnp.broadcast_to(block[None], (count,) + block.shape), axi...]
    ppermute x16 -> x13, starting transfers between devices: 54.8 us -> 47.4 us  [the longest x4 19.6 us: halo(): far = lax.ppermute(field, TILE, pairs)]
  transfers between devices with their start and end apart: 18 -> 19, of which waited for: 3 -> 8; matrix products, arithmetic and copies ran while one was open for 1% -> 11% of each run, Pallas kernels for 0% -> 0%
where the time goes in v1:
time: 207 us; the launch traced here: 206 us
  starting transfers between devices  83.2 us (40%)
  waiting for transfers between devices  45.5 us (22%)
  blocking collectives  24.6 us (12%)
  matrix products  22.5 us (11%)
  other arithmetic  15.2 us (7%)
  local copies, waits for them, and re-layouts  13.2 us (6%)
    all_to_all x4, waiting for transfers between devices, spread(): lax.all_to_all(jnp.broadcast_to(block[None], (count,) + block.shape), axi...  24.5 us
    all_to_all x4, starting transfers between devices, spread(): lax.all_to_all(jnp.broadcast_to(block[None], (count,) + block.shape), axi...  22.7 us
    ppermute x4, starting transfers between devices, halo(): far = lax.ppermute(field, TILE, pairs)  19.6 us
    ppermute x4, starting transfers between devices, halo(): edges = lax.ppermute(edges, 'x_hi', [(0, 1), (1, 0)])  17.5 us
    all_to_all x1, blocking collectives, spread(): lax.all_to_all(jnp.broadcast_to(block[None], (count,) + block.shape), axi...  10.8 us
    all_to_all x1, waiting for transfers between devices, reduce_gradients(): lax.all_to_all(total.reshape((2 * depth,) + total.shape[2:]), ('z', 'x_hi...  8.85 us
    all_gather x1, blocking collectives, gather_weights(): rows = lax.all_gather(rows, 'core', axis=0, tiled=True)  8.36 us
    ppermute x4, starting transfers between devices, halo(): near = lax.ppermute(field, 'core', [(0, 1), (1, 0)])  7.68 us
  transfers between devices with their start and end apart: 19, of which 8 were waited for; matrix products, arithmetic and copies ran while one was open for 11% of the time, Pallas kernels for 0%

profile of v1, /device:TPU:1, one launch (start us, length us, event | category | flops | bytes accessed | tf_op | source)
XLA Modules:
  0.0 205.6 jit_solution(17354390328537236878)
XLA Ops:
  0.6 0.7 convert_element_type.99
  1.4 0.7 convert_element_type.98
  2.1 0.7 maximum_bitcast_fusion
  2.8 8.4 %all-gather = bf16[2,4,1536]{2,1,0:T(4,128)(2,1)S(1)} all-gather(bf16[1,4,1536]{2,1,0:T(4,128)(2,1)S(1)} %maximum_bitcast_fusion), channel_id=1, replica_groups=mesh['x_lo'=2,'y'=4,'z'=16,'core'=2,'x_hi'=2] {'core'}, dimensions={0}, use_global_device_ids=true | all-gather | bytes 36864 | tf_op jit(solution)/shard_map/all_gather | solution.py:25
  11.2 0.7 broadcast_in_dim.24
  11.8 9.5 %all-to-all-start = ((bf16[16,8,768]{2,1,0:T(8,128)(2,1)}), bf16[16,8,768]{2,1,0:T(8,128)(2,1)S(1)}, u32[]{:S(2)}, u32[]{:S(2)}) async-start(bf16[16,8,768]{2,1,0:T(8,128)(2,1)} %broadcast_in_dim.24), calls=%async_computation | async-start | bytes 393216 | tf_op jit(solution)/shard_map/all_to_all | solution.py:18
  21.4 0.9 constant_dynamic-update-slice_fusion.1
  22.3 12.0 %all-to-all-done = bf16[16,8,768]{2,1,0:T(8,128)(2,1)S(1)} async-done(((bf16[16,8,768]{2,1,0:T(8,128)(2,1)}), bf16[16,8,768]{2,1,0:T(8,128)(2,1)S(1)}, u32[]{:S(2)}, u32[]{:S(2)}) %all-to-all-start) | async-done | bytes 196640 | tf_op jit(solution)/shard_map/all_to_all | solution.py:18
  34.3 1.3 broadcast_in_dim.52
  35.6 5.1 %all-to-all-start.1 = ((bf16[8,128,768]{2,1,0:T(8,128)(2,1)}), bf16[8,128,768]{2,1,0:T(8,128)(2,1)S(1)}, u32[]{:S(2)}, u32[]{:S(2)}) async-start(bf16[8,128,768]{2,1,0:T(8,128)(2,1)} %broadcast_in_dim.52), calls=%async_computation.1 | async-start | bytes 3145728 | tf_op jit(solution)/shard_map/all_to_all | solution.py:18
  40.8 7.6 %collective-permute-start = (f32[2,128,256]{2,1,0:T(8,128)S(1)}, f32[2,128,256]{2,1,0:T(8,128)S(1)}, u32[]{:S(2)}, u32[]{:S(2)}) collective-permute-start(f32[2,128,256]{2,1,0:T(8,128)S(1)} %get-tuple-element.32), channel_id=1, source_target_pairs={{2,4},{4,2},{6,8},{8,6},{10,12},{12,10},{14,16},{16,14},{18,20},{2... | collective-permute-start | bytes 786440 | tf_op jit(solution)/shard_map/ppermute | solution.py:44
  48.4 1.9 collective-permute-start.1
  50.4 4.4 %collective-permute-start.2 = (f32[2,2,256]{2,1,0:T(2,128)S(1)}, f32[2,2,256]{2,1,0:T(2,128)S(1)}, u32[]{:S(2)}, u32[]{:S(2)}) collective-permute-start(f32[2,2,256]{2,1,0:T(2,128)S(1)} %pad_maximum_fusion.1), channel_id=1, source_target_pairs={{0,1},{1,0},{2,3},{3,2},{4,5},{5,4},{6,7},{7,6},{8,9},{9,8},{10,11... | collective-permute-start | bytes 12296 | tf_op jit(solution)/shard_map/ppermute | solution.py:46
  54.8 3.3 %collective-permute-done.2 = f32[2,2,256]{2,1,0:T(2,128)S(1)} collective-permute-done((f32[2,2,256]{2,1,0:T(2,128)S(1)}, f32[2,2,256]{2,1,0:T(2,128)S(1)}, u32[]{:S(2)}, u32[]{:S(2)}) %collective-permute-start.2) | collective-permute-done | bytes 4128 | tf_op jit(solution)/shard_map/ppermute | solution.py:46
  58.5 10.8 %all_to_all.35 = bf16[2,1024,768]{2,1,0:T(8,128)(2,1)S(1)} all-to-all(bf16[2,1024,768]{2,1,0:T(8,128)(2,1)S(1)} %broadcast_in_dim.54), channel_id=1, replica_groups=mesh['x_lo'=2,'y'=4,'z'=16,'core'=2,'x_hi'=2] {'core'}, dimensions={0} | all-to-all | bytes 6291456 | tf_op jit(solution)/shard_map/all_to_all | solution.py:18
  69.3 0.3 fusion.38
  70.0 0.7 fusion.21
  71.6 5.7 %collective-permute-start.3 = (f32[1,128,256]{2,1,0:T(8,128)S(1)}, f32[1,128,256]{2,1,0:T(8,128)S(1)}, u32[]{:S(2)}, u32[]{:S(2)}) collective-permute-start(f32[1,128,256]{2,1,0:T(8,128)S(1)} %bitcast.152), channel_id=1, source_target_pairs={{2,4},{4,2},{6,8},{8,6},{10,12},{12,10},{14,16},{16,14},{18,20},{2... | collective-permute-start | bytes 393224 | tf_op jit(solution)/shard_map/ppermute | solution.py:44
  77.3 1.9 collective-permute-start.4
  79.7 0.7 fusion.29
  80.6 4.3 %collective-permute-start.5 = (f32[1,2,256]{2,1,0:T(2,128)S(1)}, f32[1,2,256]{2,1,0:T(2,128)S(1)}, u32[]{:S(2)}, u32[]{:S(2)}) collective-permute-start(f32[1,2,256]{2,1,0:T(2,128)S(1)} %pad_maximum_fusion.2), channel_id=1, source_target_pairs={{0,1},{1,0},{2,3},{3,2},{4,5},{5,4},{6,7},{7,6},{8,9},{9,8},{10,11... | collective-permute-start | bytes 6152 | tf_op jit(solution)/shard_map/ppermute | solution.py:46
  85.3 1.2 collective-permute-done.5
  86.5 0.4 fusion.5
  87.3 3.2 %collective-permute-start.6 = (f32[1,128,256]{2,1,0:T(8,128)S(1)}, f32[1,128,256]{2,1,0:T(8,128)}, u32[]{:S(2)}, u32[]{:S(2)}) collective-permute-start(f32[1,128,256]{2,1,0:T(8,128)S(1)} %fusion.86), channel_id=1, source_target_pairs={{2,4},{4,2},{6,8},{8,6},{10,12},{12,10},{14,16},{16,14},{18,20},{2... | collective-permute-start | bytes 393224 | tf_op jit(solution)/shard_map/ppermute | solution.py:44
  90.5 1.9 collective-permute-start.7
  92.4 1.4 fusion.108
  93.8 4.3 %collective-permute-start.8 = (f32[1,2,256]{2,1,0:T(2,128)S(1)}, f32[1,2,256]{2,1,0:T(2,128)S(1)}, u32[]{:S(2)}, u32[]{:S(2)}) collective-permute-start(f32[1,2,256]{2,1,0:T(2,128)S(1)} %pad_maximum_fusion.3), channel_id=1, source_target_pairs={{0,1},{1,0},{2,3},{3,2},{4,5},{5,4},{6,7},{7,6},{8,9},{9,8},{10,11... | collective-permute-start | bytes 6152 | tf_op jit(solution)/shard_map/ppermute | solution.py:46
  98.1 3.4 %fusion.1 = bf16[128,1024]{1,0:T(8,128)(2,1)} fusion(bf16[128,1024]{1,0:T(8,128)(2,1)} %copy-done.3, bf16[128,1024]{1,0:T(8,128)(2,1)} %copy-done.12, bf16[2,1024,768]{2,1,0:T(8,128)(2,1)S(1)} %all_to_all.35, f32[128,256]{1,0:T(8,128)S(1)} %fusion.82, f32[128]{0:T(128)S(1)} %add_bitcast_fusion, bf16[1024,512]{1,0:T(8,128)(2,1)} %copy-done.2, ...), kind=kOutput, calls=%fused_computation.12 | convolution fusion | flops 341114880 | bytes 3539456 | tf_op jit(solution)/shard_map/dot_general | solution.py:148
  101.5 2.3 %fusion.128 = f32[1024,256]{0,1:T(8,128)} fusion(bf16[128,1024]{1,0:T(8,128)(2,1)} %fusion.1, bf16[128,256]{1,0:T(8,128)(2,1)} %copy-done.7), kind=kOutput, calls=%fused_computation.183 | convolution fusion | flops 67108864 | bytes 1376256 | tf_op jit(solution)/shard_map/dot_general | solution.py:155
  103.8 1.3 convolution_add_fusion.3
  105.2 3.4 %fusion.3 = bf16[128,1024]{1,0:T(8,128)(2,1)} fusion(bf16[128,1024]{1,0:T(8,128)(2,1)} %copy-done.4, bf16[128,1024]{1,0:T(8,128)(2,1)} %copy-done.11, bf16[2,1024,768]{2,1,0:T(8,128)(2,1)S(1)} %all_to_all.35, f32[128,256]{1,0:T(8,128)S(1)} %convolution_add_fusion.3, f32[128]{0:T(128)S(1)} %add_bitcast_fusion, bf16[1024,512]{1,0:T(8,128)(2,1)} %copy-done.2, ...), kind=kOutput, calls=%fused_computation.14 | convolution fusion | flops 341114880 | bytes 3539456 | tf_op jit(solution)/shard_map/dot_general | solution.py:148
  108.6 2.6 %convolution_add_fusion.1 = f32[1024,256]{0,1:T(8,128)} fusion(f32[1024,256]{0,1:T(8,128)} %fusion.128, bf16[128,1024]{1,0:T(8,128)(2,1)} %fusion.3, bf16[128,256]{1,0:T(8,128)(2,1)S(1)} %copy-done.6), kind=kOutput, calls=%fused_computation.6 | convolution fusion | flops 67371008 | bytes 2424832 | tf_op jit(solution)/shard_map/dot_general | solution.py:155
  111.2 2.6 %copy.20 = f32[1,1024,2,128]{3,1,0,2:T(8,128)} copy(f32[1,1024,2,128]{1,3,2,0:T(8,128)} %bitcast.149) | data formatting | bytes 2097152 | tf_op jit(solution)/shard_map/stack | solution.py:56
  113.8 2.7 %convolution_add_fusion = f32[1024,256]{0,1:T(8,128)} fusion(f32[1024,256]{0,1:T(8,128)} %fusion.108, bf16[128,1024]{1,0:T(8,128)(2,1)} %copy-done.4, f32[128,256]{1,0:T(8,128)S(1)} %convolution_add_fusion.3, f32[128]{0:T(128)S(1)} %add_bitcast_fusion), kind=kOutput, calls=%fused_computation.5 | convolution fusion | flops 67436544 | bytes 2490880 | tf_op jit(solution)/shard_map/dot_general | solution.py:152
  116.5 2.5 %copy.21 = f32[1,1024,2,128]{3,1,0,2:T(8,128)} copy(f32[1,1024,2,128]{1,3,2,0:T(8,128)} %bitcast.150) | data formatting | bytes 2097152 | tf_op jit(solution)/shard_map/stack | solution.py:56
  119.0 2.1 %fusion.12 = bf16[2,1024,128]{2,1,0:T(8,128)(2,1)} fusion(s32[]{:T(128)S(6)} %select_n.15, f32[1,1024,2,128]{3,1,0,2:T(8,128)} %copy.21, f32[1,1024,2,128]{3,1,0,2:T(8,128)} %copy.20), kind=kLoop, calls=%fused_computation.29 | loop fusion | flops 262144 | bytes 2621444 | tf_op jit(solution)/shard_map/convert_element_type | solution.py:60
  121.1 2.7 %collective-permute-start.12 = (bf16[2,1024,128]{2,1,0:T(8,128)(2,1)}, bf16[2,1024,128]{2,1,0:T(8,128)(2,1)}, u32[]{:S(2)}, u32[]{:S(2)}) collective-permute-start(bf16[2,1024,128]{2,1,0:T(8,128)(2,1)} %fusion.12), channel_id=1, source_target_pairs={{0,2},{2,0},{1,3},{3,1},{4,6},{6,4},{5,7},{7,5},{8,10},{10,8},{9,1... | collective-permute-start | bytes 1572872 | tf_op jit(solution)/shard_map/ppermute | solution.py:60
  123.7 1.9 collective-permute-done.12
  125.6 2.3 %fusion.11 = bf16[2,1024,128]{2,1,0:T(8,128)(2,1)} fusion(s32[]{:T(128)S(6)} %select_n.14, f32[1,1024,2,128]{3,1,0,2:T(8,128)} %copy.20, f32[1,1024,2,128]{3,1,0,2:T(8,128)} %copy.21, bf16[2,1024,128]{2,1,0:T(8,128)(2,1)} %collective-permute-done.12), kind=kLoop, calls=%fused_computation.25 | loop fusion | flops 1048576 | bytes 3145732 | tf_op jit(solution)/shard_map/convert_element_type | solution.py:63
  127.9 6.3 %all-to-all-start.3 = ((bf16[16,128,128]{2,1,0:T(8,128)(2,1)}), bf16[16,128,128]{2,1,0:T(8,128)(2,1)}, u32[]{:S(2)}, u32[]{:S(2)}) async-start(bf16[16,128,128]{2,1,0:T(8,128)(2,1)} %bitcast.155), calls=%async_computation.3 | async-start | bytes 1048576 | tf_op jit(solution)/shard_map/all_to_all | solution.py:64
  134.2 3.1 %collective-permute-start.9 = (f32[1,128,256]{2,1,0:T(8,128)S(1)}, f32[1,128,256]{2,1,0:T(8,128)}, u32[]{:S(2)}, u32[]{:S(2)}) collective-permute-start(f32[1,128,256]{2,1,0:T(8,128)S(1)} %fusion.87), channel_id=1, source_target_pairs={{2,4},{4,2},{6,8},{8,6},{10,12},{12,10},{14,16},{16,14},{18,20},{2... | collective-permute-start | bytes 393224 | tf_op jit(solution)/shard_map/ppermute | solution.py:44
  137.3 1.9 collective-permute-start.10
  139.2 5.7 %all-to-all-done.3 = bf16[16,128,128]{2,1,0:T(8,128)(2,1)} async-done(((bf16[16,128,128]{2,1,0:T(8,128)(2,1)}), bf16[16,128,128]{2,1,0:T(8,128)(2,1)}, u32[]{:S(2)}, u32[]{:S(2)}) %all-to-all-start.3) | async-done | bytes 524320 | tf_op jit(solution)/shard_map/all_to_all | solution.py:64
  144.9 1.1 convert_reduce_fusion
  146.0 0.7 broadcast_in_dim.60
  146.7 6.8 %all-to-all-start.4 = ((f32[32,8,128]{2,1,0:T(8,128)}), f32[32,8,128]{2,1,0:T(8,128)}, u32[]{:S(2)}, u32[]{:S(2)}) async-start(f32[32,8,128]{2,1,0:T(8,128)} %bitcast.157), calls=%async_computation.4 | async-start | bytes 262144 | tf_op jit(solution)/shard_map/all_to_all | solution.py:69
  153.5 0.6 pad_maximum_fusion.4
  154.0 4.6 %collective-permute-start.11 = (f32[1,2,256]{2,1,0:T(2,128)}, f32[1,2,256]{2,1,0:T(2,128)}, u32[]{:S(2)}, u32[]{:S(2)}) collective-permute-start(f32[1,2,256]{2,1,0:T(2,128)} %pad_maximum_fusion.4), channel_id=1, source_target_pairs={{0,1},{1,0},{2,3},{3,2},{4,5},{5,4},{6,7},{7,6},{8,9},{9,8},{10,11... | collective-permute-start | bytes 6152 | tf_op jit(solution)/shard_map/ppermute | solution.py:46
  158.6 0.7 fusion.118
  159.3 8.8 %all-to-all-done.4 = f32[32,8,128]{2,1,0:T(8,128)} async-done(((f32[32,8,128]{2,1,0:T(8,128)}), f32[32,8,128]{2,1,0:T(8,128)}, u32[]{:S(2)}, u32[]{:S(2)}) %all-to-all-start.4) | async-done | bytes 131104 | tf_op jit(solution)/shard_map/all_to_all | solution.py:69
  168.2 1.5 reduce_sum.58
  169.7 5.4 %all_gather.7 = f32[2,8,256]{2,1,0:T(8,128)S(1)} all-gather(f32[2,8,128]{2,1,0:T(8,128)} %reduce_sum.58), channel_id=1, replica_groups=mesh['x_lo'=2,'y'=4,'z'=16,'core'=2,'x_hi'=2] {'core'}, dimensions={2}, use_global_device_ids=true | all-gather | bytes 24576 | tf_op jit(solution)/shard_map/all_gather | solution.py:73
  175.1 0.6 multiply_reduce_fusion
  175.7 1.2 broadcast_in_dim_broadcast_in_dim_broadcast_in_dim.3
  177.0 4.1 %all-to-all-start.5 = ((f32[16,1,128]{2,1,0:T(1,128)}), f32[16,1,128]{2,1,0:T(1,128)}, u32[]{:S(2)}, u32[]{:S(2)}) async-start(f32[16,1,128]{2,1,0:T(1,128)} %broadcast_in_dim_broadcast_in_dim_broadcast_in_dim.3), calls=%async_computation.5 | async-start | bytes 16384 | tf_op jit(solution)/shard_map/all_to_all | solution.py:18
  181.1 1.3 fusion.125
  182.5 9.7 %all-to-all-done.5 = f32[16,1,128]{2,1,0:T(1,128)} async-done(((f32[16,1,128]{2,1,0:T(1,128)}), f32[16,1,128]{2,1,0:T(1,128)}, u32[]{:S(2)}, u32[]{:S(2)}) %all-to-all-start.5) | async-done | bytes 8224 | tf_op jit(solution)/shard_map/all_to_all | solution.py:18
  192.1 1.2 reduce_sum.60
  193.4 1.2 broadcast_in_dim.61
  194.6 3.9 %all-to-all-start.6 = ((f32[8,1,128]{2,1,0:T(1,128)}), f32[8,1,128]{2,1,0:T(1,128)}, u32[]{:S(2)}, u32[]{:S(2)}) async-start(f32[8,1,128]{2,1,0:T(1,128)} %broadcast_in_dim.61), calls=%async_computation.6 | async-start | bytes 8192 | tf_op jit(solution)/shard_map/all_to_all | solution.py:18
  198.6 2.1 %fusion.4 = f32[1,128,256]{2,1,0:T(8,128)} fusion(bf16[128,1024]{1,0:T(8,128)(2,1)} %fusion.3, bf16[2,1024,768]{2,1,0:T(8,128)(2,1)S(1)} %all_to_all.35, f32[128,256]{1,0:T(8,128)S(1)} %convolution_add_fusion.3, f32[1,1,256]{2,1,0:T(1,128)} %get-tuple-element.41, f32[1,127,256]{2,1,0:T(8,128)} %get-tuple-element.21, f32[1,127,256]{2,1,0:T(8,128)} %get-tuple-element.20, ...), kind=kOutput, calls=%fused_computation.16 | convolution fusion | flops 67436544 | bytes 1703936 | tf_op jit(solution)/shard_map/dot_general | solution.py:161
  200.6 2.8 %all-to-all-done.6 = f32[8,1,128]{2,1,0:T(1,128)} async-done(((f32[8,1,128]{2,1,0:T(1,128)}), f32[8,1,128]{2,1,0:T(1,128)}, u32[]{:S(2)}, u32[]{:S(2)}) %all-to-all-start.6) | async-done | bytes 4128 | tf_op jit(solution)/shard_map/all_to_all | solution.py:18
  203.5 0.7 reduce_sum.61
  204.2 1.3 fusion.94
  (79 shorter events, 2.9 us)
Async XLA Ops:
  0.6 40.1 %copy-start.9 = (f32[1,128,256]{2,1,0:T(8,128)S(1)}, f32[1,128,256]{2,1,0:T(8,128)}, u32[]{:S(2)}) copy-start(f32[1,128,256]{2,1,0:T(8,128)} %param.12) | copy-start | bytes 393220
  11.8 22.5 %all-to-all-start = ((bf16[16,8,768]{2,1,0:T(8,128)(2,1)}), bf16[16,8,768]{2,1,0:T(8,128)(2,1)S(1)}, u32[]{:S(2)}, u32[]{:S(2)}) async-start(bf16[16,8,768]{2,1,0:T(8,128)(2,1)} %broadcast_in_dim.24), calls=%async_computation | async-start | bytes 393216 | tf_op jit(solution)/shard_map/all_to_all | solution.py:18
  22.3 46.9 %copy-start.5 = (bf16[128,256]{1,0:T(8,128)(2,1)}, bf16[128,256]{1,0:T(8,128)(2,1)S(1)}, u32[]{:S(2)}) copy-start(bf16[128,256]{1,0:T(8,128)(2,1)S(1)} %get-tuple-element.35) | copy-start | bytes 196612
  34.3 20.5 %copy-start.17 = (s32[1,128]{1,0:T(1,128)S(1)}, s32[1,128]{1,0:T(1,128)}, u32[]{:S(2)}) copy-start(s32[1,128]{1,0:T(1,128)} %param.14) | copy-start | bytes 1540
  35.6 22.6 %all-to-all-start.1 = ((bf16[8,128,768]{2,1,0:T(8,128)(2,1)}), bf16[8,128,768]{2,1,0:T(8,128)(2,1)S(1)}, u32[]{:S(2)}, u32[]{:S(2)}) async-start(bf16[8,128,768]{2,1,0:T(8,128)(2,1)} %broadcast_in_dim.52), calls=%async_computation.1 | async-start | bytes 3145728 | tf_op jit(solution)/shard_map/all_to_all | solution.py:18
  40.8 17.4 %collective-permute-start = (f32[2,128,256]{2,1,0:T(8,128)S(1)}, f32[2,128,256]{2,1,0:T(8,128)S(1)}, u32[]{:S(2)}, u32[]{:S(2)}) collective-permute-start(f32[2,128,256]{2,1,0:T(8,128)S(1)} %get-tuple-element.32), channel_id=1, source_target_pairs={{2,4},{4,2},{6,8},{8,6},{10,12},{12,10},{14,16},{16,14},{18,20},{2... | collective-permute-start | bytes 786440 | tf_op jit(solution)/shard_map/ppermute | solution.py:44
  48.4 9.7 %collective-permute-start.1 = (f32[2,128,256]{2,1,0:T(8,128)S(1)}, f32[2,128,256]{2,1,0:T(8,128)S(1)}, u32[]{:S(2)}, u32[]{:S(2)}) collective-permute-start(f32[2,128,256]{2,1,0:T(8,128)S(1)} %get-tuple-element.32), channel_id=1, source_target_pairs={{0,2},{2,0},{1,3},{3,1},{4,6},{6,4},{5,7},{7,5},{8,10},{10,8},{9,1... | collective-permute-start | bytes 786440 | tf_op jit(solution)/shard_map/ppermute | solution.py:47
  50.4 7.8 %collective-permute-start.2 = (f32[2,2,256]{2,1,0:T(2,128)S(1)}, f32[2,2,256]{2,1,0:T(2,128)S(1)}, u32[]{:S(2)}, u32[]{:S(2)}) collective-permute-start(f32[2,2,256]{2,1,0:T(2,128)S(1)} %pad_maximum_fusion.1), channel_id=1, source_target_pairs={{0,1},{1,0},{2,3},{3,2},{4,5},{5,4},{6,7},{7,6},{8,9},{9,8},{10,11... | collective-permute-start | bytes 12296 | tf_op jit(solution)/shard_map/ppermute | solution.py:46
  69.7 0.9 copy-start.11
  69.9 9.8 %copy-start.1 = (bf16[1024,512]{1,0:T(8,128)(2,1)}, bf16[1024,512]{1,0:T(8,128)(2,1)S(1)}, u32[]{:S(2)}) copy-start(bf16[1024,512]{1,0:T(8,128)(2,1)S(1)} %get-tuple-element.14) | copy-start | bytes 3145732
  69.9 9.8 %copy-start.2 = (bf16[1024,512]{1,0:T(8,128)(2,1)}, bf16[1024,512]{1,0:T(8,128)(2,1)S(1)}, u32[]{:S(2)}) copy-start(bf16[1024,512]{1,0:T(8,128)(2,1)S(1)} %get-tuple-element.15) | copy-start | bytes 3145732
  69.9 1.2 copy-start
  69.9 1.3 copy-start.8
  69.9 1.5 copy-start.10
  70.8 8.9 %copy-start.4 = (bf16[128,1024]{1,0:T(8,128)(2,1)}, bf16[128,1024]{1,0:T(8,128)(2,1)S(1)}, u32[]{:S(2)}) copy-start(bf16[128,1024]{1,0:T(8,128)(2,1)S(1)} %get-tuple-element.11) | copy-start | bytes 786436
  71.5 8.1 %copy-start.7 = (bf16[128,256]{1,0:T(8,128)(2,1)}, bf16[128,256]{1,0:T(8,128)(2,1)S(1)}, u32[]{:S(2)}) copy-start(bf16[128,256]{1,0:T(8,128)(2,1)S(1)} %get-tuple-element.4) | copy-start | bytes 196612
  71.6 14.9 %collective-permute-start.3 = (f32[1,128,256]{2,1,0:T(8,128)S(1)}, f32[1,128,256]{2,1,0:T(8,128)S(1)}, u32[]{:S(2)}, u32[]{:S(2)}) collective-permute-start(f32[1,128,256]{2,1,0:T(8,128)S(1)} %bitcast.152), channel_id=1, source_target_pairs={{2,4},{4,2},{6,8},{8,6},{10,12},{12,10},{14,16},{16,14},{18,20},{2... | collective-permute-start | bytes 393224 | tf_op jit(solution)/shard_map/ppermute | solution.py:44
  77.3 9.2 %collective-permute-start.4 = (f32[1,128,256]{2,1,0:T(8,128)S(1)}, f32[1,128,256]{2,1,0:T(8,128)S(1)}, u32[]{:S(2)}, u32[]{:S(2)}) collective-permute-start(f32[1,128,256]{2,1,0:T(8,128)S(1)} %bitcast.153), channel_id=1, source_target_pairs={{0,2},{2,0},{1,3},{3,1},{4,6},{6,4},{5,7},{7,5},{8,10},{10,8},{9,1... | collective-permute-start | bytes 393224 | tf_op jit(solution)/shard_map/ppermute | solution.py:47
  79.7 0.9 copy-start.12
  80.4 6.1 %copy-start.13 = (s32[64]{0:T(128)S(1)}, s32[64]{0:T(128)}, u32[]{:S(2)}) copy-start(s32[64]{0:T(128)} %param.19) | copy-start | bytes 772
  80.4 6.1 %copy-start.14 = (s32[64]{0:T(128)S(1)}, s32[64]{0:T(128)}, u32[]{:S(2)}) copy-start(s32[64]{0:T(128)} %param.18) | copy-start | bytes 772
  80.4 6.4 %copy-start.15 = (f32[64]{0:T(128)S(1)}, f32[64]{0:T(128)}, u32[]{:S(2)}) copy-start(f32[64]{0:T(128)} %param.21) | copy-start | bytes 772
  80.5 6.4 %copy-start.16 = (f32[64]{0:T(128)S(1)}, f32[64]{0:T(128)}, u32[]{:S(2)}) copy-start(f32[64]{0:T(128)} %param.20) | copy-start | bytes 772
  80.6 11.8 %copy-start.3 = (bf16[128,1024]{1,0:T(8,128)(2,1)}, bf16[128,1024]{1,0:T(8,128)(2,1)S(1)}, u32[]{:S(2)}) copy-start(bf16[128,1024]{1,0:T(8,128)(2,1)S(1)} %get-tuple-element.7) | copy-start | bytes 786436
  80.6 5.8 %collective-permute-start.5 = (f32[1,2,256]{2,1,0:T(2,128)S(1)}, f32[1,2,256]{2,1,0:T(2,128)S(1)}, u32[]{:S(2)}, u32[]{:S(2)}) collective-permute-start(f32[1,2,256]{2,1,0:T(2,128)S(1)} %pad_maximum_fusion.2), channel_id=1, source_target_pairs={{0,1},{1,0},{2,3},{3,2},{4,5},{5,4},{6,7},{7,6},{8,9},{9,8},{10,11... | collective-permute-start | bytes 6152 | tf_op jit(solution)/shard_map/ppermute | solution.py:46
  87.3 16.5 %collective-permute-start.6 = (f32[1,128,256]{2,1,0:T(8,128)S(1)}, f32[1,128,256]{2,1,0:T(8,128)}, u32[]{:S(2)}, u32[]{:S(2)}) collective-permute-start(f32[1,128,256]{2,1,0:T(8,128)S(1)} %fusion.86), channel_id=1, source_target_pairs={{2,4},{4,2},{6,8},{8,6},{10,12},{12,10},{14,16},{16,14},{18,20},{2... | collective-permute-start | bytes 393224 | tf_op jit(solution)/shard_map/ppermute | solution.py:44
  90.5 13.3 %collective-permute-start.7 = (f32[1,128,256]{2,1,0:T(8,128)S(1)}, f32[1,128,256]{2,1,0:T(8,128)}, u32[]{:S(2)}, u32[]{:S(2)}) collective-permute-start(f32[1,128,256]{2,1,0:T(8,128)S(1)} %fusion.86), channel_id=1, source_target_pairs={{0,2},{2,0},{1,3},{3,1},{4,6},{6,4},{5,7},{7,5},{8,10},{10,8},{9,1... | collective-permute-start | bytes 393224 | tf_op jit(solution)/shard_map/ppermute | solution.py:47
  93.8 10.0 %collective-permute-start.8 = (f32[1,2,256]{2,1,0:T(2,128)S(1)}, f32[1,2,256]{2,1,0:T(2,128)S(1)}, u32[]{:S(2)}, u32[]{:S(2)}) collective-permute-start(f32[1,2,256]{2,1,0:T(2,128)S(1)} %pad_maximum_fusion.3), channel_id=1, source_target_pairs={{0,1},{1,0},{2,3},{3,2},{4,5},{5,4},{6,7},{7,6},{8,9},{9,8},{10,11... | collective-permute-start | bytes 6152 | tf_op jit(solution)/shard_map/ppermute | solution.py:46
  105.1 3.4 %copy-start.6 = (bf16[128,256]{1,0:T(8,128)(2,1)S(1)}, bf16[128,256]{1,0:T(8,128)(2,1)}, u32[]{:S(2)}) copy-start(bf16[128,256]{1,0:T(8,128)(2,1)} %copy-done.5) | copy-start | bytes 196612
  121.1 4.5 %collective-permute-start.12 = (bf16[2,1024,128]{2,1,0:T(8,128)(2,1)}, bf16[2,1024,128]{2,1,0:T(8,128)(2,1)}, u32[]{:S(2)}, u32[]{:S(2)}) collective-permute-start(bf16[2,1024,128]{2,1,0:T(8,128)(2,1)} %fusion.12), channel_id=1, source_target_pairs={{0,2},{2,0},{1,3},{3,1},{4,6},{6,4},{5,7},{7,5},{8,10},{10,8},{9,1... | collective-permute-start | bytes 1572872 | tf_op jit(solution)/shard_map/ppermute | solution.py:60
  127.9 17.0 %all-to-all-start.3 = ((bf16[16,128,128]{2,1,0:T(8,128)(2,1)}), bf16[16,128,128]{2,1,0:T(8,128)(2,1)}, u32[]{:S(2)}, u32[]{:S(2)}) async-start(bf16[16,128,128]{2,1,0:T(8,128)(2,1)} %bitcast.155), calls=%async_computation.3 | async-start | bytes 1048576 | tf_op jit(solution)/shard_map/all_to_all | solution.py:64
  134.2 64.4 %collective-permute-start.9 = (f32[1,128,256]{2,1,0:T(8,128)S(1)}, f32[1,128,256]{2,1,0:T(8,128)}, u32[]{:S(2)}, u32[]{:S(2)}) collective-permute-start(f32[1,128,256]{2,1,0:T(8,128)S(1)} %fusion.87), channel_id=1, source_target_pairs={{2,4},{4,2},{6,8},{8,6},{10,12},{12,10},{14,16},{16,14},{18,20},{2... | collective-permute-start | bytes 393224 | tf_op jit(solution)/shard_map/ppermute | solution.py:44
  137.3 61.3 %collective-permute-start.10 = (f32[1,128,256]{2,1,0:T(8,128)S(1)}, f32[1,128,256]{2,1,0:T(8,128)}, u32[]{:S(2)}, u32[]{:S(2)}) collective-permute-start(f32[1,128,256]{2,1,0:T(8,128)S(1)} %fusion.87), channel_id=1, source_target_pairs={{0,2},{2,0},{1,3},{3,1},{4,6},{6,4},{5,7},{7,5},{8,10},{10,8},{9,1... | collective-permute-start | bytes 393224 | tf_op jit(solution)/shard_map/ppermute | solution.py:47
  146.7 21.5 %all-to-all-start.4 = ((f32[32,8,128]{2,1,0:T(8,128)}), f32[32,8,128]{2,1,0:T(8,128)}, u32[]{:S(2)}, u32[]{:S(2)}) async-start(f32[32,8,128]{2,1,0:T(8,128)} %bitcast.157), calls=%async_computation.4 | async-start | bytes 262144 | tf_op jit(solution)/shard_map/all_to_all | solution.py:69
  154.0 27.1 %collective-permute-start.11 = (f32[1,2,256]{2,1,0:T(2,128)}, f32[1,2,256]{2,1,0:T(2,128)}, u32[]{:S(2)}, u32[]{:S(2)}) collective-permute-start(f32[1,2,256]{2,1,0:T(2,128)} %pad_maximum_fusion.4), channel_id=1, source_target_pairs={{0,1},{1,0},{2,3},{3,2},{4,5},{5,4},{6,7},{7,6},{8,9},{9,8},{10,11... | collective-permute-start | bytes 6152 | tf_op jit(solution)/shard_map/ppermute | solution.py:46
  177.0 15.2 %all-to-all-start.5 = ((f32[16,1,128]{2,1,0:T(1,128)}), f32[16,1,128]{2,1,0:T(1,128)}, u32[]{:S(2)}, u32[]{:S(2)}) async-start(f32[16,1,128]{2,1,0:T(1,128)} %broadcast_in_dim_broadcast_in_dim_broadcast_in_dim.3), calls=%async_computation.5 | async-start | bytes 16384 | tf_op jit(solution)/shard_map/all_to_all | solution.py:18
  194.6 8.9 %all-to-all-start.6 = ((f32[8,1,128]{2,1,0:T(1,128)}), f32[8,1,128]{2,1,0:T(1,128)}, u32[]{:S(2)}, u32[]{:S(2)}) async-start(f32[8,1,128]{2,1,0:T(1,128)} %broadcast_in_dim.61), calls=%async_computation.6 | async-start | bytes 8192 | tf_op jit(solution)/shard_map/all_to_all | solution.py:18

commit v2 on v1

--- a/solution.py
+++ b/solution.py
@@ -1,6 +1,8 @@
 import jax
 import jax.numpy as jnp
 from jax import lax
+from jax.experimental import pallas as pl
+from jax.experimental.pallas import tpu as pltpu
 from jax.sharding import Mesh
 from jax.sharding import PartitionSpec as P
 
@@ -31,7 +33,7 @@
     features = w_in.shape[1]
     w_in_all = both[0, :, :features]
     w_mid_all = jnp.concatenate([both[0, :, features:], both[1, :, :-features]], axis=1)
-    return w_in_all, w_mid_all, both[1, :, -features:]
+    return both, w_in_all, w_mid_all, both[1, :, -features:]
 
 
 def halo(field):
@@ -50,33 +52,106 @@
     return far + near + east + west
 
 
-def reduce_gradients(grad_in, grad_out):
-    rows, features = grad_in.shape
-    part = features // 2
-    grads = jnp.stack([grad_in, grad_out]).reshape(2, rows, 2, part)
-    me = lax.axis_index("core")
-    mine = lax.dynamic_index_in_dim(grads, me, 2, keepdims=False)
-    other = lax.dynamic_index_in_dim(grads, 1 - me, 2, keepdims=False)
-    got = lax.ppermute(other.astype(jnp.bfloat16), "core", [(0, 1), (1, 0)])
-    total = mine + got.astype(jnp.float32)
-    peers = lax.axis_size(("x_hi", "x_lo", "y"))
-    total = total.reshape(peers, rows * 2 // peers, part).astype(jnp.bfloat16)
-    total = lax.all_to_all(total, ("x_hi", "x_lo", "y"), 0, 0)
-    total = jnp.sum(total.astype(jnp.float32), axis=0)
-    depth = lax.axis_size("z")
-    total = total.reshape(depth, 1, -1, part)
-    total = jnp.broadcast_to(total, (depth, 2) + total.shape[2:])
-    total = lax.all_to_all(
-        total.reshape((2 * depth,) + total.shape[2:]), ("z", "x_hi"), 0, 0
-    ).reshape(total.shape)
-    total = jnp.sum(total, axis=0)
-    both = lax.all_gather(total, "core", axis=2, tiled=True)
-    square = jnp.broadcast_to(jnp.sum(both * both), (1, 128))
-    square = jnp.sum(spread(square, "z"), axis=0)
-    square = jnp.sum(spread(square, ("x_lo", "y")), axis=0)[0, 0]
-    shard = both.shape[1] // 2
-    own = lax.dynamic_slice_in_dim(both, me * shard, shard, 1)
-    return own[0], own[1], square
+def adjoint_layers(source, hidden_one, hidden_two, weights):
+    features = source.shape[1]
+    depth = weights.shape[2] - features
+    slope_two = 1.0 - jnp.square(hidden_two.astype(jnp.float32))
+    back_two = lax.dot_general(
+        source, weights[1, :, depth:], CONTRACT_LAST, preferred_element_type=jnp.float32
+    )
+    back_two = (slope_two * back_two).astype(jnp.bfloat16)
+    back_one = lax.dot_general(
+        back_two[:, :depth],
+        weights[0, :, features:],
+        CONTRACT_LAST,
+        preferred_element_type=jnp.float32,
+    ) + lax.dot_general(
+        back_two[:, depth:],
+        weights[1, :, :depth],
+        CONTRACT_LAST,
+        preferred_element_type=jnp.float32,
+    )
+    slope_one = 1.0 - jnp.square(hidden_one.astype(jnp.float32))
+    return (slope_one * back_one).astype(jnp.bfloat16)
+
+
+def last_step_kernel(adjoint, gating, hidden_one, hidden_two, weights, source_out, one_out, back):
+    source = (gating[...] * adjoint[...]).astype(jnp.bfloat16)
+    source_out[...] = source
+    back_one = adjoint_layers(source, hidden_one[...], hidden_two[...], weights)
+    one_out[...] = back_one
+    back[...] = jnp.dot(
+        back_one, weights[0, :, : source.shape[1]], preferred_element_type=jnp.float32
+    )
+
+
+def first_step_kernel(
+    adjoint,
+    gating,
+    hidden_one,
+    hidden_two,
+    states,
+    source_late,
+    one_late,
+    hidden_late,
+    states_late,
+    weights,
+    one_out,
+    grads,
+):
+    source = (gating[...] * adjoint[...]).astype(jnp.bfloat16)
+    back_one = adjoint_layers(source, hidden_one[...], hidden_two[...], weights)
+    one_out[...] = back_one
+    pairs = (
+        (one_late[...], back_one, states_late[...], states[...]),
+        (hidden_late[...], hidden_two[...], source_late[...], source),
+    )
+    _, blocks, halves, rows, columns = grads.shape
+    for which, (left_late, left, right_late, right) in enumerate(pairs):
+        total = lax.dot_general(
+            jnp.concatenate([left_late, left]),
+            jnp.concatenate([right_late, right]),
+            CONTRACT_FIRST,
+            preferred_element_type=jnp.float32,
+        ).astype(jnp.bfloat16)
+        for block in range(blocks):
+            for half in range(halves):
+                grads[which, block, half] = total[
+                    block * rows : (block + 1) * rows, half * columns : (half + 1) * columns
+                ]
+
+
+def on_chip(kernel, outs, operands, flops):
+    size = sum(array.size * array.dtype.itemsize for array in list(operands) + list(outs))
+    return pl.pallas_call(
+        kernel,
+        out_shape=outs,
+        in_specs=[pl.BlockSpec(memory_space=pltpu.VMEM)] * len(operands),
+        out_specs=[pl.BlockSpec(memory_space=pltpu.VMEM)] * len(outs),
+        compiler_params=pltpu.CompilerParams(vmem_limit_bytes=24 * 1024 * 1024),
+        cost_estimate=pl.CostEstimate(flops=flops, bytes_accessed=size, transcendentals=0),
+    )(*operands)
+
+
+def reduce_gradients(grads):
+    kinds, blocks, halves, rows, columns = grads.shape
+    around = ("x_hi", "x_lo", "y", "core")
+    grads = grads.reshape(kinds * blocks * halves, rows, columns)
+    grads = lax.all_to_all(grads, around, 0, 0)
+    grads = jnp.sum(grads.astype(jnp.float32), axis=0).astype(jnp.bfloat16)
+    grads = jnp.sum(spread(grads, "z").astype(jnp.float32), axis=0)
+    square = jnp.broadcast_to(jnp.sum(grads * grads), (8, columns))
+    depth = rows // lax.axis_size("z")
+    own = lax.dynamic_slice_in_dim(grads, lax.axis_index("z") * depth, depth, 0)
+    parts = spread(jnp.concatenate([own, square]), around)
+    square = jnp.sum(parts[:, depth, 0])
+    parts = parts.reshape(kinds, blocks, halves, depth + 8, columns)
+    block = lax.axis_index(("x_lo", "y"))
+    parts = lax.dynamic_index_in_dim(parts, block, 1, keepdims=False)
+    shard = depth // halves
+    parts = lax.dynamic_slice_in_dim(parts, lax.axis_index("core") * shard, shard, 2)
+    parts = jnp.concatenate([parts[:, 0], parts[:, 1]], axis=2)
+    return parts[0], parts[1], square
 
 
 def local(
@@ -85,7 +160,7 @@
     _, cells, features = state.shape
     current, increment_now, diffusivity = state[0], increment[0], diffusivity[0]
     pair_sum = halo(jnp.stack([current, increment_now]))
-    w_in_b, w_mid_all, w_out_b = gather_weights(w_in, w_mid, w_out)
+    weights, w_in_b, w_mid_all, w_out_b = gather_weights(w_in, w_mid, w_out)
     hidden_units = w_in_b.shape[0]
     gating = (0.5 + land_sea.astype(jnp.float32)).reshape(cells, 1)
     saved = []
@@ -110,7 +185,7 @@
             w_out_b,
             preferred_element_type=jnp.float32,
         )
-        saved.append((states_b, hidden_two, slope_one, slope_two))
+        saved.append((states_b, hidden_one, hidden_two))
         return gating * out[:cells], gating * out[cells:]
 
     tend, tangent = network(current, increment_now)
@@ -132,35 +207,51 @@
     adjoint = lax.dot_general(
         pick_cell, weighted[:, None] * pick_level, CONTRACT_FIRST, precision=lax.Precision.HIGHEST
     )
-    grad_in = jnp.zeros((hidden_units, features), jnp.float32)
-    grad_out = jnp.zeros((hidden_units, features), jnp.float32)
-    for section_index in (1, 0):
-        states_b, hidden_two, slope_one, slope_two = saved[section_index]
-        spreading = diffusivity * adjoint
-        spread_sum = halo(spreading[None])[0]
-        source = (gating * adjoint).astype(jnp.bfloat16)
-        back_two = (
-            slope_two
-            * lax.dot_general(source, w_out_b, CONTRACT_LAST, preferred_element_type=jnp.float32)
-        ).astype(jnp.bfloat16)
-        back_one = (
-            slope_one
-            * lax.dot_general(
-                back_two, w_mid_all, CONTRACT_LAST, preferred_element_type=jnp.float32
-            )
-        ).astype(jnp.bfloat16)
-        grad_out = grad_out + lax.dot_general(
-            hidden_two, source, CONTRACT_FIRST, preferred_element_type=jnp.float32
-        )
-        grad_in = grad_in + lax.dot_general(
-            back_one, states_b, CONTRACT_FIRST, preferred_element_type=jnp.float32
-        )
-        adjoint = (
-            adjoint
-            + (spread_sum - 4.0 * spreading)
-            + jnp.dot(back_one, w_in_b, preferred_element_type=jnp.float32)
-        )
-    share_in, share_out, square_sum = reduce_gradients(grad_in, grad_out)
+    states_late, one_late, two_late = saved[1]
+    states_b, hidden_one, hidden_two = saved[0]
+    spreading = diffusivity * adjoint
+    spread_sum = halo(spreading[None])[0]
+    wide = jax.ShapeDtypeStruct((cells, hidden_units), jnp.bfloat16)
+    narrow = jax.ShapeDtypeStruct((cells, features), jnp.float32)
+    layer = 2 * cells * hidden_units
+    source_late, back_late, back_sum = on_chip(
+        last_step_kernel,
+        (jax.ShapeDtypeStruct((cells, features), jnp.bfloat16), wide, narrow),
+        (adjoint, gating, one_late, two_late, weights),
+        layer * (2 * features + hidden_units),
+    )
+    adjoint = adjoint + (spread_sum - 4.0 * spreading) + back_sum
+    blocks = lax.axis_size(("x_lo", "y"))
+    halves = lax.axis_size("core")
+    back_first, grads = on_chip(
+        first_step_kernel,
+        (
+            wide,
+            jax.ShapeDtypeStruct(
+                (2, blocks, halves, hidden_units // blocks, features // halves), jnp.bfloat16
+            ),
+        ),
+        (
+            adjoint,
+            gating,
+            hidden_one,
+            hidden_two,
+            states_b,
+            source_late,
+            back_late,
+            two_late,
+            states_late,
+            weights,
+        ),
+        layer * (5 * features + hidden_units),
+    )
+    share_in, share_out, square_sum = reduce_gradients(grads)
+    spreading = diffusivity * adjoint
+    adjoint = (
+        adjoint
+        + (halo(spreading[None])[0] - 4.0 * spreading)
+        + jnp.dot(back_first, w_in_b, preferred_element_type=jnp.float32)
+    )
     scale = LEARN_RATE / jnp.sqrt(square_sum / (2.0 * hidden_units * features) + EPSILON)
     return (adjoint[None], w_in - scale * share_in, w_out - scale * share_out)
 

time: 207 us -> 191 us (0.923)
  blocking collectives: 24.6 us -> 44.4 us
  matrix products: 22.5 us -> 5.42 us
  waiting for transfers between devices: 45.5 us -> 37.2 us
  starting transfers between devices: 83.2 us -> 77.3 us
  other arithmetic: 15.2 us -> 11.1 us
  local copies, waits for them, and re-layouts: 13.2 us -> 9.61 us
  Pallas kernels: 0 us -> 2.42 us
    all_to_all x0 -> x1, blocking collectives: none -> 25.7 us  [reduce_gradients(): grads = lax.all_to_all(grads, around, 0, 0)]
    dot_general x8 -> x1, matrix products: 19.2 us -> 2.06 us  [local(): jnp.dot(back_first, w_in_b, preferred_element_type=jnp.float32)]
    all_to_all x2 -> x0, waiting for transfers between devices: 14.5 us -> none  [the longest x1 8.85 us: reduce_gradients(): lax.all_to_all(total.reshape((2 * depth,) + total.shape[2:]), ('z', 'x_hi...]
    all_to_all x2 -> x0, starting transfers between devices: 13.1 us -> none  [the longest x1 6.78 us: reduce_gradients(): lax.all_to_all(total.reshape((2 * depth,) + total.shape[2:]), ('z', 'x_hi...]
    all_to_all x4, starting transfers between devices: 22.7 us -> 34.4 us  [spread(): lax.all_to_all(jnp.broadcast_to(block[None], (count,) + block.shape), axi...]
    all_to_all x4, waiting for transfers between devices: 24.5 us -> 31 us  [spread(): lax.all_to_all(jnp.broadcast_to(block[None], (count,) + block.shape), axi...]
    another operation x3 -> x0, local copies, waits for them, and re-layouts: 6.36 us -> none  [the longest x2 5.11 us: reduce_gradients(): grads = jnp.stack([grad_in, grad_out]).reshape(2, rows, 2, part)]
    all_gather x1 -> x0, blocking collectives: 5.42 us -> none  [reduce_gradients(): both = lax.all_gather(total, 'core', axis=2, tiled=True)]
  transfers between devices with their start and end apart: 19 -> 16, of which waited for: 8 -> 6; matrix products, arithmetic and copies ran while one was open for 11% -> 6% of each run, Pallas kernels for 0% -> 1%
where the time goes in v2:
time: 191 us; the launch traced here: 189 us
  starting transfers between devices  77.3 us (40%)
  blocking collectives  44.4 us (23%)
  waiting for transfers between devices  37.2 us (19%)
  other arithmetic  11.1 us (6%)
  local copies, waits for them, and re-layouts  9.61 us (5%)
  matrix products  5.42 us (3%)
  Pallas kernels  2.42 us (1%)
  between operations  1.92 us (1%)
    all_to_all x4, starting transfers between devices, spread(): lax.all_to_all(jnp.broadcast_to(block[None], (count,) + block.shape), axi...  34.4 us
    all_to_all x4, waiting for transfers between devices, spread(): lax.all_to_all(jnp.broadcast_to(block[None], (count,) + block.shape), axi...  31 us
    all_to_all x1, blocking collectives, reduce_gradients(): grads = lax.all_to_all(grads, around, 0, 0)  25.7 us
    ppermute x4, starting transfers between devices, halo(): far = lax.ppermute(field, TILE, pairs)  20.7 us
    ppermute x4, starting transfers between devices, halo(): edges = lax.ppermute(edges, 'x_hi', [(0, 1), (1, 0)])  14.6 us
    all_to_all x1, blocking collectives, spread(): lax.all_to_all(jnp.broadcast_to(block[None], (count,) + block.shape), axi...  10.4 us
    all_gather x1, blocking collectives, gather_weights(): rows = lax.all_gather(rows, 'core', axis=0, tiled=True)  8.36 us
    ppermute x4, starting transfers between devices, halo(): near = lax.ppermute(field, 'core', [(0, 1), (1, 0)])  7.68 us
  transfers between devices with their start and end apart: 16, of which 6 were waited for; matrix products, arithmetic and copies ran while one was open for 6% of the time, Pallas kernels for 1%

profile of v2, /device:TPU:1, one launch (start us, length us, event | category | flops | bytes accessed | tf_op | source)
XLA Modules:
  0.0 189.4 jit_solution(8205626440547827044)
XLA Ops:
  0.6 0.7 convert_element_type.68
  1.4 0.7 convert_element_type.67
  2.1 0.7 maximum_bitcast_fusion
  2.8 8.4 %all-gather = bf16[2,4,1536]{2,1,0:T(4,128)(2,1)S(1)} all-gather(bf16[1,4,1536]{2,1,0:T(4,128)(2,1)S(1)} %maximum_bitcast_fusion), channel_id=1, replica_groups=mesh['x_lo'=2,'y'=4,'z'=16,'core'=2,'x_hi'=2] {'core'}, dimensions={0}, use_global_device_ids=true | all-gather | bytes 36864 | tf_op jit(solution)/shard_map/all_gather | solution.py:27
  11.2 0.7 broadcast_in_dim.22
  11.9 9.5 %all-to-all-start = ((bf16[16,8,768]{2,1,0:T(8,128)(2,1)}), bf16[16,8,768]{2,1,0:T(8,128)(2,1)S(1)}, u32[]{:S(2)}, u32[]{:S(2)}) async-start(bf16[16,8,768]{2,1,0:T(8,128)(2,1)} %broadcast_in_dim.22), calls=%async_computation | async-start | bytes 393216 | tf_op jit(solution)/shard_map/all_to_all | solution.py:20
  21.4 0.9 constant_dynamic-update-slice_fusion.1
  22.3 12.0 %all-to-all-done = bf16[16,8,768]{2,1,0:T(8,128)(2,1)S(1)} async-done(((bf16[16,8,768]{2,1,0:T(8,128)(2,1)}), bf16[16,8,768]{2,1,0:T(8,128)(2,1)S(1)}, u32[]{:S(2)}, u32[]{:S(2)}) %all-to-all-start) | async-done | bytes 196640 | tf_op jit(solution)/shard_map/all_to_all | solution.py:20
  34.4 1.3 broadcast_in_dim.24
  35.6 5.1 %all-to-all-start.1 = ((bf16[8,128,768]{2,1,0:T(8,128)(2,1)}), bf16[8,128,768]{2,1,0:T(8,128)(2,1)S(1)}, u32[]{:S(2)}, u32[]{:S(2)}) async-start(bf16[8,128,768]{2,1,0:T(8,128)(2,1)} %broadcast_in_dim.24), calls=%async_computation.1 | async-start | bytes 3145728 | tf_op jit(solution)/shard_map/all_to_all | solution.py:20
  40.8 7.6 %collective-permute-start = (f32[2,128,256]{2,1,0:T(8,128)S(1)}, f32[2,128,256]{2,1,0:T(8,128)S(1)}, u32[]{:S(2)}, u32[]{:S(2)}) collective-permute-start(f32[2,128,256]{2,1,0:T(8,128)S(1)} %get-tuple-element.44), channel_id=1, source_target_pairs={{2,4},{4,2},{6,8},{8,6},{10,12},{12,10},{14,16},{16,14},{18,20},{2... | collective-permute-start | bytes 786440 | tf_op jit(solution)/shard_map/ppermute | solution.py:46
  48.4 1.9 %collective-permute-start.1 = (f32[2,128,256]{2,1,0:T(8,128)S(1)}, f32[2,128,256]{2,1,0:T(8,128)S(1)}, u32[]{:S(2)}, u32[]{:S(2)}) collective-permute-start(f32[2,128,256]{2,1,0:T(8,128)S(1)} %get-tuple-element.44), channel_id=1, source_target_pairs={{0,2},{2,0},{1,3},{3,1},{4,6},{6,4},{5,7},{7,5},{8,10},{10,8},{9,1... | collective-permute-start | bytes 786440 | tf_op jit(solution)/shard_map/ppermute | solution.py:49
  50.4 4.4 %collective-permute-start.2 = (f32[2,2,256]{2,1,0:T(2,128)S(1)}, f32[2,2,256]{2,1,0:T(2,128)S(1)}, u32[]{:S(2)}, u32[]{:S(2)}) collective-permute-start(f32[2,2,256]{2,1,0:T(2,128)S(1)} %pad_maximum_fusion.4), channel_id=1, source_target_pairs={{0,1},{1,0},{2,3},{3,2},{4,5},{5,4},{6,7},{7,6},{8,9},{9,8},{10,11... | collective-permute-start | bytes 12296 | tf_op jit(solution)/shard_map/ppermute | solution.py:48
  54.8 0.1 copy.24.gating
  54.9 3.2 %collective-permute-done.2 = f32[2,2,256]{2,1,0:T(2,128)S(1)} collective-permute-done((f32[2,2,256]{2,1,0:T(2,128)S(1)}, f32[2,2,256]{2,1,0:T(2,128)S(1)}, u32[]{:S(2)}, u32[]{:S(2)}) %collective-permute-start.2) | collective-permute-done | bytes 4128 | tf_op jit(solution)/shard_map/ppermute | solution.py:48
  58.2 0.8 fusion.28
  58.9 0.2 broadcast_in_dim.26
  59.1 10.4 %all_to_all.30.weights = bf16[2,1024,768]{2,1,0:T(8,128)(2,1)S(1)} all-to-all(bf16[2,1024,768]{2,1,0:T(8,128)(2,1)S(1)} %broadcast_in_dim.26), channel_id=1, replica_groups=mesh['x_lo'=2,'y'=4,'z'=16,'core'=2,'x_hi'=2] {'core'}, dimensions={0} | all-to-all | bytes 6291456 | tf_op jit(solution)/shard_map/all_to_all | solution.py:20
  69.6 0.3 fusion.27
  69.9 0.1 fusion.10
  70.0 0.2 slice_bitcast_fusion.1
  70.2 0.7 fusion.1
  70.9 0.1 fusion.8
  71.0 0.3 fusion.15
  71.4 0.1 fusion.100
  71.5 6.1 %collective-permute-start.3 = (f32[1,128,256]{2,1,0:T(8,128)S(1)}, f32[1,128,256]{2,1,0:T(8,128)S(1)}, u32[]{:S(2)}, u32[]{:S(2)}) collective-permute-start(f32[1,128,256]{2,1,0:T(8,128)S(1)} %bitcast.134), channel_id=1, source_target_pairs={{2,4},{4,2},{6,8},{8,6},{10,12},{12,10},{14,16},{16,14},{18,20},{2... | collective-permute-start | bytes 393224 | tf_op jit(solution)/shard_map/ppermute | solution.py:46
  77.6 1.9 %collective-permute-start.4 = (f32[1,128,256]{2,1,0:T(8,128)S(1)}, f32[1,128,256]{2,1,0:T(8,128)S(1)}, u32[]{:S(2)}, u32[]{:S(2)}) collective-permute-start(f32[1,128,256]{2,1,0:T(8,128)S(1)} %bitcast.135), channel_id=1, source_target_pairs={{0,2},{2,0},{1,3},{3,1},{4,6},{6,4},{5,7},{7,5},{8,10},{10,8},{9,1... | collective-permute-start | bytes 393224 | tf_op jit(solution)/shard_map/ppermute | solution.py:49
  79.5 0.3 fusion.26
  79.8 0.1 fusion.6
  79.9 0.7 fusion
  80.7 0.1 fusion.4
  80.8 3.6 %collective-permute-start.5 = (f32[1,2,256]{2,1,0:T(2,128)S(1)}, f32[1,2,256]{2,1,0:T(2,128)S(1)}, u32[]{:S(2)}, u32[]{:S(2)}) collective-permute-start(f32[1,2,256]{2,1,0:T(2,128)S(1)} %pad_maximum_fusion.5), channel_id=1, source_target_pairs={{0,1},{1,0},{2,3},{3,2},{4,5},{5,4},{6,7},{7,6},{8,9},{9,8},{10,11... | collective-permute-start | bytes 6152 | tf_op jit(solution)/shard_map/ppermute | solution.py:48
  84.5 0.3 fusion.22
  84.8 1.9 collective-permute-done.5
  86.7 0.4 fusion.3
  87.1 0.3 fusion.70.adjoint
  87.5 3.2 %collective-permute-start.6 = (f32[1,128,256]{2,1,0:T(8,128)S(1)}, f32[1,128,256]{2,1,0:T(8,128)S(1)}, u32[]{:S(2)}, u32[]{:S(2)}) collective-permute-start(f32[1,128,256]{2,1,0:T(8,128)S(1)} %fusion.74), channel_id=1, source_target_pairs={{2,4},{4,2},{6,8},{8,6},{10,12},{12,10},{14,16},{16,14},{18,20},{2... | collective-permute-start | bytes 393224 | tf_op jit(solution)/shard_map/ppermute | solution.py:46
  90.7 1.9 %collective-permute-start.7 = (f32[1,128,256]{2,1,0:T(8,128)S(1)}, f32[1,128,256]{2,1,0:T(8,128)S(1)}, u32[]{:S(2)}, u32[]{:S(2)}) collective-permute-start(f32[1,128,256]{2,1,0:T(8,128)S(1)} %fusion.74), channel_id=1, source_target_pairs={{0,2},{2,0},{1,3},{3,1},{4,6},{6,4},{5,7},{7,5},{8,10},{10,8},{9,1... | collective-permute-start | bytes 393224 | tf_op jit(solution)/shard_map/ppermute | solution.py:49
  92.7 3.6 %collective-permute-start.8 = (f32[1,2,256]{2,1,0:T(2,128)S(1)}, f32[1,2,256]{2,1,0:T(2,128)S(1)}, u32[]{:S(2)}, u32[]{:S(2)}) collective-permute-start(f32[1,2,256]{2,1,0:T(2,128)S(1)} %pad_maximum_fusion.6), channel_id=1, source_target_pairs={{0,1},{1,0},{2,3},{3,2},{4,5},{5,4},{6,7},{7,6},{8,9},{9,8},{10,11... | collective-permute-start | bytes 6152 | tf_op jit(solution)/shard_map/ppermute | solution.py:48
  96.3 1.1 shard_map.130
  97.4 1.1 collective-permute-done.8
  98.5 0.7 fusion.75
  99.2 1.3 shard_map.131
  100.6 0.7 copy-done
  101.3 25.7 %all_to_all.31 = bf16[32,128,128]{2,1,0:T(8,128)(2,1)} all-to-all(bf16[32,128,128]{2,1,0:T(8,128)(2,1)S(1)} %bitcast.131), channel_id=1, replica_groups=mesh['x_lo'=2,'y'=4,'z'=16,'core'=2,'x_hi'=2] {'x_hi','x_lo','y','core'}, dimensions={0} | all-to-all | bytes 2097152 | tf_op jit(solution)/shard_map/all_to_all | solution.py:140
  127.0 2.0 %reduce_sum.49 = bf16[128,128]{1,0:T(8,128)(2,1)} reduce(bf16[32,128,128]{2,1,0:T(8,128)(2,1)} %all_to_all.31, bf16[]{:T(256)} %constant.68.clone.1), dimensions={0}, to_apply=%region_1.0 | reduce | flops 507904 | bytes 1081346 | tf_op jit(solution)/shard_map/reduce_sum | solution.py:141
  129.0 1.7 broadcast_in_dim.59
  130.7 6.6 %all-to-all-start.4 = ((bf16[16,128,128]{2,1,0:T(8,128)(2,1)}), bf16[16,128,128]{2,1,0:T(8,128)(2,1)}, u32[]{:S(2)}, u32[]{:S(2)}) async-start(bf16[16,128,128]{2,1,0:T(8,128)(2,1)} %broadcast_in_dim.59), calls=%async_computation.4 | async-start | bytes 1048576 | tf_op jit(solution)/shard_map/all_to_all | solution.py:20
  137.3 3.8 %collective-permute-start.9 = (f32[1,128,256]{2,1,0:T(8,128)}, f32[1,128,256]{2,1,0:T(8,128)}, u32[]{:S(2)}, u32[]{:S(2)}) collective-permute-start(f32[1,128,256]{2,1,0:T(8,128)} %get-tuple-element.13), channel_id=1, source_target_pairs={{2,4},{4,2},{6,8},{8,6},{10,12},{12,10},{14,16},{16,14},{18,20},{2... | collective-permute-start | bytes 393224 | tf_op jit(solution)/shard_map/ppermute | solution.py:46
  141.1 1.9 %collective-permute-start.10 = (f32[1,128,256]{2,1,0:T(8,128)}, f32[1,128,256]{2,1,0:T(8,128)}, u32[]{:S(2)}, u32[]{:S(2)}) collective-permute-start(f32[1,128,256]{2,1,0:T(8,128)} %get-tuple-element.13), channel_id=1, source_target_pairs={{0,2},{2,0},{1,3},{3,1},{4,6},{6,4},{5,7},{7,5},{8,10},{10,8},{9,1... | collective-permute-start | bytes 393224 | tf_op jit(solution)/shard_map/ppermute | solution.py:49
  143.0 0.7 fusion.110
  143.7 3.0 %collective-permute-start.11 = (f32[1,2,256]{2,1,0:T(2,128)S(1)}, f32[1,2,256]{2,1,0:T(2,128)S(1)}, u32[]{:S(2)}, u32[]{:S(2)}) collective-permute-start(f32[1,2,256]{2,1,0:T(2,128)S(1)} %pad_maximum_fusion.7), channel_id=1, source_target_pairs={{0,1},{1,0},{2,3},{3,2},{4,5},{5,4},{6,7},{7,6},{8,9},{9,8},{10,11... | collective-permute-start | bytes 6152 | tf_op jit(solution)/shard_map/ppermute | solution.py:48
  146.7 1.7 fusion.109
  148.4 11.9 %all-to-all-done.4 = bf16[16,128,128]{2,1,0:T(8,128)(2,1)} async-done(((bf16[16,128,128]{2,1,0:T(8,128)(2,1)}), bf16[16,128,128]{2,1,0:T(8,128)(2,1)}, u32[]{:S(2)}, u32[]{:S(2)}) %all-to-all-start.4) | async-done | bytes 524320 | tf_op jit(solution)/shard_map/all_to_all | solution.py:20
  160.3 1.1 convert_reduce_fusion
  161.4 0.6 multiply_reduce_fusion
  162.1 0.6 concatenate.86
  162.7 0.7 broadcast_in_dim.60
  163.4 13.1 %all-to-all-start.5 = ((f32[32,16,128]{2,1,0:T(8,128)}), f32[32,16,128]{2,1,0:T(8,128)}, u32[]{:S(2)}, u32[]{:S(2)}) async-start(f32[32,16,128]{2,1,0:T(8,128)} %broadcast_in_dim.60), calls=%async_computation.5 | async-start | bytes 524288 | tf_op jit(solution)/shard_map/all_to_all | solution.py:20
  176.6 2.1 %fusion.2 = f32[1,128,256]{2,1,0:T(8,128)} fusion(bf16[128,1024]{1,0:T(8,128)(2,1)S(1)} %copy-done.1, bf16[2,1024,768]{2,1,0:T(8,128)(2,1)S(1)} %all_to_all.30.weights, f32[128,256]{1,0:T(8,128)S(1)} %get-tuple-element.14.adjoint, f32[1,1,256]{2,1,0:T(1,128)S(1)} %get-tuple-element.55, f32[1,127,256]{2,1,0:T(8,128)} %get-tuple-element.33, ...), kind=kOutput, calls=%fused_computation.4 | convolution fusion | flops 67436544 | bytes 1703936 | tf_op jit(solution)/shard_map/dot_general | solution.py:253
  178.7 7.0 %all-to-all-done.5 = f32[32,16,128]{2,1,0:T(8,128)} async-done(((f32[32,16,128]{2,1,0:T(8,128)}), f32[32,16,128]{2,1,0:T(8,128)}, u32[]{:S(2)}, u32[]{:S(2)}) %all-to-all-start.5) | async-done | bytes 262176 | tf_op jit(solution)/shard_map/all_to_all | solution.py:20
  185.7 0.8 dynamic-slice_bitcast_fusion
  186.5 1.5 slice_reduce_fusion
  188.8 0.6 fusion.87
  (57 shorter events, 0.3 us)
Async XLA Ops:
  0.6 40.1 %copy-start.5 = (f32[1,128,256]{2,1,0:T(8,128)S(1)}, f32[1,128,256]{2,1,0:T(8,128)}, u32[]{:S(2)}) copy-start(f32[1,128,256]{2,1,0:T(8,128)} %param.12) | copy-start | bytes 393220
  11.9 22.5 %all-to-all-start = ((bf16[16,8,768]{2,1,0:T(8,128)(2,1)}), bf16[16,8,768]{2,1,0:T(8,128)(2,1)S(1)}, u32[]{:S(2)}, u32[]{:S(2)}) async-start(bf16[16,8,768]{2,1,0:T(8,128)(2,1)} %broadcast_in_dim.22), calls=%async_computation | async-start | bytes 393216 | tf_op jit(solution)/shard_map/all_to_all | solution.py:20
  34.4 20.5 %copy-start.12 = (s32[1,128]{1,0:T(1,128)S(1)}, s32[1,128]{1,0:T(1,128)}, u32[]{:S(2)}) copy-start(s32[1,128]{1,0:T(1,128)} %param.14) | copy-start | bytes 1540
  35.6 23.3 %all-to-all-start.1 = ((bf16[8,128,768]{2,1,0:T(8,128)(2,1)}), bf16[8,128,768]{2,1,0:T(8,128)(2,1)S(1)}, u32[]{:S(2)}, u32[]{:S(2)}) async-start(bf16[8,128,768]{2,1,0:T(8,128)(2,1)} %broadcast_in_dim.24), calls=%async_computation.1 | async-start | bytes 3145728 | tf_op jit(solution)/shard_map/all_to_all | solution.py:20
  40.8 17.4 %collective-permute-start = (f32[2,128,256]{2,1,0:T(8,128)S(1)}, f32[2,128,256]{2,1,0:T(8,128)S(1)}, u32[]{:S(2)}, u32[]{:S(2)}) collective-permute-start(f32[2,128,256]{2,1,0:T(8,128)S(1)} %get-tuple-element.44), channel_id=1, source_target_pairs={{2,4},{4,2},{6,8},{8,6},{10,12},{12,10},{14,16},{16,14},{18,20},{2... | collective-permute-start | bytes 786440 | tf_op jit(solution)/shard_map/ppermute | solution.py:46
  48.4 9.7 %collective-permute-start.1 = (f32[2,128,256]{2,1,0:T(8,128)S(1)}, f32[2,128,256]{2,1,0:T(8,128)S(1)}, u32[]{:S(2)}, u32[]{:S(2)}) collective-permute-start(f32[2,128,256]{2,1,0:T(8,128)S(1)} %get-tuple-element.44), channel_id=1, source_target_pairs={{0,2},{2,0},{1,3},{3,1},{4,6},{6,4},{5,7},{7,5},{8,10},{10,8},{9,1... | collective-permute-start | bytes 786440 | tf_op jit(solution)/shard_map/ppermute | solution.py:49
  50.4 7.8 %collective-permute-start.2 = (f32[2,2,256]{2,1,0:T(2,128)S(1)}, f32[2,2,256]{2,1,0:T(2,128)S(1)}, u32[]{:S(2)}, u32[]{:S(2)}) collective-permute-start(f32[2,2,256]{2,1,0:T(2,128)S(1)} %pad_maximum_fusion.4), channel_id=1, source_target_pairs={{0,1},{1,0},{2,3},{3,2},{4,5},{5,4},{6,7},{7,6},{8,9},{9,8},{10,11... | collective-permute-start | bytes 12296 | tf_op jit(solution)/shard_map/ppermute | solution.py:48
  70.2 1.2 copy-start.2
  70.2 1.2 copy-start.3
  70.2 1.2 copy-start.4
  71.5 15.2 %collective-permute-start.3 = (f32[1,128,256]{2,1,0:T(8,128)S(1)}, f32[1,128,256]{2,1,0:T(8,128)S(1)}, u32[]{:S(2)}, u32[]{:S(2)}) collective-permute-start(f32[1,128,256]{2,1,0:T(8,128)S(1)} %bitcast.134), channel_id=1, source_target_pairs={{2,4},{4,2},{6,8},{8,6},{10,12},{12,10},{14,16},{16,14},{18,20},{2... | collective-permute-start | bytes 393224 | tf_op jit(solution)/shard_map/ppermute | solution.py:46
  77.6 9.1 %collective-permute-start.4 = (f32[1,128,256]{2,1,0:T(8,128)S(1)}, f32[1,128,256]{2,1,0:T(8,128)S(1)}, u32[]{:S(2)}, u32[]{:S(2)}) collective-permute-start(f32[1,128,256]{2,1,0:T(8,128)S(1)} %bitcast.135), channel_id=1, source_target_pairs={{0,2},{2,0},{1,3},{3,1},{4,6},{6,4},{5,7},{7,5},{8,10},{10,8},{9,1... | collective-permute-start | bytes 393224 | tf_op jit(solution)/shard_map/ppermute | solution.py:49
  80.7 6.0 %copy-start.8 = (s32[64]{0:T(128)S(1)}, s32[64]{0:T(128)}, u32[]{:S(2)}) copy-start(s32[64]{0:T(128)} %param.19) | copy-start | bytes 772
  80.7 6.0 %copy-start.9 = (s32[64]{0:T(128)S(1)}, s32[64]{0:T(128)}, u32[]{:S(2)}) copy-start(s32[64]{0:T(128)} %param.18) | copy-start | bytes 772
  80.7 6.4 %copy-start.10 = (f32[64]{0:T(128)S(1)}, f32[64]{0:T(128)}, u32[]{:S(2)}) copy-start(f32[64]{0:T(128)} %param.21) | copy-start | bytes 772
  80.7 6.4 %copy-start.11 = (f32[64]{0:T(128)S(1)}, f32[64]{0:T(128)}, u32[]{:S(2)}) copy-start(f32[64]{0:T(128)} %param.20) | copy-start | bytes 772
  80.8 5.8 %collective-permute-start.5 = (f32[1,2,256]{2,1,0:T(2,128)S(1)}, f32[1,2,256]{2,1,0:T(2,128)S(1)}, u32[]{:S(2)}, u32[]{:S(2)}) collective-permute-start(f32[1,2,256]{2,1,0:T(2,128)S(1)} %pad_maximum_fusion.5), channel_id=1, source_target_pairs={{0,1},{1,0},{2,3},{3,2},{4,5},{5,4},{6,7},{7,6},{8,9},{9,8},{10,11... | collective-permute-start | bytes 6152 | tf_op jit(solution)/shard_map/ppermute | solution.py:48
  87.5 11.0 %collective-permute-start.6 = (f32[1,128,256]{2,1,0:T(8,128)S(1)}, f32[1,128,256]{2,1,0:T(8,128)S(1)}, u32[]{:S(2)}, u32[]{:S(2)}) collective-permute-start(f32[1,128,256]{2,1,0:T(8,128)S(1)} %fusion.74), channel_id=1, source_target_pairs={{2,4},{4,2},{6,8},{8,6},{10,12},{12,10},{14,16},{16,14},{18,20},{2... | collective-permute-start | bytes 393224 | tf_op jit(solution)/shard_map/ppermute | solution.py:46
  90.7 7.8 %collective-permute-start.7 = (f32[1,128,256]{2,1,0:T(8,128)S(1)}, f32[1,128,256]{2,1,0:T(8,128)S(1)}, u32[]{:S(2)}, u32[]{:S(2)}) collective-permute-start(f32[1,128,256]{2,1,0:T(8,128)S(1)} %fusion.74), channel_id=1, source_target_pairs={{0,2},{2,0},{1,3},{3,1},{4,6},{6,4},{5,7},{7,5},{8,10},{10,8},{9,1... | collective-permute-start | bytes 393224 | tf_op jit(solution)/shard_map/ppermute | solution.py:49
  92.7 5.8 %collective-permute-start.8 = (f32[1,2,256]{2,1,0:T(2,128)S(1)}, f32[1,2,256]{2,1,0:T(2,128)S(1)}, u32[]{:S(2)}, u32[]{:S(2)}) collective-permute-start(f32[1,2,256]{2,1,0:T(2,128)S(1)} %pad_maximum_fusion.6), channel_id=1, source_target_pairs={{0,1},{1,0},{2,3},{3,2},{4,5},{5,4},{6,7},{7,6},{8,9},{9,8},{10,11... | collective-permute-start | bytes 6152 | tf_op jit(solution)/shard_map/ppermute | solution.py:48
  100.6 0.7 copy-start
  101.3 75.3 %copy-start.1 = (bf16[128,1024]{1,0:T(8,128)(2,1)S(1)}, bf16[128,1024]{1,0:T(8,128)(2,1)}, u32[]{:S(2)}) copy-start(bf16[128,1024]{1,0:T(8,128)(2,1)} %copy-done) | copy-start | bytes 786436
  127.0 61.8 %copy-start.6 = (f32[4,256]{1,0:T(4,128)S(1)}, f32[4,256]{1,0:T(4,128)}, u32[]{:S(2)}) copy-start(f32[4,256]{1,0:T(4,128)} %param.17) | copy-start | bytes 12292
  127.0 61.8 %copy-start.7 = (f32[4,256]{1,0:T(4,128)S(1)}, f32[4,256]{1,0:T(4,128)}, u32[]{:S(2)}) copy-start(f32[4,256]{1,0:T(4,128)} %param.15) | copy-start | bytes 12292
  130.7 29.7 %all-to-all-start.4 = ((bf16[16,128,128]{2,1,0:T(8,128)(2,1)}), bf16[16,128,128]{2,1,0:T(8,128)(2,1)}, u32[]{:S(2)}, u32[]{:S(2)}) async-start(bf16[16,128,128]{2,1,0:T(8,128)(2,1)} %broadcast_in_dim.59), calls=%async_computation.4 | async-start | bytes 1048576 | tf_op jit(solution)/shard_map/all_to_all | solution.py:20
  137.3 39.3 %collective-permute-start.9 = (f32[1,128,256]{2,1,0:T(8,128)}, f32[1,128,256]{2,1,0:T(8,128)}, u32[]{:S(2)}, u32[]{:S(2)}) collective-permute-start(f32[1,128,256]{2,1,0:T(8,128)} %get-tuple-element.13), channel_id=1, source_target_pairs={{2,4},{4,2},{6,8},{8,6},{10,12},{12,10},{14,16},{16,14},{18,20},{2... | collective-permute-start | bytes 393224 | tf_op jit(solution)/shard_map/ppermute | solution.py:46
  141.1 35.6 %collective-permute-start.10 = (f32[1,128,256]{2,1,0:T(8,128)}, f32[1,128,256]{2,1,0:T(8,128)}, u32[]{:S(2)}, u32[]{:S(2)}) collective-permute-start(f32[1,128,256]{2,1,0:T(8,128)} %get-tuple-element.13), channel_id=1, source_target_pairs={{0,2},{2,0},{1,3},{3,1},{4,6},{6,4},{5,7},{7,5},{8,10},{10,8},{9,1... | collective-permute-start | bytes 393224 | tf_op jit(solution)/shard_map/ppermute | solution.py:49
  143.7 32.9 %collective-permute-start.11 = (f32[1,2,256]{2,1,0:T(2,128)S(1)}, f32[1,2,256]{2,1,0:T(2,128)S(1)}, u32[]{:S(2)}, u32[]{:S(2)}) collective-permute-start(f32[1,2,256]{2,1,0:T(2,128)S(1)} %pad_maximum_fusion.7), channel_id=1, source_target_pairs={{0,1},{1,0},{2,3},{3,2},{4,5},{5,4},{6,7},{7,6},{8,9},{9,8},{10,11... | collective-permute-start | bytes 6152 | tf_op jit(solution)/shard_map/ppermute | solution.py:48
  163.4 22.3 %all-to-all-start.5 = ((f32[32,16,128]{2,1,0:T(8,128)}), f32[32,16,128]{2,1,0:T(8,128)}, u32[]{:S(2)}, u32[]{:S(2)}) async-start(f32[32,16,128]{2,1,0:T(8,128)} %broadcast_in_dim.60), calls=%async_computation.5 | async-start | bytes 524288 | tf_op jit(solution)/shard_map/all_to_all | solution.py:20

commit v3 on v2

--- a/solution.py
+++ b/solution.py
@@ -1,3 +1,5 @@
+import functools
+
 import jax
 import jax.numpy as jnp
 from jax import lax
@@ -10,9 +12,11 @@
 EPSILON = 1e-06
 CONTRACT_LAST = (((1,), (1,)), ((), ()))
 CONTRACT_FIRST = (((0,), (0,)), ((), ()))
-FINE_AXES = ("x_lo", "y", "z", "core", "x_hi")
-FINE_SIZES = (2, 4, 16, 2, 2)
-TILE = ("x_lo", "y", "z", "core")
+FINE_AXES = ("x_lo", "y", "z_hi", "z_lo", "core", "x_hi")
+FINE_SIZES = (2, 4, 4, 4, 2, 2)
+Z = ("z_hi", "z_lo")
+TILE = ("x_lo", "y", "z_hi", "z_lo", "core")
+AROUND = ("x_hi", "x_lo", "y", "core")
 
 
 def spread(block, axis):
@@ -21,13 +25,17 @@
 
 
 def gather_weights(w_in, w_mid, w_out):
-    rows = jnp.concatenate(
-        [w_in.astype(jnp.bfloat16), w_mid, w_out.astype(jnp.bfloat16)], axis=1
+    columns = 2 * w_in.shape[1] + w_mid.shape[1]
+    (rows,) = on_chip(
+        pack_kernel,
+        (jax.ShapeDtypeStruct((w_in.shape[0], columns), jnp.bfloat16),),
+        (w_in, w_mid, w_out),
+        0,
     )
     rows = lax.all_gather(rows, "core", axis=0, tiled=True)
     width = rows.shape[1] // 2
     half = lax.dynamic_slice_in_dim(rows, lax.axis_index("core") * width, width, 1)
-    half = spread(half, "z").reshape(-1, width)
+    half = spread(half, Z).reshape(-1, width)
     half = spread(half, ("x_lo", "y")).reshape(-1, width)
     both = spread(half, "core")
     features = w_in.shape[1]
@@ -121,37 +129,87 @@
                 ]
 
 
-def on_chip(kernel, outs, operands, flops):
+def on_chip(kernel, outs, operands, flops, scratch=(), scalars=0):
     size = sum(array.size * array.dtype.itemsize for array in list(operands) + list(outs))
+    places = [pltpu.SMEM] * scalars + [pltpu.VMEM] * (len(operands) - scalars)
     return pl.pallas_call(
         kernel,
         out_shape=outs,
-        in_specs=[pl.BlockSpec(memory_space=pltpu.VMEM)] * len(operands),
+        in_specs=[pl.BlockSpec(memory_space=place) for place in places],
         out_specs=[pl.BlockSpec(memory_space=pltpu.VMEM)] * len(outs),
+        scratch_shapes=scratch,
         compiler_params=pltpu.CompilerParams(vmem_limit_bytes=24 * 1024 * 1024),
         cost_estimate=pl.CostEstimate(flops=flops, bytes_accessed=size, transcendentals=0),
     )(*operands)
 
 
-def reduce_gradients(grads):
+def pack_kernel(w_in, w_mid, w_out, rows):
+    features = w_in.shape[1]
+    rows[:, :features] = w_in[...].astype(jnp.bfloat16)
+    rows[:, features:-features] = w_mid[...]
+    rows[:, -features:] = w_out[...].astype(jnp.bfloat16)
+
+
+def sum_and_spread_kernel(parts, copies):
+    total = jnp.sum(parts[...].astype(jnp.float32), axis=0).astype(jnp.bfloat16)
+    copies[...] = jnp.broadcast_to(total[None], copies.shape)
+
+
+def sum_and_square_kernel(place, parts, copies, total):
+    total[...] = jnp.sum(parts[...].astype(jnp.float32), axis=0)
+    depth = copies.shape[1] // 2
+    own = total[pl.ds(pl.multiple_of(place[0] * depth, depth), depth), :]
+    squares = jnp.sum(total[...] * total[...], axis=0, keepdims=True)
+    both = jnp.concatenate([own, jnp.broadcast_to(squares, own.shape)])
+    copies[...] = jnp.broadcast_to(both[None], copies.shape)
+
+
+def update_kernel(blocks, count, place, parts, w_in, w_out, new_in, new_out):
+    depth = parts.shape[1] // 2
+    shard = w_in.shape[0]
+    squares = jnp.sum(parts[:, depth, :], axis=0, keepdims=True)
+    square_sum = jnp.sum(squares, axis=1, keepdims=True)
+    scale = LEARN_RATE / jnp.sqrt(square_sum / count + EPSILON)
+    for which, (old, new) in enumerate(((w_in, new_in), (w_out, new_out))):
+        sides = []
+        for half in range(2):
+            rows = parts[(which * blocks + place[0]) * 2 + half, :depth, :]
+            sides.append(jnp.where(place[1] == 0, rows[:shard], rows[shard:]))
+        new[...] = old[...] - scale * jnp.concatenate(sides, axis=1)
+
+
+def updated(grads, w_in, w_out):
     kinds, blocks, halves, rows, columns = grads.shape
-    around = ("x_hi", "x_lo", "y", "core")
-    grads = grads.reshape(kinds * blocks * halves, rows, columns)
-    grads = lax.all_to_all(grads, around, 0, 0)
-    grads = jnp.sum(grads.astype(jnp.float32), axis=0).astype(jnp.bfloat16)
-    grads = jnp.sum(spread(grads, "z").astype(jnp.float32), axis=0)
-    square = jnp.broadcast_to(jnp.sum(grads * grads), (8, columns))
-    depth = rows // lax.axis_size("z")
-    own = lax.dynamic_slice_in_dim(grads, lax.axis_index("z") * depth, depth, 0)
-    parts = spread(jnp.concatenate([own, square]), around)
-    square = jnp.sum(parts[:, depth, 0])
-    parts = parts.reshape(kinds, blocks, halves, depth + 8, columns)
-    block = lax.axis_index(("x_lo", "y"))
-    parts = lax.dynamic_index_in_dim(parts, block, 1, keepdims=False)
-    shard = depth // halves
-    parts = lax.dynamic_slice_in_dim(parts, lax.axis_index("core") * shard, shard, 2)
-    parts = jnp.concatenate([parts[:, 0], parts[:, 1]], axis=2)
-    return parts[0], parts[1], square
+    peers = kinds * blocks * halves
+    grads = lax.all_to_all(grads.reshape(peers, rows, columns), AROUND, 0, 0)
+    for axis in ("z_lo", "z_hi"):
+        count = lax.axis_size(axis)
+        (copies,) = on_chip(
+            sum_and_spread_kernel,
+            (jax.ShapeDtypeStruct((count, rows, columns), jnp.bfloat16),),
+            (grads,),
+            grads.size,
+        )
+        grads = lax.all_to_all(copies, axis, 0, 0)
+    depth = rows // lax.axis_size(Z)
+    (copies,) = on_chip(
+        sum_and_square_kernel,
+        (jax.ShapeDtypeStruct((peers, 2 * depth, columns), jnp.float32),),
+        (lax.axis_index(Z)[None], grads),
+        grads.size,
+        scratch=(pltpu.VMEM((rows, columns), jnp.float32),),
+        scalars=1,
+    )
+    parts = lax.all_to_all(copies, AROUND, 0, 0)
+    place = jnp.stack([lax.axis_index(("x_lo", "y")), lax.axis_index("core")])
+    shape = jax.ShapeDtypeStruct(w_in.shape, jnp.float32)
+    return on_chip(
+        functools.partial(update_kernel, blocks, float(peers * rows * columns)),
+        (shape, shape),
+        (place, parts, w_in, w_out),
+        parts.size,
+        scalars=1,
+    )
 
 
 def local(
@@ -245,15 +303,14 @@
         ),
         layer * (5 * features + hidden_units),
     )
-    share_in, share_out, square_sum = reduce_gradients(grads)
+    w_in_new, w_out_new = updated(grads, w_in, w_out)
     spreading = diffusivity * adjoint
     adjoint = (
         adjoint
         + (halo(spreading[None])[0] - 4.0 * spreading)
         + jnp.dot(back_first, w_in_b, preferred_element_type=jnp.float32)
     )
-    scale = LEARN_RATE / jnp.sqrt(square_sum / (2.0 * hidden_units * features) + EPSILON)
-    return (adjoint[None], w_in - scale * share_in, w_out - scale * share_out)
+    return adjoint[None], w_in_new, w_out_new
 
 
 def solution(mesh):

time: 191 us -> 176 us (0.921)
  other arithmetic: 11.1 us -> 3.72 us
  waiting for transfers between devices: 37.2 us -> 30 us
  Pallas kernels: 2.42 us -> 5.18 us
    all_to_all x4 -> x2, starting transfers between devices: 34.4 us -> 14.7 us  [spread(): lax.all_to_all(jnp.broadcast_to(block[None], (count,) + block.shape), axi...]
    all_to_all x4 -> x2, waiting for transfers between devices: 31 us -> 12 us  [spread(): lax.all_to_all(jnp.broadcast_to(block[None], (count,) + block.shape), axi...]
    all_to_all x0 -> x3, starting transfers between devices: none -> 17.7 us  [the longest x2 10.7 us: updated(): grads = lax.all_to_all(copies, axis, 0, 0)]
    all_to_all x0 -> x3, waiting for transfers between devices: none -> 11.7 us  [the longest x1 6.97 us: updated(): parts = lax.all_to_all(copies, AROUND, 0, 0)]
    reduce_sum x4 -> x0, other arithmetic: 5.31 us -> none  [the longest x1 2.03 us: reduce_gradients(): grads = jnp.sum(grads.astype(jnp.float32), axis=0).astype(jnp.bfloat16)]
    unnamed x27 -> x33, local copies, waits for them, and re-layouts: 0.78 us -> 3.55 us
    pallas_call x2 -> x7, Pallas kernels: 2.42 us -> 5.18 us  [on_chip(): pl.pallas_call(kernel, out_shape=outs, in_specs=[pl.BlockSpec(memory_spac...]
    broadcast_in_dim x5 -> x3, local copies, waits for them, and re-layouts: 4.57 us -> 2.18 us  [spread(): jnp.broadcast_to(block[None], (count,) + block.shape)]
  transfers between devices with their start and end apart: 16 -> 17, of which waited for: 6 -> 6; matrix products, arithmetic and copies ran while one was open for 6% -> 5% of each run, Pallas kernels for 1% -> 1%
where the time goes in v3:
time: 176 us; the launch traced here: 175 us
  starting transfers between devices  76.7 us (44%)
  blocking collectives  44.5 us (25%)
  waiting for transfers between devices  30 us (17%)
  local copies, waits for them, and re-layouts  8.54 us (5%)
  matrix products  5.45 us (3%)
  Pallas kernels  5.18 us (3%)
  other arithmetic  3.72 us (2%)
    all_to_all x1, blocking collectives, updated(): grads = lax.all_to_all(grads.reshape(peers, rows, columns), AROUND, 0, 0)  25.5 us
    ppermute x4, starting transfers between devices, halo(): far = lax.ppermute(field, TILE, pairs)  21.9 us
    ppermute x4, starting transfers between devices, halo(): edges = lax.ppermute(edges, 'x_hi', [(0, 1), (1, 0)])  14.7 us
    all_to_all x2, starting transfers between devices, spread(): lax.all_to_all(jnp.broadcast_to(block[None], (count,) + block.shape), axi...  14.7 us
    all_to_all x2, waiting for transfers between devices, spread(): lax.all_to_all(jnp.broadcast_to(block[None], (count,) + block.shape), axi...  12 us
    all_to_all x2, starting transfers between devices, updated(): grads = lax.all_to_all(copies, axis, 0, 0)  10.7 us
    all_to_all x1, blocking collectives, spread(): lax.all_to_all(jnp.broadcast_to(block[None], (count,) + block.shape), axi...  10.4 us
    all_gather x1, blocking collectives, gather_weights(): rows = lax.all_gather(rows, 'core', axis=0, tiled=True)  8.49 us
  transfers between devices with their start and end apart: 17, of which 6 were waited for; matrix products, arithmetic and copies ran while one was open for 5% of the time, Pallas kernels for 1%

profile of v3, /device:TPU:1, one launch (start us, length us, event | category | flops | bytes accessed | tf_op | source)
XLA Modules:
  0.0 175.3 jit_solution(16037637145239362140)
XLA Ops:
  0.6 0.7 copy-done.2
  1.3 0.7 copy-done.4
  2.0 0.7 copy-done.6
  2.7 8.5 %all-gather = bf16[2,4,1536]{2,1,0:T(4,128)(2,1)S(1)} all-gather(bf16[1,4,1536]{2,1,0:T(4,128)(2,1)S(1)} %bitcast.117), channel_id=1, replica_groups=mesh['x_lo'=2,'y'=4,'z_hi'=4,'z_lo'=4,'core'=2,'x_hi'=2] {'core'}, dimensions={0}, use_global_device_ids=true | all-gather | bytes 36864 | tf_op jit(solution)/shard_map/all_gather | solution.py:35
  11.2 0.7 broadcast_in_dim.40
  11.9 9.5 %all-to-all-start = ((bf16[16,8,768]{2,1,0:T(8,128)(2,1)}), bf16[16,8,768]{2,1,0:T(8,128)(2,1)S(1)}, u32[]{:S(2)}, u32[]{:S(2)}) async-start(bf16[16,8,768]{2,1,0:T(8,128)(2,1)} %broadcast_in_dim.40), calls=%async_computation | async-start | bytes 393216 | tf_op jit(solution)/shard_map/all_to_all | solution.py:24
  21.5 0.9 constant_dynamic-update-slice_fusion.1
  22.4 12.0 %all-to-all-done = bf16[16,8,768]{2,1,0:T(8,128)(2,1)S(1)} async-done(((bf16[16,8,768]{2,1,0:T(8,128)(2,1)}), bf16[16,8,768]{2,1,0:T(8,128)(2,1)S(1)}, u32[]{:S(2)}, u32[]{:S(2)}) %all-to-all-start) | async-done | bytes 196640 | tf_op jit(solution)/shard_map/all_to_all | solution.py:24
  34.4 1.3 broadcast_in_dim.42
  35.7 5.1 %all-to-all-start.1 = ((bf16[8,128,768]{2,1,0:T(8,128)(2,1)}), bf16[8,128,768]{2,1,0:T(8,128)(2,1)S(1)}, u32[]{:S(2)}, u32[]{:S(2)}) async-start(bf16[8,128,768]{2,1,0:T(8,128)(2,1)} %broadcast_in_dim.42), calls=%async_computation.1 | async-start | bytes 3145728 | tf_op jit(solution)/shard_map/all_to_all | solution.py:24
  40.9 7.6 %collective-permute-start = (f32[2,128,256]{2,1,0:T(8,128)S(1)}, f32[2,128,256]{2,1,0:T(8,128)S(1)}, u32[]{:S(2)}, u32[]{:S(2)}) collective-permute-start(f32[2,128,256]{2,1,0:T(8,128)S(1)} %get-tuple-element.48), channel_id=1, source_target_pairs={{2,4},{4,2},{6,8},{8,6},{10,12},{12,10},{14,16},{16,14},{18,20},{2... | collective-permute-start | bytes 786440 | tf_op jit(solution)/shard_map/ppermute | solution.py:54
  48.5 1.9 %collective-permute-start.1 = (f32[2,128,256]{2,1,0:T(8,128)S(1)}, f32[2,128,256]{2,1,0:T(8,128)S(1)}, u32[]{:S(2)}, u32[]{:S(2)}) collective-permute-start(f32[2,128,256]{2,1,0:T(8,128)S(1)} %get-tuple-element.48), channel_id=1, source_target_pairs={{0,2},{2,0},{1,3},{3,1},{4,6},{6,4},{5,7},{7,5},{8,10},{10,8},{9,1... | collective-permute-start | bytes 786440 | tf_op jit(solution)/shard_map/ppermute | solution.py:57
  50.5 4.4 %collective-permute-start.2 = (f32[2,2,256]{2,1,0:T(2,128)S(1)}, f32[2,2,256]{2,1,0:T(2,128)S(1)}, u32[]{:S(2)}, u32[]{:S(2)}) collective-permute-start(f32[2,2,256]{2,1,0:T(2,128)S(1)} %pad_maximum_fusion.3), channel_id=1, source_target_pairs={{0,1},{1,0},{2,3},{3,2},{4,5},{5,4},{6,7},{7,6},{8,9},{9,8},{10,11... | collective-permute-start | bytes 12296 | tf_op jit(solution)/shard_map/ppermute | solution.py:56
  54.9 0.1 copy.18.gating
  55.0 3.2 %collective-permute-done.2 = f32[2,2,256]{2,1,0:T(2,128)S(1)} collective-permute-done((f32[2,2,256]{2,1,0:T(2,128)S(1)}, f32[2,2,256]{2,1,0:T(2,128)S(1)}, u32[]{:S(2)}, u32[]{:S(2)}) %collective-permute-start.2) | collective-permute-done | bytes 4128 | tf_op jit(solution)/shard_map/ppermute | solution.py:56
  58.2 0.8 fusion.28
  59.0 0.2 broadcast_in_dim.44
  59.2 10.4 %all_to_all.35.weights = bf16[2,1024,768]{2,1,0:T(8,128)(2,1)S(1)} all-to-all(bf16[2,1024,768]{2,1,0:T(8,128)(2,1)S(1)} %broadcast_in_dim.44), channel_id=1, replica_groups=mesh['x_lo'=2,'y'=4,'z_hi'=4,'z_lo'=4,'core'=2,'x_hi'=2] {'core'}, dimensions={0} | all-to-all | bytes 6291456 | tf_op jit(solution)/shard_map/all_to_all | solution.py:24
  69.7 0.3 fusion.27
  70.0 0.1 fusion.10
  70.1 0.2 slice_bitcast_fusion.1
  70.3 0.0 copy-start.7
  70.3 0.7 fusion.1
  71.0 0.1 fusion.8
  71.1 0.3 fusion.15
  71.5 0.1 fusion.93
  71.6 6.1 %collective-permute-start.3 = (f32[1,128,256]{2,1,0:T(8,128)S(1)}, f32[1,128,256]{2,1,0:T(8,128)S(1)}, u32[]{:S(2)}, u32[]{:S(2)}) collective-permute-start(f32[1,128,256]{2,1,0:T(8,128)S(1)} %bitcast.120), channel_id=1, source_target_pairs={{2,4},{4,2},{6,8},{8,6},{10,12},{12,10},{14,16},{16,14},{18,20},{2... | collective-permute-start | bytes 393224 | tf_op jit(solution)/shard_map/ppermute | solution.py:54
  77.7 1.9 %collective-permute-start.4 = (f32[1,128,256]{2,1,0:T(8,128)S(1)}, f32[1,128,256]{2,1,0:T(8,128)S(1)}, u32[]{:S(2)}, u32[]{:S(2)}) collective-permute-start(f32[1,128,256]{2,1,0:T(8,128)S(1)} %bitcast.121), channel_id=1, source_target_pairs={{0,2},{2,0},{1,3},{3,1},{4,6},{6,4},{5,7},{7,5},{8,10},{10,8},{9,1... | collective-permute-start | bytes 393224 | tf_op jit(solution)/shard_map/ppermute | solution.py:57
  79.6 0.3 fusion.26
  79.9 0.1 fusion.6
  80.1 0.7 fusion
  80.8 0.1 fusion.4
  81.0 3.6 %collective-permute-start.5 = (f32[1,2,256]{2,1,0:T(2,128)S(1)}, f32[1,2,256]{2,1,0:T(2,128)S(1)}, u32[]{:S(2)}, u32[]{:S(2)}) collective-permute-start(f32[1,2,256]{2,1,0:T(2,128)S(1)} %pad_maximum_fusion.4), channel_id=1, source_target_pairs={{0,1},{1,0},{2,3},{3,2},{4,5},{5,4},{6,7},{7,6},{8,9},{9,8},{10,11... | collective-permute-start | bytes 6152 | tf_op jit(solution)/shard_map/ppermute | solution.py:56
  84.6 0.3 fusion.22
  84.9 1.9 %collective-permute-done.5 = f32[1,2,256]{2,1,0:T(2,128)S(1)} collective-permute-done((f32[1,2,256]{2,1,0:T(2,128)S(1)}, f32[1,2,256]{2,1,0:T(2,128)S(1)}, u32[]{:S(2)}, u32[]{:S(2)}) %collective-permute-start.5) | collective-permute-done | bytes 2080 | tf_op jit(solution)/shard_map/ppermute | solution.py:56
  86.8 0.4 fusion.3
  87.2 0.3 fusion.70.adjoint
  87.6 3.2 %collective-permute-start.6 = (f32[1,128,256]{2,1,0:T(8,128)S(1)}, f32[1,128,256]{2,1,0:T(8,128)S(1)}, u32[]{:S(2)}, u32[]{:S(2)}) collective-permute-start(f32[1,128,256]{2,1,0:T(8,128)S(1)} %fusion.74), channel_id=1, source_target_pairs={{2,4},{4,2},{6,8},{8,6},{10,12},{12,10},{14,16},{16,14},{18,20},{2... | collective-permute-start | bytes 393224 | tf_op jit(solution)/shard_map/ppermute | solution.py:54
  90.8 1.9 %collective-permute-start.7 = (f32[1,128,256]{2,1,0:T(8,128)S(1)}, f32[1,128,256]{2,1,0:T(8,128)S(1)}, u32[]{:S(2)}, u32[]{:S(2)}) collective-permute-start(f32[1,128,256]{2,1,0:T(8,128)S(1)} %fusion.74), channel_id=1, source_target_pairs={{0,2},{2,0},{1,3},{3,1},{4,6},{6,4},{5,7},{7,5},{8,10},{10,8},{9,1... | collective-permute-start | bytes 393224 | tf_op jit(solution)/shard_map/ppermute | solution.py:57
  92.8 3.6 %collective-permute-start.8 = (f32[1,2,256]{2,1,0:T(2,128)S(1)}, f32[1,2,256]{2,1,0:T(2,128)S(1)}, u32[]{:S(2)}, u32[]{:S(2)}) collective-permute-start(f32[1,2,256]{2,1,0:T(2,128)S(1)} %pad_maximum_fusion.5), channel_id=1, source_target_pairs={{0,1},{1,0},{2,3},{3,2},{4,5},{5,4},{6,7},{7,6},{8,9},{9,8},{10,11... | collective-permute-start | bytes 6152 | tf_op jit(solution)/shard_map/ppermute | solution.py:56
  96.4 1.1 shard_map.131
  97.5 1.1 collective-permute-done.8
  98.6 0.7 fusion.75
  99.4 1.3 shard_map.132
  100.7 0.7 copy-done.1
  101.4 25.5 %all_to_all.36.parts = bf16[32,128,128]{2,1,0:T(8,128)(2,1)S(1)} all-to-all(bf16[32,128,128]{2,1,0:T(8,128)(2,1)S(1)} %bitcast.116), channel_id=1, replica_groups=mesh['x_lo'=2,'y'=4,'z_hi'=4,'z_lo'=4,'core'=2,'x_hi'=2] {'x_hi','x_lo',..., dimensions={0} | all-to-all | bytes 2097152 | tf_op jit(solution)/shard_map/all_to_all | solution.py:184
  127.0 0.8 shard_map.133
  127.8 3.3 %all-to-all-start.4 = ((bf16[4,128,128]{2,1,0:T(8,128)(2,1)}), bf16[4,128,128]{2,1,0:T(8,128)(2,1)S(1)}, u32[]{:S(2)}, u32[]{:S(2)}) async-start(bf16[4,128,128]{2,1,0:T(8,128)(2,1)} %shard_map.133), calls=%async_computation.4 | async-start | bytes 262144 | tf_op jit(solution)/shard_map/all_to_all | solution.py:193
  131.1 0.1 pad_add_fusion.place
  131.2 4.8 %all-to-all-done.4.parts = bf16[4,128,128]{2,1,0:T(8,128)(2,1)S(1)} async-done(((bf16[4,128,128]{2,1,0:T(8,128)(2,1)}), bf16[4,128,128]{2,1,0:T(8,128)(2,1)S(1)}, u32[]{:S(2)}, u32[]{:S(2)}) %all-to-all-start.4) | async-done | bytes 131104 | tf_op jit(solution)/shard_map/all_to_all | solution.py:193
  135.9 0.7 shard_map.134
  136.6 7.4 %all-to-all-start.5 = ((bf16[4,128,128]{2,1,0:T(8,128)(2,1)}), bf16[4,128,128]{2,1,0:T(8,128)(2,1)S(1)}, u32[]{:S(2)}, u32[]{:S(2)}) async-start(bf16[4,128,128]{2,1,0:T(8,128)(2,1)} %shard_map.134), calls=%async_computation.5 | async-start | bytes 262144 | tf_op jit(solution)/shard_map/all_to_all | solution.py:193
  144.0 0.7 fusion.103
  144.7 0.6 pad_maximum_fusion.6
  145.3 3.2 %collective-permute-start.11 = (f32[1,2,256]{2,1,0:T(2,128)}, f32[1,2,256]{2,1,0:T(2,128)S(1)}, u32[]{:S(2)}, u32[]{:S(2)}) collective-permute-start(f32[1,2,256]{2,1,0:T(2,128)} %pad_maximum_fusion.6), channel_id=1, source_target_pairs={{0,1},{1,0},{2,3},{3,2},{4,5},{5,4},{6,7},{7,6},{8,9},{9,8},{10,11... | collective-permute-start | bytes 6152 | tf_op jit(solution)/shard_map/ppermute | solution.py:56
  148.5 1.7 fusion.102
  150.2 5.0 %collective-permute-start.9 = (f32[1,128,256]{2,1,0:T(8,128)}, f32[1,128,256]{2,1,0:T(8,128)}, u32[]{:S(2)}, u32[]{:S(2)}) collective-permute-start(f32[1,128,256]{2,1,0:T(8,128)} %get-tuple-element.17), channel_id=1, source_target_pairs={{2,4},{4,2},{6,8},{8,6},{10,12},{12,10},{14,16},{16,14},{18,20},{2... | collective-permute-start | bytes 393224 | tf_op jit(solution)/shard_map/ppermute | solution.py:54
  155.1 1.9 %collective-permute-start.10 = (f32[1,128,256]{2,1,0:T(8,128)}, f32[1,128,256]{2,1,0:T(8,128)}, u32[]{:S(2)}, u32[]{:S(2)}) collective-permute-start(f32[1,128,256]{2,1,0:T(8,128)} %get-tuple-element.17), channel_id=1, source_target_pairs={{0,2},{2,0},{1,3},{3,1},{4,6},{6,4},{5,7},{7,5},{8,10},{10,8},{9,1... | collective-permute-start | bytes 393224 | tf_op jit(solution)/shard_map/ppermute | solution.py:57
  157.1 0.1 shard_map.135
  157.1 0.7 copy-done
  157.9 7.0 %all-to-all-start.6 = ((f32[32,16,128]{2,1,0:T(8,128)}), f32[32,16,128]{2,1,0:T(8,128)S(1)}, u32[]{:S(2)}, u32[]{:S(2)}) async-start(f32[32,16,128]{2,1,0:T(8,128)} %copy-done), calls=%async_computation.6 | async-start | bytes 524288 | tf_op jit(solution)/shard_map/all_to_all | solution.py:203
  164.9 2.1 %fusion.2 = f32[1,128,256]{2,1,0:T(8,128)} fusion(bf16[128,1024]{1,0:T(8,128)(2,1)} %copy-done.1, bf16[2,1024,768]{2,1,0:T(8,128)(2,1)S(1)} %all_to_all.35.weights, f32[128,256]{1,0:T(8,128)S(1)} %get-tuple-element.18.adjoint, f32[1,1,256]{2,1,0:T(1,128)S(1)} %get-tuple-element.55, f32[1,127,256]{2,1,0:T(8,128)} %get-tuple-element.37, ...), kind=kOutput, calls=%fused_computation.4 | convolution fusion | flops 67436544 | bytes 1703936 | tf_op jit(solution)/shard_map/dot_general | solution.py:311
  167.0 7.0 %all-to-all-done.6.parts = f32[32,16,128]{2,1,0:T(8,128)S(1)} async-done(((f32[32,16,128]{2,1,0:T(8,128)}), f32[32,16,128]{2,1,0:T(8,128)S(1)}, u32[]{:S(2)}, u32[]{:S(2)}) %all-to-all-start.6) | async-done | bytes 262176 | tf_op jit(solution)/shard_map/all_to_all | solution.py:203
  174.0 1.3 shard_map.136
  (57 shorter events, 0.3 us)
Async XLA Ops:
  0.6 0.7 copy-start.2
  1.3 0.7 copy-start.4
  2.0 0.7 copy-start.6
  2.7 38.1 %copy-start.10 = (f32[1,128,256]{2,1,0:T(8,128)S(1)}, f32[1,128,256]{2,1,0:T(8,128)}, u32[]{:S(2)}) copy-start(f32[1,128,256]{2,1,0:T(8,128)} %param.12) | copy-start | bytes 393220
  11.9 22.5 %all-to-all-start = ((bf16[16,8,768]{2,1,0:T(8,128)(2,1)}), bf16[16,8,768]{2,1,0:T(8,128)(2,1)S(1)}, u32[]{:S(2)}, u32[]{:S(2)}) async-start(bf16[16,8,768]{2,1,0:T(8,128)(2,1)} %broadcast_in_dim.40), calls=%async_computation | async-start | bytes 393216 | tf_op jit(solution)/shard_map/all_to_all | solution.py:24
  34.4 20.5 %copy-start.15 = (s32[1,128]{1,0:T(1,128)S(1)}, s32[1,128]{1,0:T(1,128)}, u32[]{:S(2)}) copy-start(s32[1,128]{1,0:T(1,128)} %param.14) | copy-start | bytes 1540
  35.7 23.3 %all-to-all-start.1 = ((bf16[8,128,768]{2,1,0:T(8,128)(2,1)}), bf16[8,128,768]{2,1,0:T(8,128)(2,1)S(1)}, u32[]{:S(2)}, u32[]{:S(2)}) async-start(bf16[8,128,768]{2,1,0:T(8,128)(2,1)} %broadcast_in_dim.42), calls=%async_computation.1 | async-start | bytes 3145728 | tf_op jit(solution)/shard_map/all_to_all | solution.py:24
  40.9 17.4 %collective-permute-start = (f32[2,128,256]{2,1,0:T(8,128)S(1)}, f32[2,128,256]{2,1,0:T(8,128)S(1)}, u32[]{:S(2)}, u32[]{:S(2)}) collective-permute-start(f32[2,128,256]{2,1,0:T(8,128)S(1)} %get-tuple-element.48), channel_id=1, source_target_pairs={{2,4},{4,2},{6,8},{8,6},{10,12},{12,10},{14,16},{16,14},{18,20},{2... | collective-permute-start | bytes 786440 | tf_op jit(solution)/shard_map/ppermute | solution.py:54
  48.5 9.7 %collective-permute-start.1 = (f32[2,128,256]{2,1,0:T(8,128)S(1)}, f32[2,128,256]{2,1,0:T(8,128)S(1)}, u32[]{:S(2)}, u32[]{:S(2)}) collective-permute-start(f32[2,128,256]{2,1,0:T(8,128)S(1)} %get-tuple-element.48), channel_id=1, source_target_pairs={{0,2},{2,0},{1,3},{3,1},{4,6},{6,4},{5,7},{7,5},{8,10},{10,8},{9,1... | collective-permute-start | bytes 786440 | tf_op jit(solution)/shard_map/ppermute | solution.py:57
  50.5 7.8 %collective-permute-start.2 = (f32[2,2,256]{2,1,0:T(2,128)S(1)}, f32[2,2,256]{2,1,0:T(2,128)S(1)}, u32[]{:S(2)}, u32[]{:S(2)}) collective-permute-start(f32[2,2,256]{2,1,0:T(2,128)S(1)} %pad_maximum_fusion.3), channel_id=1, source_target_pairs={{0,1},{1,0},{2,3},{3,2},{4,5},{5,4},{6,7},{7,6},{8,9},{9,8},{10,11... | collective-permute-start | bytes 12296 | tf_op jit(solution)/shard_map/ppermute | solution.py:56
  70.3 1.2 copy-start.7
  70.3 1.2 copy-start.8
  70.3 1.2 copy-start.9
  71.6 15.2 %collective-permute-start.3 = (f32[1,128,256]{2,1,0:T(8,128)S(1)}, f32[1,128,256]{2,1,0:T(8,128)S(1)}, u32[]{:S(2)}, u32[]{:S(2)}) collective-permute-start(f32[1,128,256]{2,1,0:T(8,128)S(1)} %bitcast.120), channel_id=1, source_target_pairs={{2,4},{4,2},{6,8},{8,6},{10,12},{12,10},{14,16},{16,14},{18,20},{2... | collective-permute-start | bytes 393224 | tf_op jit(solution)/shard_map/ppermute | solution.py:54
  77.7 9.1 %collective-permute-start.4 = (f32[1,128,256]{2,1,0:T(8,128)S(1)}, f32[1,128,256]{2,1,0:T(8,128)S(1)}, u32[]{:S(2)}, u32[]{:S(2)}) collective-permute-start(f32[1,128,256]{2,1,0:T(8,128)S(1)} %bitcast.121), channel_id=1, source_target_pairs={{0,2},{2,0},{1,3},{3,1},{4,6},{6,4},{5,7},{7,5},{8,10},{10,8},{9,1... | collective-permute-start | bytes 393224 | tf_op jit(solution)/shard_map/ppermute | solution.py:57
  80.8 6.0 %copy-start.11 = (s32[64]{0:T(128)S(1)}, s32[64]{0:T(128)}, u32[]{:S(2)}) copy-start(s32[64]{0:T(128)} %param.19) | copy-start | bytes 772
  80.8 6.0 %copy-start.12 = (s32[64]{0:T(128)S(1)}, s32[64]{0:T(128)}, u32[]{:S(2)}) copy-start(s32[64]{0:T(128)} %param.18) | copy-start | bytes 772
  80.8 6.4 %copy-start.13 = (f32[64]{0:T(128)S(1)}, f32[64]{0:T(128)}, u32[]{:S(2)}) copy-start(f32[64]{0:T(128)} %param.21) | copy-start | bytes 772
  80.8 6.4 %copy-start.14 = (f32[64]{0:T(128)S(1)}, f32[64]{0:T(128)}, u32[]{:S(2)}) copy-start(f32[64]{0:T(128)} %param.20) | copy-start | bytes 772
  81.0 5.8 %collective-permute-start.5 = (f32[1,2,256]{2,1,0:T(2,128)S(1)}, f32[1,2,256]{2,1,0:T(2,128)S(1)}, u32[]{:S(2)}, u32[]{:S(2)}) collective-permute-start(f32[1,2,256]{2,1,0:T(2,128)S(1)} %pad_maximum_fusion.4), channel_id=1, source_target_pairs={{0,1},{1,0},{2,3},{3,2},{4,5},{5,4},{6,7},{7,6},{8,9},{9,8},{10,11... | collective-permute-start | bytes 6152 | tf_op jit(solution)/shard_map/ppermute | solution.py:56
  87.6 11.0 %collective-permute-start.6 = (f32[1,128,256]{2,1,0:T(8,128)S(1)}, f32[1,128,256]{2,1,0:T(8,128)S(1)}, u32[]{:S(2)}, u32[]{:S(2)}) collective-permute-start(f32[1,128,256]{2,1,0:T(8,128)S(1)} %fusion.74), channel_id=1, source_target_pairs={{2,4},{4,2},{6,8},{8,6},{10,12},{12,10},{14,16},{16,14},{18,20},{2... | collective-permute-start | bytes 393224 | tf_op jit(solution)/shard_map/ppermute | solution.py:54
  90.8 7.8 %collective-permute-start.7 = (f32[1,128,256]{2,1,0:T(8,128)S(1)}, f32[1,128,256]{2,1,0:T(8,128)S(1)}, u32[]{:S(2)}, u32[]{:S(2)}) collective-permute-start(f32[1,128,256]{2,1,0:T(8,128)S(1)} %fusion.74), channel_id=1, source_target_pairs={{0,2},{2,0},{1,3},{3,1},{4,6},{6,4},{5,7},{7,5},{8,10},{10,8},{9,1... | collective-permute-start | bytes 393224 | tf_op jit(solution)/shard_map/ppermute | solution.py:57
  92.8 5.8 %collective-permute-start.8 = (f32[1,2,256]{2,1,0:T(2,128)S(1)}, f32[1,2,256]{2,1,0:T(2,128)S(1)}, u32[]{:S(2)}, u32[]{:S(2)}) collective-permute-start(f32[1,2,256]{2,1,0:T(2,128)S(1)} %pad_maximum_fusion.5), channel_id=1, source_target_pairs={{0,1},{1,0},{2,3},{3,2},{4,5},{5,4},{6,7},{7,6},{8,9},{9,8},{10,11... | collective-permute-start | bytes 6152 | tf_op jit(solution)/shard_map/ppermute | solution.py:56
  100.7 0.7 copy-start.1
  101.4 72.6 %copy-start.3 = (f32[4,256]{1,0:T(4,128)S(1)}, f32[4,256]{1,0:T(4,128)}, u32[]{:S(2)}) copy-start(f32[4,256]{1,0:T(4,128)} %w_in.3) | copy-start | bytes 12292
  101.4 72.6 %copy-start.5 = (f32[4,256]{1,0:T(4,128)S(1)}, f32[4,256]{1,0:T(4,128)}, u32[]{:S(2)}) copy-start(f32[4,256]{1,0:T(4,128)} %w_out.3) | copy-start | bytes 12292
  127.8 8.2 %all-to-all-start.4 = ((bf16[4,128,128]{2,1,0:T(8,128)(2,1)}), bf16[4,128,128]{2,1,0:T(8,128)(2,1)S(1)}, u32[]{:S(2)}, u32[]{:S(2)}) async-start(bf16[4,128,128]{2,1,0:T(8,128)(2,1)} %shard_map.133), calls=%async_computation.4 | async-start | bytes 262144 | tf_op jit(solution)/shard_map/all_to_all | solution.py:193
  136.6 20.5 %all-to-all-start.5 = ((bf16[4,128,128]{2,1,0:T(8,128)(2,1)}), bf16[4,128,128]{2,1,0:T(8,128)(2,1)S(1)}, u32[]{:S(2)}, u32[]{:S(2)}) async-start(bf16[4,128,128]{2,1,0:T(8,128)(2,1)} %shard_map.134), calls=%async_computation.5 | async-start | bytes 262144 | tf_op jit(solution)/shard_map/all_to_all | solution.py:193
  145.3 19.6 %collective-permute-start.11 = (f32[1,2,256]{2,1,0:T(2,128)}, f32[1,2,256]{2,1,0:T(2,128)S(1)}, u32[]{:S(2)}, u32[]{:S(2)}) collective-permute-start(f32[1,2,256]{2,1,0:T(2,128)} %pad_maximum_fusion.6), channel_id=1, source_target_pairs={{0,1},{1,0},{2,3},{3,2},{4,5},{5,4},{6,7},{7,6},{8,9},{9,8},{10,11... | collective-permute-start | bytes 6152 | tf_op jit(solution)/shard_map/ppermute | solution.py:56
  150.2 14.8 %collective-permute-start.9 = (f32[1,128,256]{2,1,0:T(8,128)}, f32[1,128,256]{2,1,0:T(8,128)}, u32[]{:S(2)}, u32[]{:S(2)}) collective-permute-start(f32[1,128,256]{2,1,0:T(8,128)} %get-tuple-element.17), channel_id=1, source_target_pairs={{2,4},{4,2},{6,8},{8,6},{10,12},{12,10},{14,16},{16,14},{18,20},{2... | collective-permute-start | bytes 393224 | tf_op jit(solution)/shard_map/ppermute | solution.py:54
  155.1 9.8 %collective-permute-start.10 = (f32[1,128,256]{2,1,0:T(8,128)}, f32[1,128,256]{2,1,0:T(8,128)}, u32[]{:S(2)}, u32[]{:S(2)}) collective-permute-start(f32[1,128,256]{2,1,0:T(8,128)} %get-tuple-element.17), channel_id=1, source_target_pairs={{0,2},{2,0},{1,3},{3,1},{4,6},{6,4},{5,7},{7,5},{8,10},{10,8},{9,1... | collective-permute-start | bytes 393224 | tf_op jit(solution)/shard_map/ppermute | solution.py:57
  157.1 0.7 copy-start
  157.9 16.1 %all-to-all-start.6 = ((f32[32,16,128]{2,1,0:T(8,128)}), f32[32,16,128]{2,1,0:T(8,128)S(1)}, u32[]{:S(2)}, u32[]{:S(2)}) async-start(f32[32,16,128]{2,1,0:T(8,128)} %copy-done), calls=%async_computation.6 | async-start | bytes 524288 | tf_op jit(solution)/shard_map/all_to_all | solution.py:203

commit v4 on v3

--- a/solution.py
+++ b/solution.py
@@ -17,6 +17,7 @@
 Z = ("z_hi", "z_lo")
 TILE = ("x_lo", "y", "z_hi", "z_lo", "core")
 AROUND = ("x_hi", "x_lo", "y", "core")
+REACH = 3
 
 
 def spread(block, axis):
@@ -37,26 +38,26 @@
     half = lax.dynamic_slice_in_dim(rows, lax.axis_index("core") * width, width, 1)
     half = spread(half, Z).reshape(-1, width)
     half = spread(half, ("x_lo", "y")).reshape(-1, width)
-    both = spread(half, "core")
-    features = w_in.shape[1]
-    w_in_all = both[0, :, :features]
-    w_mid_all = jnp.concatenate([both[0, :, features:], both[1, :, :-features]], axis=1)
-    return both, w_in_all, w_mid_all, both[1, :, -features:]
-
-
-def halo(field):
-    count = 1
-    for axis in TILE:
-        count *= lax.axis_size(axis)
+    return spread(half, "core")
+
+
+def swapped(array, axis):
+    return lax.ppermute(array, axis, [(0, 1), (1, 0)])
+
+
+def swapped_between_chips(array):
     pairs = []
-    for row in range(1, count - 1, 2):
+    for row in range(1, lax.axis_size(TILE) - 1, 2):
         pairs += [(row, row + 1), (row + 1, row)]
-    far = lax.ppermute(field, TILE, pairs)
-    edges = jnp.concatenate([field[:, :1], field[:, -1:]], axis=1)
-    edges = lax.ppermute(edges, "x_hi", [(0, 1), (1, 0)])
-    near = lax.ppermute(field, "core", [(0, 1), (1, 0)])
-    east = jnp.concatenate([field[:, 1:], edges[:, :1]], axis=1)
-    west = jnp.concatenate([edges[:, 1:], field[:, :-1]], axis=1)
+    return lax.ppermute(array, TILE, pairs)
+
+
+def neighbour_sum(field):
+    far = swapped_between_chips(field)
+    edges = swapped(jnp.concatenate([field[:1], field[-1:]]), "x_hi")
+    near = swapped(field, "core")
+    east = jnp.concatenate([field[1:], edges[:1]])
+    west = jnp.concatenate([edges[1:], field[:-1]])
     return far + near + east + west
 
 
@@ -83,19 +84,20 @@
     return (slope_one * back_one).astype(jnp.bfloat16)
 
 
-def last_step_kernel(adjoint, gating, hidden_one, hidden_two, weights, source_out, one_out, back):
-    source = (gating[...] * adjoint[...]).astype(jnp.bfloat16)
-    source_out[...] = source
-    back_one = adjoint_layers(source, hidden_one[...], hidden_two[...], weights)
+def last_step_kernel(source, hidden_one, hidden_two, weights, one_out, back):
+    features = source.shape[1]
+    back_one = adjoint_layers(source[...], hidden_one[...], hidden_two[...], weights)
     one_out[...] = back_one
-    back[...] = jnp.dot(
-        back_one, weights[0, :, : source.shape[1]], preferred_element_type=jnp.float32
-    )
+    back[...] = jnp.dot(back_one, weights[0, :, :features], preferred_element_type=jnp.float32)
 
 
 def first_step_kernel(
-    adjoint,
+    partial,
+    near,
+    far,
+    back,
     gating,
+    diffusivity,
     hidden_one,
     hidden_two,
     states,
@@ -104,10 +106,15 @@
     hidden_late,
     states_late,
     weights,
+    adjoint_out,
+    spreading_out,
     one_out,
     grads,
 ):
-    source = (gating[...] * adjoint[...]).astype(jnp.bfloat16)
+    adjoint = partial[...] + (near[...] + far[...]) + back[...]
+    adjoint_out[...] = adjoint
+    spreading_out[...] = diffusivity[...] * adjoint
+    source = (gating[...] * adjoint).astype(jnp.bfloat16)
     back_one = adjoint_layers(source, hidden_one[...], hidden_two[...], weights)
     one_out[...] = back_one
     pairs = (
@@ -127,6 +134,163 @@
                 grads[which, block, half] = total[
                     block * rows : (block + 1) * rows, half * columns : (half + 1) * columns
                 ]
+
+
+def edge_kernel(state, increment, diffusivity, land_sea, col, lev, val, prec, edges):
+    edges[...] = jnp.zeros_like(edges)
+    cells = state.shape[1]
+    for which, field in enumerate((state, increment, diffusivity)):
+        start = 2 * REACH * which
+        edges[start : start + REACH] = field[0, :REACH]
+        edges[start + REACH : start + 2 * REACH] = field[0, cells - REACH :]
+    edges[18:19, :cells] = 0.5 + land_sea[...].astype(jnp.float32)
+    count = col.shape[1]
+    for row, numbers in enumerate((col, lev, val, prec)):
+        edges[19 + row : 20 + row, :count] = numbers[...].astype(jnp.float32)
+
+
+def widen_kernel(state, increment, diffusivity, land_sea, edges, wide):
+    cells = state.shape[1]
+    length = cells + 8
+    for which, field in enumerate((state, increment, diffusivity)):
+        base, start = length * which, 2 * REACH * which
+        wide[base : base + cells] = field[0]
+        wide[base + cells : base + length] = jnp.zeros((8, field.shape[2]), jnp.float32)
+        wide[base + cells : base + cells + REACH] = edges[start : start + REACH]
+        wide[base + length - REACH : base + length] = edges[start + REACH : start + 2 * REACH]
+    own = 0.5 + land_sea[...].astype(jnp.float32)
+    other = jnp.broadcast_to(edges[18:19, :cells], (8, cells))
+    lane = lax.broadcasted_iota(jnp.int32, (8, cells), 1)
+    other = jnp.where(lane < REACH, other, pltpu.roll(other, 8, 1))
+    wide[3 * length :, :cells] = jnp.broadcast_to(own, (8, cells))
+    wide[3 * length :, cells:] = other
+
+
+def forward_kernel(
+    own,
+    near,
+    far,
+    beyond,
+    edges,
+    col,
+    lev,
+    val,
+    prec,
+    weights,
+    first_one,
+    first_two,
+    first_states,
+    last_one,
+    last_two,
+    last_states,
+    source,
+    gating_out,
+    spreading_out,
+    partial,
+):
+    cells, features = first_states.shape
+    depth = weights.shape[2] - features
+    length = cells + 8
+    counted = (length, own.shape[1])
+    diagonal = lax.broadcasted_iota(jnp.int32, counted, 0) == lax.broadcasted_iota(
+        jnp.int32, counted, 1
+    )
+
+    def row(ref, which):
+        return ref[which * length : (which + 1) * length, :]
+
+    def gating(ref):
+        return jnp.sum(
+            jnp.where(diagonal, ref[3 * length : 3 * length + 1, :], 0.0), axis=1, keepdims=True
+        )
+
+    def laplace(field, lat):
+        return (
+            lat + pltpu.roll(field, 1, 0) + pltpu.roll(field, length - 1, 0) - 4.0 * field
+        )
+
+    def activate(both):
+        hidden = jnp.tanh(both[:length]).astype(jnp.bfloat16).astype(jnp.float32)
+        tangent = (1.0 - hidden * hidden) * both[length:]
+        return jnp.concatenate([hidden, tangent]).astype(jnp.bfloat16)
+
+    def network(states, tangents, saved=None):
+        stacked = jnp.concatenate([states, tangents]).astype(jnp.bfloat16)
+        one = activate(
+            lax.dot_general(
+                stacked,
+                weights[0, :, :features],
+                CONTRACT_LAST,
+                preferred_element_type=jnp.float32,
+            )
+        )
+        low = activate(jnp.dot(one, weights[0, :, features:], preferred_element_type=jnp.float32))
+        high = activate(jnp.dot(one, weights[1, :, :depth], preferred_element_type=jnp.float32))
+        if saved is not None:
+            saved[0][...] = one[:cells]
+            saved[1][:, :depth] = low[:cells]
+            saved[1][:, depth:] = high[:cells]
+            saved[2][...] = stacked[:cells]
+        out = jnp.dot(
+            low, weights[1, :depth, depth:], preferred_element_type=jnp.float32
+        ) + jnp.dot(high, weights[1, depth:, depth:], preferred_element_type=jnp.float32)
+        return out[:length], out[length:]
+
+    gate, diffuse = gating(own), row(own, 2)
+    states, tangents = row(own, 0), row(own, 1)
+    tend, tangent = network(states, tangents, (first_one, first_two, first_states))
+    state_one = states + diffuse * laplace(states, row(near, 0) + row(far, 0)) + gate * tend
+    increment_one = (
+        tangents + diffuse * laplace(tangents, row(near, 1) + row(far, 1)) + gate * tangent
+    )
+    middle = states + tangents
+    lat = jnp.zeros_like(middle)
+    for ref, outer, start in ((near, beyond, 0), (far, far, 3 * length + 8)):
+        states, tangents = row(ref, 0), row(ref, 1)
+        both = states + tangents
+        outside = outer[start : start + length, :] + outer[start + length : start + 2 * length, :]
+        tend, tangent = network(states, tangents)
+        lat = lat + (
+            both
+            + row(ref, 2) * laplace(both, middle + outside)
+            + gating(ref) * (tend + tangent)
+        )
+    tend, tangent = network(state_one, increment_one, (last_one, last_two, last_states))
+    final = state_one + increment_one
+    final = final + diffuse * laplace(final, lat) + gate * (tend + tangent)
+
+    count = col.shape[1]
+    columns = edges[19:20, :count]
+    columns = jnp.where(
+        columns == 0.0, float(cells), jnp.where(columns == cells - 1.0, length - 1.0, -1.0)
+    )
+    columns = jnp.concatenate([col[...].astype(jnp.float32), columns], axis=1)
+    chosen = [lev, val, prec]
+    chosen = [
+        jnp.concatenate([here[...].astype(jnp.float32), edges[20 + i : 21 + i, :count]], axis=1)
+        for i, here in enumerate(chosen)
+    ]
+    cell_ids = lax.broadcasted_iota(jnp.int32, (length, 2 * count), 0).astype(jnp.float32)
+    level_ids = lax.broadcasted_iota(jnp.int32, (features, 2 * count), 0).astype(jnp.float32)
+    pick_cell = (cell_ids == columns).astype(jnp.float32)
+    pick_level = (level_ids == chosen[0]).astype(jnp.float32)
+    at_level = jnp.dot(
+        final, pick_level, precision=lax.Precision.HIGHEST, preferred_element_type=jnp.float32
+    )
+    modelled = jnp.sum(pick_cell * at_level, axis=0, keepdims=True)
+    weighted = chosen[2] * (modelled - chosen[1])
+    adjoint = lax.dot_general(
+        pick_cell * weighted,
+        pick_level,
+        CONTRACT_LAST,
+        precision=lax.Precision.HIGHEST,
+        preferred_element_type=jnp.float32,
+    )
+    spreading = diffuse * adjoint
+    spreading_out[...] = spreading[:cells]
+    partial[...] = (adjoint + laplace(spreading, jnp.zeros_like(spreading)))[:cells]
+    source[...] = (gate * adjoint)[:cells].astype(jnp.bfloat16)
+    gating_out[...] = gate[:cells]
 
 
 def on_chip(kernel, outs, operands, flops, scratch=(), scalars=0):
@@ -216,99 +380,91 @@
     state, increment, diffusivity, land_sea, w_in, w_mid, w_out, obs_col, obs_lev, obs_val, obs_prec
 ):
     _, cells, features = state.shape
-    current, increment_now, diffusivity = state[0], increment[0], diffusivity[0]
-    pair_sum = halo(jnp.stack([current, increment_now]))
-    weights, w_in_b, w_mid_all, w_out_b = gather_weights(w_in, w_mid, w_out)
-    hidden_units = w_in_b.shape[0]
-    gating = (0.5 + land_sea.astype(jnp.float32)).reshape(cells, 1)
-    saved = []
-
-    def network(current, increment_now):
-        states_b = current.astype(jnp.bfloat16)
-        stacked = jnp.concatenate([states_b, increment_now.astype(jnp.bfloat16)])
-        one = lax.dot_general(stacked, w_in_b, CONTRACT_LAST, preferred_element_type=jnp.float32)
-        hidden_one = jnp.tanh(one[:cells]).astype(jnp.bfloat16)
-        slope_one = 1.0 - jnp.square(hidden_one.astype(jnp.float32))
-        tangent_one = (slope_one * one[cells:]).astype(jnp.bfloat16)
-        two = jnp.dot(
-            jnp.concatenate([hidden_one, tangent_one]),
-            w_mid_all,
-            preferred_element_type=jnp.float32,
-        )
-        hidden_two = jnp.tanh(two[:cells]).astype(jnp.bfloat16)
-        slope_two = 1.0 - jnp.square(hidden_two.astype(jnp.float32))
-        tangent_two = (slope_two * two[cells:]).astype(jnp.bfloat16)
-        out = jnp.dot(
-            jnp.concatenate([hidden_two, tangent_two]),
-            w_out_b,
-            preferred_element_type=jnp.float32,
-        )
-        saved.append((states_b, hidden_one, hidden_two))
-        return gating * out[:cells], gating * out[cells:]
-
-    tend, tangent = network(current, increment_now)
-    current = current + diffusivity * (pair_sum[0] - 4.0 * current) + tend
-    increment_now = increment_now + diffusivity * (pair_sum[1] - 4.0 * increment_now) + tangent
-    final = current + increment_now
-    final_sum = halo(final[None])[0]
-    tend, tangent = network(current, increment_now)
-    final = final + diffusivity * (final_sum - 4.0 * final) + (tend + tangent)
-
-    cell_ids = jnp.arange(cells, dtype=jnp.int32)
-    level_ids = jnp.arange(features, dtype=jnp.int32)
-    pick_cell = (obs_col[:, None] == cell_ids[None, :]).astype(jnp.float32)
-    pick_level = (obs_lev[:, None] == level_ids[None, :]).astype(jnp.float32)
-    modelled = jnp.sum(
-        jnp.dot(pick_cell, final, precision=lax.Precision.HIGHEST) * pick_level, axis=1
-    )
-    weighted = obs_prec * (modelled - obs_val)
-    adjoint = lax.dot_general(
-        pick_cell, weighted[:, None] * pick_level, CONTRACT_FIRST, precision=lax.Precision.HIGHEST
-    )
-    states_late, one_late, two_late = saved[1]
-    states_b, hidden_one, hidden_two = saved[0]
-    spreading = diffusivity * adjoint
-    spread_sum = halo(spreading[None])[0]
-    wide = jax.ShapeDtypeStruct((cells, hidden_units), jnp.bfloat16)
-    narrow = jax.ShapeDtypeStruct((cells, features), jnp.float32)
+    length = cells + 8
+    fields = (state, increment, diffusivity, land_sea)
+    observed = [numbers[None] for numbers in (obs_col, obs_lev, obs_val, obs_prec)]
+
+    def outs(*shapes):
+        return tuple(jax.ShapeDtypeStruct(shape, kind) for shape, kind in shapes)
+
+    (edges,) = on_chip(
+        edge_kernel, outs(((24, features), jnp.float32)), fields + tuple(observed), 0
+    )
+    edges = swapped(edges, "x_hi")
+    (own,) = on_chip(
+        widen_kernel, outs(((3 * length + 8, features), jnp.float32)), fields + (edges,), 0
+    )
+    near = swapped(own, "core")
+    far = swapped_between_chips(jnp.concatenate([own, near[: 2 * length]]))
+    beyond = swapped(far[: 2 * length], "core")
+
+    weights = gather_weights(w_in, w_mid, w_out)
+    hidden_units = weights.shape[1]
     layer = 2 * cells * hidden_units
-    source_late, back_late, back_sum = on_chip(
+    wide = ((cells, hidden_units), jnp.bfloat16)
+    narrow_b = ((cells, features), jnp.bfloat16)
+    narrow = ((cells, features), jnp.float32)
+    (
+        hidden_one,
+        hidden_two,
+        states_b,
+        late_one,
+        late_two,
+        states_late,
+        source_late,
+        gating,
+        spreading,
+        partial,
+    ) = on_chip(
+        forward_kernel,
+        outs(
+            wide, wide, narrow_b, wide, wide, narrow_b, narrow_b, ((cells, 1), jnp.float32),
+            narrow, narrow,
+        ),
+        (own, near, far, beyond, edges, *observed, weights),
+        8 * layer * (2 * features + hidden_units),
+    )
+    near = swapped(spreading, "core")
+    far = swapped_between_chips(spreading)
+    back_late, back_sum = on_chip(
         last_step_kernel,
-        (jax.ShapeDtypeStruct((cells, features), jnp.bfloat16), wide, narrow),
-        (adjoint, gating, one_late, two_late, weights),
+        outs(wide, narrow),
+        (source_late, late_one, late_two, weights),
         layer * (2 * features + hidden_units),
     )
-    adjoint = adjoint + (spread_sum - 4.0 * spreading) + back_sum
     blocks = lax.axis_size(("x_lo", "y"))
     halves = lax.axis_size("core")
-    back_first, grads = on_chip(
+    adjoint, spreading, back_first, grads = on_chip(
         first_step_kernel,
-        (
+        outs(
+            narrow,
+            narrow,
             wide,
-            jax.ShapeDtypeStruct(
-                (2, blocks, halves, hidden_units // blocks, features // halves), jnp.bfloat16
-            ),
+            ((2, blocks, halves, hidden_units // blocks, features // halves), jnp.bfloat16),
         ),
         (
-            adjoint,
+            partial,
+            near,
+            far,
+            back_sum,
             gating,
+            diffusivity[0],
             hidden_one,
             hidden_two,
             states_b,
             source_late,
             back_late,
-            two_late,
+            late_two,
             states_late,
             weights,
         ),
         layer * (5 * features + hidden_units),
     )
     w_in_new, w_out_new = updated(grads, w_in, w_out)
-    spreading = diffusivity * adjoint
     adjoint = (
         adjoint
-        + (halo(spreading[None])[0] - 4.0 * spreading)
-        + jnp.dot(back_first, w_in_b, preferred_element_type=jnp.float32)
+        + (neighbour_sum(spreading) - 4.0 * spreading)
+        + jnp.dot(back_first, weights[0, :, :features], preferred_element_type=jnp.float32)
     )
     return adjoint[None], w_in_new, w_out_new
 

time: 176 us -> 175 us (level)
  starting transfers between devices: 76.7 us -> 65.2 us
  waiting for transfers between devices: 30 us -> 40.7 us
  local copies, waits for them, and re-layouts: 8.54 us -> 19.1 us
  blocking collectives: 44.5 us -> 35 us
  Pallas kernels: 5.18 us -> 10.2 us
  matrix products: 5.45 us -> 2.1 us
  other arithmetic: 3.72 us -> 0.71 us
    ppermute x12 -> x9, starting transfers between devices: 44.3 us -> 28 us  [the longest x6 17.4 us: swapped(): return lax.ppermute(array, axis, [(0, 1), (1, 0)])]
    all_to_all x1 -> x0, blocking collectives: 10.4 us -> none  [spread(): lax.all_to_all(jnp.broadcast_to(block[None], (count,) + block.shape), axi...]
    unnamed x33 -> x59, local copies, waits for them, and re-layouts: 3.55 us -> 13.7 us
    ppermute x12 -> x9, waiting for transfers between devices: 6.26 us -> 14.1 us  [the longest x3 12.4 us: swapped_between_chips(): return lax.ppermute(array, TILE, pairs)]
    all_to_all x2 -> x3, starting transfers between devices: 14.7 us -> 19.9 us  [spread(): lax.all_to_all(jnp.broadcast_to(block[None], (count,) + block.shape), axi...]
    pallas_call x7 -> x10, Pallas kernels: 5.18 us -> 10.2 us  [on_chip(): pl.pallas_call(kernel, out_shape=outs, in_specs=[pl.BlockSpec(memory_spac...]
    dot_general x9 -> x1, matrix products: 5.45 us -> 2.1 us  [local(): jnp.dot(back_first, weights[0, :, :features], preferred_element_type=jnp....]
    all_to_all x2 -> x3, waiting for transfers between devices: 12 us -> 14.1 us  [spread(): lax.all_to_all(jnp.broadcast_to(block[None], (count,) + block.shape), axi...]
  transfers between devices with their start and end apart: 17 -> 15, of which waited for: 6 -> 8; matrix products, arithmetic and copies ran while one was open for 5% -> 4% of each run, Pallas kernels for 1% -> 1%
where the time goes in v4:
time: 175 us; the launch traced here: 174 us
  starting transfers between devices  65.2 us (37%)
  waiting for transfers between devices  40.7 us (23%)
  blocking collectives  35 us (20%)
  local copies, waits for them, and re-layouts  19.1 us (11%)
  Pallas kernels  10.2 us (6%)
  matrix products  2.1 us (1%)
    all_to_all x1, blocking collectives, updated(): grads = lax.all_to_all(grads.reshape(peers, rows, columns), AROUND, 0, 0)  26.7 us
    all_to_all x3, starting transfers between devices, spread(): lax.all_to_all(jnp.broadcast_to(block[None], (count,) + block.shape), axi...  19.9 us
    ppermute x6, starting transfers between devices, swapped(): return lax.ppermute(array, axis, [(0, 1), (1, 0)])  17.4 us
    all_to_all x3, waiting for transfers between devices, spread(): lax.all_to_all(jnp.broadcast_to(block[None], (count,) + block.shape), axi...  14.1 us
    unnamed x59, local copies, waits for them, and re-layouts  13.7 us
    ppermute x3, waiting for transfers between devices, swapped_between_chips(): return lax.ppermute(array, TILE, pairs)  12.4 us
    ppermute x3, starting transfers between devices, swapped_between_chips(): return lax.ppermute(array, TILE, pairs)  10.6 us
    pallas_call x10, Pallas kernels, on_chip(): pl.pallas_call(kernel, out_shape=outs, in_specs=[pl.BlockSpec(memory_spac...  10.2 us
  transfers between devices with their start and end apart: 15, of which 8 were waited for; matrix products, arithmetic and copies ran while one was open for 4% of the time, Pallas kernels for 1%

profile of v4, /device:TPU:1, one launch (start us, length us, event | category | flops | bytes accessed | tf_op | source)
XLA Modules:
  0.0 174.1 jit_solution(6626826565697438091)
XLA Ops:
  0.6 0.0 copy-start.15
  0.6 0.7 copy-done.15
  1.3 0.7 copy-done.17
  2.0 0.7 copy-done.19
  2.7 8.4 %all-gather = bf16[2,4,1536]{2,1,0:T(4,128)(2,1)S(1)} all-gather(bf16[1,4,1536]{2,1,0:T(4,128)(2,1)S(1)} %bitcast.22), channel_id=1, replica_groups=mesh['x_lo'=2,'y'=4,'z_hi'=4,'z_lo'=4,'core'=2,'x_hi'=2] {'core'}, dimensions={0}, use_global_device_ids=true | all-gather | bytes 36864 | tf_op jit(solution)/shard_map/all_gather | solution.py:36
  11.1 0.7 broadcast_in_dim.42
  11.8 9.5 %all-to-all-start = ((bf16[16,8,768]{2,1,0:T(8,128)(2,1)}), bf16[16,8,768]{2,1,0:T(8,128)(2,1)S(1)}, u32[]{:S(2)}, u32[]{:S(2)}) async-start(bf16[16,8,768]{2,1,0:T(8,128)(2,1)} %broadcast_in_dim.42), calls=%async_computation | async-start | bytes 393216 | tf_op jit(solution)/shard_map/all_to_all | solution.py:25
  21.4 0.0 copy-start.2
  21.4 0.9 copy-done.2
  22.3 0.9 copy-done.5
  23.2 0.9 copy-done.7
  24.1 0.7 copy-done.20
  24.7 0.7 copy-done.21
  25.4 0.7 copy-done.23
  26.0 0.7 copy-done.25
  26.7 0.7 copy-done.27
  27.4 4.7 %collective-permute-start = (f32[24,256]{1,0:T(8,128)S(1)}, f32[24,256]{1,0:T(8,128)S(1)}, u32[]{:S(2)}, u32[]{:S(2)}) collective-permute-start(f32[24,256]{1,0:T(8,128)S(1)} %shard_map.130), channel_id=1, source_target_pairs={{0,1},{1,0},{2,3},{3,2},{4,5},{5,4},{6,7},{7,6},{8,9},{9,8},{10,11... | collective-permute-start | bytes 73736 | tf_op jit(solution)/shard_map/ppermute | solution.py:45
  32.0 1.7 collective-permute-done.edges
  33.7 0.9 copy-done.6
  34.6 0.9 copy-done.8
  35.5 0.1 shard_map.131.own
  35.6 3.4 %collective-permute-start.1 = (f32[416,256]{1,0:T(8,128)S(1)}, f32[416,256]{1,0:T(8,128)S(1)}, u32[]{:S(2)}, u32[]{:S(2)}) collective-permute-start(f32[416,256]{1,0:T(8,128)S(1)} %shard_map.131.own), channel_id=1, source_target_pairs={{0,2},{2,0},{1,3},{3,1},{4,6},{6,4},{5,7},{7,5},{8,10},{10,8},{9,1... | collective-permute-start | bytes 1277960 | tf_op jit(solution)/shard_map/ppermute | solution.py:45
  39.0 1.3 broadcast_in_dim.44
  40.3 5.1 %all-to-all-start.1 = ((bf16[8,128,768]{2,1,0:T(8,128)(2,1)}), bf16[8,128,768]{2,1,0:T(8,128)(2,1)S(1)}, u32[]{:S(2)}, u32[]{:S(2)}) async-start(bf16[8,128,768]{2,1,0:T(8,128)(2,1)} %broadcast_in_dim.44), calls=%async_computation.1 | async-start | bytes 3145728 | tf_op jit(solution)/shard_map/all_to_all | solution.py:25
  45.6 3.7 %collective-permute-start.2 = (f32[688,256]{1,0:T(8,128)S(1)}, f32[688,256]{1,0:T(8,128)S(1)}, u32[]{:S(2)}, u32[]{:S(2)}) collective-permute-start(f32[688,256]{1,0:T(8,128)S(1)} %pad_maximum_fusion), channel_id=1, source_target_pairs={{2,4},{4,2},{6,8},{8,6},{10,12},{12,10},{14,16},{16,14},{18,20},{2... | collective-permute-start | bytes 2113544 | tf_op jit(solution)/shard_map/ppermute | solution.py:52
  49.3 9.1 %collective-permute-done.2.far = f32[688,256]{1,0:T(8,128)S(1)} collective-permute-done((f32[688,256]{1,0:T(8,128)S(1)}, f32[688,256]{1,0:T(8,128)S(1)}, u32[]{:S(2)}, u32[]{:S(2)}) %collective-permute-start.2) | collective-permute-done | bytes 704544 | tf_op jit(solution)/shard_map/ppermute | solution.py:52
  58.4 0.8 slice.37
  59.1 1.9 %collective-permute-start.3 = (f32[272,256]{1,0:T(8,128)}, f32[272,256]{1,0:T(8,128)S(1)}, u32[]{:S(2)}, u32[]{:S(2)}) collective-permute-start(f32[272,256]{1,0:T(8,128)} %slice.37), channel_id=1, source_target_pairs={{0,2},{2,0},{1,3},{3,1},{4,6},{6,4},{5,7},{7,5},{8,10},{10,8},{9,1... | collective-permute-start | bytes 835592 | tf_op jit(solution)/shard_map/ppermute | solution.py:45
  61.1 10.9 %all-to-all-done.1 = bf16[8,128,768]{2,1,0:T(8,128)(2,1)S(1)} async-done(((bf16[8,128,768]{2,1,0:T(8,128)(2,1)}), bf16[8,128,768]{2,1,0:T(8,128)(2,1)S(1)}, u32[]{:S(2)}, u32[]{:S(2)}) %all-to-all-start.1) | async-done | bytes 1572896 | tf_op jit(solution)/shard_map/all_to_all | solution.py:25
  72.0 1.8 %broadcast_in_dim.46 = bf16[2,1024,768]{2,1,0:T(8,128)(2,1)} broadcast(bf16[1024,768]{1,0:T(8,128)(2,1)S(1)} %bitcast.31), dimensions={1,2} | broadcast | bytes 4718592 | tf_op jit(solution)/shard_map/broadcast_in_dim | solution.py:25
  73.8 0.0 copy-start.28
  73.8 5.2 %all-to-all-start.2 = ((bf16[2,1024,768]{2,1,0:T(8,128)(2,1)}), bf16[2,1024,768]{2,1,0:T(8,128)(2,1)S(1)}, u32[]{:S(2)}, u32[]{:S(2)}) async-start(bf16[2,1024,768]{2,1,0:T(8,128)(2,1)} %broadcast_in_dim.46), calls=%async_computation.2 | async-start | bytes 6291456 | tf_op jit(solution)/shard_map/all_to_all | solution.py:25
  79.0 3.2 %all-to-all-done.2.weights = bf16[2,1024,768]{2,1,0:T(8,128)(2,1)S(1)} async-done(((bf16[2,1024,768]{2,1,0:T(8,128)(2,1)}), bf16[2,1024,768]{2,1,0:T(8,128)(2,1)S(1)}, u32[]{:S(2)}, u32[]{:S(2)}) %all-to-all-start.2) | async-done | bytes 3145760 | tf_op jit(solution)/shard_map/all_to_all | solution.py:25
  82.3 1.0 copy-done.1
  83.3 1.0 copy-done.11
  84.3 1.1 copy-done.14
  85.4 4.9 %shard_map.133 = (bf16[128,1024]{1,0:T(8,128)(2,1)S(1)}, bf16[128,1024]{1,0:T(8,128)(2,1)S(1)}, bf16[128,256]{1,0:T(8,128)(2,1)S(1)}, bf16[128,1024]{1,0:T(8,128...) custom-call(f32[416,256]{1,0:T(8,128)S(1)} %copy-done.1, ...), custom_call_target="tpu_custom_call" | custom-call | flops 3221225472 | bytes 6514176 | tf_op jit(solution)/shard_map/pallas_call | solution.py:299
  90.3 0.0 copy-start.3
  90.3 2.4 %collective-permute-start.4 = (f32[128,256]{1,0:T(8,128)S(1)}, f32[128,256]{1,0:T(8,128)S(1)}, u32[]{:S(2)}, u32[]{:S(2)}) collective-permute-start(f32[128,256]{1,0:T(8,128)S(1)} %get-tuple-element.22), channel_id=1, source_target_pairs={{0,2},{2,0},{1,3},{3,1},{4,6},{6,4},{5,7},{7,5},{8,10},{10,8},{9,1... | collective-permute-start | bytes 393224 | tf_op jit(solution)/shard_map/ppermute | solution.py:45
  92.7 1.9 %collective-permute-start.5 = (f32[128,256]{1,0:T(8,128)S(1)}, f32[128,256]{1,0:T(8,128)S(1)}, u32[]{:S(2)}, u32[]{:S(2)}) collective-permute-start(f32[128,256]{1,0:T(8,128)S(1)} %get-tuple-element.22), channel_id=1, source_target_pairs={{2,4},{4,2},{6,8},{8,6},{10,12},{12,10},{14,16},{16,14},{18,20},{2... | collective-permute-start | bytes 393224 | tf_op jit(solution)/shard_map/ppermute | solution.py:52
  94.6 1.1 shard_map.134
  95.7 3.3 %collective-permute-done.5.far = f32[128,256]{1,0:T(8,128)S(1)} collective-permute-done((f32[128,256]{1,0:T(8,128)S(1)}, f32[128,256]{1,0:T(8,128)S(1)}, u32[]{:S(2)}, u32[]{:S(2)}) %collective-permute-start.5) | collective-permute-done | bytes 131104 | tf_op jit(solution)/shard_map/ppermute | solution.py:52
  99.0 1.3 shard_map.135
  100.4 0.0 copy-start.12
  100.4 0.0 copy-start.16
  100.4 0.0 copy-start.18
  100.4 26.7 %all_to_all.35.parts = bf16[32,128,128]{2,1,0:T(8,128)(2,1)S(1)} all-to-all(bf16[32,128,128]{2,1,0:T(8,128)(2,1)S(1)} %bitcast.21), channel_id=1, replica_groups=mesh['x_lo'=2,'y'=4,'z_hi'=4,'z_lo'=4,'core'=2,'x_hi'=2] {'x_hi','x_lo',..., dimensions={0} | all-to-all | bytes 2097152 | tf_op jit(solution)/shard_map/all_to_all | solution.py:348
  127.1 0.8 shard_map.136
  127.9 3.3 %all-to-all-start.4 = ((bf16[4,128,128]{2,1,0:T(8,128)(2,1)}), bf16[4,128,128]{2,1,0:T(8,128)(2,1)S(1)}, u32[]{:S(2)}, u32[]{:S(2)}) async-start(bf16[4,128,128]{2,1,0:T(8,128)(2,1)} %shard_map.136), calls=%async_computation.4 | async-start | bytes 262144 | tf_op jit(solution)/shard_map/all_to_all | solution.py:357
  131.2 0.1 pad_add_fusion.place
  131.3 4.8 %all-to-all-done.4.parts = bf16[4,128,128]{2,1,0:T(8,128)(2,1)S(1)} async-done(((bf16[4,128,128]{2,1,0:T(8,128)(2,1)}), bf16[4,128,128]{2,1,0:T(8,128)(2,1)S(1)}, u32[]{:S(2)}, u32[]{:S(2)}) %all-to-all-start.4) | async-done | bytes 131104 | tf_op jit(solution)/shard_map/all_to_all | solution.py:357
  136.1 0.7 shard_map.137
  136.7 6.0 %all-to-all-start.5 = ((bf16[4,128,128]{2,1,0:T(8,128)(2,1)}), bf16[4,128,128]{2,1,0:T(8,128)(2,1)S(1)}, u32[]{:S(2)}, u32[]{:S(2)}) async-start(bf16[4,128,128]{2,1,0:T(8,128)(2,1)} %shard_map.137), calls=%async_computation.5 | async-start | bytes 262144 | tf_op jit(solution)/shard_map/all_to_all | solution.py:357
  142.7 0.6 pad_maximum_fusion.1
  143.3 3.2 %collective-permute-start.8 = (f32[2,256]{1,0:T(2,128)}, f32[2,256]{1,0:T(2,128)S(1)}, u32[]{:S(2)}, u32[]{:S(2)}) collective-permute-start(f32[2,256]{1,0:T(2,128)} %pad_maximum_fusion.1), channel_id=1, source_target_pairs={{0,1},{1,0},{2,3},{3,2},{4,5},{5,4},{6,7},{7,6},{8,9},{9,8},{10,11... | collective-permute-start | bytes 6152 | tf_op jit(solution)/shard_map/ppermute | solution.py:45
  146.5 0.7 fusion.6
  147.2 5.0 %collective-permute-start.6 = (f32[128,256]{1,0:T(8,128)S(1)}, f32[128,256]{1,0:T(8,128)}, u32[]{:S(2)}, u32[]{:S(2)}) collective-permute-start(f32[128,256]{1,0:T(8,128)S(1)} %get-tuple-element.34), channel_id=1, source_target_pairs={{2,4},{4,2},{6,8},{8,6},{10,12},{12,10},{14,16},{16,14},{18,20},{2... | collective-permute-start | bytes 393224 | tf_op jit(solution)/shard_map/ppermute | solution.py:52
  152.2 1.9 %collective-permute-start.7 = (f32[128,256]{1,0:T(8,128)S(1)}, f32[128,256]{1,0:T(8,128)}, u32[]{:S(2)}, u32[]{:S(2)}) collective-permute-start(f32[128,256]{1,0:T(8,128)S(1)} %get-tuple-element.34), channel_id=1, source_target_pairs={{0,2},{2,0},{1,3},{3,1},{4,6},{6,4},{5,7},{7,5},{8,10},{10,8},{9,1... | collective-permute-start | bytes 393224 | tf_op jit(solution)/shard_map/ppermute | solution.py:45
  154.1 0.8 all-to-all-done.5.parts
  154.9 0.7 copy-done.4
  155.6 8.1 %all-to-all-start.6 = ((f32[32,16,128]{2,1,0:T(8,128)}), f32[32,16,128]{2,1,0:T(8,128)S(1)}, u32[]{:S(2)}, u32[]{:S(2)}) async-start(f32[32,16,128]{2,1,0:T(8,128)} %copy-done.4), calls=%async_computation.6 | async-start | bytes 524288 | tf_op jit(solution)/shard_map/all_to_all | solution.py:367
  163.8 2.1 %fusion.5 = f32[1,128,256]{2,1,0:T(8,128)} fusion(f32[128,256]{1,0:T(8,128)} %copy-done.12, f32[1,256]{1,0:T(1,128)S(1)} %get-tuple-element.44, f32[127,256]{1,0:T(8,128)} %get-tuple-element.40, f32[127,256]{1,0:T(8,128)} %get-tuple-element.39, f32[1,256]{1,0:T(1,128)S(1)} %get-tuple-element.43, f32[128,256]{1,0:T(8,128)S(1)} %get-tuple-element.34, ...), kind=kOutput, calls=%fused_computation.8 | convolution fusion | flops 67403776 | bytes 1703936 | tf_op jit(solution)/shard_map/dot_general | solution.py:467
  165.9 7.0 %all-to-all-done.6.parts = f32[32,16,128]{2,1,0:T(8,128)S(1)} async-done(((f32[32,16,128]{2,1,0:T(8,128)}), f32[32,16,128]{2,1,0:T(8,128)S(1)}, u32[]{:S(2)}, u32[]{:S(2)}) %all-to-all-start.6) | async-done | bytes 262176 | tf_op jit(solution)/shard_map/all_to_all | solution.py:367
  172.8 1.3 shard_map.139
  (50 shorter events, 0.2 us)
Async XLA Ops:
  0.6 0.7 copy-start.15
  1.3 0.7 copy-start.17
  2.0 0.7 copy-start.19
  11.8 27.2 %all-to-all-start = ((bf16[16,8,768]{2,1,0:T(8,128)(2,1)}), bf16[16,8,768]{2,1,0:T(8,128)(2,1)S(1)}, u32[]{:S(2)}, u32[]{:S(2)}) async-start(bf16[16,8,768]{2,1,0:T(8,128)(2,1)} %broadcast_in_dim.42), calls=%async_computation | async-start | bytes 393216 | tf_op jit(solution)/shard_map/all_to_all | solution.py:25
  21.4 0.9 copy-start.2
  22.3 0.9 copy-start.5
  23.2 0.9 copy-start.7
  24.1 0.7 copy-start.20
  24.7 0.7 copy-start.21
  25.4 0.7 copy-start.23
  26.0 0.7 copy-start.25
  26.7 0.7 copy-start.27
  27.4 6.4 %collective-permute-start = (f32[24,256]{1,0:T(8,128)S(1)}, f32[24,256]{1,0:T(8,128)S(1)}, u32[]{:S(2)}, u32[]{:S(2)}) collective-permute-start(f32[24,256]{1,0:T(8,128)S(1)} %shard_map.130), channel_id=1, source_target_pairs={{0,1},{1,0},{2,3},{3,2},{4,5},{5,4},{6,7},{7,6},{8,9},{9,8},{10,11... | collective-permute-start | bytes 73736 | tf_op jit(solution)/shard_map/ppermute | solution.py:45
  33.7 0.9 copy-start.6
  34.6 0.9 copy-start.8
  35.6 9.9 %copy-start = (f32[416,256]{1,0:T(8,128)}, f32[416,256]{1,0:T(8,128)S(1)}, u32[]{:S(2)}) copy-start(f32[416,256]{1,0:T(8,128)S(1)} %shard_map.131.own) | copy-start | bytes 1277956
  35.6 9.8 %collective-permute-start.1 = (f32[416,256]{1,0:T(8,128)S(1)}, f32[416,256]{1,0:T(8,128)S(1)}, u32[]{:S(2)}, u32[]{:S(2)}) collective-permute-start(f32[416,256]{1,0:T(8,128)S(1)} %shard_map.131.own), channel_id=1, source_target_pairs={{0,2},{2,0},{1,3},{3,1},{4,6},{6,4},{5,7},{7,5},{8,10},{10,8},{9,1... | collective-permute-start | bytes 1277960 | tf_op jit(solution)/shard_map/ppermute | solution.py:45
  40.3 31.6 %all-to-all-start.1 = ((bf16[8,128,768]{2,1,0:T(8,128)(2,1)}), bf16[8,128,768]{2,1,0:T(8,128)(2,1)S(1)}, u32[]{:S(2)}, u32[]{:S(2)}) async-start(bf16[8,128,768]{2,1,0:T(8,128)(2,1)} %broadcast_in_dim.44), calls=%async_computation.1 | async-start | bytes 3145728 | tf_op jit(solution)/shard_map/all_to_all | solution.py:25
  45.4 28.3 %copy-start.10 = (f32[416,256]{1,0:T(8,128)}, f32[416,256]{1,0:T(8,128)S(1)}, u32[]{:S(2)}) copy-start(f32[416,256]{1,0:T(8,128)S(1)} %collective-permute-done.1.near) | copy-start | bytes 1277956
  45.6 12.8 %collective-permute-start.2 = (f32[688,256]{1,0:T(8,128)S(1)}, f32[688,256]{1,0:T(8,128)S(1)}, u32[]{:S(2)}, u32[]{:S(2)}) collective-permute-start(f32[688,256]{1,0:T(8,128)S(1)} %pad_maximum_fusion), channel_id=1, source_target_pairs={{2,4},{4,2},{6,8},{8,6},{10,12},{12,10},{14,16},{16,14},{18,20},{2... | collective-permute-start | bytes 2113544 | tf_op jit(solution)/shard_map/ppermute | solution.py:52
  58.4 15.5 %copy-start.13 = (f32[688,256]{1,0:T(8,128)}, f32[688,256]{1,0:T(8,128)S(1)}, u32[]{:S(2)}) copy-start(f32[688,256]{1,0:T(8,128)S(1)} %collective-permute-done.2.far) | copy-start | bytes 2113540
  59.1 19.9 %collective-permute-start.3 = (f32[272,256]{1,0:T(8,128)}, f32[272,256]{1,0:T(8,128)S(1)}, u32[]{:S(2)}, u32[]{:S(2)}) collective-permute-start(f32[272,256]{1,0:T(8,128)} %slice.37), channel_id=1, source_target_pairs={{0,2},{2,0},{1,3},{3,1},{4,6},{6,4},{5,7},{7,5},{8,10},{10,8},{9,1... | collective-permute-start | bytes 835592 | tf_op jit(solution)/shard_map/ppermute | solution.py:45
  73.8 8.5 %copy-start.22 = (s32[64]{0:T(128)S(1)}, s32[64]{0:T(128)}, u32[]{:S(2)}) copy-start(s32[64]{0:T(128)} %param.18) | copy-start | bytes 772
  73.8 8.5 %copy-start.24 = (s32[64]{0:T(128)S(1)}, s32[64]{0:T(128)}, u32[]{:S(2)}) copy-start(s32[64]{0:T(128)} %param.19) | copy-start | bytes 772
  73.8 8.5 %copy-start.26 = (f32[64]{0:T(128)S(1)}, f32[64]{0:T(128)}, u32[]{:S(2)}) copy-start(f32[64]{0:T(128)} %param.20) | copy-start | bytes 772
  73.8 8.5 %copy-start.28 = (f32[64]{0:T(128)S(1)}, f32[64]{0:T(128)}, u32[]{:S(2)}) copy-start(f32[64]{0:T(128)} %param.21) | copy-start | bytes 772
  73.8 8.4 %all-to-all-start.2 = ((bf16[2,1024,768]{2,1,0:T(8,128)(2,1)}), bf16[2,1024,768]{2,1,0:T(8,128)(2,1)S(1)}, u32[]{:S(2)}, u32[]{:S(2)}) async-start(bf16[2,1024,768]{2,1,0:T(8,128)(2,1)} %broadcast_in_dim.46), calls=%async_computation.2 | async-start | bytes 6291456 | tf_op jit(solution)/shard_map/all_to_all | solution.py:25
  82.3 1.0 copy-start.1
  83.3 1.0 copy-start.11
  84.3 1.1 copy-start.14
  90.3 8.7 %copy-start.3 = (f32[1,128,256]{2,1,0:T(8,128)S(1)}, f32[1,128,256]{2,1,0:T(8,128)}, u32[]{:S(2)}) copy-start(f32[1,128,256]{2,1,0:T(8,128)} %diffusivity.3) | copy-start | bytes 393220
  90.3 5.4 %collective-permute-start.4 = (f32[128,256]{1,0:T(8,128)S(1)}, f32[128,256]{1,0:T(8,128)S(1)}, u32[]{:S(2)}, u32[]{:S(2)}) collective-permute-start(f32[128,256]{1,0:T(8,128)S(1)} %get-tuple-element.22), channel_id=1, source_target_pairs={{0,2},{2,0},{1,3},{3,1},{4,6},{6,4},{5,7},{7,5},{8,10},{10,8},{9,1... | collective-permute-start | bytes 393224 | tf_op jit(solution)/shard_map/ppermute | solution.py:45
  92.7 6.3 %collective-permute-start.5 = (f32[128,256]{1,0:T(8,128)S(1)}, f32[128,256]{1,0:T(8,128)S(1)}, u32[]{:S(2)}, u32[]{:S(2)}) collective-permute-start(f32[128,256]{1,0:T(8,128)S(1)} %get-tuple-element.22), channel_id=1, source_target_pairs={{2,4},{4,2},{6,8},{8,6},{10,12},{12,10},{14,16},{16,14},{18,20},{2... | collective-permute-start | bytes 393224 | tf_op jit(solution)/shard_map/ppermute | solution.py:52
  100.4 26.7 %copy-start.9 = (bf16[128,1024]{1,0:T(8,128)(2,1)}, bf16[128,1024]{1,0:T(8,128)(2,1)S(1)}, u32[]{:S(2)}) copy-start(bf16[128,1024]{1,0:T(8,128)(2,1)S(1)} %get-tuple-element.35) | copy-start | bytes 786436
  100.4 26.7 %copy-start.12 = (f32[128,256]{1,0:T(8,128)}, f32[128,256]{1,0:T(8,128)S(1)}, u32[]{:S(2)}) copy-start(f32[128,256]{1,0:T(8,128)S(1)} %get-tuple-element.33) | copy-start | bytes 393220
  100.4 72.4 %copy-start.16 = (f32[4,256]{1,0:T(4,128)S(1)}, f32[4,256]{1,0:T(4,128)}, u32[]{:S(2)}) copy-start(f32[4,256]{1,0:T(4,128)} %w_in.3) | copy-start | bytes 12292
  100.4 72.4 %copy-start.18 = (f32[4,256]{1,0:T(4,128)S(1)}, f32[4,256]{1,0:T(4,128)}, u32[]{:S(2)}) copy-start(f32[4,256]{1,0:T(4,128)} %w_out.3) | copy-start | bytes 12292
  127.9 8.2 %all-to-all-start.4 = ((bf16[4,128,128]{2,1,0:T(8,128)(2,1)}), bf16[4,128,128]{2,1,0:T(8,128)(2,1)S(1)}, u32[]{:S(2)}, u32[]{:S(2)}) async-start(bf16[4,128,128]{2,1,0:T(8,128)(2,1)} %shard_map.136), calls=%async_computation.4 | async-start | bytes 262144 | tf_op jit(solution)/shard_map/all_to_all | solution.py:357
  136.7 18.1 %all-to-all-start.5 = ((bf16[4,128,128]{2,1,0:T(8,128)(2,1)}), bf16[4,128,128]{2,1,0:T(8,128)(2,1)S(1)}, u32[]{:S(2)}, u32[]{:S(2)}) async-start(bf16[4,128,128]{2,1,0:T(8,128)(2,1)} %shard_map.137), calls=%async_computation.5 | async-start | bytes 262144 | tf_op jit(solution)/shard_map/all_to_all | solution.py:357
  143.3 20.4 %collective-permute-start.8 = (f32[2,256]{1,0:T(2,128)}, f32[2,256]{1,0:T(2,128)S(1)}, u32[]{:S(2)}, u32[]{:S(2)}) collective-permute-start(f32[2,256]{1,0:T(2,128)} %pad_maximum_fusion.1), channel_id=1, source_target_pairs={{0,1},{1,0},{2,3},{3,2},{4,5},{5,4},{6,7},{7,6},{8,9},{9,8},{10,11... | collective-permute-start | bytes 6152 | tf_op jit(solution)/shard_map/ppermute | solution.py:45
  147.2 16.6 %collective-permute-start.6 = (f32[128,256]{1,0:T(8,128)S(1)}, f32[128,256]{1,0:T(8,128)}, u32[]{:S(2)}, u32[]{:S(2)}) collective-permute-start(f32[128,256]{1,0:T(8,128)S(1)} %get-tuple-element.34), channel_id=1, source_target_pairs={{2,4},{4,2},{6,8},{8,6},{10,12},{12,10},{14,16},{16,14},{18,20},{2... | collective-permute-start | bytes 393224 | tf_op jit(solution)/shard_map/ppermute | solution.py:52
  152.2 11.6 %collective-permute-start.7 = (f32[128,256]{1,0:T(8,128)S(1)}, f32[128,256]{1,0:T(8,128)}, u32[]{:S(2)}, u32[]{:S(2)}) collective-permute-start(f32[128,256]{1,0:T(8,128)S(1)} %get-tuple-element.34), channel_id=1, source_target_pairs={{0,2},{2,0},{1,3},{3,1},{4,6},{6,4},{5,7},{7,5},{8,10},{10,8},{9,1... | collective-permute-start | bytes 393224 | tf_op jit(solution)/shard_map/ppermute | solution.py:45
  154.9 0.7 copy-start.4
  155.6 17.2 %all-to-all-start.6 = ((f32[32,16,128]{2,1,0:T(8,128)}), f32[32,16,128]{2,1,0:T(8,128)S(1)}, u32[]{:S(2)}, u32[]{:S(2)}) async-start(f32[32,16,128]{2,1,0:T(8,128)} %copy-done.4), calls=%async_computation.6 | async-start | bytes 524288 | tf_op jit(solution)/shard_map/all_to_all | solution.py:367

commit v5 on v3

v5 whole, which is shorter than its diff:
```python
import functools

import jax
import jax.numpy as jnp
from jax import lax
from jax.experimental import pallas as pl
from jax.experimental.pallas import tpu as pltpu
from jax.sharding import Mesh
from jax.sharding import PartitionSpec as P

LEARN_RATE = 0.02
EPSILON = 1e-06
CONTRACT_LAST = (((1,), (1,)), ((), ()))
CONTRACT_FIRST = (((0,), (0,)), ((), ()))
FINE_AXES = ("x_lo", "y", "z_hi", "z_lo", "core", "x_hi")
FINE_SIZES = (2, 4, 4, 4, 2, 2)
Z = ("z_hi", "z_lo")
TILE = ("x_lo", "y", "z_hi", "z_lo", "core")
AROUND = ("x_hi", "x_lo", "y", "core")
REACH = 3
BLOCK = 144


def spread(block, axis):
    count = lax.axis_size(axis)
    return lax.all_to_all(jnp.broadcast_to(block[None], (count,) + block.shape), axis, 0, 0)


def gather_weights(w_in, w_mid, w_out):
    columns = 2 * w_in.shape[1] + w_mid.shape[1]
    (rows,) = on_chip(
        pack_kernel,
        (jax.ShapeDtypeStruct((w_in.shape[0], columns), jnp.bfloat16),),
        (w_in, w_mid, w_out),
        0,
        fetched=3,
    )
    rows = lax.all_gather(rows, "core", axis=0, tiled=True)
    width = rows.shape[1] // 2
    half = lax.dynamic_slice_in_dim(rows, lax.axis_index("core") * width, width, 1)
    half = spread(half, Z).reshape(-1, width)
    half = spread(half, ("x_lo", "y")).reshape(-1, width)
    return half


def swapped(array, axis):
    return lax.ppermute(array, axis, [(0, 1), (1, 0)])


def swapped_between_chips(array):
    pairs = []
    for row in range(1, lax.axis_size(TILE) - 1, 2):
        pairs += [(row, row + 1), (row + 1, row)]
    return lax.ppermute(array, TILE, pairs)


def swapped_three_apart(array):
    count = lax.axis_size(TILE)
    pairs = [(row, row + 3) for row in range(1, count - 3, 2)]
    return lax.ppermute(array, TILE, pairs + [(after, row) for row, after in pairs])


def neighbour_sum(field):
    far = swapped_between_chips(field)
    edges = swapped(jnp.concatenate([field[:1], field[-1:]]), "x_hi")
    near = swapped(field, "core")
    east = jnp.concatenate([field[1:], edges[:1]])
    west = jnp.concatenate([edges[1:], field[:-1]])
    return far + near + east + west


def adjoint_layers(source, hidden_one, hidden_two, weights):
    features = source.shape[1]
    depth = weights.shape[2] - features
    slope_two = 1.0 - jnp.square(hidden_two.astype(jnp.float32))
    back_two = lax.dot_general(
        source, weights[1, :, depth:], CONTRACT_LAST, preferred_element_type=jnp.float32
    )
    back_two = (slope_two * back_two).astype(jnp.bfloat16)
    back_one = lax.dot_general(
        back_two[:, :depth],
        weights[0, :, features:],
        CONTRACT_LAST,
        preferred_element_type=jnp.float32,
    ) + lax.dot_general(
        back_two[:, depth:],
        weights[1, :, :depth],
        CONTRACT_LAST,
        preferred_element_type=jnp.float32,
    )
    slope_one = 1.0 - jnp.square(hidden_one.astype(jnp.float32))
    return (slope_one * back_one).astype(jnp.bfloat16)


def edge_kernel(state, increment, diffusivity, land_sea, col, lev, val, prec, edges, outer):
    edges[...] = jnp.zeros_like(edges)
    cells = state.shape[1]
    for which, field in enumerate((state, increment, diffusivity)):
        start = 2 * REACH * which
        edges[start : start + REACH] = field[0, :REACH]
        edges[start + REACH : start + 2 * REACH] = field[0, cells - REACH :]
    edges[18:19, :cells] = 0.5 + land_sea[...].astype(jnp.float32)
    count = col.shape[1]
    for row, numbers in enumerate((col, lev, val, prec)):
        edges[19 + row : 20 + row, :count] = numbers[...].astype(jnp.float32)
    outer[...] = (state[0] + increment[0]).astype(jnp.bfloat16)


def ring_gating(mine, other):
    cells = mine.shape[1]
    lane = lax.broadcasted_iota(jnp.int32, (8, cells), 1)
    mine, other = (jnp.broadcast_to(row, (8, cells)) for row in (mine, other))
    other = jnp.where(lane < REACH, other, pltpu.roll(other, 8, 1))
    return jnp.concatenate([mine, other], axis=1)


def ring_field(field, edges, which):
    start = 2 * REACH * which
    return jnp.concatenate(
        [
            field,
            edges[start : start + REACH],
            jnp.zeros((8 - 2 * REACH, field.shape[1]), jnp.float32),
            edges[start + REACH : start + 2 * REACH],
        ]
    )


def pack_row_kernel(state, increment, diffusivity, mine, other, pack):
    cells, features = state.shape[1:]
    for which, field in enumerate((state, increment, diffusivity)):
        ring = ring_field(field[0], other, which)
        ring = jnp.concatenate([ring, jnp.zeros((8, features), jnp.float32)])
        pack[BLOCK * which : BLOCK * (which + 1)] = ring.astype(jnp.bfloat16)
    gating = ring_gating(mine[18:19, :cells], other[18:19, :cells])[:1]
    numbers = mine[21:23, :]
    coarse = numbers.astype(jnp.bfloat16).astype(jnp.float32)
    fine = numbers - coarse
    rest = [gating, mine[19:21, :], coarse, fine, jnp.zeros((16 - 7, features), jnp.float32)]
    pack[3 * BLOCK :] = jnp.concatenate(rest).astype(jnp.bfloat16)


def whole_kernel(
    observations,
    state,
    increment,
    diffusivity,
    mine,
    other,
    near,
    far,
    beyond,
    outer,
    settled_out,
    spreading_out,
    grads,
    weights,
):
    cells, features = state.shape[1:]
    depth = weights.shape[2] - features
    length = cells + 8
    pack = 3 * BLOCK + 16
    square = (length, 2 * cells)
    diagonal = lax.broadcasted_iota(jnp.int32, square, 0) == lax.broadcasted_iota(
        jnp.int32, square, 1
    )

    def column(row):
        return jnp.sum(jnp.where(diagonal, row, 0.0), axis=1, keepdims=True)

    def laplace(field, lat):
        return lat + pltpu.roll(field, 1, 0) + pltpu.roll(field, length - 1, 0) - 4.0 * field

    def unpack(ref, start):
        fields = [
            ref[start + BLOCK * i : start + BLOCK * (i + 1), :].astype(jnp.float32)[:length]
            for i in range(3)
        ]
        rest = ref[start + 3 * BLOCK : start + pack, :].astype(jnp.float32)
        return fields + [column(rest[:1])], rest

    def activate(both):
        hidden = jnp.tanh(both[:length]).astype(jnp.bfloat16).astype(jnp.float32)
        tangent = (1.0 - hidden * hidden) * both[length:]
        return jnp.concatenate([hidden, tangent]).astype(jnp.bfloat16)

    def network(states, tangents):
        stacked = jnp.concatenate([states, tangents]).astype(jnp.bfloat16)
        one = activate(
            lax.dot_general(
                stacked,
                weights[0, :, :features],
                CONTRACT_LAST,
                preferred_element_type=jnp.float32,
            )
        )
        low = activate(jnp.dot(one, weights[0, :, features:], preferred_element_type=jnp.float32))
        high = activate(jnp.dot(one, weights[1, :, :depth], preferred_element_type=jnp.float32))
        out = jnp.dot(
            low, weights[1, :depth, depth:], preferred_element_type=jnp.float32
        ) + jnp.dot(high, weights[1, depth:, depth:], preferred_element_type=jnp.float32)
        saved = (one[:cells], jnp.concatenate([low[:cells], high[:cells]], axis=1), stacked[:cells])
        return out[:length], out[length:], saved

    def observed(final, columns, levels, values, precisions):
        count = columns.shape[1]
        cell_ids = lax.broadcasted_iota(jnp.int32, (length, count), 0).astype(jnp.float32)
        level_ids = lax.broadcasted_iota(jnp.int32, (features, count), 0).astype(jnp.float32)
        pick_cell = (cell_ids == columns).astype(jnp.float32)
        pick_level = (level_ids == levels).astype(jnp.float32)
        at_level = jnp.dot(
            final, pick_level, precision=lax.Precision.HIGHEST, preferred_element_type=jnp.float32
        )
        modelled = jnp.sum(pick_cell * at_level, axis=0, keepdims=True)
        return lax.dot_general(
            pick_cell * (precisions * (modelled - values)),
            pick_level,
            CONTRACT_LAST,
            precision=lax.Precision.HIGHEST,
            preferred_element_type=jnp.float32,
        )

    own = [ring_field(ref[0], other, i) for i, ref in enumerate((state, increment, diffusivity))]
    gate = column(ring_gating(mine[18:19, :cells], other[18:19, :cells])[:1])
    own.append(gate)
    beside, beside_rest = zip(unpack(near, 0), unpack(far, 0))
    second = [unpack(beyond, 0)[0], unpack(far, pack)[0]]
    third = [unpack(beyond, pack)[0]]
    third = [
        third[0][0] + third[0][1],
        jnp.concatenate(
            [outer[...].astype(jnp.float32), jnp.zeros((length - cells, features), jnp.float32)]
        ),
    ]

    def advance(row, lats):
        states, tangents, diffuse, gated = row
        tend, tangent, saved = network(states, tangents)
        return (
            states + diffuse * laplace(states, lats[0]) + gated * tend,
            tangents + diffuse * laplace(tangents, lats[1]) + gated * tangent,
            saved,
        )

    def advance_sum(row, middle, lat):
        tend, tangent, saved = network(row[0], row[1])
        return middle + row[2] * laplace(middle, lat) + row[3] * (tend + tangent), saved

    state_one, increment_one, first = advance(
        own, [beside[0][i] + beside[1][i] for i in range(2)]
    )
    middle_one = state_one + increment_one
    beside_one, beside_middle, second_middle = [], [], []
    for row, next_row, last in zip(beside, second, third):
        one = advance(row, [own[i] + next_row[i] for i in range(2)])[:2]
        beside_one.append(one)
        beside_middle.append(one[0] + one[1])
        next_sum = next_row[0] + next_row[1]
        second_middle.append(
            advance_sum(next_row, next_sum, row[0] + row[1] + last)[0]
        )
    final, late = advance_sum(
        [state_one, increment_one, own[2], gate],
        middle_one,
        beside_middle[0] + beside_middle[1],
    )

    count = observations
    columns = other[19:20, :count]
    columns = jnp.where(
        columns == 0.0, float(cells), jnp.where(columns == cells - 1.0, length - 1.0, -1.0)
    )
    columns = jnp.concatenate([mine[19:20, :count], columns], axis=1)
    chosen = [
        jnp.concatenate([mine[i : i + 1, :count], other[i : i + 1, :count]], axis=1)
        for i in (20, 21, 22)
    ]
    adjoint = observed(final, columns, *chosen)
    around = jnp.zeros_like(adjoint)
    for row, one, middle, next_middle, rest in zip(
        beside, beside_one, beside_middle, second_middle, beside_rest
    ):
        total = advance_sum(
            [one[0], one[1], row[2], row[3]], middle, middle_one + next_middle
        )[0]
        around = around + row[2] * observed(
            total,
            rest[1:2, :cells],
            rest[2:3, :cells],
            rest[3:4, :cells] + rest[5:6, :cells],
            rest[4:5, :cells] + rest[6:7, :cells],
        )
    spreading = own[2] * adjoint
    adjoint_one = (adjoint + laplace(spreading, around))[:cells]
    gate = gate[:cells]
    source_late = (gate * adjoint[:cells]).astype(jnp.bfloat16)
    back_late = adjoint_layers(source_late, late[0], late[1], weights)
    adjoint_one = adjoint_one + jnp.dot(
        back_late, weights[0, :, :features], preferred_element_type=jnp.float32
    )
    spreading = own[2][:cells] * adjoint_one
    spreading_out[...] = spreading
    source = (gate * adjoint_one).astype(jnp.bfloat16)
    back_one = adjoint_layers(source, first[0], first[1], weights)
    settled_out[...] = (
        adjoint_one
        - 4.0 * spreading
        + jnp.dot(back_one, weights[0, :, :features], preferred_element_type=jnp.float32)
    )
    pairs = (
        (back_late, back_one, late[2], first[2]),
        (late[1], first[1], source_late, source),
    )
    _, blocks, halves, rows, width = grads.shape
    for which, (left_late, left, right_late, right) in enumerate(pairs):
        total = lax.dot_general(
            jnp.concatenate([left_late, left]),
            jnp.concatenate([right_late, right]),
            CONTRACT_FIRST,
            preferred_element_type=jnp.float32,
        ).astype(jnp.bfloat16)
        for block in range(blocks):
            for half in range(halves):
                grads[which, block, half] = total[
                    block * rows : (block + 1) * rows, half * width : (half + 1) * width
                ]


def on_chip(kernel, outs, operands, flops, scratch=(), scalars=0, fetched=0, place=None):
    size = sum(array.size * array.dtype.itemsize for array in list(operands) + list(outs))
    count = len(operands) - scalars
    by_kernel = fetched > 0
    places = [pltpu.SMEM] * scalars + [pl.ANY if by_kernel else pltpu.VMEM] * count
    body = kernel
    if by_kernel:
        copies = tuple(
            pltpu.VMEM(array.shape, array.dtype)
            for array in operands[scalars : scalars + fetched]
        )
        scratch = copies + (pltpu.SemaphoreType.DMA((count,)),) + tuple(scratch)

        def body(*refs):
            numbers, sources, refs = refs[:scalars], refs[scalars : scalars + count], refs[scalars + count :]
            results, refs = refs[: len(outs)], refs[len(outs) :]
            held, done, rest = refs[:fetched], refs[fetched], refs[fetched + 1 :]
            targets = list(held)
            if place is not None:
                targets += place(numbers, rest)
            moves = [
                pltpu.make_async_copy(source, target, done.at[i])
                for i, (source, target) in enumerate(zip(sources, targets))
            ]
            for move in moves:
                move.start()
            for move in moves:
                move.wait()
            kernel(*held, *results, *rest)

    return pl.pallas_call(
        body,
        out_shape=outs,
        in_specs=[pl.BlockSpec(memory_space=place_) for place_ in places],
        out_specs=[pl.BlockSpec(memory_space=pltpu.VMEM)] * len(outs),
        scratch_shapes=scratch,
        compiler_params=pltpu.CompilerParams(vmem_limit_bytes=32 * 1024 * 1024),
        cost_estimate=pl.CostEstimate(flops=flops, bytes_accessed=size, transcendentals=0),
    )(*operands)


def pack_kernel(w_in, w_mid, w_out, rows):
    features = w_in.shape[1]
    rows[:, :features] = w_in[...].astype(jnp.bfloat16)
    rows[:, features:-features] = w_mid[...]
    rows[:, -features:] = w_out[...].astype(jnp.bfloat16)


def sum_and_spread_kernel(parts, copies):
    total = jnp.sum(parts[...].astype(jnp.float32), axis=0).astype(jnp.bfloat16)
    copies[...] = jnp.broadcast_to(total[None], copies.shape)


def sum_and_square_kernel(place, parts, copies, total):
    total[...] = jnp.sum(parts[...].astype(jnp.float32), axis=0)
    depth = copies.shape[1] // 2
    own = total[pl.ds(pl.multiple_of(place[0] * depth, depth), depth), :]
    squares = jnp.sum(total[...] * total[...], axis=0, keepdims=True)
    both = jnp.concatenate([own, jnp.broadcast_to(squares, own.shape)])
    copies[...] = jnp.broadcast_to(both[None], copies.shape)


def update_kernel(blocks, count, place, parts, w_in, w_out, new_in, new_out):
    depth = parts.shape[1] // 2
    shard = w_in.shape[0]
    squares = jnp.sum(parts[:, depth, :], axis=0, keepdims=True)
    square_sum = jnp.sum(squares, axis=1, keepdims=True)
    scale = LEARN_RATE / jnp.sqrt(square_sum / count + EPSILON)
    for which, (old, new) in enumerate(((w_in, new_in), (w_out, new_out))):
        sides = []
        for half in range(2):
            rows = parts[(which * blocks + place[0]) * 2 + half, :depth, :]
            sides.append(jnp.where(place[1] == 0, rows[:shard], rows[shard:]))
        new[...] = old[...] - scale * jnp.concatenate(sides, axis=1)


def updated(grads, w_in, w_out):
    kinds, blocks, halves, rows, columns = grads.shape
    peers = kinds * blocks * halves
    grads = lax.all_to_all(grads.reshape(peers, rows, columns), AROUND, 0, 0)
    for axis in ("z_lo", "z_hi"):
        count = lax.axis_size(axis)
        (copies,) = on_chip(
            sum_and_spread_kernel,
            (jax.ShapeDtypeStruct((count, rows, columns), jnp.bfloat16),),
            (grads,),
            grads.size,
        )
        grads = lax.all_to_all(copies, axis, 0, 0)
    depth = rows // lax.axis_size(Z)
    (copies,) = on_chip(
        sum_and_square_kernel,
        (jax.ShapeDtypeStruct((peers, 2 * depth, columns), jnp.float32),),
        (lax.axis_index(Z)[None], grads),
        grads.size,
        scratch=(pltpu.VMEM((rows, columns), jnp.float32),),
        scalars=1,
    )
    parts = lax.all_to_all(copies, AROUND, 0, 0)
    place = jnp.stack([lax.axis_index(("x_lo", "y")), lax.axis_index("core")])
    shape = jax.ShapeDtypeStruct(w_in.shape, jnp.float32)
    return on_chip(
        functools.partial(update_kernel, blocks, float(peers * rows * columns)),
        (shape, shape),
        (place, parts, w_in, w_out),
        parts.size,
        scalars=1,
    )


def local(
    state, increment, diffusivity, land_sea, w_in, w_mid, w_out, obs_col, obs_lev, obs_val, obs_prec
):
    _, cells, features = state.shape
    length = cells + 8
    fields = (state, increment, diffusivity, land_sea)
    observed = [numbers[None] for numbers in (obs_col, obs_lev, obs_val, obs_prec)]

    def outs(*shapes):
        return tuple(jax.ShapeDtypeStruct(shape, kind) for shape, kind in shapes)

    mine, outer = on_chip(
        edge_kernel,
        outs(((24, features), jnp.float32), ((cells, features), jnp.bfloat16)),
        fields + tuple(observed),
        0,
        fetched=8,
    )
    outer = swapped_three_apart(outer)
    other = swapped(mine, "x_hi")
    (own,) = on_chip(
        pack_row_kernel,
        outs(((3 * BLOCK + 16, features), jnp.bfloat16)),
        fields[:3] + (mine, other),
        0,
        fetched=5,
    )
    near = swapped(own, "core")
    far = swapped_between_chips(jnp.concatenate([own, near]))
    beyond = swapped(far, "core")

    half = gather_weights(w_in, w_mid, w_out)
    hidden_units, width = half.shape
    blocks = lax.axis_size(("x_lo", "y"))
    halves = lax.axis_size("core")
    narrow = ((cells, features), jnp.float32)
    settled, spreading, grads = on_chip(
        functools.partial(whole_kernel, obs_col.shape[0]),
        outs(
            narrow,
            narrow,
            ((2, blocks, halves, hidden_units // blocks, features // halves), jnp.bfloat16),
        ),
        (lax.axis_index("core")[None], *fields[:3], mine, other, near, far, beyond, outer)
        + (half, swapped(half, "core")),
        40 * cells * hidden_units * (2 * features + hidden_units),
        scratch=(pltpu.VMEM((2, hidden_units, width), jnp.bfloat16),),
        scalars=1,
        fetched=9,
        place=lambda numbers, rest: [
            rest[0].at[numbers[0][0]],
            rest[0].at[1 - numbers[0][0]],
        ],
    )
    w_in_new, w_out_new = updated(grads, w_in, w_out)
    adjoint = settled + neighbour_sum(spreading)
    return adjoint[None], w_in_new, w_out_new


def solution(mesh):
    fine = Mesh(mesh.devices.reshape(FINE_SIZES), FINE_AXES)
    everywhere = TILE + ("x_hi",)
    return jax.shard_map(
        local,
        mesh=fine,
        in_specs=(
            P(TILE, "x_hi", None),
            P(TILE, "x_hi", None),
            P(TILE, "x_hi", None),
            P(TILE, "x_hi"),
            P(TILE, None),
            P(TILE, None),
            P(TILE, None),
            P(everywhere),
            P(everywhere),
            P(everywhere),
            P(everywhere),
        ),
        out_specs=(P(TILE, "x_hi", None), P(TILE, None), P(TILE, None)),
        check_vma=False,
    )
```

time: 176 us -> 184 us (1.045)
  blocking collectives: 44.5 us -> 78.8 us
  starting transfers between devices: 76.7 us -> 54.8 us
  Pallas kernels: 5.18 us -> 18.5 us
  local copies, waits for them, and re-layouts: 8.54 us -> 2.29 us
  matrix products: 5.45 us -> 0 us
  other arithmetic: 3.72 us -> 0.82 us
  waiting for transfers between devices: 30 us -> 27.3 us
    all_to_all x1 -> x2, blocking collectives: 10.4 us -> 44.5 us  [spread(): lax.all_to_all(jnp.broadcast_to(block[None], (count,) + block.shape), axi...]
    all_to_all x2 -> x0, starting transfers between devices: 14.7 us -> none  [spread(): lax.all_to_all(jnp.broadcast_to(block[None], (count,) + block.shape), axi...]
    pallas_call x7 -> x8, Pallas kernels: 5.18 us -> 18.5 us  [on_chip(): pl.pallas_call(body, out_shape=outs, in_specs=[pl.BlockSpec(memory_space=...]
    all_to_all x2 -> x0, waiting for transfers between devices: 12 us -> none  [spread(): lax.all_to_all(jnp.broadcast_to(block[None], (count,) + block.shape), axi...]
    ppermute x12 -> x9, starting transfers between devices: 44.3 us -> 36.2 us  [the longest x6 21.5 us: swapped(): return lax.ppermute(array, axis, [(0, 1), (1, 0)])]
    ppermute x12 -> x9, waiting for transfers between devices: 6.26 us -> 12.2 us  [the longest x2 6.15 us: swapped_between_chips(): return lax.ppermute(array, TILE, pairs)]
    dot_general x9 -> x0, matrix products: 5.45 us -> none  [the longest x1 2.09 us: local(): jnp.dot(back_first, w_in_b, preferred_element_type=jnp.float32)]
    slice x12 -> x3, local copies, waits for them, and re-layouts: 2.53 us -> 0.03 us  [the longest x2 0.02 us: neighbour_sum(): west = jnp.concatenate([edges[1:], field[:-1]])]
  transfers between devices with their start and end apart: 17 -> 12, of which waited for: 6 -> 7; matrix products, arithmetic and copies ran while one was open for 5% -> 0% of each run, Pallas kernels for 1% -> 1%
where the time goes in v5:
time: 184 us
  blocking collectives  78.8 us (43%)
  starting transfers between devices  54.8 us (30%)
  waiting for transfers between devices  27.3 us (15%)
  Pallas kernels  18.5 us (10%)
  local copies, waits for them, and re-layouts  2.29 us (1%)
    all_to_all x2, blocking collectives, spread(): lax.all_to_all(jnp.broadcast_to(block[None], (count,) + block.shape), axi...  44.5 us
    all_to_all x1, blocking collectives, updated(): grads = lax.all_to_all(grads.reshape(peers, rows, columns), AROUND, 0, 0)  25.9 us
    ppermute x6, starting transfers between devices, swapped(): return lax.ppermute(array, axis, [(0, 1), (1, 0)])  21.5 us
    pallas_call x8, Pallas kernels, on_chip(): pl.pallas_call(body, out_shape=outs, in_specs=[pl.BlockSpec(memory_space=...  18.5 us
    ppermute x2, starting transfers between devices, swapped_between_chips(): return lax.ppermute(array, TILE, pairs)  11.5 us
    all_to_all x2, starting transfers between devices, updated(): grads = lax.all_to_all(copies, axis, 0, 0)  10.6 us
    all_gather x1, blocking collectives, gather_weights(): rows = lax.all_gather(rows, 'core', axis=0, tiled=True)  8.37 us
    all_to_all x1, waiting for transfers between devices, updated(): parts = lax.all_to_all(copies, AROUND, 0, 0)  8.26 us
  transfers between devices with their start and end apart: 12, of which 7 were waited for; matrix products, arithmetic and copies ran while one was open for 0% of the time, Pallas kernels for 1%

profile of v5, /device:TPU:1, one launch (start us, length us, event | category | flops | bytes accessed | tf_op | source)
XLA Modules:
  0.0 183.6 jit_solution(1625501497669416964)
XLA Ops:
  0.6 0.0 copy-start.3
  0.6 0.7 copy-done.3
  1.3 0.0 copy-start.5
  1.3 0.7 copy-done.5
  2.0 0.0 copy-start.7
  2.0 0.7 copy-done.7
  2.8 8.4 %all-gather = bf16[2,4,1536]{2,1,0:T(4,128)(2,1)S(1)} all-gather(bf16[1,4,1536]{2,1,0:T(4,128)(2,1)S(1)} %bitcast.16), channel_id=1, replica_groups=mesh['x_lo'=2,'y'=4,'z_hi'=4,'z_lo'=4,'core'=2,'x_hi'=2] {'core'}, dimensions={0}, use_global_device_ids=true | all-gather | bytes 36864 | tf_op jit(solution)/shard_map/all_gather | solution.py:38
  11.2 22.3 %all_to_all.30 = bf16[16,8,768]{2,1,0:T(8,128)(2,1)S(1)} all-to-all(bf16[16,8,768]{2,1,0:T(8,128)(2,1)S(1)} %broadcast_in_dim.39), channel_id=1, replica_groups=mesh['x_lo'=2,'y'=4,'z_hi'=4,'z_lo'=4,'core'=2,'x_hi'=2] {'z_hi','z_lo'}, dimensions={0} | all-to-all | bytes 393216 | tf_op jit(solution)/shard_map/all_to_all | solution.py:26
  33.5 0.1 broadcast_in_dim.41
  33.6 0.0 copy-start
  33.6 0.0 copy-start.1
  33.6 0.0 copy-start.2
  33.6 0.0 copy-start.8
  33.6 0.0 copy-start.9
  33.6 0.0 copy-start.10
  33.7 0.0 copy-start.11
  33.7 0.0 copy-start.12
  33.7 22.2 %all_to_all.31 = bf16[8,128,768]{2,1,0:T(8,128)(2,1)S(1)} all-to-all(bf16[8,128,768]{2,1,0:T(8,128)(2,1)S(1)} %broadcast_in_dim.41), channel_id=1, replica_groups=mesh['x_lo'=2,'y'=4,'z_hi'=4,'z_lo'=4,'core'=2,'x_hi'=2] {'x_lo','y'}, dimensions={0} | all-to-all | bytes 3145728 | tf_op jit(solution)/shard_map/all_to_all | solution.py:26
  55.9 7.1 %collective-permute-start.5 = (bf16[1024,768]{1,0:T(8,128)(2,1)S(1)}, bf16[1024,768]{1,0:T(8,128)(2,1)S(1)}, u32[]{:S(2)}, u32[]{:S(2)}) collective-permute-start(bf16[1024,768]{1,0:T(8,128)(2,1)S(1)} %bitcast.13), channel_id=1, source_target_pairs={{0,2},{2,0},{1,3},{3,1},{4,6},{6,4},{5,7},{7,5},{8,10},{10,8},{9,1... | collective-permute-start | bytes 4718600 | tf_op jit(solution)/shard_map/ppermute | solution.py:47
  63.0 0.0 copy-done
  63.0 0.0 copy-done.1
  63.0 0.0 copy-done.2
  63.0 0.0 copy-done.8
  63.0 0.0 copy-done.9
  63.0 0.0 copy-done.10
  63.0 0.0 copy-done.11
  63.1 0.0 copy-done.12
  63.1 0.6 shard_map.130
  63.7 4.4 %collective-permute-start = (f32[24,256]{1,0:T(8,128)S(1)}, f32[24,256]{1,0:T(8,128)S(1)}, u32[]{:S(2)}, u32[]{:S(2)}) collective-permute-start(f32[24,256]{1,0:T(8,128)S(1)} %get-tuple-element.10.refs_3_.refs_4_), channel_id=1, source_target_pairs={{0,1},{1,0},{2,3},{3,2},{4,5},{5,4},{6,7},{7,6},{8,9},{9,8},{10,11... | collective-permute-start | bytes 73736 | tf_op jit(solution)/shard_map/ppermute | solution.py:47
  68.1 1.7 collective-permute-done.refs_4_.refs_5_
  69.8 0.7 shard_map.131
  70.5 3.1 %collective-permute-start.1 = (bf16[448,256]{1,0:T(8,128)(2,1)S(1)}, bf16[448,256]{1,0:T(8,128)(2,1)S(1)}, u32[]{:S(2)}, u32[]{:S(2)}) collective-permute-start(bf16[448,256]{1,0:T(8,128)(2,1)S(1)} %shard_map.131), channel_id=1, source_target_pairs={{0,2},{2,0},{1,3},{3,1},{4,6},{6,4},{5,7},{7,5},{8,10},{10,8},{9,1... | collective-permute-start | bytes 688136 | tf_op jit(solution)/shard_map/ppermute | solution.py:47
  73.5 1.1 collective-permute-done.1.refs_6_
  74.7 6.5 %collective-permute-start.2 = (bf16[896,256]{1,0:T(8,128)(2,1)S(1)}, bf16[896,256]{1,0:T(8,128)(2,1)S(1)}, u32[]{:S(2)}, u32[]{:S(2)}) collective-permute-start(bf16[896,256]{1,0:T(8,128)(2,1)S(1)} %pad_maximum_fusion), channel_id=1, source_target_pairs={{2,4},{4,2},{6,8},{8,6},{10,12},{12,10},{14,16},{16,14},{18,20},{2... | collective-permute-start | bytes 1376264 | tf_op jit(solution)/shard_map/ppermute | solution.py:54
  81.2 6.1 %collective-permute-done.2.refs_7_ = bf16[896,256]{1,0:T(8,128)(2,1)S(1)} collective-permute-done((bf16[896,256]{1,0:T(8,128)(2,1)S(1)}, bf16[896,256]{1,0:T(8,128)(2,1)S(1)}, u32[]{:S(2)}, u32[]{:S(2)}) %collective-permute-start.2) | collective-permute-done | bytes 458784 | tf_op jit(solution)/shard_map/ppermute | solution.py:54
  87.3 1.9 %collective-permute-start.3 = (bf16[896,256]{1,0:T(8,128)(2,1)S(1)}, bf16[896,256]{1,0:T(8,128)(2,1)S(1)}, u32[]{:S(2)}, u32[]{:S(2)}) collective-permute-start(bf16[896,256]{1,0:T(8,128)(2,1)S(1)} %collective-permute-done.2.refs_7_), channel_id=1, source_target_pairs={{0,2},{2,0},{1,3},{3,1},{4,6},{6,4},{5,7},{7,5},{8,10},{10,8},{9,1... | collective-permute-start | bytes 1376264 | tf_op jit(solution)/shard_map/ppermute | solution.py:47
  89.3 3.2 %collective-permute-start.4 = (bf16[128,256]{1,0:T(8,128)(2,1)S(1)}, bf16[128,256]{1,0:T(8,128)(2,1)S(1)}, u32[]{:S(2)}, u32[]{:S(2)}) collective-permute-start(bf16[128,256]{1,0:T(8,128)(2,1)S(1)} %get-tuple-element.11), channel_id=1, source_target_pairs={{2,8},{6,12},{10,16},{14,20},{18,24},{22,28},{26,32},{30,36},{34,4... | collective-permute-start | bytes 196616 | tf_op jit(solution)/shard_map/ppermute | solution.py:60
  92.5 3.3 %collective-permute-done.4.refs_9_ = bf16[128,256]{1,0:T(8,128)(2,1)S(1)} collective-permute-done((bf16[128,256]{1,0:T(8,128)(2,1)S(1)}, bf16[128,256]{1,0:T(8,128)(2,1)S(1)}, u32[]{:S(2)}, u32[]{:S(2)}) %collective-permute-start.4) | collective-permute-done | bytes 65568 | tf_op jit(solution)/shard_map/ppermute | solution.py:60
  95.7 0.0 collective-permute-done.3.refs_8_
  95.8 0.0 collective-permute-done.5.refs_11_
  95.8 13.7 %shard_map.133 = (f32[128,256]{1,0:T(8,128)S(1)}, f32[128,256]{1,0:T(8,128)S(1)}, bf16[2,8,2,128,128]{4,3,2,1,0:T(8,128)(2,1)S(1)}) custom-call(s32[1]{0:T(128)} %bitcast.refs_0_, f32[1,128,256]{2,1,0:T(8,128)S(1)} %copy-done, f32[1,128,256]{2,1,0:T(8,128)S(1)} %copy-done.1, f32[1,128,256]{2,1,0:T(8,128)S(1)} %copy-done.2, ...), custom_call_target="tpu_custom_call" | custom-call | flops 8053063680 | bytes 6111236 | tf_op jit(solution)/shard_map/pallas_call | solution.py:359
  109.5 25.9 %all_to_all.32.parts = bf16[32,128,128]{2,1,0:T(8,128)(2,1)S(1)} all-to-all(bf16[32,128,128]{2,1,0:T(8,128)(2,1)S(1)} %bitcast.15), channel_id=1, replica_groups=mesh['x_lo'=2,'y'=4,'z_hi'=4,'z_lo'=4,'core'=2,'x_hi'=2] {'x_hi','x_lo',..., dimensions={0} | all-to-all | bytes 2097152 | tf_op jit(solution)/shard_map/all_to_all | solution.py:408
  135.4 0.8 shard_map.134
  136.2 0.0 copy-start.4
  136.2 0.0 copy-start.6
  136.2 3.5 %all-to-all-start.3 = ((bf16[4,128,128]{2,1,0:T(8,128)(2,1)}), bf16[4,128,128]{2,1,0:T(8,128)(2,1)S(1)}, u32[]{:S(2)}, u32[]{:S(2)}) async-start(bf16[4,128,128]{2,1,0:T(8,128)(2,1)} %shard_map.134), calls=%async_computation.3 | async-start | bytes 262144 | tf_op jit(solution)/shard_map/all_to_all | solution.py:417
  139.7 0.1 pad_add_fusion.place
  139.8 4.8 %all-to-all-done.3.parts = bf16[4,128,128]{2,1,0:T(8,128)(2,1)S(1)} async-done(((bf16[4,128,128]{2,1,0:T(8,128)(2,1)}), bf16[4,128,128]{2,1,0:T(8,128)(2,1)S(1)}, u32[]{:S(2)}, u32[]{:S(2)}) %all-to-all-start.3) | async-done | bytes 131104 | tf_op jit(solution)/shard_map/all_to_all | solution.py:417
  144.5 0.7 shard_map.135
  145.2 7.1 %all-to-all-start.4 = ((bf16[4,128,128]{2,1,0:T(8,128)(2,1)}), bf16[4,128,128]{2,1,0:T(8,128)(2,1)S(1)}, u32[]{:S(2)}, u32[]{:S(2)}) async-start(bf16[4,128,128]{2,1,0:T(8,128)(2,1)} %shard_map.135), calls=%async_computation.4 | async-start | bytes 262144 | tf_op jit(solution)/shard_map/all_to_all | solution.py:417
  152.3 3.2 %collective-permute-start.8 = (f32[2,256]{1,0:T(2,128)S(1)}, f32[2,256]{1,0:T(2,128)S(1)}, u32[]{:S(2)}, u32[]{:S(2)}) collective-permute-start(f32[2,256]{1,0:T(2,128)S(1)} %pad_maximum_fusion.1), channel_id=1, source_target_pairs={{0,1},{1,0},{2,3},{3,2},{4,5},{5,4},{6,7},{7,6},{8,9},{9,8},{10,11... | collective-permute-start | bytes 6152 | tf_op jit(solution)/shard_map/ppermute | solution.py:47
  155.5 5.0 %collective-permute-start.6 = (f32[128,256]{1,0:T(8,128)S(1)}, f32[128,256]{1,0:T(8,128)S(1)}, u32[]{:S(2)}, u32[]{:S(2)}) collective-permute-start(f32[128,256]{1,0:T(8,128)S(1)} %get-tuple-element.13), channel_id=1, source_target_pairs={{2,4},{4,2},{6,8},{8,6},{10,12},{12,10},{14,16},{16,14},{18,20},{2... | collective-permute-start | bytes 393224 | tf_op jit(solution)/shard_map/ppermute | solution.py:54
  160.5 1.9 %collective-permute-start.7 = (f32[128,256]{1,0:T(8,128)S(1)}, f32[128,256]{1,0:T(8,128)S(1)}, u32[]{:S(2)}, u32[]{:S(2)}) collective-permute-start(f32[128,256]{1,0:T(8,128)S(1)} %get-tuple-element.13), channel_id=1, source_target_pairs={{0,2},{2,0},{1,3},{3,1},{4,6},{6,4},{5,7},{7,5},{8,10},{10,8},{9,1... | collective-permute-start | bytes 393224 | tf_op jit(solution)/shard_map/ppermute | solution.py:47
  162.5 2.1 %all-to-all-done.4.parts = bf16[4,128,128]{2,1,0:T(8,128)(2,1)S(1)} async-done(((bf16[4,128,128]{2,1,0:T(8,128)(2,1)}), bf16[4,128,128]{2,1,0:T(8,128)(2,1)S(1)}, u32[]{:S(2)}, u32[]{:S(2)}) %all-to-all-start.4) | async-done | bytes 131104 | tf_op jit(solution)/shard_map/all_to_all | solution.py:417
  164.5 0.7 shard_map.136
  165.2 8.1 %all-to-all-start.5 = ((f32[32,16,128]{2,1,0:T(8,128)}), f32[32,16,128]{2,1,0:T(8,128)S(1)}, u32[]{:S(2)}, u32[]{:S(2)}) async-start(f32[32,16,128]{2,1,0:T(8,128)} %shard_map.136), calls=%async_computation.5 | async-start | bytes 524288 | tf_op jit(solution)/shard_map/all_to_all | solution.py:427
  173.3 0.0 collective-permute-done.8
  173.3 0.0 collective-permute-done.6
  173.3 0.0 collective-permute-done.7
  173.4 0.7 fusion.2
  174.1 8.3 %all-to-all-done.5.parts = f32[32,16,128]{2,1,0:T(8,128)S(1)} async-done(((f32[32,16,128]{2,1,0:T(8,128)}), f32[32,16,128]{2,1,0:T(8,128)S(1)}, u32[]{:S(2)}, u32[]{:S(2)}) %all-to-all-start.5) | async-done | bytes 262176 | tf_op jit(solution)/shard_map/all_to_all | solution.py:427
  182.3 0.0 copy-done.4
  182.3 0.0 copy-done.6
  182.3 1.3 shard_map.137
  (9 shorter events, 0.1 us)
Async XLA Ops:
  0.6 0.7 copy-start.3
  1.3 0.7 copy-start.5
  2.0 0.7 copy-start.7
  33.6 29.4 %copy-start = (f32[1,128,256]{2,1,0:T(8,128)S(1)}, f32[1,128,256]{2,1,0:T(8,128)}, u32[]{:S(2)}) copy-start(f32[1,128,256]{2,1,0:T(8,128)} %refs_1_.7) | copy-start | bytes 393220
  33.6 29.4 %copy-start.1 = (f32[1,128,256]{2,1,0:T(8,128)S(1)}, f32[1,128,256]{2,1,0:T(8,128)}, u32[]{:S(2)}) copy-start(f32[1,128,256]{2,1,0:T(8,128)} %refs_2_.7) | copy-start | bytes 393220
  33.6 29.4 %copy-start.2 = (f32[1,128,256]{2,1,0:T(8,128)S(1)}, f32[1,128,256]{2,1,0:T(8,128)}, u32[]{:S(2)}) copy-start(f32[1,128,256]{2,1,0:T(8,128)} %refs_3_.3) | copy-start | bytes 393220
  33.6 29.4 %copy-start.8 = (s32[1,128]{1,0:T(1,128)S(1)}, s32[1,128]{1,0:T(1,128)}, u32[]{:S(2)}) copy-start(s32[1,128]{1,0:T(1,128)} %refs_3_.2) | copy-start | bytes 1540
  33.6 29.4 %copy-start.9 = (s32[64]{0:T(128)S(1)}, s32[64]{0:T(128)}, u32[]{:S(2)}) copy-start(s32[64]{0:T(128)} %param.18) | copy-start | bytes 772
  33.6 29.4 %copy-start.10 = (s32[64]{0:T(128)S(1)}, s32[64]{0:T(128)}, u32[]{:S(2)}) copy-start(s32[64]{0:T(128)} %param.19) | copy-start | bytes 772
  33.7 29.4 %copy-start.11 = (f32[64]{0:T(128)S(1)}, f32[64]{0:T(128)}, u32[]{:S(2)}) copy-start(f32[64]{0:T(128)} %param.20) | copy-start | bytes 772
  33.7 29.4 %copy-start.12 = (f32[64]{0:T(128)S(1)}, f32[64]{0:T(128)}, u32[]{:S(2)}) copy-start(f32[64]{0:T(128)} %param.21) | copy-start | bytes 772
  55.9 39.8 %collective-permute-start.5 = (bf16[1024,768]{1,0:T(8,128)(2,1)S(1)}, bf16[1024,768]{1,0:T(8,128)(2,1)S(1)}, u32[]{:S(2)}, u32[]{:S(2)}) collective-permute-start(bf16[1024,768]{1,0:T(8,128)(2,1)S(1)} %bitcast.13), channel_id=1, source_target_pairs={{0,2},{2,0},{1,3},{3,1},{4,6},{6,4},{5,7},{7,5},{8,10},{10,8},{9,1... | collective-permute-start | bytes 4718600 | tf_op jit(solution)/shard_map/ppermute | solution.py:47
  63.7 6.1 %collective-permute-start = (f32[24,256]{1,0:T(8,128)S(1)}, f32[24,256]{1,0:T(8,128)S(1)}, u32[]{:S(2)}, u32[]{:S(2)}) collective-permute-start(f32[24,256]{1,0:T(8,128)S(1)} %get-tuple-element.10.refs_3_.refs_4_), channel_id=1, source_target_pairs={{0,1},{1,0},{2,3},{3,2},{4,5},{5,4},{6,7},{7,6},{8,9},{9,8},{10,11... | collective-permute-start | bytes 73736 | tf_op jit(solution)/shard_map/ppermute | solution.py:47
  70.5 4.2 %collective-permute-start.1 = (bf16[448,256]{1,0:T(8,128)(2,1)S(1)}, bf16[448,256]{1,0:T(8,128)(2,1)S(1)}, u32[]{:S(2)}, u32[]{:S(2)}) collective-permute-start(bf16[448,256]{1,0:T(8,128)(2,1)S(1)} %shard_map.131), channel_id=1, source_target_pairs={{0,2},{2,0},{1,3},{3,1},{4,6},{6,4},{5,7},{7,5},{8,10},{10,8},{9,1... | collective-permute-start | bytes 688136 | tf_op jit(solution)/shard_map/ppermute | solution.py:47
  74.7 12.7 %collective-permute-start.2 = (bf16[896,256]{1,0:T(8,128)(2,1)S(1)}, bf16[896,256]{1,0:T(8,128)(2,1)S(1)}, u32[]{:S(2)}, u32[]{:S(2)}) collective-permute-start(bf16[896,256]{1,0:T(8,128)(2,1)S(1)} %pad_maximum_fusion), channel_id=1, source_target_pairs={{2,4},{4,2},{6,8},{8,6},{10,12},{12,10},{14,16},{16,14},{18,20},{2... | collective-permute-start | bytes 1376264 | tf_op jit(solution)/shard_map/ppermute | solution.py:54
  87.3 8.4 %collective-permute-start.3 = (bf16[896,256]{1,0:T(8,128)(2,1)S(1)}, bf16[896,256]{1,0:T(8,128)(2,1)S(1)}, u32[]{:S(2)}, u32[]{:S(2)}) collective-permute-start(bf16[896,256]{1,0:T(8,128)(2,1)S(1)} %collective-permute-done.2.refs_7_), channel_id=1, source_target_pairs={{0,2},{2,0},{1,3},{3,1},{4,6},{6,4},{5,7},{7,5},{8,10},{10,8},{9,1... | collective-permute-start | bytes 1376264 | tf_op jit(solution)/shard_map/ppermute | solution.py:47
  89.3 6.5 %collective-permute-start.4 = (bf16[128,256]{1,0:T(8,128)(2,1)S(1)}, bf16[128,256]{1,0:T(8,128)(2,1)S(1)}, u32[]{:S(2)}, u32[]{:S(2)}) collective-permute-start(bf16[128,256]{1,0:T(8,128)(2,1)S(1)} %get-tuple-element.11), channel_id=1, source_target_pairs={{2,8},{6,12},{10,16},{14,20},{18,24},{22,28},{26,32},{30,36},{34,4... | collective-permute-start | bytes 196616 | tf_op jit(solution)/shard_map/ppermute | solution.py:60
  136.2 46.1 %copy-start.4 = (f32[4,256]{1,0:T(4,128)S(1)}, f32[4,256]{1,0:T(4,128)}, u32[]{:S(2)}) copy-start(f32[4,256]{1,0:T(4,128)} %w_in.1) | copy-start | bytes 12292
  136.2 46.1 %copy-start.6 = (f32[4,256]{1,0:T(4,128)S(1)}, f32[4,256]{1,0:T(4,128)}, u32[]{:S(2)}) copy-start(f32[4,256]{1,0:T(4,128)} %w_out.1) | copy-start | bytes 12292
  136.2 8.3 %all-to-all-start.3 = ((bf16[4,128,128]{2,1,0:T(8,128)(2,1)}), bf16[4,128,128]{2,1,0:T(8,128)(2,1)S(1)}, u32[]{:S(2)}, u32[]{:S(2)}) async-start(bf16[4,128,128]{2,1,0:T(8,128)(2,1)} %shard_map.134), calls=%async_computation.3 | async-start | bytes 262144 | tf_op jit(solution)/shard_map/all_to_all | solution.py:417
  145.2 19.3 %all-to-all-start.4 = ((bf16[4,128,128]{2,1,0:T(8,128)(2,1)}), bf16[4,128,128]{2,1,0:T(8,128)(2,1)S(1)}, u32[]{:S(2)}, u32[]{:S(2)}) async-start(bf16[4,128,128]{2,1,0:T(8,128)(2,1)} %shard_map.135), calls=%async_computation.4 | async-start | bytes 262144 | tf_op jit(solution)/shard_map/all_to_all | solution.py:417
  152.3 21.0 %collective-permute-start.8 = (f32[2,256]{1,0:T(2,128)S(1)}, f32[2,256]{1,0:T(2,128)S(1)}, u32[]{:S(2)}, u32[]{:S(2)}) collective-permute-start(f32[2,256]{1,0:T(2,128)S(1)} %pad_maximum_fusion.1), channel_id=1, source_target_pairs={{0,1},{1,0},{2,3},{3,2},{4,5},{5,4},{6,7},{7,6},{8,9},{9,8},{10,11... | collective-permute-start | bytes 6152 | tf_op jit(solution)/shard_map/ppermute | solution.py:47
  155.5 17.8 %collective-permute-start.6 = (f32[128,256]{1,0:T(8,128)S(1)}, f32[128,256]{1,0:T(8,128)S(1)}, u32[]{:S(2)}, u32[]{:S(2)}) collective-permute-start(f32[128,256]{1,0:T(8,128)S(1)} %get-tuple-element.13), channel_id=1, source_target_pairs={{2,4},{4,2},{6,8},{8,6},{10,12},{12,10},{14,16},{16,14},{18,20},{2... | collective-permute-start | bytes 393224 | tf_op jit(solution)/shard_map/ppermute | solution.py:54
  160.5 12.8 %collective-permute-start.7 = (f32[128,256]{1,0:T(8,128)S(1)}, f32[128,256]{1,0:T(8,128)S(1)}, u32[]{:S(2)}, u32[]{:S(2)}) collective-permute-start(f32[128,256]{1,0:T(8,128)S(1)} %get-tuple-element.13), channel_id=1, source_target_pairs={{0,2},{2,0},{1,3},{3,1},{4,6},{6,4},{5,7},{7,5},{8,10},{10,8},{9,1... | collective-permute-start | bytes 393224 | tf_op jit(solution)/shard_map/ppermute | solution.py:47
  165.2 17.1 %all-to-all-start.5 = ((f32[32,16,128]{2,1,0:T(8,128)}), f32[32,16,128]{2,1,0:T(8,128)S(1)}, u32[]{:S(2)}, u32[]{:S(2)}) async-start(f32[32,16,128]{2,1,0:T(8,128)} %shard_map.136), calls=%async_computation.5 | async-start | bytes 524288 | tf_op jit(solution)/shard_map/all_to_all | solution.py:427

commit v6 on v5

--- a/solution.py
+++ b/solution.py
@@ -26,7 +26,7 @@
     return lax.all_to_all(jnp.broadcast_to(block[None], (count,) + block.shape), axis, 0, 0)
 
 
-def gather_weights(w_in, w_mid, w_out):
+def chip_rows(w_in, w_mid, w_out):
     columns = 2 * w_in.shape[1] + w_mid.shape[1]
     (rows,) = on_chip(
         pack_kernel,
@@ -34,13 +34,11 @@
         (w_in, w_mid, w_out),
         0,
         fetched=3,
+        room=56,
     )
     rows = lax.all_gather(rows, "core", axis=0, tiled=True)
-    width = rows.shape[1] // 2
-    half = lax.dynamic_slice_in_dim(rows, lax.axis_index("core") * width, width, 1)
-    half = spread(half, Z).reshape(-1, width)
-    half = spread(half, ("x_lo", "y")).reshape(-1, width)
-    return half
+    width = columns // 2
+    return lax.dynamic_slice_in_dim(rows, lax.axis_index("core") * width, width, 1)
 
 
 def swapped(array, axis):
@@ -326,7 +324,7 @@
                 ]
 
 
-def on_chip(kernel, outs, operands, flops, scratch=(), scalars=0, fetched=0, place=None):
+def on_chip(kernel, outs, operands, flops, scratch=(), scalars=0, fetched=0, place=None, room=32):
     size = sum(array.size * array.dtype.itemsize for array in list(operands) + list(outs))
     count = len(operands) - scalars
     by_kernel = fetched > 0
@@ -362,7 +360,7 @@
         in_specs=[pl.BlockSpec(memory_space=place_) for place_ in places],
         out_specs=[pl.BlockSpec(memory_space=pltpu.VMEM)] * len(outs),
         scratch_shapes=scratch,
-        compiler_params=pltpu.CompilerParams(vmem_limit_bytes=32 * 1024 * 1024),
+        compiler_params=pltpu.CompilerParams(vmem_limit_bytes=room * 1024 * 1024),
         cost_estimate=pl.CostEstimate(flops=flops, bytes_accessed=size, transcendentals=0),
     )(*operands)
 
@@ -441,33 +439,40 @@
 ):
     _, cells, features = state.shape
     length = cells + 8
-    fields = (state, increment, diffusivity, land_sea)
     observed = [numbers[None] for numbers in (obs_col, obs_lev, obs_val, obs_prec)]
 
     def outs(*shapes):
         return tuple(jax.ShapeDtypeStruct(shape, kind) for shape, kind in shapes)
 
+    half = chip_rows(w_in, w_mid, w_out)
+    width = half.shape[1]
+    half, land_sea = lax.optimization_barrier((half, land_sea))
+    fields = (state, increment, diffusivity, land_sea)
     mine, outer = on_chip(
         edge_kernel,
         outs(((24, features), jnp.float32), ((cells, features), jnp.bfloat16)),
         fields + tuple(observed),
         0,
         fetched=8,
-    )
+        room=56,
+    )
+    half = spread(half, Z).reshape(-1, width)
+    other = swapped(mine, "x_hi")
     outer = swapped_three_apart(outer)
-    other = swapped(mine, "x_hi")
     (own,) = on_chip(
         pack_row_kernel,
         outs(((3 * BLOCK + 16, features), jnp.bfloat16)),
         fields[:3] + (mine, other),
         0,
         fetched=5,
+        room=56,
     )
     near = swapped(own, "core")
+    half, near, outer = lax.optimization_barrier((half, near, outer))
+    half = spread(half, ("x_lo", "y")).reshape(-1, width)
     far = swapped_between_chips(jnp.concatenate([own, near]))
     beyond = swapped(far, "core")
-
-    half = gather_weights(w_in, w_mid, w_out)
+    half, far, beyond = lax.optimization_barrier((half, far, beyond))
     hidden_units, width = half.shape
     blocks = lax.axis_size(("x_lo", "y"))
     halves = lax.axis_size("core")

time: 184 us -> 166 us (0.902)
  blocking collectives: 78.8 us -> 33.5 us
  starting transfers between devices: 54.8 us -> 71.3 us
  waiting for transfers between devices: 27.3 us -> 33.6 us
  Pallas kernels: 18.5 us -> 22.2 us
    all_to_all x2 -> x0, blocking collectives: 44.5 us -> none  [spread(): lax.all_to_all(jnp.broadcast_to(block[None], (count,) + block.shape), axi...]
    all_to_all x0 -> x2, starting transfers between devices: none -> 14.8 us  [spread(): lax.all_to_all(jnp.broadcast_to(block[None], (count,) + block.shape), axi...]
    pallas_call x8, Pallas kernels: 18.5 us -> 22.2 us  [on_chip(): pl.pallas_call(body, out_shape=outs, in_specs=[pl.BlockSpec(memory_space=...]
    ppermute x6, waiting for transfers between devices: 2.81 us -> 6.43 us  [swapped(): return lax.ppermute(array, axis, [(0, 1), (1, 0)])]
    ppermute x6, starting transfers between devices: 21.5 us -> 24.5 us  [swapped(): return lax.ppermute(array, axis, [(0, 1), (1, 0)])]
    broadcast_in_dim x2, local copies, waits for them, and re-layouts: 0.12 us -> 1.98 us  [spread(): jnp.broadcast_to(block[None], (count,) + block.shape)]
  transfers between devices with their start and end apart: 12 -> 14, of which waited for: 7 -> 9; matrix products, arithmetic and copies ran while one was open for 0% -> 1% of each run, Pallas kernels for 1% -> 3%
where the time goes in v6:
time: 166 us; the launch traced here: 165 us
  starting transfers between devices  71.3 us (43%)
  waiting for transfers between devices  33.6 us (20%)
  blocking collectives  33.5 us (20%)
  Pallas kernels  22.2 us (13%)
  local copies, waits for them, and re-layouts  2.66 us (2%)
    all_to_all x1, blocking collectives, updated(): grads = lax.all_to_all(grads.reshape(peers, rows, columns), AROUND, 0, 0)  24.9 us
    ppermute x6, starting transfers between devices, swapped(): return lax.ppermute(array, axis, [(0, 1), (1, 0)])  24.5 us
    pallas_call x8, Pallas kernels, on_chip(): pl.pallas_call(body, out_shape=outs, in_specs=[pl.BlockSpec(memory_space=...  22.2 us
    all_to_all x2, starting transfers between devices, spread(): lax.all_to_all(jnp.broadcast_to(block[None], (count,) + block.shape), axi...  14.8 us
    all_to_all x2, starting transfers between devices, updated(): grads = lax.all_to_all(copies, axis, 0, 0)  10.6 us
    ppermute x2, starting transfers between devices, swapped_between_chips(): return lax.ppermute(array, TILE, pairs)  10.2 us
    all_gather x1, blocking collectives, chip_rows(): rows = lax.all_gather(rows, 'core', axis=0, tiled=True)  8.58 us
    all_to_all x1, waiting for transfers between devices, updated(): parts = lax.all_to_all(copies, AROUND, 0, 0)  8.35 us
  transfers between devices with their start and end apart: 14, of which 9 were waited for; matrix products, arithmetic and copies ran while one was open for 1% of the time, Pallas kernels for 3%

profile of v6, /device:TPU:1, one launch (start us, length us, event | category | flops | bytes accessed | tf_op | source)
XLA Modules:
  0.0 165.0 jit_solution(15210378954422602747)
XLA Ops:
  0.6 1.3 shard_map.130
  2.0 8.6 %all-gather = bf16[2,4,1536]{2,1,0:T(4,128)(2,1)S(1)} all-gather(bf16[1,4,1536]{2,1,0:T(4,128)(2,1)} %bitcast.17), channel_id=1, replica_groups=mesh['x_lo'=2,'y'=4,'z_hi'=4,'z_lo'=4,'core'=2,'x_hi'=2] {'core'}, dimensions={0}, use_global_device_ids=true | all-gather | bytes 36864 | tf_op jit(solution)/shard_map/all_gather | solution.py:39
  10.6 0.7 broadcast_in_dim.38
  11.3 9.5 %all-to-all-start = ((bf16[16,8,768]{2,1,0:T(8,128)(2,1)}), bf16[16,8,768]{2,1,0:T(8,128)(2,1)S(1)}, u32[]{:S(2)}, u32[]{:S(2)}) async-start(bf16[16,8,768]{2,1,0:T(8,128)(2,1)} %broadcast_in_dim.38), calls=%async_computation | async-start | bytes 393216 | tf_op jit(solution)/shard_map/all_to_all | solution.py:26
  20.8 1.8 %shard_map.131 = (f32[24,256]{1,0:T(8,128)}, bf16[128,256]{1,0:T(8,128)(2,1)}) custom-call(f32[1,128,256]{2,1,0:T(8,128)} %refs_1_.7, f32[1,128,256]{2,1,0:T(8,128)} %refs_2_.7, f32[1,128,256]{2,1,0:T(8,128)} %refs_3_.2, s32[1,128]{1,0:T(1,128)} %refs_3_.1, s32[1,64]{1,0:T(1,128)} %bitcast.18, s32[1,64]{1,0:T(1,128)} %bitcast.19, f32[1,64]{1,0:T(1,128)} %bitcast.20, ...), custom_call_target="tpu_custom_call" | custom-call | bytes 484864 | tf_op jit(solution)/shard_map/pallas_call | solution.py:357
  22.6 4.7 %collective-permute-start = (f32[24,256]{1,0:T(8,128)}, f32[24,256]{1,0:T(8,128)S(1)}, u32[]{:S(2)}, u32[]{:S(2)}) collective-permute-start(f32[24,256]{1,0:T(8,128)} %get-tuple-element.19.refs_3_.refs_4_), channel_id=1, source_target_pairs={{0,1},{1,0},{2,3},{3,2},{4,5},{5,4},{6,7},{7,6},{8,9},{9,8},{10,11... | collective-permute-start | bytes 73736 | tf_op jit(solution)/shard_map/ppermute | solution.py:45
  27.3 1.6 collective-permute-done.refs_4_.refs_5_
  28.9 0.0 copy-start.4
  28.9 0.6 copy-done.4
  29.5 1.9 %shard_map.132 = bf16[448,256]{1,0:T(8,128)(2,1)} custom-call(f32[1,128,256]{2,1,0:T(8,128)} %refs_1_.7, f32[1,128,256]{2,1,0:T(8,128)} %refs_2_.7, f32[1,128,256]{2,1,0:T(8,128)} %refs_3_.2, f32[24,256]{1,0:T(8,128)} %get-tuple-element.19.refs_3_.refs_4_, f32[24,256]{1,0:T(8,128)} %copy-done.4), custom_call_target="tpu_custom_call" | custom-call | bytes 671744 | tf_op jit(solution)/shard_map/pallas_call | solution.py:357
  31.4 3.7 %collective-permute-start.1 = (bf16[448,256]{1,0:T(8,128)(2,1)}, bf16[448,256]{1,0:T(8,128)(2,1)S(1)}, u32[]{:S(2)}, u32[]{:S(2)}) collective-permute-start(bf16[448,256]{1,0:T(8,128)(2,1)} %shard_map.132), channel_id=1, source_target_pairs={{0,2},{2,0},{1,3},{3,1},{4,6},{6,4},{5,7},{7,5},{8,10},{10,8},{9,1... | collective-permute-start | bytes 688136 | tf_op jit(solution)/shard_map/ppermute | solution.py:45
  35.1 4.3 %collective-permute-start.2 = (bf16[128,256]{1,0:T(8,128)(2,1)}, bf16[128,256]{1,0:T(8,128)(2,1)S(1)}, u32[]{:S(2)}, u32[]{:S(2)}) collective-permute-start(bf16[128,256]{1,0:T(8,128)(2,1)} %get-tuple-element.21), channel_id=1, source_target_pairs={{2,8},{6,12},{10,16},{14,20},{18,24},{22,28},{26,32},{30,36},{34,4... | collective-permute-start | bytes 196616 | tf_op jit(solution)/shard_map/ppermute | solution.py:58
  39.4 2.3 %collective-permute-done.2.refs_9_ = bf16[128,256]{1,0:T(8,128)(2,1)S(1)} collective-permute-done((bf16[128,256]{1,0:T(8,128)(2,1)}, bf16[128,256]{1,0:T(8,128)(2,1)S(1)}, u32[]{:S(2)}, u32[]{:S(2)}) %collective-permute-start.2) | collective-permute-done | bytes 65568 | tf_op jit(solution)/shard_map/ppermute | solution.py:58
  41.8 0.0 collective-permute-done.1.refs_6_
  41.8 0.0 all-to-all-done
  41.8 1.3 broadcast_in_dim.39
  43.1 0.0 copy-start.8
  43.1 0.0 copy-start
  43.1 0.0 copy-start.1
  43.1 0.0 copy-start.2
  43.1 0.0 copy-start.3
  43.1 0.0 copy-start.5
  43.1 5.3 %all-to-all-start.1 = ((bf16[8,128,768]{2,1,0:T(8,128)(2,1)}), bf16[8,128,768]{2,1,0:T(8,128)(2,1)S(1)}, u32[]{:S(2)}, u32[]{:S(2)}) async-start(bf16[8,128,768]{2,1,0:T(8,128)(2,1)} %broadcast_in_dim.39), calls=%async_computation.1 | async-start | bytes 3145728 | tf_op jit(solution)/shard_map/all_to_all | solution.py:26
  48.4 0.0 copy-done.8
  48.4 5.9 %collective-permute-start.3 = (bf16[896,256]{1,0:T(8,128)(2,1)S(1)}, bf16[896,256]{1,0:T(8,128)(2,1)S(1)}, u32[]{:S(2)}, u32[]{:S(2)}) collective-permute-start(bf16[896,256]{1,0:T(8,128)(2,1)S(1)} %pad_maximum_fusion), channel_id=1, source_target_pairs={{2,4},{4,2},{6,8},{8,6},{10,12},{12,10},{14,16},{16,14},{18,20},{2... | collective-permute-start | bytes 1376264 | tf_op jit(solution)/shard_map/ppermute | solution.py:52
  54.3 6.4 %collective-permute-done.3.refs_7_ = bf16[896,256]{1,0:T(8,128)(2,1)S(1)} collective-permute-done((bf16[896,256]{1,0:T(8,128)(2,1)S(1)}, bf16[896,256]{1,0:T(8,128)(2,1)S(1)}, u32[]{:S(2)}, u32[]{:S(2)}) %collective-permute-start.3) | collective-permute-done | bytes 458784 | tf_op jit(solution)/shard_map/ppermute | solution.py:52
  60.8 1.9 %collective-permute-start.4 = (bf16[896,256]{1,0:T(8,128)(2,1)S(1)}, bf16[896,256]{1,0:T(8,128)(2,1)S(1)}, u32[]{:S(2)}, u32[]{:S(2)}) collective-permute-start(bf16[896,256]{1,0:T(8,128)(2,1)S(1)} %collective-permute-done.3.refs_7_), channel_id=1, source_target_pairs={{0,2},{2,0},{1,3},{3,1},{4,6},{6,4},{5,7},{7,5},{8,10},{10,8},{9,1... | collective-permute-start | bytes 1376264 | tf_op jit(solution)/shard_map/ppermute | solution.py:45
  62.7 1.8 %collective-permute-done.4.refs_8_ = bf16[896,256]{1,0:T(8,128)(2,1)S(1)} collective-permute-done((bf16[896,256]{1,0:T(8,128)(2,1)S(1)}, bf16[896,256]{1,0:T(8,128)(2,1)S(1)}, u32[]{:S(2)}, u32[]{:S(2)}) %collective-permute-start.4) | collective-permute-done | bytes 458784 | tf_op jit(solution)/shard_map/ppermute | solution.py:45
  64.5 1.8 %all-to-all-done.1 = bf16[8,128,768]{2,1,0:T(8,128)(2,1)S(1)} async-done(((bf16[8,128,768]{2,1,0:T(8,128)(2,1)}), bf16[8,128,768]{2,1,0:T(8,128)(2,1)S(1)}, u32[]{:S(2)}, u32[]{:S(2)}) %all-to-all-start.1) | async-done | bytes 1572896 | tf_op jit(solution)/shard_map/all_to_all | solution.py:26
  66.2 8.5 %collective-permute-start.5 = (bf16[1024,768]{1,0:T(8,128)(2,1)S(1)}, bf16[1024,768]{1,0:T(8,128)(2,1)S(1)}, u32[]{:S(2)}, u32[]{:S(2)}) collective-permute-start(bf16[1024,768]{1,0:T(8,128)(2,1)S(1)} %bitcast.13), channel_id=1, source_target_pairs={{0,2},{2,0},{1,3},{3,1},{4,6},{6,4},{5,7},{7,5},{8,10},{10,8},{9,1... | collective-permute-start | bytes 4718600 | tf_op jit(solution)/shard_map/ppermute | solution.py:45
  74.8 3.0 %collective-permute-done.5.refs_11_ = bf16[1024,768]{1,0:T(8,128)(2,1)S(1)} collective-permute-done((bf16[1024,768]{1,0:T(8,128)(2,1)S(1)}, bf16[1024,768]{1,0:T(8,128)(2,1)S(1)}, u32[]{:S(2)}, u32[]{:S(2)}) %collective-permute-start.5) | collective-permute-done | bytes 1572896 | tf_op jit(solution)/shard_map/ppermute | solution.py:45
  77.8 0.0 copy-done
  77.8 0.0 copy-done.1
  77.8 0.0 copy-done.2
  77.8 0.0 copy-done.3
  77.8 0.0 copy-done.5
  77.8 13.7 %shard_map.133 = (f32[128,256]{1,0:T(8,128)S(1)}, f32[128,256]{1,0:T(8,128)S(1)}, bf16[2,8,2,128,128]{4,3,2,1,0:T(8,128)(2,1)S(1)}) custom-call(s32[1]{0:T(128)} %bitcast.refs_0_, f32[1,128,256]{2,1,0:T(8,128)S(1)} %copy-done, f32[1,128,256]{2,1,0:T(8,128)S(1)} %copy-done.1, f32[1,128,256]{2,1,0:T(8,128)S(1)} %copy-done.2, f32[24,256]{1,0:T(8,128)S(1)} %copy-done.3, ...), custom_call_target="tpu_custom_call" | custom-call | flops 8053063680 | bytes 6111236 | tf_op jit(solution)/shard_map/pallas_call | solution.py:357
  91.6 24.9 %all_to_all.30.parts = bf16[32,128,128]{2,1,0:T(8,128)(2,1)S(1)} all-to-all(bf16[32,128,128]{2,1,0:T(8,128)(2,1)S(1)} %bitcast.15), channel_id=1, replica_groups=mesh['x_lo'=2,'y'=4,'z_hi'=4,'z_lo'=4,'core'=2,'x_hi'=2] {'x_hi','x_lo',..., dimensions={0} | all-to-all | bytes 2097152 | tf_op jit(solution)/shard_map/all_to_all | solution.py:406
  116.5 0.8 shard_map.134
  117.3 0.0 copy-start.6
  117.3 0.0 copy-start.7
  117.3 3.5 %all-to-all-start.3 = ((bf16[4,128,128]{2,1,0:T(8,128)(2,1)}), bf16[4,128,128]{2,1,0:T(8,128)(2,1)S(1)}, u32[]{:S(2)}, u32[]{:S(2)}) async-start(bf16[4,128,128]{2,1,0:T(8,128)(2,1)} %shard_map.134), calls=%async_computation.3 | async-start | bytes 262144 | tf_op jit(solution)/shard_map/all_to_all | solution.py:415
  120.8 0.1 pad_add_fusion.place
  120.9 4.8 %all-to-all-done.3.parts = bf16[4,128,128]{2,1,0:T(8,128)(2,1)S(1)} async-done(((bf16[4,128,128]{2,1,0:T(8,128)(2,1)}), bf16[4,128,128]{2,1,0:T(8,128)(2,1)S(1)}, u32[]{:S(2)}, u32[]{:S(2)}) %all-to-all-start.3) | async-done | bytes 131104 | tf_op jit(solution)/shard_map/all_to_all | solution.py:415
  125.6 0.7 shard_map.135
  126.3 7.1 %all-to-all-start.4 = ((bf16[4,128,128]{2,1,0:T(8,128)(2,1)}), bf16[4,128,128]{2,1,0:T(8,128)(2,1)S(1)}, u32[]{:S(2)}, u32[]{:S(2)}) async-start(bf16[4,128,128]{2,1,0:T(8,128)(2,1)} %shard_map.135), calls=%async_computation.4 | async-start | bytes 262144 | tf_op jit(solution)/shard_map/all_to_all | solution.py:415
  133.4 3.8 %collective-permute-start.8 = (f32[2,256]{1,0:T(2,128)S(1)}, f32[2,256]{1,0:T(2,128)S(1)}, u32[]{:S(2)}, u32[]{:S(2)}) collective-permute-start(f32[2,256]{1,0:T(2,128)S(1)} %pad_maximum_fusion.1), channel_id=1, source_target_pairs={{0,1},{1,0},{2,3},{3,2},{4,5},{5,4},{6,7},{7,6},{8,9},{9,8},{10,11... | collective-permute-start | bytes 6152 | tf_op jit(solution)/shard_map/ppermute | solution.py:45
  137.3 4.3 %collective-permute-start.6 = (f32[128,256]{1,0:T(8,128)S(1)}, f32[128,256]{1,0:T(8,128)S(1)}, u32[]{:S(2)}, u32[]{:S(2)}) collective-permute-start(f32[128,256]{1,0:T(8,128)S(1)} %get-tuple-element.29), channel_id=1, source_target_pairs={{2,4},{4,2},{6,8},{8,6},{10,12},{12,10},{14,16},{16,14},{18,20},{2... | collective-permute-start | bytes 393224 | tf_op jit(solution)/shard_map/ppermute | solution.py:52
  141.6 1.9 %collective-permute-start.7 = (f32[128,256]{1,0:T(8,128)S(1)}, f32[128,256]{1,0:T(8,128)S(1)}, u32[]{:S(2)}, u32[]{:S(2)}) collective-permute-start(f32[128,256]{1,0:T(8,128)S(1)} %get-tuple-element.29), channel_id=1, source_target_pairs={{0,2},{2,0},{1,3},{3,1},{4,6},{6,4},{5,7},{7,5},{8,10},{10,8},{9,1... | collective-permute-start | bytes 393224 | tf_op jit(solution)/shard_map/ppermute | solution.py:45
  143.6 3.5 %all-to-all-done.4.parts = bf16[4,128,128]{2,1,0:T(8,128)(2,1)S(1)} async-done(((bf16[4,128,128]{2,1,0:T(8,128)(2,1)}), bf16[4,128,128]{2,1,0:T(8,128)(2,1)S(1)}, u32[]{:S(2)}, u32[]{:S(2)}) %all-to-all-start.4) | async-done | bytes 131104 | tf_op jit(solution)/shard_map/all_to_all | solution.py:415
  147.0 0.7 shard_map.136
  147.8 6.9 %all-to-all-start.5 = ((f32[32,16,128]{2,1,0:T(8,128)}), f32[32,16,128]{2,1,0:T(8,128)S(1)}, u32[]{:S(2)}, u32[]{:S(2)}) async-start(f32[32,16,128]{2,1,0:T(8,128)} %shard_map.136), calls=%async_computation.5 | async-start | bytes 524288 | tf_op jit(solution)/shard_map/all_to_all | solution.py:425
  154.7 0.0 collective-permute-done.8
  154.7 0.0 collective-permute-done.6
  154.7 0.0 collective-permute-done.7
  154.7 0.7 fusion.2
  155.4 8.4 %all-to-all-done.5.parts = f32[32,16,128]{2,1,0:T(8,128)S(1)} async-done(((f32[32,16,128]{2,1,0:T(8,128)}), f32[32,16,128]{2,1,0:T(8,128)S(1)}, u32[]{:S(2)}, u32[]{:S(2)}) %all-to-all-start.5) | async-done | bytes 262176 | tf_op jit(solution)/shard_map/all_to_all | solution.py:425
  163.8 0.0 copy-done.6
  163.8 0.0 copy-done.7
  163.8 1.3 shard_map.137
  (7 shorter events, 0.1 us)
Async XLA Ops:
  11.3 30.5 %all-to-all-start = ((bf16[16,8,768]{2,1,0:T(8,128)(2,1)}), bf16[16,8,768]{2,1,0:T(8,128)(2,1)S(1)}, u32[]{:S(2)}, u32[]{:S(2)}) async-start(bf16[16,8,768]{2,1,0:T(8,128)(2,1)} %broadcast_in_dim.38), calls=%async_computation | async-start | bytes 393216 | tf_op jit(solution)/shard_map/all_to_all | solution.py:26
  22.6 6.3 %collective-permute-start = (f32[24,256]{1,0:T(8,128)}, f32[24,256]{1,0:T(8,128)S(1)}, u32[]{:S(2)}, u32[]{:S(2)}) collective-permute-start(f32[24,256]{1,0:T(8,128)} %get-tuple-element.19.refs_3_.refs_4_), channel_id=1, source_target_pairs={{0,1},{1,0},{2,3},{3,2},{4,5},{5,4},{6,7},{7,6},{8,9},{9,8},{10,11... | collective-permute-start | bytes 73736 | tf_op jit(solution)/shard_map/ppermute | solution.py:45
  28.9 0.6 copy-start.4
  31.4 10.4 %collective-permute-start.1 = (bf16[448,256]{1,0:T(8,128)(2,1)}, bf16[448,256]{1,0:T(8,128)(2,1)S(1)}, u32[]{:S(2)}, u32[]{:S(2)}) collective-permute-start(bf16[448,256]{1,0:T(8,128)(2,1)} %shard_map.132), channel_id=1, source_target_pairs={{0,2},{2,0},{1,3},{3,1},{4,6},{6,4},{5,7},{7,5},{8,10},{10,8},{9,1... | collective-permute-start | bytes 688136 | tf_op jit(solution)/shard_map/ppermute | solution.py:45
  35.1 6.7 %collective-permute-start.2 = (bf16[128,256]{1,0:T(8,128)(2,1)}, bf16[128,256]{1,0:T(8,128)(2,1)S(1)}, u32[]{:S(2)}, u32[]{:S(2)}) collective-permute-start(bf16[128,256]{1,0:T(8,128)(2,1)} %get-tuple-element.21), channel_id=1, source_target_pairs={{2,8},{6,12},{10,16},{14,20},{18,24},{22,28},{26,32},{30,36},{34,4... | collective-permute-start | bytes 196616 | tf_op jit(solution)/shard_map/ppermute | solution.py:58
  43.1 5.3 %copy-start.8 = (bf16[448,256]{1,0:T(8,128)(2,1)S(1)}, bf16[448,256]{1,0:T(8,128)(2,1)}, u32[]{:S(2)}) copy-start(bf16[448,256]{1,0:T(8,128)(2,1)} %shard_map.132) | copy-start | bytes 688132
  43.1 34.7 %copy-start = (f32[1,128,256]{2,1,0:T(8,128)S(1)}, f32[1,128,256]{2,1,0:T(8,128)}, u32[]{:S(2)}) copy-start(f32[1,128,256]{2,1,0:T(8,128)} %refs_1_.7) | copy-start | bytes 393220
  43.1 34.7 %copy-start.1 = (f32[1,128,256]{2,1,0:T(8,128)S(1)}, f32[1,128,256]{2,1,0:T(8,128)}, u32[]{:S(2)}) copy-start(f32[1,128,256]{2,1,0:T(8,128)} %refs_2_.7) | copy-start | bytes 393220
  43.1 34.7 %copy-start.2 = (f32[1,128,256]{2,1,0:T(8,128)S(1)}, f32[1,128,256]{2,1,0:T(8,128)}, u32[]{:S(2)}) copy-start(f32[1,128,256]{2,1,0:T(8,128)} %refs_3_.2) | copy-start | bytes 393220
  43.1 34.7 %copy-start.3 = (f32[24,256]{1,0:T(8,128)S(1)}, f32[24,256]{1,0:T(8,128)}, u32[]{:S(2)}) copy-start(f32[24,256]{1,0:T(8,128)} %get-tuple-element.19.refs_3_.refs_4_) | copy-start | bytes 73732
  43.1 34.7 %copy-start.5 = (f32[24,256]{1,0:T(8,128)S(1)}, f32[24,256]{1,0:T(8,128)}, u32[]{:S(2)}) copy-start(f32[24,256]{1,0:T(8,128)} %copy-done.4) | copy-start | bytes 73732
  43.1 23.2 %all-to-all-start.1 = ((bf16[8,128,768]{2,1,0:T(8,128)(2,1)}), bf16[8,128,768]{2,1,0:T(8,128)(2,1)S(1)}, u32[]{:S(2)}, u32[]{:S(2)}) async-start(bf16[8,128,768]{2,1,0:T(8,128)(2,1)} %broadcast_in_dim.39), calls=%async_computation.1 | async-start | bytes 3145728 | tf_op jit(solution)/shard_map/all_to_all | solution.py:26
  48.4 12.4 %collective-permute-start.3 = (bf16[896,256]{1,0:T(8,128)(2,1)S(1)}, bf16[896,256]{1,0:T(8,128)(2,1)S(1)}, u32[]{:S(2)}, u32[]{:S(2)}) collective-permute-start(bf16[896,256]{1,0:T(8,128)(2,1)S(1)} %pad_maximum_fusion), channel_id=1, source_target_pairs={{2,4},{4,2},{6,8},{8,6},{10,12},{12,10},{14,16},{16,14},{18,20},{2... | collective-permute-start | bytes 1376264 | tf_op jit(solution)/shard_map/ppermute | solution.py:52
  60.8 3.7 %collective-permute-start.4 = (bf16[896,256]{1,0:T(8,128)(2,1)S(1)}, bf16[896,256]{1,0:T(8,128)(2,1)S(1)}, u32[]{:S(2)}, u32[]{:S(2)}) collective-permute-start(bf16[896,256]{1,0:T(8,128)(2,1)S(1)} %collective-permute-done.3.refs_7_), channel_id=1, source_target_pairs={{0,2},{2,0},{1,3},{3,1},{4,6},{6,4},{5,7},{7,5},{8,10},{10,8},{9,1... | collective-permute-start | bytes 1376264 | tf_op jit(solution)/shard_map/ppermute | solution.py:45
  66.2 11.6 %collective-permute-start.5 = (bf16[1024,768]{1,0:T(8,128)(2,1)S(1)}, bf16[1024,768]{1,0:T(8,128)(2,1)S(1)}, u32[]{:S(2)}, u32[]{:S(2)}) collective-permute-start(bf16[1024,768]{1,0:T(8,128)(2,1)S(1)} %bitcast.13), channel_id=1, source_target_pairs={{0,2},{2,0},{1,3},{3,1},{4,6},{6,4},{5,7},{7,5},{8,10},{10,8},{9,1... | collective-permute-start | bytes 4718600 | tf_op jit(solution)/shard_map/ppermute | solution.py:45
  117.3 46.5 %copy-start.6 = (f32[4,256]{1,0:T(4,128)S(1)}, f32[4,256]{1,0:T(4,128)}, u32[]{:S(2)}) copy-start(f32[4,256]{1,0:T(4,128)} %w_in.1) | copy-start | bytes 12292
  117.3 46.5 %copy-start.7 = (f32[4,256]{1,0:T(4,128)S(1)}, f32[4,256]{1,0:T(4,128)}, u32[]{:S(2)}) copy-start(f32[4,256]{1,0:T(4,128)} %w_out.1) | copy-start | bytes 12292
  117.3 8.3 %all-to-all-start.3 = ((bf16[4,128,128]{2,1,0:T(8,128)(2,1)}), bf16[4,128,128]{2,1,0:T(8,128)(2,1)S(1)}, u32[]{:S(2)}, u32[]{:S(2)}) async-start(bf16[4,128,128]{2,1,0:T(8,128)(2,1)} %shard_map.134), calls=%async_computation.3 | async-start | bytes 262144 | tf_op jit(solution)/shard_map/all_to_all | solution.py:415
  126.3 20.7 %all-to-all-start.4 = ((bf16[4,128,128]{2,1,0:T(8,128)(2,1)}), bf16[4,128,128]{2,1,0:T(8,128)(2,1)S(1)}, u32[]{:S(2)}, u32[]{:S(2)}) async-start(bf16[4,128,128]{2,1,0:T(8,128)(2,1)} %shard_map.135), calls=%async_computation.4 | async-start | bytes 262144 | tf_op jit(solution)/shard_map/all_to_all | solution.py:415
  133.4 21.2 %collective-permute-start.8 = (f32[2,256]{1,0:T(2,128)S(1)}, f32[2,256]{1,0:T(2,128)S(1)}, u32[]{:S(2)}, u32[]{:S(2)}) collective-permute-start(f32[2,256]{1,0:T(2,128)S(1)} %pad_maximum_fusion.1), channel_id=1, source_target_pairs={{0,1},{1,0},{2,3},{3,2},{4,5},{5,4},{6,7},{7,6},{8,9},{9,8},{10,11... | collective-permute-start | bytes 6152 | tf_op jit(solution)/shard_map/ppermute | solution.py:45
  137.3 17.4 %collective-permute-start.6 = (f32[128,256]{1,0:T(8,128)S(1)}, f32[128,256]{1,0:T(8,128)S(1)}, u32[]{:S(2)}, u32[]{:S(2)}) collective-permute-start(f32[128,256]{1,0:T(8,128)S(1)} %get-tuple-element.29), channel_id=1, source_target_pairs={{2,4},{4,2},{6,8},{8,6},{10,12},{12,10},{14,16},{16,14},{18,20},{2... | collective-permute-start | bytes 393224 | tf_op jit(solution)/shard_map/ppermute | solution.py:52
  141.6 13.1 %collective-permute-start.7 = (f32[128,256]{1,0:T(8,128)S(1)}, f32[128,256]{1,0:T(8,128)S(1)}, u32[]{:S(2)}, u32[]{:S(2)}) collective-permute-start(f32[128,256]{1,0:T(8,128)S(1)} %get-tuple-element.29), channel_id=1, source_target_pairs={{0,2},{2,0},{1,3},{3,1},{4,6},{6,4},{5,7},{7,5},{8,10},{10,8},{9,1... | collective-permute-start | bytes 393224 | tf_op jit(solution)/shard_map/ppermute | solution.py:45
  147.8 16.0 %all-to-all-start.5 = ((f32[32,16,128]{2,1,0:T(8,128)}), f32[32,16,128]{2,1,0:T(8,128)S(1)}, u32[]{:S(2)}, u32[]{:S(2)}) async-start(f32[32,16,128]{2,1,0:T(8,128)} %shard_map.136), calls=%async_computation.5 | async-start | bytes 524288 | tf_op jit(solution)/shard_map/all_to_all | solution.py:425

commit v7 on v6

--- a/solution.py
+++ b/solution.py
@@ -37,8 +37,8 @@
         room=56,
     )
     rows = lax.all_gather(rows, "core", axis=0, tiled=True)
-    width = columns // 2
-    return lax.dynamic_slice_in_dim(rows, lax.axis_index("core") * width, width, 1)
+    width = columns // lax.axis_size(("core", "x_hi"))
+    return lax.dynamic_slice_in_dim(rows, lax.axis_index(("core", "x_hi")) * width, width, 1)
 
 
 def swapped(array, axis):
@@ -335,18 +335,19 @@
             pltpu.VMEM(array.shape, array.dtype)
             for array in operands[scalars : scalars + fetched]
         )
-        scratch = copies + (pltpu.SemaphoreType.DMA((count,)),) + tuple(scratch)
+        scratch = copies + (pltpu.SemaphoreType.DMA((2 * count,)),) + tuple(scratch)
 
         def body(*refs):
             numbers, sources, refs = refs[:scalars], refs[scalars : scalars + count], refs[scalars + count :]
             results, refs = refs[: len(outs)], refs[len(outs) :]
             held, done, rest = refs[:fetched], refs[fetched], refs[fetched + 1 :]
-            targets = list(held)
+            pairs = list(zip(sources, held))
             if place is not None:
-                targets += place(numbers, rest)
+                for source, targets in zip(sources[fetched:], place(numbers, rest)):
+                    pairs += [(source.at[i], target) for i, target in enumerate(targets)]
             moves = [
                 pltpu.make_async_copy(source, target, done.at[i])
-                for i, (source, target) in enumerate(zip(sources, targets))
+                for i, (source, target) in enumerate(pairs)
             ]
             for move in moves:
                 move.start()
@@ -382,20 +383,26 @@
     depth = copies.shape[1] // 2
     own = total[pl.ds(pl.multiple_of(place[0] * depth, depth), depth), :]
     squares = jnp.sum(total[...] * total[...], axis=0, keepdims=True)
-    both = jnp.concatenate([own, jnp.broadcast_to(squares, own.shape)])
+    terms = []
+    for _ in range(3):
+        terms.append(squares.astype(jnp.bfloat16).astype(jnp.float32))
+        squares = squares - terms[-1]
+    rest = jnp.zeros((depth - len(terms), squares.shape[1]), jnp.float32)
+    both = jnp.concatenate([own] + terms + [rest]).astype(jnp.bfloat16)
     copies[...] = jnp.broadcast_to(both[None], copies.shape)
 
 
-def update_kernel(blocks, count, place, parts, w_in, w_out, new_in, new_out):
-    depth = parts.shape[1] // 2
+def update_kernel(blocks, count, place, parts_ref, w_in, w_out, new_in, new_out):
+    depth = parts_ref.shape[1] // 2
     shard = w_in.shape[0]
-    squares = jnp.sum(parts[:, depth, :], axis=0, keepdims=True)
-    square_sum = jnp.sum(squares, axis=1, keepdims=True)
+    parts = parts_ref[...].astype(jnp.float32)
+    squares = jnp.sum(parts, axis=0)[depth:]
+    square_sum = jnp.sum(jnp.sum(squares, axis=0, keepdims=True), axis=1, keepdims=True)
     scale = LEARN_RATE / jnp.sqrt(square_sum / count + EPSILON)
     for which, (old, new) in enumerate(((w_in, new_in), (w_out, new_out))):
         sides = []
         for half in range(2):
-            rows = parts[(which * blocks + place[0]) * 2 + half, :depth, :]
+            rows = parts_ref[(which * blocks + place[0]) * 2 + half].astype(jnp.float32)[:depth]
             sides.append(jnp.where(place[1] == 0, rows[:shard], rows[shard:]))
         new[...] = old[...] - scale * jnp.concatenate(sides, axis=1)
 
@@ -416,7 +423,7 @@
     depth = rows // lax.axis_size(Z)
     (copies,) = on_chip(
         sum_and_square_kernel,
-        (jax.ShapeDtypeStruct((peers, 2 * depth, columns), jnp.float32),),
+        (jax.ShapeDtypeStruct((peers, 2 * depth, columns), jnp.bfloat16),),
         (lax.axis_index(Z)[None], grads),
         grads.size,
         scratch=(pltpu.VMEM((rows, columns), jnp.float32),),
@@ -468,12 +475,15 @@
         room=56,
     )
     near = swapped(own, "core")
-    half, near, outer = lax.optimization_barrier((half, near, outer))
-    half = spread(half, ("x_lo", "y")).reshape(-1, width)
+    half, near = lax.optimization_barrier((half, near))
+    half = spread(half, ("x_hi", "x_lo", "y"))
     far = swapped_between_chips(jnp.concatenate([own, near]))
+    far, outer = lax.optimization_barrier((far, outer))
     beyond = swapped(far, "core")
     half, far, beyond = lax.optimization_barrier((half, far, beyond))
-    hidden_units, width = half.shape
+    pieces = lax.axis_size("x_hi")
+    half = half.reshape(pieces, -1, width)
+    hidden_units = half.shape[1]
     blocks = lax.axis_size(("x_lo", "y"))
     halves = lax.axis_size("core")
     narrow = ((cells, features), jnp.float32)
@@ -487,12 +497,12 @@
         (lax.axis_index("core")[None], *fields[:3], mine, other, near, far, beyond, outer)
         + (half, swapped(half, "core")),
         40 * cells * hidden_units * (2 * features + hidden_units),
-        scratch=(pltpu.VMEM((2, hidden_units, width), jnp.bfloat16),),
+        scratch=(pltpu.VMEM((2, hidden_units, pieces * width), jnp.bfloat16),),
         scalars=1,
         fetched=9,
         place=lambda numbers, rest: [
-            rest[0].at[numbers[0][0]],
-            rest[0].at[1 - numbers[0][0]],
+            [rest[0].at[side, :, pl.ds(piece * width, width)] for piece in range(pieces)]
+            for side in (numbers[0][0], 1 - numbers[0][0])
         ],
     )
     w_in_new, w_out_new = updated(grads, w_in, w_out)

time: 166 us -> 163 us (0.982)
  blocking collectives: 33.5 us -> 8.58 us
  waiting for transfers between devices: 33.6 us -> 57.3 us
  starting transfers between devices: 71.3 us -> 68.6 us
    all_to_all x1 -> x0, blocking collectives: 24.9 us -> none  [updated(): grads = lax.all_to_all(grads.reshape(peers, rows, columns), AROUND, 0, 0)]
    all_to_all x0 -> x1, waiting for transfers between devices: none -> 16.9 us  [updated(): grads = lax.all_to_all(grads.reshape(peers, rows, columns), AROUND, 0, 0)]
    all_to_all x2, waiting for transfers between devices: 1.8 us -> 11.4 us  [spread(): lax.all_to_all(jnp.broadcast_to(block[None], (count,) + block.shape), axi...]
    ppermute x2, waiting for transfers between devices: 6.45 us -> 0.01 us  [swapped_between_chips(): return lax.ppermute(array, TILE, pairs)]
    all_to_all x0 -> x1, starting transfers between devices: none -> 5.77 us  [updated(): grads = lax.all_to_all(grads.reshape(peers, rows, columns), AROUND, 0, 0)]
    ppermute x6, starting transfers between devices: 24.5 us -> 19.9 us  [swapped(): return lax.ppermute(array, axis, [(0, 1), (1, 0)])]
    ppermute x1, waiting for transfers between devices: 2.34 us -> 5.21 us  [swapped_three_apart(): lax.ppermute(array, TILE, pairs + [(after, row) for row, after in pairs])]
    all_to_all x2, starting transfers between devices: 10.6 us -> 8.1 us  [updated(): grads = lax.all_to_all(copies, axis, 0, 0)]
  transfers between devices with their start and end apart: 14 -> 15, of which waited for: 9 -> 10; matrix products, arithmetic and copies ran while one was open for 1% -> 1% of each run, Pallas kernels for 3% -> 3%
where the time goes in v7:
time: 163 us; the launch traced here: 162 us
  starting transfers between devices  68.6 us (42%)
  waiting for transfers between devices  57.3 us (35%)
  Pallas kernels  23.5 us (14%)
  blocking collectives  8.58 us (5%)
  local copies, waits for them, and re-layouts  2.71 us (2%)
    pallas_call x8, Pallas kernels, on_chip(): pl.pallas_call(body, out_shape=outs, in_specs=[pl.BlockSpec(memory_space=...  23.5 us
    ppermute x6, starting transfers between devices, swapped(): return lax.ppermute(array, axis, [(0, 1), (1, 0)])  19.9 us
    all_to_all x1, waiting for transfers between devices, updated(): grads = lax.all_to_all(grads.reshape(peers, rows, columns), AROUND, 0, 0)  16.9 us
    all_to_all x2, starting transfers between devices, spread(): lax.all_to_all(jnp.broadcast_to(block[None], (count,) + block.shape), axi...  16.4 us
    all_to_all x2, waiting for transfers between devices, spread(): lax.all_to_all(jnp.broadcast_to(block[None], (count,) + block.shape), axi...  11.4 us
    ppermute x2, starting transfers between devices, swapped_between_chips(): return lax.ppermute(array, TILE, pairs)  8.78 us
    all_to_all x2, waiting for transfers between devices, updated(): grads = lax.all_to_all(copies, axis, 0, 0)  8.6 us
    all_gather x1, blocking collectives, chip_rows(): rows = lax.all_gather(rows, 'core', axis=0, tiled=True)  8.58 us
  transfers between devices with their start and end apart: 15, of which 10 were waited for; matrix products, arithmetic and copies ran while one was open for 1% of the time, Pallas kernels for 3%

profile of v7, /device:TPU:1, one launch (start us, length us, event | category | flops | bytes accessed | tf_op | source)
XLA Modules:
  0.0 162.4 jit_solution(10641285215384012469)
XLA Ops:
  0.6 1.4 shard_map.130
  2.0 8.6 %all-gather = bf16[2,4,1536]{2,1,0:T(4,128)(2,1)S(1)} all-gather(bf16[1,4,1536]{2,1,0:T(4,128)(2,1)} %bitcast.16), channel_id=1, replica_groups=mesh['x_lo'=2,'y'=4,'z_hi'=4,'z_lo'=4,'core'=2,'x_hi'=2] {'core'}, dimensions={0}, use_global_device_ids=true | all-gather | bytes 36864 | tf_op jit(solution)/shard_map/all_gather | solution.py:39
  10.6 0.7 broadcast_in_dim.38
  11.3 9.5 %all-to-all-start = ((bf16[16,8,384]{2,1,0:T(8,128)(2,1)}), bf16[16,8,384]{2,1,0:T(8,128)(2,1)S(1)}, u32[]{:S(2)}, u32[]{:S(2)}) async-start(bf16[16,8,384]{2,1,0:T(8,128)(2,1)} %broadcast_in_dim.38), calls=%async_computation | async-start | bytes 196608 | tf_op jit(solution)/shard_map/all_to_all | solution.py:26
  20.8 1.8 %shard_map.131 = (f32[24,256]{1,0:T(8,128)}, bf16[128,256]{1,0:T(8,128)(2,1)}) custom-call(f32[1,128,256]{2,1,0:T(8,128)} %refs_1_.7, f32[1,128,256]{2,1,0:T(8,128)} %refs_2_.7, f32[1,128,256]{2,1,0:T(8,128)} %refs_3_.2, s32[1,128]{1,0:T(1,128)} %refs_3_.1, s32[1,64]{1,0:T(1,128)} %bitcast.17, s32[1,64]{1,0:T(1,128)} %bitcast.18, f32[1,64]{1,0:T(1,128)} %bitcast.19, ...), custom_call_target="tpu_custom_call" | custom-call | bytes 484864 | tf_op jit(solution)/shard_map/pallas_call | solution.py:358
  22.7 4.7 %collective-permute-start = (f32[24,256]{1,0:T(8,128)}, f32[24,256]{1,0:T(8,128)S(1)}, u32[]{:S(2)}, u32[]{:S(2)}) collective-permute-start(f32[24,256]{1,0:T(8,128)} %get-tuple-element.20.refs_3_.refs_4_), channel_id=1, source_target_pairs={{0,1},{1,0},{2,3},{3,2},{4,5},{5,4},{6,7},{7,6},{8,9},{9,8},{10,11... | collective-permute-start | bytes 73736 | tf_op jit(solution)/shard_map/ppermute | solution.py:45
  27.3 1.9 %collective-permute-done.refs_4_.refs_5_ = f32[24,256]{1,0:T(8,128)S(1)} collective-permute-done((f32[24,256]{1,0:T(8,128)}, f32[24,256]{1,0:T(8,128)S(1)}, u32[]{:S(2)}, u32[]{:S(2)}) %collective-permute-start) | collective-permute-done | bytes 24608 | tf_op jit(solution)/shard_map/ppermute | solution.py:45
  29.3 0.0 copy-start.4
  29.3 0.6 copy-done.4
  29.9 1.9 %shard_map.132 = bf16[448,256]{1,0:T(8,128)(2,1)} custom-call(f32[1,128,256]{2,1,0:T(8,128)} %refs_1_.7, f32[1,128,256]{2,1,0:T(8,128)} %refs_2_.7, f32[1,128,256]{2,1,0:T(8,128)} %refs_3_.2, f32[24,256]{1,0:T(8,128)} %get-tuple-element.20.refs_3_.refs_4_, f32[24,256]{1,0:T(8,128)} %copy-done.4), custom_call_target="tpu_custom_call" | custom-call | bytes 671744 | tf_op jit(solution)/shard_map/pallas_call | solution.py:358
  31.8 3.4 %collective-permute-start.1 = (bf16[448,256]{1,0:T(8,128)(2,1)}, bf16[448,256]{1,0:T(8,128)(2,1)S(1)}, u32[]{:S(2)}, u32[]{:S(2)}) collective-permute-start(bf16[448,256]{1,0:T(8,128)(2,1)} %shard_map.132), channel_id=1, source_target_pairs={{0,2},{2,0},{1,3},{3,1},{4,6},{6,4},{5,7},{7,5},{8,10},{10,8},{9,1... | collective-permute-start | bytes 688136 | tf_op jit(solution)/shard_map/ppermute | solution.py:45
  35.1 1.3 collective-permute-done.1.refs_6_
  36.5 0.0 all-to-all-done
  36.5 1.4 broadcast_in_dim.39
  37.8 0.0 copy-start.8
  37.8 0.0 copy-start.9
  37.8 0.0 copy-start
  37.8 0.0 copy-start.1
  37.8 0.0 copy-start.2
  37.9 0.0 copy-start.3
  37.9 0.0 copy-start.5
  37.9 6.9 %all-to-all-start.1 = ((bf16[16,128,384]{2,1,0:T(8,128)(2,1)}), bf16[16,128,384]{2,1,0:T(8,128)(2,1)S(1)}, u32[]{:S(2)}, u32[]{:S(2)}) async-start(bf16[16,128,384]{2,1,0:T(8,128)(2,1)} %broadcast_in_dim.39), calls=%async_computation.1 | async-start | bytes 3145728 | tf_op jit(solution)/shard_map/all_to_all | solution.py:26
  44.8 0.0 copy-done.8
  44.8 4.1 %collective-permute-start.2 = (bf16[896,256]{1,0:T(8,128)(2,1)S(1)}, bf16[896,256]{1,0:T(8,128)(2,1)S(1)}, u32[]{:S(2)}, u32[]{:S(2)}) collective-permute-start(bf16[896,256]{1,0:T(8,128)(2,1)S(1)} %pad_maximum_fusion), channel_id=1, source_target_pairs={{2,4},{4,2},{6,8},{8,6},{10,12},{12,10},{14,16},{16,14},{18,20},{2... | collective-permute-start | bytes 1376264 | tf_op jit(solution)/shard_map/ppermute | solution.py:52
  48.9 0.0 copy-done.9
  48.9 2.8 %collective-permute-start.3 = (bf16[128,256]{1,0:T(8,128)(2,1)S(1)}, bf16[128,256]{1,0:T(8,128)(2,1)S(1)}, u32[]{:S(2)}, u32[]{:S(2)}) collective-permute-start(bf16[128,256]{1,0:T(8,128)(2,1)S(1)} %copy-done.9), channel_id=1, source_target_pairs={{2,8},{6,12},{10,16},{14,20},{18,24},{22,28},{26,32},{30,36},{34,4... | collective-permute-start | bytes 196616 | tf_op jit(solution)/shard_map/ppermute | solution.py:58
  51.8 5.2 %collective-permute-done.3.refs_9_ = bf16[128,256]{1,0:T(8,128)(2,1)S(1)} collective-permute-done((bf16[128,256]{1,0:T(8,128)(2,1)S(1)}, bf16[128,256]{1,0:T(8,128)(2,1)S(1)}, u32[]{:S(2)}, u32[]{:S(2)}) %collective-permute-start.3) | collective-permute-done | bytes 65568 | tf_op jit(solution)/shard_map/ppermute | solution.py:58
  57.0 0.0 collective-permute-done.2.refs_7_
  57.0 1.9 %collective-permute-start.4 = (bf16[896,256]{1,0:T(8,128)(2,1)S(1)}, bf16[896,256]{1,0:T(8,128)(2,1)S(1)}, u32[]{:S(2)}, u32[]{:S(2)}) collective-permute-start(bf16[896,256]{1,0:T(8,128)(2,1)S(1)} %collective-permute-done.2.refs_7_), channel_id=1, source_target_pairs={{0,2},{2,0},{1,3},{3,1},{4,6},{6,4},{5,7},{7,5},{8,10},{10,8},{9,1... | collective-permute-start | bytes 1376264 | tf_op jit(solution)/shard_map/ppermute | solution.py:45
  58.9 1.8 %collective-permute-done.4.refs_8_ = bf16[896,256]{1,0:T(8,128)(2,1)S(1)} collective-permute-done((bf16[896,256]{1,0:T(8,128)(2,1)S(1)}, bf16[896,256]{1,0:T(8,128)(2,1)S(1)}, u32[]{:S(2)}, u32[]{:S(2)}) %collective-permute-start.4) | collective-permute-done | bytes 458784 | tf_op jit(solution)/shard_map/ppermute | solution.py:45
  60.7 11.4 %all-to-all-done.1 = bf16[16,128,384]{2,1,0:T(8,128)(2,1)S(1)} async-done(((bf16[16,128,384]{2,1,0:T(8,128)(2,1)}), bf16[16,128,384]{2,1,0:T(8,128)(2,1)S(1)}, u32[]{:S(2)}, u32[]{:S(2)}) %all-to-all-start.1) | async-done | bytes 1572896 | tf_op jit(solution)/shard_map/all_to_all | solution.py:26
  72.1 4.8 %collective-permute-start.5 = (bf16[2,1024,384]{2,1,0:T(8,128)(2,1)S(1)}, bf16[2,1024,384]{2,1,0:T(8,128)(2,1)S(1)}, u32[]{:S(2)}, u32[]{:S(2)}) collective-permute-start(bf16[2,1024,384]{2,1,0:T(8,128)(2,1)S(1)} %bitcast.13), channel_id=1, source_target_pairs={{0,2},{2,0},{1,3},{3,1},{4,6},{6,4},{5,7},{7,5},{8,10},{10,8},{9,1... | collective-permute-start | bytes 4718600 | tf_op jit(solution)/shard_map/ppermute | solution.py:45
  77.0 3.0 %collective-permute-done.5.refs_11_ = bf16[2,1024,384]{2,1,0:T(8,128)(2,1)S(1)} collective-permute-done((bf16[2,1024,384]{2,1,0:T(8,128)(2,1)S(1)}, bf16[2,1024,384]{2,1,0:T(8,128)(2,1)S(1)}, u32[]{:S(2)}, u32[]{:S(2)}) %collective-permute-start.5) | collective-permute-done | bytes 1572896 | tf_op jit(solution)/shard_map/ppermute | solution.py:45
  80.0 0.0 copy-done
  80.0 0.0 copy-done.1
  80.0 0.0 copy-done.2
  80.0 0.0 copy-done.3
  80.0 0.0 copy-done.5
  80.0 14.9 %shard_map.133 = (f32[128,256]{1,0:T(8,128)S(1)}, f32[128,256]{1,0:T(8,128)S(1)}, bf16[2,8,2,128,128]{4,3,2,1,0:T(8,128)(2,1)}) custom-call(s32[1]{0:T(128)} %bitcast.refs_0_, f32[1,128,256]{2,1,0:T(8,128)S(1)} %copy-done, f32[1,128,256]{2,1,0:T(8,128)S(1)} %copy-done.1, f32[1,128,256]{2,1,0:T(8,128)S(1)} %copy-done.2, f32[24,256]{1,0:T(8,128)S(1)} %copy-done.3, ...), custom_call_target="tpu_custom_call" | custom-call | flops 8053063680 | bytes 6111236 | tf_op jit(solution)/shard_map/pallas_call | solution.py:358
  94.9 5.8 %all-to-all-start.2 = ((bf16[32,128,128]{2,1,0:T(8,128)(2,1)}), bf16[32,128,128]{2,1,0:T(8,128)(2,1)S(1)}, u32[]{:S(2)}, u32[]{:S(2)}) async-start(bf16[32,128,128]{2,1,0:T(8,128)(2,1)} %bitcast.11), calls=%async_computation.2 | async-start | bytes 2097152 | tf_op jit(solution)/shard_map/all_to_all | solution.py:413
  100.7 16.9 %all-to-all-done.2.parts = bf16[32,128,128]{2,1,0:T(8,128)(2,1)S(1)} async-done(((bf16[32,128,128]{2,1,0:T(8,128)(2,1)}), bf16[32,128,128]{2,1,0:T(8,128)(2,1)S(1)}, u32[]{:S(2)}, u32[]{:S(2)}) %all-to-all-start.2) | async-done | bytes 1048608 | tf_op jit(solution)/shard_map/all_to_all | solution.py:413
  117.6 0.8 shard_map.134
  118.4 0.0 copy-start.6
  118.4 0.0 copy-start.7
  118.4 3.5 %all-to-all-start.3 = ((bf16[4,128,128]{2,1,0:T(8,128)(2,1)}), bf16[4,128,128]{2,1,0:T(8,128)(2,1)S(1)}, u32[]{:S(2)}, u32[]{:S(2)}) async-start(bf16[4,128,128]{2,1,0:T(8,128)(2,1)} %shard_map.134), calls=%async_computation.3 | async-start | bytes 262144 | tf_op jit(solution)/shard_map/all_to_all | solution.py:422
  121.9 0.1 pad_add_fusion.place
  122.0 3.2 %collective-permute-start.8 = (f32[2,256]{1,0:T(2,128)S(1)}, f32[2,256]{1,0:T(2,128)S(1)}, u32[]{:S(2)}, u32[]{:S(2)}) collective-permute-start(f32[2,256]{1,0:T(2,128)S(1)} %pad_maximum_fusion.1), channel_id=1, source_target_pairs={{0,1},{1,0},{2,3},{3,2},{4,5},{5,4},{6,7},{7,6},{8,9},{9,8},{10,11... | collective-permute-start | bytes 6152 | tf_op jit(solution)/shard_map/ppermute | solution.py:45
  125.2 1.6 all-to-all-done.3.parts
  126.7 0.7 shard_map.135
  127.4 4.6 %all-to-all-start.4 = ((bf16[4,128,128]{2,1,0:T(8,128)(2,1)}), bf16[4,128,128]{2,1,0:T(8,128)(2,1)S(1)}, u32[]{:S(2)}, u32[]{:S(2)}) async-start(bf16[4,128,128]{2,1,0:T(8,128)(2,1)} %shard_map.135), calls=%async_computation.4 | async-start | bytes 262144 | tf_op jit(solution)/shard_map/all_to_all | solution.py:422
  132.1 4.7 %collective-permute-start.6 = (f32[128,256]{1,0:T(8,128)S(1)}, f32[128,256]{1,0:T(8,128)S(1)}, u32[]{:S(2)}, u32[]{:S(2)}) collective-permute-start(f32[128,256]{1,0:T(8,128)S(1)} %get-tuple-element.31), channel_id=1, source_target_pairs={{2,4},{4,2},{6,8},{8,6},{10,12},{12,10},{14,16},{16,14},{18,20},{2... | collective-permute-start | bytes 393224 | tf_op jit(solution)/shard_map/ppermute | solution.py:52
  136.8 1.9 %collective-permute-start.7 = (f32[128,256]{1,0:T(8,128)S(1)}, f32[128,256]{1,0:T(8,128)S(1)}, u32[]{:S(2)}, u32[]{:S(2)}) collective-permute-start(f32[128,256]{1,0:T(8,128)S(1)} %get-tuple-element.31), channel_id=1, source_target_pairs={{0,2},{2,0},{1,3},{3,1},{4,6},{6,4},{5,7},{7,5},{8,10},{10,8},{9,1... | collective-permute-start | bytes 393224 | tf_op jit(solution)/shard_map/ppermute | solution.py:45
  138.7 0.0 collective-permute-done.8
  138.7 7.0 %all-to-all-done.4.parts = bf16[4,128,128]{2,1,0:T(8,128)(2,1)S(1)} async-done(((bf16[4,128,128]{2,1,0:T(8,128)(2,1)}), bf16[4,128,128]{2,1,0:T(8,128)(2,1)S(1)}, u32[]{:S(2)}, u32[]{:S(2)}) %all-to-all-start.4) | async-done | bytes 131104 | tf_op jit(solution)/shard_map/all_to_all | solution.py:422
  145.8 0.7 shard_map.136
  146.5 6.8 %all-to-all-start.5 = ((bf16[32,16,128]{2,1,0:T(8,128)(2,1)}), bf16[32,16,128]{2,1,0:T(8,128)(2,1)S(1)}, u32[]{:S(2)}, u32[]{:S(2)}) async-start(bf16[32,16,128]{2,1,0:T(8,128)(2,1)} %shard_map.136), calls=%async_computation.5 | async-start | bytes 262144 | tf_op jit(solution)/shard_map/all_to_all | solution.py:432
  153.3 0.0 collective-permute-done.6
  153.3 0.0 collective-permute-done.7
  153.3 0.7 fusion.2
  154.0 7.1 %all-to-all-done.5.parts_ref = bf16[32,16,128]{2,1,0:T(8,128)(2,1)S(1)} async-done(((bf16[32,16,128]{2,1,0:T(8,128)(2,1)}), bf16[32,16,128]{2,1,0:T(8,128)(2,1)S(1)}, u32[]{:S(2)}, u32[]{:S(2)}) %all-to-all-start.5) | async-done | bytes 131104 | tf_op jit(solution)/shard_map/all_to_all | solution.py:432
  161.1 0.0 copy-done.6
  161.1 0.0 copy-done.7
  161.1 1.3 shard_map.137
  (7 shorter events, 0.1 us)
Async XLA Ops:
  11.3 25.2 %all-to-all-start = ((bf16[16,8,384]{2,1,0:T(8,128)(2,1)}), bf16[16,8,384]{2,1,0:T(8,128)(2,1)S(1)}, u32[]{:S(2)}, u32[]{:S(2)}) async-start(bf16[16,8,384]{2,1,0:T(8,128)(2,1)} %broadcast_in_dim.38), calls=%async_computation | async-start | bytes 196608 | tf_op jit(solution)/shard_map/all_to_all | solution.py:26
  22.7 6.6 %collective-permute-start = (f32[24,256]{1,0:T(8,128)}, f32[24,256]{1,0:T(8,128)S(1)}, u32[]{:S(2)}, u32[]{:S(2)}) collective-permute-start(f32[24,256]{1,0:T(8,128)} %get-tuple-element.20.refs_3_.refs_4_), channel_id=1, source_target_pairs={{0,1},{1,0},{2,3},{3,2},{4,5},{5,4},{6,7},{7,6},{8,9},{9,8},{10,11... | collective-permute-start | bytes 73736 | tf_op jit(solution)/shard_map/ppermute | solution.py:45
  29.3 0.6 copy-start.4
  31.8 4.7 %collective-permute-start.1 = (bf16[448,256]{1,0:T(8,128)(2,1)}, bf16[448,256]{1,0:T(8,128)(2,1)S(1)}, u32[]{:S(2)}, u32[]{:S(2)}) collective-permute-start(bf16[448,256]{1,0:T(8,128)(2,1)} %shard_map.132), channel_id=1, source_target_pairs={{0,2},{2,0},{1,3},{3,1},{4,6},{6,4},{5,7},{7,5},{8,10},{10,8},{9,1... | collective-permute-start | bytes 688136 | tf_op jit(solution)/shard_map/ppermute | solution.py:45
  37.8 7.0 %copy-start.8 = (bf16[448,256]{1,0:T(8,128)(2,1)S(1)}, bf16[448,256]{1,0:T(8,128)(2,1)}, u32[]{:S(2)}) copy-start(bf16[448,256]{1,0:T(8,128)(2,1)} %shard_map.132) | copy-start | bytes 688132
  37.8 11.1 %copy-start.9 = (bf16[128,256]{1,0:T(8,128)(2,1)S(1)}, bf16[128,256]{1,0:T(8,128)(2,1)}, u32[]{:S(2)}) copy-start(bf16[128,256]{1,0:T(8,128)(2,1)} %get-tuple-element.24) | copy-start | bytes 196612
  37.8 42.2 %copy-start = (f32[1,128,256]{2,1,0:T(8,128)S(1)}, f32[1,128,256]{2,1,0:T(8,128)}, u32[]{:S(2)}) copy-start(f32[1,128,256]{2,1,0:T(8,128)} %refs_1_.7) | copy-start | bytes 393220
  37.8 42.2 %copy-start.1 = (f32[1,128,256]{2,1,0:T(8,128)S(1)}, f32[1,128,256]{2,1,0:T(8,128)}, u32[]{:S(2)}) copy-start(f32[1,128,256]{2,1,0:T(8,128)} %refs_2_.7) | copy-start | bytes 393220
  37.8 42.2 %copy-start.2 = (f32[1,128,256]{2,1,0:T(8,128)S(1)}, f32[1,128,256]{2,1,0:T(8,128)}, u32[]{:S(2)}) copy-start(f32[1,128,256]{2,1,0:T(8,128)} %refs_3_.2) | copy-start | bytes 393220
  37.9 42.2 %copy-start.3 = (f32[24,256]{1,0:T(8,128)S(1)}, f32[24,256]{1,0:T(8,128)}, u32[]{:S(2)}) copy-start(f32[24,256]{1,0:T(8,128)} %get-tuple-element.20.refs_3_.refs_4_) | copy-start | bytes 73732
  37.9 42.1 %copy-start.5 = (f32[24,256]{1,0:T(8,128)S(1)}, f32[24,256]{1,0:T(8,128)}, u32[]{:S(2)}) copy-start(f32[24,256]{1,0:T(8,128)} %copy-done.4) | copy-start | bytes 73732
  37.9 34.3 %all-to-all-start.1 = ((bf16[16,128,384]{2,1,0:T(8,128)(2,1)}), bf16[16,128,384]{2,1,0:T(8,128)(2,1)S(1)}, u32[]{:S(2)}, u32[]{:S(2)}) async-start(bf16[16,128,384]{2,1,0:T(8,128)(2,1)} %broadcast_in_dim.39), calls=%async_computation.1 | async-start | bytes 3145728 | tf_op jit(solution)/shard_map/all_to_all | solution.py:26
  44.8 12.2 %collective-permute-start.2 = (bf16[896,256]{1,0:T(8,128)(2,1)S(1)}, bf16[896,256]{1,0:T(8,128)(2,1)S(1)}, u32[]{:S(2)}, u32[]{:S(2)}) collective-permute-start(bf16[896,256]{1,0:T(8,128)(2,1)S(1)} %pad_maximum_fusion), channel_id=1, source_target_pairs={{2,4},{4,2},{6,8},{8,6},{10,12},{12,10},{14,16},{16,14},{18,20},{2... | collective-permute-start | bytes 1376264 | tf_op jit(solution)/shard_map/ppermute | solution.py:52
  48.9 8.0 %collective-permute-start.3 = (bf16[128,256]{1,0:T(8,128)(2,1)S(1)}, bf16[128,256]{1,0:T(8,128)(2,1)S(1)}, u32[]{:S(2)}, u32[]{:S(2)}) collective-permute-start(bf16[128,256]{1,0:T(8,128)(2,1)S(1)} %copy-done.9), channel_id=1, source_target_pairs={{2,8},{6,12},{10,16},{14,20},{18,24},{22,28},{26,32},{30,36},{34,4... | collective-permute-start | bytes 196616 | tf_op jit(solution)/shard_map/ppermute | solution.py:58
  57.0 3.7 %collective-permute-start.4 = (bf16[896,256]{1,0:T(8,128)(2,1)S(1)}, bf16[896,256]{1,0:T(8,128)(2,1)S(1)}, u32[]{:S(2)}, u32[]{:S(2)}) collective-permute-start(bf16[896,256]{1,0:T(8,128)(2,1)S(1)} %collective-permute-done.2.refs_7_), channel_id=1, source_target_pairs={{0,2},{2,0},{1,3},{3,1},{4,6},{6,4},{5,7},{7,5},{8,10},{10,8},{9,1... | collective-permute-start | bytes 1376264 | tf_op jit(solution)/shard_map/ppermute | solution.py:45
  72.1 7.9 %collective-permute-start.5 = (bf16[2,1024,384]{2,1,0:T(8,128)(2,1)S(1)}, bf16[2,1024,384]{2,1,0:T(8,128)(2,1)S(1)}, u32[]{:S(2)}, u32[]{:S(2)}) collective-permute-start(bf16[2,1024,384]{2,1,0:T(8,128)(2,1)S(1)} %bitcast.13), channel_id=1, source_target_pairs={{0,2},{2,0},{1,3},{3,1},{4,6},{6,4},{5,7},{7,5},{8,10},{10,8},{9,1... | collective-permute-start | bytes 4718600 | tf_op jit(solution)/shard_map/ppermute | solution.py:45
  94.9 22.7 %all-to-all-start.2 = ((bf16[32,128,128]{2,1,0:T(8,128)(2,1)}), bf16[32,128,128]{2,1,0:T(8,128)(2,1)S(1)}, u32[]{:S(2)}, u32[]{:S(2)}) async-start(bf16[32,128,128]{2,1,0:T(8,128)(2,1)} %bitcast.11), calls=%async_computation.2 | async-start | bytes 2097152 | tf_op jit(solution)/shard_map/all_to_all | solution.py:413
  118.4 42.6 %copy-start.6 = (f32[4,256]{1,0:T(4,128)S(1)}, f32[4,256]{1,0:T(4,128)}, u32[]{:S(2)}) copy-start(f32[4,256]{1,0:T(4,128)} %w_in.1) | copy-start | bytes 12292
  118.4 42.6 %copy-start.7 = (f32[4,256]{1,0:T(4,128)S(1)}, f32[4,256]{1,0:T(4,128)}, u32[]{:S(2)}) copy-start(f32[4,256]{1,0:T(4,128)} %w_out.1) | copy-start | bytes 12292
  118.4 8.3 %all-to-all-start.3 = ((bf16[4,128,128]{2,1,0:T(8,128)(2,1)}), bf16[4,128,128]{2,1,0:T(8,128)(2,1)S(1)}, u32[]{:S(2)}, u32[]{:S(2)}) async-start(bf16[4,128,128]{2,1,0:T(8,128)(2,1)} %shard_map.134), calls=%async_computation.3 | async-start | bytes 262144 | tf_op jit(solution)/shard_map/all_to_all | solution.py:422
  122.0 16.7 %collective-permute-start.8 = (f32[2,256]{1,0:T(2,128)S(1)}, f32[2,256]{1,0:T(2,128)S(1)}, u32[]{:S(2)}, u32[]{:S(2)}) collective-permute-start(f32[2,256]{1,0:T(2,128)S(1)} %pad_maximum_fusion.1), channel_id=1, source_target_pairs={{0,1},{1,0},{2,3},{3,2},{4,5},{5,4},{6,7},{7,6},{8,9},{9,8},{10,11... | collective-permute-start | bytes 6152 | tf_op jit(solution)/shard_map/ppermute | solution.py:45
  127.4 18.3 %all-to-all-start.4 = ((bf16[4,128,128]{2,1,0:T(8,128)(2,1)}), bf16[4,128,128]{2,1,0:T(8,128)(2,1)S(1)}, u32[]{:S(2)}, u32[]{:S(2)}) async-start(bf16[4,128,128]{2,1,0:T(8,128)(2,1)} %shard_map.135), calls=%async_computation.4 | async-start | bytes 262144 | tf_op jit(solution)/shard_map/all_to_all | solution.py:422
  132.1 21.2 %collective-permute-start.6 = (f32[128,256]{1,0:T(8,128)S(1)}, f32[128,256]{1,0:T(8,128)S(1)}, u32[]{:S(2)}, u32[]{:S(2)}) collective-permute-start(f32[128,256]{1,0:T(8,128)S(1)} %get-tuple-element.31), channel_id=1, source_target_pairs={{2,4},{4,2},{6,8},{8,6},{10,12},{12,10},{14,16},{16,14},{18,20},{2... | collective-permute-start | bytes 393224 | tf_op jit(solution)/shard_map/ppermute | solution.py:52
  136.8 16.5 %collective-permute-start.7 = (f32[128,256]{1,0:T(8,128)S(1)}, f32[128,256]{1,0:T(8,128)S(1)}, u32[]{:S(2)}, u32[]{:S(2)}) collective-permute-start(f32[128,256]{1,0:T(8,128)S(1)} %get-tuple-element.31), channel_id=1, source_target_pairs={{0,2},{2,0},{1,3},{3,1},{4,6},{6,4},{5,7},{7,5},{8,10},{10,8},{9,1... | collective-permute-start | bytes 393224 | tf_op jit(solution)/shard_map/ppermute | solution.py:45
  146.5 14.6 %all-to-all-start.5 = ((bf16[32,16,128]{2,1,0:T(8,128)(2,1)}), bf16[32,16,128]{2,1,0:T(8,128)(2,1)S(1)}, u32[]{:S(2)}, u32[]{:S(2)}) async-start(bf16[32,16,128]{2,1,0:T(8,128)(2,1)} %shard_map.136), calls=%async_computation.5 | async-start | bytes 262144 | tf_op jit(solution)/shard_map/all_to_all | solution.py:432

commit v8 on v7

--- a/solution.py
+++ b/solution.py
@@ -26,21 +26,6 @@
     return lax.all_to_all(jnp.broadcast_to(block[None], (count,) + block.shape), axis, 0, 0)
 
 
-def chip_rows(w_in, w_mid, w_out):
-    columns = 2 * w_in.shape[1] + w_mid.shape[1]
-    (rows,) = on_chip(
-        pack_kernel,
-        (jax.ShapeDtypeStruct((w_in.shape[0], columns), jnp.bfloat16),),
-        (w_in, w_mid, w_out),
-        0,
-        fetched=3,
-        room=56,
-    )
-    rows = lax.all_gather(rows, "core", axis=0, tiled=True)
-    width = columns // lax.axis_size(("core", "x_hi"))
-    return lax.dynamic_slice_in_dim(rows, lax.axis_index(("core", "x_hi")) * width, width, 1)
-
-
 def swapped(array, axis):
     return lax.ppermute(array, axis, [(0, 1), (1, 0)])
 
@@ -56,15 +41,6 @@
     count = lax.axis_size(TILE)
     pairs = [(row, row + 3) for row in range(1, count - 3, 2)]
     return lax.ppermute(array, TILE, pairs + [(after, row) for row, after in pairs])
-
-
-def neighbour_sum(field):
-    far = swapped_between_chips(field)
-    edges = swapped(jnp.concatenate([field[:1], field[-1:]]), "x_hi")
-    near = swapped(field, "core")
-    east = jnp.concatenate([field[1:], edges[:1]])
-    west = jnp.concatenate([edges[1:], field[:-1]])
-    return far + near + east + west
 
 
 def adjoint_layers(source, hidden_one, hidden_two, weights):
@@ -90,7 +66,26 @@
     return (slope_one * back_one).astype(jnp.bfloat16)
 
 
-def edge_kernel(state, increment, diffusivity, land_sea, col, lev, val, prec, edges, outer):
+def first_kernel(
+    state,
+    increment,
+    diffusivity,
+    land_sea,
+    col,
+    lev,
+    val,
+    prec,
+    w_in,
+    w_mid,
+    w_out,
+    rows,
+    edges,
+    outer,
+):
+    features = w_in.shape[1]
+    rows[:, :features] = w_in[...].astype(jnp.bfloat16)
+    rows[:, features:-features] = w_mid[...]
+    rows[:, -features:] = w_out[...].astype(jnp.bfloat16)
     edges[...] = jnp.zeros_like(edges)
     cells = state.shape[1]
     for which, field in enumerate((state, increment, diffusivity)):
@@ -124,7 +119,7 @@
     )
 
 
-def pack_row_kernel(state, increment, diffusivity, mine, other, pack):
+def pack_row_kernel(mine, other, state, increment, diffusivity, pack):
     cells, features = state.shape[1:]
     for which, field in enumerate((state, increment, diffusivity)):
         ring = ring_field(field[0], other, which)
@@ -151,6 +146,7 @@
     outer,
     settled_out,
     spreading_out,
+    ends_out,
     grads,
     weights,
 ):
@@ -298,6 +294,7 @@
     )
     spreading = own[2][:cells] * adjoint_one
     spreading_out[...] = spreading
+    ends_out[...] = jnp.concatenate([spreading[:1], spreading[cells - 7 :]])
     source = (gate * adjoint_one).astype(jnp.bfloat16)
     back_one = adjoint_layers(source, first[0], first[1], weights)
     settled_out[...] = (
@@ -324,36 +321,37 @@
                 ]
 
 
-def on_chip(kernel, outs, operands, flops, scratch=(), scalars=0, fetched=0, place=None, room=32):
+def on_chip(kernel, outs, operands, flops, scratch=(), scalars=0, direct=0, fetched=0, place=None, room=32):
     size = sum(array.size * array.dtype.itemsize for array in list(operands) + list(outs))
-    count = len(operands) - scalars
     by_kernel = fetched > 0
-    places = [pltpu.SMEM] * scalars + [pl.ANY if by_kernel else pltpu.VMEM] * count
+    before = scalars + (direct if by_kernel else len(operands) - scalars)
+    count = len(operands) - before
+    places = [pltpu.SMEM] * scalars + [pltpu.VMEM] * (before - scalars) + [pl.ANY] * count
     body = kernel
     if by_kernel:
         copies = tuple(
             pltpu.VMEM(array.shape, array.dtype)
-            for array in operands[scalars : scalars + fetched]
-        )
-        scratch = copies + (pltpu.SemaphoreType.DMA((2 * count,)),) + tuple(scratch)
+            for array in operands[before : before + fetched]
+        )
+        scratch = copies + (pltpu.SemaphoreType.DMA((count,)),) + tuple(scratch)
 
         def body(*refs):
-            numbers, sources, refs = refs[:scalars], refs[scalars : scalars + count], refs[scalars + count :]
+            numbers, ready = refs[:scalars], refs[scalars:before]
+            sources, refs = refs[before : before + count], refs[before + count :]
             results, refs = refs[: len(outs)], refs[len(outs) :]
             held, done, rest = refs[:fetched], refs[fetched], refs[fetched + 1 :]
-            pairs = list(zip(sources, held))
+            targets = list(held)
             if place is not None:
-                for source, targets in zip(sources[fetched:], place(numbers, rest)):
-                    pairs += [(source.at[i], target) for i, target in enumerate(targets)]
+                targets += place(numbers, rest)
             moves = [
                 pltpu.make_async_copy(source, target, done.at[i])
-                for i, (source, target) in enumerate(pairs)
+                for i, (source, target) in enumerate(zip(sources, targets))
             ]
             for move in moves:
                 move.start()
             for move in moves:
                 move.wait()
-            kernel(*held, *results, *rest)
+            kernel(*ready, *held, *results, *rest)
 
     return pl.pallas_call(
         body,
@@ -364,13 +362,6 @@
         compiler_params=pltpu.CompilerParams(vmem_limit_bytes=room * 1024 * 1024),
         cost_estimate=pl.CostEstimate(flops=flops, bytes_accessed=size, transcendentals=0),
     )(*operands)
-
-
-def pack_kernel(w_in, w_mid, w_out, rows):
-    features = w_in.shape[1]
-    rows[:, :features] = w_in[...].astype(jnp.bfloat16)
-    rows[:, features:-features] = w_mid[...]
-    rows[:, -features:] = w_out[...].astype(jnp.bfloat16)
 
 
 def sum_and_spread_kernel(parts, copies):
@@ -407,10 +398,11 @@
         new[...] = old[...] - scale * jnp.concatenate(sides, axis=1)
 
 
-def updated(grads, w_in, w_out):
+def updated(grads, w_in, w_out, arriving):
     kinds, blocks, halves, rows, columns = grads.shape
     peers = kinds * blocks * halves
     grads = lax.all_to_all(grads.reshape(peers, rows, columns), AROUND, 0, 0)
+    grads, arriving = lax.optimization_barrier((grads, arriving))
     for axis in ("z_lo", "z_hi"):
         count = lax.axis_size(axis)
         (copies,) = on_chip(
@@ -432,13 +424,14 @@
     parts = lax.all_to_all(copies, AROUND, 0, 0)
     place = jnp.stack([lax.axis_index(("x_lo", "y")), lax.axis_index("core")])
     shape = jax.ShapeDtypeStruct(w_in.shape, jnp.float32)
-    return on_chip(
+    new_in, new_out = on_chip(
         functools.partial(update_kernel, blocks, float(peers * rows * columns)),
         (shape, shape),
         (place, parts, w_in, w_out),
         parts.size,
         scalars=1,
     )
+    return new_in, new_out, arriving
 
 
 def local(
@@ -451,62 +444,74 @@
     def outs(*shapes):
         return tuple(jax.ShapeDtypeStruct(shape, kind) for shape, kind in shapes)
 
-    half = chip_rows(w_in, w_mid, w_out)
-    width = half.shape[1]
-    half, land_sea = lax.optimization_barrier((half, land_sea))
-    fields = (state, increment, diffusivity, land_sea)
-    mine, outer = on_chip(
-        edge_kernel,
-        outs(((24, features), jnp.float32), ((cells, features), jnp.bfloat16)),
-        fields + tuple(observed),
+    columns = 2 * features + w_mid.shape[1]
+    width = columns // lax.axis_size("core")
+    rows, mine, outer = on_chip(
+        first_kernel,
+        outs(
+            ((w_in.shape[0], columns), jnp.bfloat16),
+            ((24, features), jnp.float32),
+            ((cells, features), jnp.bfloat16),
+        ),
+        (state, increment, diffusivity, land_sea, *observed, w_in, w_mid, w_out),
         0,
-        fetched=8,
+        fetched=11,
         room=56,
     )
+    rows = lax.all_gather(rows, "core", axis=0, tiled=True)
+    half = lax.dynamic_slice_in_dim(rows, lax.axis_index("core") * width, width, 1)
+    half, mine, outer = lax.optimization_barrier((half, mine, outer))
     half = spread(half, Z).reshape(-1, width)
     other = swapped(mine, "x_hi")
     outer = swapped_three_apart(outer)
     (own,) = on_chip(
         pack_row_kernel,
         outs(((3 * BLOCK + 16, features), jnp.bfloat16)),
-        fields[:3] + (mine, other),
+        (mine, other, state, increment, diffusivity),
         0,
-        fetched=5,
+        direct=2,
+        fetched=3,
         room=56,
     )
     near = swapped(own, "core")
     half, near = lax.optimization_barrier((half, near))
-    half = spread(half, ("x_hi", "x_lo", "y"))
+    half = spread(half, ("x_lo", "y")).reshape(-1, width)
     far = swapped_between_chips(jnp.concatenate([own, near]))
     far, outer = lax.optimization_barrier((far, outer))
     beyond = swapped(far, "core")
     half, far, beyond = lax.optimization_barrier((half, far, beyond))
-    pieces = lax.axis_size("x_hi")
-    half = half.reshape(pieces, -1, width)
-    hidden_units = half.shape[1]
+    hidden_units = half.shape[0]
     blocks = lax.axis_size(("x_lo", "y"))
     halves = lax.axis_size("core")
     narrow = ((cells, features), jnp.float32)
-    settled, spreading, grads = on_chip(
+    settled, spreading, ends, grads = on_chip(
         functools.partial(whole_kernel, obs_col.shape[0]),
         outs(
             narrow,
             narrow,
+            ((8, features), jnp.float32),
             ((2, blocks, halves, hidden_units // blocks, features // halves), jnp.bfloat16),
         ),
-        (lax.axis_index("core")[None], *fields[:3], mine, other, near, far, beyond, outer)
+        (lax.axis_index("core")[None], state, increment, diffusivity, mine, other, near, far, beyond, outer)
         + (half, swapped(half, "core")),
         40 * cells * hidden_units * (2 * features + hidden_units),
-        scratch=(pltpu.VMEM((2, hidden_units, pieces * width), jnp.bfloat16),),
+        scratch=(pltpu.VMEM((2, hidden_units, width), jnp.bfloat16),),
         scalars=1,
         fetched=9,
         place=lambda numbers, rest: [
-            [rest[0].at[side, :, pl.ds(piece * width, width)] for piece in range(pieces)]
-            for side in (numbers[0][0], 1 - numbers[0][0])
+            rest[0].at[numbers[0][0]],
+            rest[0].at[1 - numbers[0][0]],
         ],
     )
-    w_in_new, w_out_new = updated(grads, w_in, w_out)
-    adjoint = settled + neighbour_sum(spreading)
+    arriving = (
+        swapped_between_chips(spreading),
+        swapped(spreading, "core"),
+        swapped(ends, "x_hi"),
+    )
+    w_in_new, w_out_new, (far, near, ends) = updated(grads, w_in, w_out, arriving)
+    east = jnp.concatenate([spreading[1:], ends[:1]])
+    west = jnp.concatenate([ends[-1:], spreading[:-1]])
+    adjoint = settled + (far + near + east + west)
     return adjoint[None], w_in_new, w_out_new
 
 

time: 163 us -> 159 us (0.975)
  waiting for transfers between devices: 57.3 us -> 50.4 us
  starting transfers between devices: 68.6 us -> 72 us
    all_to_all x1, waiting for transfers between devices: 16.9 us -> 1.72 us  [updated(): grads = lax.all_to_all(grads.reshape(peers, rows, columns), AROUND, 0, 0)]
    all_to_all x2, waiting for transfers between devices: 8.6 us -> 18.3 us  [updated(): grads = lax.all_to_all(copies, axis, 0, 0)]
    all_to_all x2, waiting for transfers between devices: 11.4 us -> 3.08 us  [spread(): lax.all_to_all(jnp.broadcast_to(block[None], (count,) + block.shape), axi...]
    ppermute x6, waiting for transfers between devices: 8.03 us -> 14.2 us  [swapped(): return lax.ppermute(array, axis, [(0, 1), (1, 0)])]
    ppermute x6, starting transfers between devices: 19.9 us -> 22.5 us  [swapped(): return lax.ppermute(array, axis, [(0, 1), (1, 0)])]
    all_to_all x1, starting transfers between devices: 5.77 us -> 7.41 us  [updated(): grads = lax.all_to_all(grads.reshape(peers, rows, columns), AROUND, 0, 0)]
    all_to_all x2, starting transfers between devices: 8.1 us -> 9.74 us  [updated(): grads = lax.all_to_all(copies, axis, 0, 0)]
    all_to_all x2, starting transfers between devices: 16.4 us -> 14.8 us  [spread(): lax.all_to_all(jnp.broadcast_to(block[None], (count,) + block.shape), axi...]
  transfers between devices with their start and end apart: 15 -> 15, of which waited for: 10 -> 11; matrix products, arithmetic and copies ran while one was open for 1% -> 1% of each run, Pallas kernels for 3% -> 2%
where the time goes in v8:
time: 159 us; the launch traced here: 158 us
  starting transfers between devices  72 us (45%)
  waiting for transfers between devices  50.4 us (32%)
  Pallas kernels  22.6 us (14%)
  blocking collectives  8.58 us (5%)
  local copies, waits for them, and re-layouts  2.65 us (2%)
    pallas_call x7, Pallas kernels, on_chip(): pl.pallas_call(body, out_shape=outs, in_specs=[pl.BlockSpec(memory_space=...  22.6 us
    ppermute x6, starting transfers between devices, swapped(): return lax.ppermute(array, axis, [(0, 1), (1, 0)])  22.5 us
    all_to_all x2, waiting for transfers between devices, updated(): grads = lax.all_to_all(copies, axis, 0, 0)  18.3 us
    all_to_all x2, starting transfers between devices, spread(): lax.all_to_all(jnp.broadcast_to(block[None], (count,) + block.shape), axi...  14.8 us
    ppermute x6, waiting for transfers between devices, swapped(): return lax.ppermute(array, axis, [(0, 1), (1, 0)])  14.2 us
    all_to_all x2, starting transfers between devices, updated(): grads = lax.all_to_all(copies, axis, 0, 0)  9.74 us
    all_gather x1, blocking collectives, local(): rows = lax.all_gather(rows, 'core', axis=0, tiled=True)  8.58 us
    ppermute x2, starting transfers between devices, swapped_between_chips(): return lax.ppermute(array, TILE, pairs)  8.02 us
  transfers between devices with their start and end apart: 15, of which 11 were waited for; matrix products, arithmetic and copies ran while one was open for 1% of the time, Pallas kernels for 2%

profile of v8, /device:TPU:1, one launch (start us, length us, event | category | flops | bytes accessed | tf_op | source)
XLA Modules:
  0.0 157.9 jit_solution(14727959931197561695)
XLA Ops:
  0.6 1.8 %shard_map.130 = (bf16[4,1536]{1,0:T(4,128)(2,1)}, f32[24,256]{1,0:T(8,128)}, bf16[128,256]{1,0:T(8,128)(2,1)}) custom-call(f32[1,128,256]{2,1,0:T(8,128)} %refs_1_.3, f32[1,128,256]{2,1,0:T(8,128)} %refs_2_.5, f32[1,128,256]{2,1,0:T(8,128)} %refs_3_.5, s32[1,128]{1,0:T(1,128)} %refs_3_.3, s32[1,64]{1,0:T(1,128)} %bitcast.17, s32[1,64]{1,0:T(1,128)} %bitcast.18, ...), custom_call_target="tpu_custom_call" | custom-call | bytes 513536 | tf_op jit(solution)/shard_map/pallas_call | solution.py:356
  2.4 8.6 %all-gather = bf16[2,4,1536]{2,1,0:T(4,128)(2,1)S(1)} all-gather(bf16[1,4,1536]{2,1,0:T(4,128)(2,1)} %bitcast.16), channel_id=1, replica_groups=mesh['x_lo'=2,'y'=4,'z_hi'=4,'z_lo'=4,'core'=2,'x_hi'=2] {'core'}, dimensions={0}, use_global_device_ids=true | all-gather | bytes 36864 | tf_op jit(solution)/shard_map/all_gather | solution.py:461
  11.1 0.7 broadcast_in_dim.38
  11.7 9.5 %all-to-all-start = ((bf16[16,8,768]{2,1,0:T(8,128)(2,1)}), bf16[16,8,768]{2,1,0:T(8,128)(2,1)S(1)}, u32[]{:S(2)}, u32[]{:S(2)}) async-start(bf16[16,8,768]{2,1,0:T(8,128)(2,1)} %broadcast_in_dim.38), calls=%async_computation | async-start | bytes 393216 | tf_op jit(solution)/shard_map/all_to_all | solution.py:26
  21.3 4.7 %collective-permute-start = (f32[24,256]{1,0:T(8,128)}, f32[24,256]{1,0:T(8,128)S(1)}, u32[]{:S(2)}, u32[]{:S(2)}) collective-permute-start(f32[24,256]{1,0:T(8,128)} %get-tuple-element.29.refs_0_.refs_4_), channel_id=1, source_target_pairs={{0,1},{1,0},{2,3},{3,2},{4,5},{5,4},{6,7},{7,6},{8,9},{9,8},{10,11... | collective-permute-start | bytes 73736 | tf_op jit(solution)/shard_map/ppermute | solution.py:30
  26.0 1.6 %collective-permute-done.refs_1_.refs_5_ = f32[24,256]{1,0:T(8,128)S(1)} collective-permute-done((f32[24,256]{1,0:T(8,128)}, f32[24,256]{1,0:T(8,128)S(1)}, u32[]{:S(2)}, u32[]{:S(2)}) %collective-permute-start) | collective-permute-done | bytes 24608 | tf_op jit(solution)/shard_map/ppermute | solution.py:30
  27.6 0.0 copy-start.4
  27.6 0.6 copy-done.4
  28.2 2.6 %shard_map.131 = bf16[448,256]{1,0:T(8,128)(2,1)} custom-call(f32[24,256]{1,0:T(8,128)} %get-tuple-element.29.refs_0_.refs_4_, f32[24,256]{1,0:T(8,128)} %copy-done.4, f32[1,128,256]{2,1,0:T(8,128)} %refs_1_.3, f32[1,128,256]{2,1,0:T(8,128)} %refs_2_.5, f32[1,128,256]{2,1,0:T(8,128)} %refs_3_.5), custom_call_target="tpu_custom_call" | custom-call | bytes 671744 | tf_op jit(solution)/shard_map/pallas_call | solution.py:356
  30.8 3.7 %collective-permute-start.1 = (bf16[448,256]{1,0:T(8,128)(2,1)}, bf16[448,256]{1,0:T(8,128)(2,1)S(1)}, u32[]{:S(2)}, u32[]{:S(2)}) collective-permute-start(bf16[448,256]{1,0:T(8,128)(2,1)} %shard_map.131), channel_id=1, source_target_pairs={{0,2},{2,0},{1,3},{3,1},{4,6},{6,4},{5,7},{7,5},{8,10},{10,8},{9,1... | collective-permute-start | bytes 688136 | tf_op jit(solution)/shard_map/ppermute | solution.py:30
  34.5 1.3 collective-permute-done.1.refs_6_
  35.8 0.0 all-to-all-done
  35.8 1.3 broadcast_in_dim.39
  37.1 0.0 copy-start.8
  37.1 0.0 copy-start.9
  37.1 0.0 copy-start
  37.1 0.0 copy-start.1
  37.1 0.0 copy-start.2
  37.1 0.0 copy-start.3
  37.1 0.0 copy-start.5
  37.1 5.3 %all-to-all-start.1 = ((bf16[8,128,768]{2,1,0:T(8,128)(2,1)}), bf16[8,128,768]{2,1,0:T(8,128)(2,1)S(1)}, u32[]{:S(2)}, u32[]{:S(2)}) async-start(bf16[8,128,768]{2,1,0:T(8,128)(2,1)} %broadcast_in_dim.39), calls=%async_computation.1 | async-start | bytes 3145728 | tf_op jit(solution)/shard_map/all_to_all | solution.py:26
  42.4 0.0 copy-done.8
  42.4 6.1 %collective-permute-start.2 = (bf16[896,256]{1,0:T(8,128)(2,1)S(1)}, bf16[896,256]{1,0:T(8,128)(2,1)S(1)}, u32[]{:S(2)}, u32[]{:S(2)}) collective-permute-start(bf16[896,256]{1,0:T(8,128)(2,1)S(1)} %pad_maximum_fusion), channel_id=1, source_target_pairs={{2,4},{4,2},{6,8},{8,6},{10,12},{12,10},{14,16},{16,14},{18,20},{2... | collective-permute-start | bytes 1376264 | tf_op jit(solution)/shard_map/ppermute | solution.py:37
  48.5 0.0 copy-done.9
  48.5 2.8 %collective-permute-start.3 = (bf16[128,256]{1,0:T(8,128)(2,1)S(1)}, bf16[128,256]{1,0:T(8,128)(2,1)S(1)}, u32[]{:S(2)}, u32[]{:S(2)}) collective-permute-start(bf16[128,256]{1,0:T(8,128)(2,1)S(1)} %copy-done.9), channel_id=1, source_target_pairs={{2,8},{6,12},{10,16},{14,20},{18,24},{22,28},{26,32},{30,36},{34,4... | collective-permute-start | bytes 196616 | tf_op jit(solution)/shard_map/ppermute | solution.py:43
  51.3 5.9 %collective-permute-done.3.refs_9_ = bf16[128,256]{1,0:T(8,128)(2,1)S(1)} collective-permute-done((bf16[128,256]{1,0:T(8,128)(2,1)S(1)}, bf16[128,256]{1,0:T(8,128)(2,1)S(1)}, u32[]{:S(2)}, u32[]{:S(2)}) %collective-permute-start.3) | collective-permute-done | bytes 65568 | tf_op jit(solution)/shard_map/ppermute | solution.py:43
  57.2 0.0 collective-permute-done.2.refs_7_
  57.2 1.9 %collective-permute-start.4 = (bf16[896,256]{1,0:T(8,128)(2,1)S(1)}, bf16[896,256]{1,0:T(8,128)(2,1)S(1)}, u32[]{:S(2)}, u32[]{:S(2)}) collective-permute-start(bf16[896,256]{1,0:T(8,128)(2,1)S(1)} %collective-permute-done.2.refs_7_), channel_id=1, source_target_pairs={{0,2},{2,0},{1,3},{3,1},{4,6},{6,4},{5,7},{7,5},{8,10},{10,8},{9,1... | collective-permute-start | bytes 1376264 | tf_op jit(solution)/shard_map/ppermute | solution.py:30
  59.1 1.8 %collective-permute-done.4.refs_8_ = bf16[896,256]{1,0:T(8,128)(2,1)S(1)} collective-permute-done((bf16[896,256]{1,0:T(8,128)(2,1)S(1)}, bf16[896,256]{1,0:T(8,128)(2,1)S(1)}, u32[]{:S(2)}, u32[]{:S(2)}) %collective-permute-start.4) | collective-permute-done | bytes 458784 | tf_op jit(solution)/shard_map/ppermute | solution.py:30
  60.9 3.1 %all-to-all-done.1 = bf16[8,128,768]{2,1,0:T(8,128)(2,1)S(1)} async-done(((bf16[8,128,768]{2,1,0:T(8,128)(2,1)}), bf16[8,128,768]{2,1,0:T(8,128)(2,1)S(1)}, u32[]{:S(2)}, u32[]{:S(2)}) %all-to-all-start.1) | async-done | bytes 1572896 | tf_op jit(solution)/shard_map/all_to_all | solution.py:26
  64.0 5.5 %collective-permute-start.5 = (bf16[1024,768]{1,0:T(8,128)(2,1)S(1)}, bf16[1024,768]{1,0:T(8,128)(2,1)S(1)}, u32[]{:S(2)}, u32[]{:S(2)}) collective-permute-start(bf16[1024,768]{1,0:T(8,128)(2,1)S(1)} %bitcast.13), channel_id=1, source_target_pairs={{0,2},{2,0},{1,3},{3,1},{4,6},{6,4},{5,7},{7,5},{8,10},{10,8},{9,1... | collective-permute-start | bytes 4718600 | tf_op jit(solution)/shard_map/ppermute | solution.py:30
  69.5 3.0 %collective-permute-done.5.refs_11_ = bf16[1024,768]{1,0:T(8,128)(2,1)S(1)} collective-permute-done((bf16[1024,768]{1,0:T(8,128)(2,1)S(1)}, bf16[1024,768]{1,0:T(8,128)(2,1)S(1)}, u32[]{:S(2)}, u32[]{:S(2)}) %collective-permute-start.5) | collective-permute-done | bytes 1572896 | tf_op jit(solution)/shard_map/ppermute | solution.py:30
  72.5 0.0 copy-done
  72.5 0.0 copy-done.1
  72.5 0.0 copy-done.2
  72.5 0.0 copy-done.3
  72.5 0.0 copy-done.5
  72.5 14.7 %shard_map.132 = (f32[128,256]{1,0:T(8,128)S(1)}, f32[128,256]{1,0:T(8,128)S(1)}, f32[8,256]{1,0:T(8,128)S(1)}, bf16[2,8,2,128,128]{4,3,2,1,0:T(8,128)(2,1)}) custom-call(s32[1]{0:T(128)} %bitcast.refs_0_, f32[1,128,256]{2,1,0:T(8,128)S(1)} %copy-done, f32[1,128,256]{2,1,0:T(8,128)S(1)} %copy-done.1, f32[1,128,256]{2,1,0:T(8,128)S(1)} %copy-done.2, ...), custom_call_target="tpu_custom_call" | custom-call | flops 8053063680 | bytes 6119428 | tf_op jit(solution)/shard_map/pallas_call | solution.py:356
  87.2 7.4 %all-to-all-start.2 = ((bf16[32,128,128]{2,1,0:T(8,128)(2,1)}), bf16[32,128,128]{2,1,0:T(8,128)(2,1)S(1)}, u32[]{:S(2)}, u32[]{:S(2)}) async-start(bf16[32,128,128]{2,1,0:T(8,128)(2,1)} %bitcast.8), calls=%async_computation.2 | async-start | bytes 2097152 | tf_op jit(solution)/shard_map/all_to_all | solution.py:404
  94.7 1.9 %collective-permute-start.6 = (f32[128,256]{1,0:T(8,128)S(1)}, f32[128,256]{1,0:T(8,128)S(1)}, u32[]{:S(2)}, u32[]{:S(2)}) collective-permute-start(f32[128,256]{1,0:T(8,128)S(1)} %get-tuple-element.41), channel_id=1, source_target_pairs={{2,4},{4,2},{6,8},{8,6},{10,12},{12,10},{14,16},{16,14},{18,20},{2... | collective-permute-start | bytes 393224 | tf_op jit(solution)/shard_map/ppermute | solution.py:37
  96.6 1.9 %collective-permute-start.7 = (f32[128,256]{1,0:T(8,128)S(1)}, f32[128,256]{1,0:T(8,128)S(1)}, u32[]{:S(2)}, u32[]{:S(2)}) collective-permute-start(f32[128,256]{1,0:T(8,128)S(1)} %get-tuple-element.41), channel_id=1, source_target_pairs={{0,2},{2,0},{1,3},{3,1},{4,6},{6,4},{5,7},{7,5},{8,10},{10,8},{9,1... | collective-permute-start | bytes 393224 | tf_op jit(solution)/shard_map/ppermute | solution.py:30
  98.5 4.8 %collective-permute-start.8 = (f32[8,256]{1,0:T(8,128)S(1)}, f32[8,256]{1,0:T(8,128)S(1)}, u32[]{:S(2)}, u32[]{:S(2)}) collective-permute-start(f32[8,256]{1,0:T(8,128)S(1)} %get-tuple-element.42), channel_id=1, source_target_pairs={{0,1},{1,0},{2,3},{3,2},{4,5},{5,4},{6,7},{7,6},{8,9},{9,8},{10,11... | collective-permute-start | bytes 24584 | tf_op jit(solution)/shard_map/ppermute | solution.py:30
  103.3 6.5 %collective-permute-done.8 = f32[8,256]{1,0:T(8,128)S(1)} collective-permute-done((f32[8,256]{1,0:T(8,128)S(1)}, f32[8,256]{1,0:T(8,128)S(1)}, u32[]{:S(2)}, u32[]{:S(2)}) %collective-permute-start.8) | collective-permute-done | bytes 8224 | tf_op jit(solution)/shard_map/ppermute | solution.py:30
  109.8 0.0 collective-permute-done.6
  109.8 0.0 collective-permute-done.7
  109.8 1.7 %all-to-all-done.2.parts = bf16[32,128,128]{2,1,0:T(8,128)(2,1)S(1)} async-done(((bf16[32,128,128]{2,1,0:T(8,128)(2,1)}), bf16[32,128,128]{2,1,0:T(8,128)(2,1)S(1)}, u32[]{:S(2)}, u32[]{:S(2)}) %all-to-all-start.2) | async-done | bytes 1048608 | tf_op jit(solution)/shard_map/all_to_all | solution.py:404
  111.6 0.8 shard_map.133
  112.4 0.0 copy-start.6
  112.4 0.0 copy-start.7
  112.4 3.5 %all-to-all-start.3 = ((bf16[4,128,128]{2,1,0:T(8,128)(2,1)}), bf16[4,128,128]{2,1,0:T(8,128)(2,1)S(1)}, u32[]{:S(2)}, u32[]{:S(2)}) async-start(bf16[4,128,128]{2,1,0:T(8,128)(2,1)} %shard_map.133), calls=%async_computation.3 | async-start | bytes 262144 | tf_op jit(solution)/shard_map/all_to_all | solution.py:414
  115.8 0.1 pad_add_fusion.place
  115.9 4.8 %all-to-all-done.3.parts = bf16[4,128,128]{2,1,0:T(8,128)(2,1)S(1)} async-done(((bf16[4,128,128]{2,1,0:T(8,128)(2,1)}), bf16[4,128,128]{2,1,0:T(8,128)(2,1)S(1)}, u32[]{:S(2)}, u32[]{:S(2)}) %all-to-all-start.3) | async-done | bytes 131104 | tf_op jit(solution)/shard_map/all_to_all | solution.py:414
  120.7 0.7 shard_map.134
  121.4 6.3 %all-to-all-start.4 = ((bf16[4,128,128]{2,1,0:T(8,128)(2,1)}), bf16[4,128,128]{2,1,0:T(8,128)(2,1)S(1)}, u32[]{:S(2)}, u32[]{:S(2)}) async-start(bf16[4,128,128]{2,1,0:T(8,128)(2,1)} %shard_map.134), calls=%async_computation.4 | async-start | bytes 262144 | tf_op jit(solution)/shard_map/all_to_all | solution.py:414
  127.7 13.6 %all-to-all-done.4.parts = bf16[4,128,128]{2,1,0:T(8,128)(2,1)S(1)} async-done(((bf16[4,128,128]{2,1,0:T(8,128)(2,1)}), bf16[4,128,128]{2,1,0:T(8,128)(2,1)S(1)}, u32[]{:S(2)}, u32[]{:S(2)}) %all-to-all-start.4) | async-done | bytes 131104 | tf_op jit(solution)/shard_map/all_to_all | solution.py:414
  141.2 0.7 shard_map.135
  141.9 6.8 %all-to-all-start.5 = ((bf16[32,16,128]{2,1,0:T(8,128)(2,1)}), bf16[32,16,128]{2,1,0:T(8,128)(2,1)S(1)}, u32[]{:S(2)}, u32[]{:S(2)}) async-start(bf16[32,16,128]{2,1,0:T(8,128)(2,1)} %shard_map.135), calls=%async_computation.5 | async-start | bytes 262144 | tf_op jit(solution)/shard_map/all_to_all | solution.py:424
  148.8 0.7 fusion.2
  149.5 7.1 %all-to-all-done.5.parts_ref = bf16[32,16,128]{2,1,0:T(8,128)(2,1)S(1)} async-done(((bf16[32,16,128]{2,1,0:T(8,128)(2,1)}), bf16[32,16,128]{2,1,0:T(8,128)(2,1)S(1)}, u32[]{:S(2)}, u32[]{:S(2)}) %all-to-all-start.5) | async-done | bytes 131104 | tf_op jit(solution)/shard_map/all_to_all | solution.py:424
  156.6 0.0 copy-done.6
  156.6 0.0 copy-done.7
  156.6 1.3 shard_map.136
  (5 shorter events, 0.1 us)
Async XLA Ops:
  11.7 24.0 %all-to-all-start = ((bf16[16,8,768]{2,1,0:T(8,128)(2,1)}), bf16[16,8,768]{2,1,0:T(8,128)(2,1)S(1)}, u32[]{:S(2)}, u32[]{:S(2)}) async-start(bf16[16,8,768]{2,1,0:T(8,128)(2,1)} %broadcast_in_dim.38), calls=%async_computation | async-start | bytes 393216 | tf_op jit(solution)/shard_map/all_to_all | solution.py:26
  21.3 6.3 %collective-permute-start = (f32[24,256]{1,0:T(8,128)}, f32[24,256]{1,0:T(8,128)S(1)}, u32[]{:S(2)}, u32[]{:S(2)}) collective-permute-start(f32[24,256]{1,0:T(8,128)} %get-tuple-element.29.refs_0_.refs_4_), channel_id=1, source_target_pairs={{0,1},{1,0},{2,3},{3,2},{4,5},{5,4},{6,7},{7,6},{8,9},{9,8},{10,11... | collective-permute-start | bytes 73736 | tf_op jit(solution)/shard_map/ppermute | solution.py:30
  27.6 0.6 copy-start.4
  30.8 5.0 %collective-permute-start.1 = (bf16[448,256]{1,0:T(8,128)(2,1)}, bf16[448,256]{1,0:T(8,128)(2,1)S(1)}, u32[]{:S(2)}, u32[]{:S(2)}) collective-permute-start(bf16[448,256]{1,0:T(8,128)(2,1)} %shard_map.131), channel_id=1, source_target_pairs={{0,2},{2,0},{1,3},{3,1},{4,6},{6,4},{5,7},{7,5},{8,10},{10,8},{9,1... | collective-permute-start | bytes 688136 | tf_op jit(solution)/shard_map/ppermute | solution.py:30
  37.1 5.3 %copy-start.8 = (bf16[448,256]{1,0:T(8,128)(2,1)S(1)}, bf16[448,256]{1,0:T(8,128)(2,1)}, u32[]{:S(2)}) copy-start(bf16[448,256]{1,0:T(8,128)(2,1)} %shard_map.131) | copy-start | bytes 688132
  37.1 11.5 %copy-start.9 = (bf16[128,256]{1,0:T(8,128)(2,1)S(1)}, bf16[128,256]{1,0:T(8,128)(2,1)}, u32[]{:S(2)}) copy-start(bf16[128,256]{1,0:T(8,128)(2,1)} %get-tuple-element.33) | copy-start | bytes 196612
  37.1 35.4 %copy-start = (f32[1,128,256]{2,1,0:T(8,128)S(1)}, f32[1,128,256]{2,1,0:T(8,128)}, u32[]{:S(2)}) copy-start(f32[1,128,256]{2,1,0:T(8,128)} %refs_1_.3) | copy-start | bytes 393220
  37.1 35.4 %copy-start.1 = (f32[1,128,256]{2,1,0:T(8,128)S(1)}, f32[1,128,256]{2,1,0:T(8,128)}, u32[]{:S(2)}) copy-start(f32[1,128,256]{2,1,0:T(8,128)} %refs_2_.5) | copy-start | bytes 393220
  37.1 35.4 %copy-start.2 = (f32[1,128,256]{2,1,0:T(8,128)S(1)}, f32[1,128,256]{2,1,0:T(8,128)}, u32[]{:S(2)}) copy-start(f32[1,128,256]{2,1,0:T(8,128)} %refs_3_.5) | copy-start | bytes 393220
  37.1 35.4 %copy-start.3 = (f32[24,256]{1,0:T(8,128)S(1)}, f32[24,256]{1,0:T(8,128)}, u32[]{:S(2)}) copy-start(f32[24,256]{1,0:T(8,128)} %get-tuple-element.29.refs_0_.refs_4_) | copy-start | bytes 73732
  37.1 35.4 %copy-start.5 = (f32[24,256]{1,0:T(8,128)S(1)}, f32[24,256]{1,0:T(8,128)}, u32[]{:S(2)}) copy-start(f32[24,256]{1,0:T(8,128)} %copy-done.4) | copy-start | bytes 73732
  37.1 26.9 %all-to-all-start.1 = ((bf16[8,128,768]{2,1,0:T(8,128)(2,1)}), bf16[8,128,768]{2,1,0:T(8,128)(2,1)S(1)}, u32[]{:S(2)}, u32[]{:S(2)}) async-start(bf16[8,128,768]{2,1,0:T(8,128)(2,1)} %broadcast_in_dim.39), calls=%async_computation.1 | async-start | bytes 3145728 | tf_op jit(solution)/shard_map/all_to_all | solution.py:26
  42.4 14.8 %collective-permute-start.2 = (bf16[896,256]{1,0:T(8,128)(2,1)S(1)}, bf16[896,256]{1,0:T(8,128)(2,1)S(1)}, u32[]{:S(2)}, u32[]{:S(2)}) collective-permute-start(bf16[896,256]{1,0:T(8,128)(2,1)S(1)} %pad_maximum_fusion), channel_id=1, source_target_pairs={{2,4},{4,2},{6,8},{8,6},{10,12},{12,10},{14,16},{16,14},{18,20},{2... | collective-permute-start | bytes 1376264 | tf_op jit(solution)/shard_map/ppermute | solution.py:37
  48.5 8.7 %collective-permute-start.3 = (bf16[128,256]{1,0:T(8,128)(2,1)S(1)}, bf16[128,256]{1,0:T(8,128)(2,1)S(1)}, u32[]{:S(2)}, u32[]{:S(2)}) collective-permute-start(bf16[128,256]{1,0:T(8,128)(2,1)S(1)} %copy-done.9), channel_id=1, source_target_pairs={{2,8},{6,12},{10,16},{14,20},{18,24},{22,28},{26,32},{30,36},{34,4... | collective-permute-start | bytes 196616 | tf_op jit(solution)/shard_map/ppermute | solution.py:43
  57.2 3.7 %collective-permute-start.4 = (bf16[896,256]{1,0:T(8,128)(2,1)S(1)}, bf16[896,256]{1,0:T(8,128)(2,1)S(1)}, u32[]{:S(2)}, u32[]{:S(2)}) collective-permute-start(bf16[896,256]{1,0:T(8,128)(2,1)S(1)} %collective-permute-done.2.refs_7_), channel_id=1, source_target_pairs={{0,2},{2,0},{1,3},{3,1},{4,6},{6,4},{5,7},{7,5},{8,10},{10,8},{9,1... | collective-permute-start | bytes 1376264 | tf_op jit(solution)/shard_map/ppermute | solution.py:30
  64.0 8.5 %collective-permute-start.5 = (bf16[1024,768]{1,0:T(8,128)(2,1)S(1)}, bf16[1024,768]{1,0:T(8,128)(2,1)S(1)}, u32[]{:S(2)}, u32[]{:S(2)}) collective-permute-start(bf16[1024,768]{1,0:T(8,128)(2,1)S(1)} %bitcast.13), channel_id=1, source_target_pairs={{0,2},{2,0},{1,3},{3,1},{4,6},{6,4},{5,7},{7,5},{8,10},{10,8},{9,1... | collective-permute-start | bytes 4718600 | tf_op jit(solution)/shard_map/ppermute | solution.py:30
  87.2 24.3 %all-to-all-start.2 = ((bf16[32,128,128]{2,1,0:T(8,128)(2,1)}), bf16[32,128,128]{2,1,0:T(8,128)(2,1)S(1)}, u32[]{:S(2)}, u32[]{:S(2)}) async-start(bf16[32,128,128]{2,1,0:T(8,128)(2,1)} %bitcast.8), calls=%async_computation.2 | async-start | bytes 2097152 | tf_op jit(solution)/shard_map/all_to_all | solution.py:404
  94.7 15.2 %collective-permute-start.6 = (f32[128,256]{1,0:T(8,128)S(1)}, f32[128,256]{1,0:T(8,128)S(1)}, u32[]{:S(2)}, u32[]{:S(2)}) collective-permute-start(f32[128,256]{1,0:T(8,128)S(1)} %get-tuple-element.41), channel_id=1, source_target_pairs={{2,4},{4,2},{6,8},{8,6},{10,12},{12,10},{14,16},{16,14},{18,20},{2... | collective-permute-start | bytes 393224 | tf_op jit(solution)/shard_map/ppermute | solution.py:37
  96.6 13.2 %collective-permute-start.7 = (f32[128,256]{1,0:T(8,128)S(1)}, f32[128,256]{1,0:T(8,128)S(1)}, u32[]{:S(2)}, u32[]{:S(2)}) collective-permute-start(f32[128,256]{1,0:T(8,128)S(1)} %get-tuple-element.41), channel_id=1, source_target_pairs={{0,2},{2,0},{1,3},{3,1},{4,6},{6,4},{5,7},{7,5},{8,10},{10,8},{9,1... | collective-permute-start | bytes 393224 | tf_op jit(solution)/shard_map/ppermute | solution.py:30
  98.5 11.3 %collective-permute-start.8 = (f32[8,256]{1,0:T(8,128)S(1)}, f32[8,256]{1,0:T(8,128)S(1)}, u32[]{:S(2)}, u32[]{:S(2)}) collective-permute-start(f32[8,256]{1,0:T(8,128)S(1)} %get-tuple-element.42), channel_id=1, source_target_pairs={{0,1},{1,0},{2,3},{3,2},{4,5},{5,4},{6,7},{7,6},{8,9},{9,8},{10,11... | collective-permute-start | bytes 24584 | tf_op jit(solution)/shard_map/ppermute | solution.py:30
  112.4 44.2 %copy-start.6 = (f32[4,256]{1,0:T(4,128)S(1)}, f32[4,256]{1,0:T(4,128)}, u32[]{:S(2)}) copy-start(f32[4,256]{1,0:T(4,128)} %w_in.1) | copy-start | bytes 12292
  112.4 44.2 %copy-start.7 = (f32[4,256]{1,0:T(4,128)S(1)}, f32[4,256]{1,0:T(4,128)}, u32[]{:S(2)}) copy-start(f32[4,256]{1,0:T(4,128)} %w_out.1) | copy-start | bytes 12292
  112.4 8.3 %all-to-all-start.3 = ((bf16[4,128,128]{2,1,0:T(8,128)(2,1)}), bf16[4,128,128]{2,1,0:T(8,128)(2,1)S(1)}, u32[]{:S(2)}, u32[]{:S(2)}) async-start(bf16[4,128,128]{2,1,0:T(8,128)(2,1)} %shard_map.133), calls=%async_computation.3 | async-start | bytes 262144 | tf_op jit(solution)/shard_map/all_to_all | solution.py:414
  121.4 19.9 %all-to-all-start.4 = ((bf16[4,128,128]{2,1,0:T(8,128)(2,1)}), bf16[4,128,128]{2,1,0:T(8,128)(2,1)S(1)}, u32[]{:S(2)}, u32[]{:S(2)}) async-start(bf16[4,128,128]{2,1,0:T(8,128)(2,1)} %shard_map.134), calls=%async_computation.4 | async-start | bytes 262144 | tf_op jit(solution)/shard_map/all_to_all | solution.py:414
  141.9 14.7 %all-to-all-start.5 = ((bf16[32,16,128]{2,1,0:T(8,128)(2,1)}), bf16[32,16,128]{2,1,0:T(8,128)(2,1)S(1)}, u32[]{:S(2)}, u32[]{:S(2)}) async-start(bf16[32,16,128]{2,1,0:T(8,128)(2,1)} %shard_map.135), calls=%async_computation.5 | async-start | bytes 262144 | tf_op jit(solution)/shard_map/all_to_all | solution.py:424

commit v9 on v8

--- a/solution.py
+++ b/solution.py
@@ -119,12 +119,25 @@
     )
 
 
-def pack_row_kernel(mine, other, state, increment, diffusivity, pack):
-    cells, features = state.shape[1:]
+def pack_fields_kernel(state, increment, diffusivity, pack):
+    cells = state.shape[1]
     for which, field in enumerate((state, increment, diffusivity)):
-        ring = ring_field(field[0], other, which)
-        ring = jnp.concatenate([ring, jnp.zeros((8, features), jnp.float32)])
-        pack[BLOCK * which : BLOCK * (which + 1)] = ring.astype(jnp.bfloat16)
+        pack[BLOCK * which : BLOCK * which + cells] = field[0].astype(jnp.bfloat16)
+
+
+def pack_edges_kernel(fields, mine, other, pack):
+    features = fields.shape[1]
+    cells = BLOCK - 16
+    for which in range(3):
+        base, start = BLOCK * which, 2 * REACH * which
+        pack[base : base + cells] = fields[base : base + cells]
+        edges = [
+            other[start : start + REACH],
+            jnp.zeros((8 - 2 * REACH, features), jnp.float32),
+            other[start + REACH : start + 2 * REACH],
+            jnp.zeros((8, features), jnp.float32),
+        ]
+        pack[base + cells : base + BLOCK] = jnp.concatenate(edges).astype(jnp.bfloat16)
     gating = ring_gating(mine[18:19, :cells], other[18:19, :cells])[:1]
     numbers = mine[21:23, :]
     coarse = numbers.astype(jnp.bfloat16).astype(jnp.float32)
@@ -135,6 +148,7 @@
 
 def whole_kernel(
     observations,
+    core,
     state,
     increment,
     diffusivity,
@@ -147,7 +161,8 @@
     settled_out,
     spreading_out,
     ends_out,
-    grads,
+    kept,
+    given,
     weights,
 ):
     cells, features = state.shape[1:]
@@ -174,12 +189,14 @@
         return fields + [column(rest[:1])], rest
 
     def activate(both):
-        hidden = jnp.tanh(both[:length]).astype(jnp.bfloat16).astype(jnp.float32)
-        tangent = (1.0 - hidden * hidden) * both[length:]
+        middle = both.shape[0] // 2
+        hidden = jnp.tanh(both[:middle]).astype(jnp.bfloat16).astype(jnp.float32)
+        tangent = (1.0 - hidden * hidden) * both[middle:]
         return jnp.concatenate([hidden, tangent]).astype(jnp.bfloat16)
 
-    def network(states, tangents):
-        stacked = jnp.concatenate([states, tangents]).astype(jnp.bfloat16)
+    def networks(rows):
+        stacked = jnp.concatenate([row[0] for row in rows] + [row[1] for row in rows])
+        stacked = stacked.astype(jnp.bfloat16)
         one = activate(
             lax.dot_general(
                 stacked,
@@ -194,7 +211,8 @@
             low, weights[1, :depth, depth:], preferred_element_type=jnp.float32
         ) + jnp.dot(high, weights[1, depth:, depth:], preferred_element_type=jnp.float32)
         saved = (one[:cells], jnp.concatenate([low[:cells], high[:cells]], axis=1), stacked[:cells])
-        return out[:length], out[length:], saved
+        outs = [out[i * length : (i + 1) * length] for i in range(2 * len(rows))]
+        return list(zip(outs[: len(rows)], outs[len(rows) :])), saved
 
     def observed(final, columns, levels, values, precisions):
         count = columns.shape[1]
@@ -227,38 +245,42 @@
         ),
     ]
 
-    def advance(row, lats):
+    def advance(row, lats, moved):
         states, tangents, diffuse, gated = row
-        tend, tangent, saved = network(states, tangents)
         return (
-            states + diffuse * laplace(states, lats[0]) + gated * tend,
-            tangents + diffuse * laplace(tangents, lats[1]) + gated * tangent,
-            saved,
-        )
-
-    def advance_sum(row, middle, lat):
-        tend, tangent, saved = network(row[0], row[1])
-        return middle + row[2] * laplace(middle, lat) + row[3] * (tend + tangent), saved
-
-    state_one, increment_one, first = advance(
-        own, [beside[0][i] + beside[1][i] for i in range(2)]
+            states + diffuse * laplace(states, lats[0]) + gated * moved[0],
+            tangents + diffuse * laplace(tangents, lats[1]) + gated * moved[1],
+        )
+
+    def advance_sum(row, middle, lat, moved):
+        return middle + row[2] * laplace(middle, lat) + row[3] * (moved[0] + moved[1])
+
+    groups = ((0,), (1, 2), (3, 4))
+    all_rows = [own] + list(beside) + second
+    moved = []
+    first = None
+    for group in groups:
+        got, saved = networks([all_rows[i] for i in group])
+        moved += got
+        first = saved if first is None else first
+    state_one, increment_one = advance(
+        own, [beside[0][i] + beside[1][i] for i in range(2)], moved[0]
     )
     middle_one = state_one + increment_one
     beside_one, beside_middle, second_middle = [], [], []
-    for row, next_row, last in zip(beside, second, third):
-        one = advance(row, [own[i] + next_row[i] for i in range(2)])[:2]
+    for i, (row, next_row, last) in enumerate(zip(beside, second, third)):
+        one = advance(row, [own[j] + next_row[j] for j in range(2)], moved[1 + i])
         beside_one.append(one)
         beside_middle.append(one[0] + one[1])
         next_sum = next_row[0] + next_row[1]
-        second_middle.append(
-            advance_sum(next_row, next_sum, row[0] + row[1] + last)[0]
-        )
-    final, late = advance_sum(
-        [state_one, increment_one, own[2], gate],
-        middle_one,
-        beside_middle[0] + beside_middle[1],
-    )
-
+        second_middle.append(advance_sum(next_row, next_sum, row[0] + row[1] + last, moved[3 + i]))
+    all_rows = [(state_one, increment_one)] + beside_one
+    late, moved = None, []
+    for group in ((0,), (1, 2)):
+        got, saved = networks([all_rows[i] for i in group])
+        moved += got
+        late = saved if late is None else late
+    final = advance_sum(own, middle_one, beside_middle[0] + beside_middle[1], moved[0])
     count = observations
     columns = other[19:20, :count]
     columns = jnp.where(
@@ -271,12 +293,10 @@
     ]
     adjoint = observed(final, columns, *chosen)
     around = jnp.zeros_like(adjoint)
-    for row, one, middle, next_middle, rest in zip(
-        beside, beside_one, beside_middle, second_middle, beside_rest
+    for row, middle, next_middle, rest, moves in zip(
+        beside, beside_middle, second_middle, beside_rest, moved[1:]
     ):
-        total = advance_sum(
-            [one[0], one[1], row[2], row[3]], middle, middle_one + next_middle
-        )[0]
+        total = advance_sum(row, middle, middle_one + next_middle, moves)
         around = around + row[2] * observed(
             total,
             rest[1:2, :cells],
@@ -302,28 +322,27 @@
         - 4.0 * spreading
         + jnp.dot(back_one, weights[0, :, :features], preferred_element_type=jnp.float32)
     )
-    pairs = (
-        (back_late, back_one, late[2], first[2]),
-        (late[1], first[1], source_late, source),
-    )
-    _, blocks, halves, rows, width = grads.shape
-    for which, (left_late, left, right_late, right) in enumerate(pairs):
+    first_core = core[0] == 0
+    lefts = [jnp.concatenate([back_late, back_one]), jnp.concatenate([late[1], first[1]])]
+    rights = [jnp.concatenate([late[2], first[2]]), jnp.concatenate([source_late, source])]
+    halves, blocks, rows, width = kept.shape
+    for out, which in ((given, 1), (kept, 0)):
         total = lax.dot_general(
-            jnp.concatenate([left_late, left]),
-            jnp.concatenate([right_late, right]),
+            jnp.where(first_core, lefts[which], lefts[1 - which]),
+            jnp.where(first_core, rights[which], rights[1 - which]),
             CONTRACT_FIRST,
             preferred_element_type=jnp.float32,
         ).astype(jnp.bfloat16)
-        for block in range(blocks):
-            for half in range(halves):
-                grads[which, block, half] = total[
+        for half in range(halves):
+            for block in range(blocks):
+                out[half, block] = total[
                     block * rows : (block + 1) * rows, half * width : (half + 1) * width
                 ]
 
 
 def on_chip(kernel, outs, operands, flops, scratch=(), scalars=0, direct=0, fetched=0, place=None, room=32):
     size = sum(array.size * array.dtype.itemsize for array in list(operands) + list(outs))
-    by_kernel = fetched > 0
+    by_kernel = fetched > 0 or place is not None
     before = scalars + (direct if by_kernel else len(operands) - scalars)
     count = len(operands) - before
     places = [pltpu.SMEM] * scalars + [pltpu.VMEM] * (before - scalars) + [pl.ANY] * count
@@ -351,7 +370,7 @@
                 move.start()
             for move in moves:
                 move.wait()
-            kernel(*ready, *held, *results, *rest)
+            kernel(*numbers, *ready, *held, *results, *rest)
 
     return pl.pallas_call(
         body,
@@ -393,15 +412,27 @@
     for which, (old, new) in enumerate(((w_in, new_in), (w_out, new_out))):
         sides = []
         for half in range(2):
-            rows = parts_ref[(which * blocks + place[0]) * 2 + half].astype(jnp.float32)[:depth]
+            rows = parts_ref[(half * blocks + place[0]) * 2 + which].astype(jnp.float32)[:depth]
             sides.append(jnp.where(place[1] == 0, rows[:shard], rows[shard:]))
         new[...] = old[...] - scale * jnp.concatenate(sides, axis=1)
 
 
-def updated(grads, w_in, w_out, arriving):
-    kinds, blocks, halves, rows, columns = grads.shape
-    peers = kinds * blocks * halves
-    grads = lax.all_to_all(grads.reshape(peers, rows, columns), AROUND, 0, 0)
+def add_kernel(left, right, total):
+    total[...] = (left[...].astype(jnp.float32) + right[...].astype(jnp.float32)).astype(
+        jnp.bfloat16
+    )
+
+
+def updated(kept, given, w_in, w_out, arriving):
+    halves, blocks, rows, columns = kept.shape
+    peers = halves * blocks
+    (grads,) = on_chip(
+        add_kernel,
+        (jax.ShapeDtypeStruct((peers, rows, columns), jnp.bfloat16),),
+        (kept.reshape(peers, rows, columns), swapped(given, "core").reshape(peers, rows, columns)),
+        kept.size,
+    )
+    grads = lax.all_to_all(grads, AROUND[:-1], 0, 0)
     grads, arriving = lax.optimization_barrier((grads, arriving))
     for axis in ("z_lo", "z_hi"):
         count = lax.axis_size(axis)
@@ -412,6 +443,7 @@
             grads.size,
         )
         grads = lax.all_to_all(copies, axis, 0, 0)
+    peers *= lax.axis_size("core")
     depth = rows // lax.axis_size(Z)
     (copies,) = on_chip(
         sum_and_square_kernel,
@@ -460,19 +492,14 @@
     )
     rows = lax.all_gather(rows, "core", axis=0, tiled=True)
     half = lax.dynamic_slice_in_dim(rows, lax.axis_index("core") * width, width, 1)
-    half, mine, outer = lax.optimization_barrier((half, mine, outer))
+    fields = (state, increment, diffusivity)
+    half, mine, outer, fields = lax.optimization_barrier((half, mine, outer, fields))
     half = spread(half, Z).reshape(-1, width)
     other = swapped(mine, "x_hi")
     outer = swapped_three_apart(outer)
-    (own,) = on_chip(
-        pack_row_kernel,
-        outs(((3 * BLOCK + 16, features), jnp.bfloat16)),
-        (mine, other, state, increment, diffusivity),
-        0,
-        direct=2,
-        fetched=3,
-        room=56,
-    )
+    packed = outs(((3 * BLOCK + 16, features), jnp.bfloat16))
+    (packs,) = on_chip(pack_fields_kernel, packed, fields, 0, fetched=3)
+    (own,) = on_chip(pack_edges_kernel, packed, (packs, mine, other), 0)
     near = swapped(own, "core")
     half, near = lax.optimization_barrier((half, near))
     half = spread(half, ("x_lo", "y")).reshape(-1, width)
@@ -482,22 +509,25 @@
     half, far, beyond = lax.optimization_barrier((half, far, beyond))
     hidden_units = half.shape[0]
     blocks = lax.axis_size(("x_lo", "y"))
-    halves = lax.axis_size("core")
+    halves = lax.axis_size("x_hi")
+    part = ((halves, blocks, hidden_units // blocks, features // halves), jnp.bfloat16)
     narrow = ((cells, features), jnp.float32)
-    settled, spreading, ends, grads = on_chip(
+    settled, spreading, ends, kept, given = on_chip(
         functools.partial(whole_kernel, obs_col.shape[0]),
         outs(
             narrow,
             narrow,
             ((8, features), jnp.float32),
-            ((2, blocks, halves, hidden_units // blocks, features // halves), jnp.bfloat16),
+            part,
+            part,
         ),
         (lax.axis_index("core")[None], state, increment, diffusivity, mine, other, near, far, beyond, outer)
         + (half, swapped(half, "core")),
         40 * cells * hidden_units * (2 * features + hidden_units),
         scratch=(pltpu.VMEM((2, hidden_units, width), jnp.bfloat16),),
         scalars=1,
-        fetched=9,
+        direct=9,
+        fetched=0,
         place=lambda numbers, rest: [
             rest[0].at[numbers[0][0]],
             rest[0].at[1 - numbers[0][0]],
@@ -508,7 +538,7 @@
         swapped(spreading, "core"),
         swapped(ends, "x_hi"),
     )
-    w_in_new, w_out_new, (far, near, ends) = updated(grads, w_in, w_out, arriving)
+    w_in_new, w_out_new, (far, near, ends) = updated(kept, given, w_in, w_out, arriving)
     east = jnp.concatenate([spreading[1:], ends[:1]])
     west = jnp.concatenate([ends[-1:], spreading[:-1]])
     adjoint = settled + (far + near + east + west)

time: 159 us -> 154 us (0.969)
  waiting for transfers between devices: 50.4 us -> 39.1 us
  starting transfers between devices: 72 us -> 80.6 us
  Pallas kernels: 22.6 us -> 17.8 us
  local copies, waits for them, and re-layouts: 2.65 us -> 5.49 us
    ppermute x6 -> x7, waiting for transfers between devices: 14.2 us -> 8.73 us  [swapped(): return lax.ppermute(array, axis, [(0, 1), (1, 0)])]
    pallas_call x7 -> x9, Pallas kernels: 22.6 us -> 17.8 us  [on_chip(): pl.pallas_call(body, out_shape=outs, in_specs=[pl.BlockSpec(memory_space=...]
    all_to_all x1, starting transfers between devices: 6.85 us -> 11.5 us  [updated(): parts = lax.all_to_all(copies, AROUND, 0, 0)]
    ppermute x6 -> x7, starting transfers between devices: 22.5 us -> 25.7 us  [swapped(): return lax.ppermute(array, axis, [(0, 1), (1, 0)])]
    unnamed x21 -> x23, local copies, waits for them, and re-layouts: 0.65 us -> 3.48 us
    all_to_all x2, waiting for transfers between devices: 3.08 us -> 0.32 us  [spread(): lax.all_to_all(jnp.broadcast_to(block[None], (count,) + block.shape), axi...]
    ppermute x2, starting transfers between devices: 8.02 us -> 9.68 us  [swapped_between_chips(): return lax.ppermute(array, TILE, pairs)]
  transfers between devices with their start and end apart: 15 -> 16, of which waited for: 11 -> 11; matrix products, arithmetic and copies ran while one was open for 1% -> 1% of each run, Pallas kernels for 2% -> 0%
where the time goes in v9:
time: 154 us; the launch traced here: 153 us
  starting transfers between devices  80.6 us (52%)
  waiting for transfers between devices  39.1 us (25%)
  Pallas kernels  17.8 us (12%)
  blocking collectives  8.58 us (6%)
  local copies, waits for them, and re-layouts  5.49 us (4%)
    ppermute x7, starting transfers between devices, swapped(): return lax.ppermute(array, axis, [(0, 1), (1, 0)])  25.7 us
    pallas_call x9, Pallas kernels, on_chip(): pl.pallas_call(body, out_shape=outs, in_specs=[pl.BlockSpec(memory_space=...  17.8 us
    all_to_all x2, waiting for transfers between devices, updated(): grads = lax.all_to_all(copies, axis, 0, 0)  16.8 us
    all_to_all x2, starting transfers between devices, spread(): lax.all_to_all(jnp.broadcast_to(block[None], (count,) + block.shape), axi...  14.8 us
    all_to_all x1, starting transfers between devices, updated(): parts = lax.all_to_all(copies, AROUND, 0, 0)  11.5 us
    all_to_all x2, starting transfers between devices, updated(): grads = lax.all_to_all(copies, axis, 0, 0)  10.1 us
    ppermute x2, starting transfers between devices, swapped_between_chips(): return lax.ppermute(array, TILE, pairs)  9.68 us
    ppermute x7, waiting for transfers between devices, swapped(): return lax.ppermute(array, axis, [(0, 1), (1, 0)])  8.73 us
  transfers between devices with their start and end apart: 16, of which 11 were waited for; matrix products, arithmetic and copies ran while one was open for 1% of the time, Pallas kernels for 0%

profile of v9, /device:TPU:1, one launch (start us, length us, event | category | flops | bytes accessed | tf_op | source)
XLA Modules:
  0.0 153.3 jit_solution(10291613022902403166)
XLA Ops:
  0.6 1.8 %shard_map.130 = (bf16[4,1536]{1,0:T(4,128)(2,1)}, f32[24,256]{1,0:T(8,128)}, bf16[128,256]{1,0:T(8,128)(2,1)}) custom-call(f32[1,128,256]{2,1,0:T(8,128)} %refs_1_.4, f32[1,128,256]{2,1,0:T(8,128)} %refs_2_.4, f32[1,128,256]{2,1,0:T(8,128)} %refs_3_.3, s32[1,128]{1,0:T(1,128)} %refs_3_.2, s32[1,64]{1,0:T(1,128)} %bitcast.20, s32[1,64]{1,0:T(1,128)} %bitcast.21, ...), custom_call_target="tpu_custom_call" | custom-call | bytes 513536 | tf_op jit(solution)/shard_map/pallas_call | solution.py:375
  2.4 8.6 %all-gather = bf16[2,4,1536]{2,1,0:T(4,128)(2,1)S(1)} all-gather(bf16[1,4,1536]{2,1,0:T(4,128)(2,1)} %bitcast.19), channel_id=1, replica_groups=mesh['x_lo'=2,'y'=4,'z_hi'=4,'z_lo'=4,'core'=2,'x_hi'=2] {'core'}, dimensions={0}, use_global_device_ids=true | all-gather | bytes 36864 | tf_op jit(solution)/shard_map/all_gather | solution.py:493
  11.1 0.7 broadcast_in_dim.38
  11.7 9.5 %all-to-all-start = ((bf16[16,8,768]{2,1,0:T(8,128)(2,1)}), bf16[16,8,768]{2,1,0:T(8,128)(2,1)S(1)}, u32[]{:S(2)}, u32[]{:S(2)}) async-start(bf16[16,8,768]{2,1,0:T(8,128)(2,1)} %broadcast_in_dim.38), calls=%async_computation | async-start | bytes 393216 | tf_op jit(solution)/shard_map/all_to_all | solution.py:26
  21.3 4.7 %collective-permute-start = (f32[24,256]{1,0:T(8,128)}, f32[24,256]{1,0:T(8,128)S(1)}, u32[]{:S(2)}, u32[]{:S(2)}) collective-permute-start(f32[24,256]{1,0:T(8,128)} %get-tuple-element.33.mine.refs_4_), channel_id=1, source_target_pairs={{0,1},{1,0},{2,3},{3,2},{4,5},{5,4},{6,7},{7,6},{8,9},{9,8},{10,11... | collective-permute-start | bytes 73736 | tf_op jit(solution)/shard_map/ppermute | solution.py:30
  25.9 0.0 copy-start
  26.0 0.9 copy-done
  26.9 0.0 copy-start.2
  26.9 0.9 copy-done.2
  27.8 0.0 copy-start.4
  27.8 0.9 copy-done.4
  28.7 0.5 shard_map.131.fields
  29.2 0.0 collective-permute-done.other.refs_5_
  29.2 0.0 copy-start.6
  29.2 0.7 copy-done.6
  29.9 0.1 shard_map.132
  30.0 2.8 %collective-permute-start.1 = (bf16[448,256]{1,0:T(8,128)(2,1)S(1)}, bf16[448,256]{1,0:T(8,128)(2,1)S(1)}, u32[]{:S(2)}, u32[]{:S(2)}) collective-permute-start(bf16[448,256]{1,0:T(8,128)(2,1)S(1)} %shard_map.132), channel_id=1, source_target_pairs={{0,2},{2,0},{1,3},{3,1},{4,6},{6,4},{5,7},{7,5},{8,10},{10,8},{9,1... | collective-permute-start | bytes 688136 | tf_op jit(solution)/shard_map/ppermute | solution.py:30
  32.8 1.1 collective-permute-done.1.refs_6_
  33.9 0.3 all-to-all-done
  34.2 1.3 broadcast_in_dim.39
  35.5 0.0 copy-start.7
  35.5 5.3 %all-to-all-start.1 = ((bf16[8,128,768]{2,1,0:T(8,128)(2,1)}), bf16[8,128,768]{2,1,0:T(8,128)(2,1)S(1)}, u32[]{:S(2)}, u32[]{:S(2)}) async-start(bf16[8,128,768]{2,1,0:T(8,128)(2,1)} %broadcast_in_dim.39), calls=%async_computation.1 | async-start | bytes 3145728 | tf_op jit(solution)/shard_map/all_to_all | solution.py:26
  40.8 7.6 %collective-permute-start.2 = (bf16[896,256]{1,0:T(8,128)(2,1)S(1)}, bf16[896,256]{1,0:T(8,128)(2,1)S(1)}, u32[]{:S(2)}, u32[]{:S(2)}) collective-permute-start(bf16[896,256]{1,0:T(8,128)(2,1)S(1)} %pad_maximum_fusion), channel_id=1, source_target_pairs={{2,4},{4,2},{6,8},{8,6},{10,12},{12,10},{14,16},{16,14},{18,20},{2... | collective-permute-start | bytes 1376264 | tf_op jit(solution)/shard_map/ppermute | solution.py:37
  48.5 0.0 copy-done.10
  48.5 2.8 %collective-permute-start.3 = (bf16[128,256]{1,0:T(8,128)(2,1)S(1)}, bf16[128,256]{1,0:T(8,128)(2,1)S(1)}, u32[]{:S(2)}, u32[]{:S(2)}) collective-permute-start(bf16[128,256]{1,0:T(8,128)(2,1)S(1)} %copy-done.10), channel_id=1, source_target_pairs={{2,8},{6,12},{10,16},{14,20},{18,24},{22,28},{26,32},{30,36},{34,4... | collective-permute-start | bytes 196616 | tf_op jit(solution)/shard_map/ppermute | solution.py:43
  51.3 5.9 %collective-permute-done.3.refs_9_ = bf16[128,256]{1,0:T(8,128)(2,1)S(1)} collective-permute-done((bf16[128,256]{1,0:T(8,128)(2,1)S(1)}, bf16[128,256]{1,0:T(8,128)(2,1)S(1)}, u32[]{:S(2)}, u32[]{:S(2)}) %collective-permute-start.3) | collective-permute-done | bytes 65568 | tf_op jit(solution)/shard_map/ppermute | solution.py:43
  57.2 0.0 collective-permute-done.2.refs_7_
  57.2 1.9 %collective-permute-start.4 = (bf16[896,256]{1,0:T(8,128)(2,1)S(1)}, bf16[896,256]{1,0:T(8,128)(2,1)S(1)}, u32[]{:S(2)}, u32[]{:S(2)}) collective-permute-start(bf16[896,256]{1,0:T(8,128)(2,1)S(1)} %collective-permute-done.2.refs_7_), channel_id=1, source_target_pairs={{0,2},{2,0},{1,3},{3,1},{4,6},{6,4},{5,7},{7,5},{8,10},{10,8},{9,1... | collective-permute-start | bytes 1376264 | tf_op jit(solution)/shard_map/ppermute | solution.py:30
  59.1 1.8 %collective-permute-done.4.refs_8_ = bf16[896,256]{1,0:T(8,128)(2,1)S(1)} collective-permute-done((bf16[896,256]{1,0:T(8,128)(2,1)S(1)}, bf16[896,256]{1,0:T(8,128)(2,1)S(1)}, u32[]{:S(2)}, u32[]{:S(2)}) %collective-permute-start.4) | collective-permute-done | bytes 458784 | tf_op jit(solution)/shard_map/ppermute | solution.py:30
  60.9 0.0 all-to-all-done.1
  60.9 7.0 %collective-permute-start.5 = (bf16[1024,768]{1,0:T(8,128)(2,1)S(1)}, bf16[1024,768]{1,0:T(8,128)(2,1)S(1)}, u32[]{:S(2)}, u32[]{:S(2)}) collective-permute-start(bf16[1024,768]{1,0:T(8,128)(2,1)S(1)} %bitcast.14), channel_id=1, source_target_pairs={{0,2},{2,0},{1,3},{3,1},{4,6},{6,4},{5,7},{7,5},{8,10},{10,8},{9,1... | collective-permute-start | bytes 4718600 | tf_op jit(solution)/shard_map/ppermute | solution.py:30
  67.9 3.0 %collective-permute-done.5.refs_11_ = bf16[1024,768]{1,0:T(8,128)(2,1)S(1)} collective-permute-done((bf16[1024,768]{1,0:T(8,128)(2,1)S(1)}, bf16[1024,768]{1,0:T(8,128)(2,1)S(1)}, u32[]{:S(2)}, u32[]{:S(2)}) %collective-permute-start.5) | collective-permute-done | bytes 1572896 | tf_op jit(solution)/shard_map/ppermute | solution.py:30
  71.0 0.0 copy-done.1
  71.0 0.0 copy-done.3
  71.0 0.0 copy-done.5
  71.0 0.0 copy-done.7
  71.0 11.1 %shard_map.133 = (f32[128,256]{1,0:T(8,128)S(1)}, f32[128,256]{1,0:T(8,128)S(1)}, f32[8,256]{1,0:T(8,128)S(1)}, bf16[2,8,128,128]{3,2,1,0:T(8,128)(2,1)S(1)}, bf16[2,8,128,128]{3,2,1,0:T(8,128)(2,1)S(1)}) custom-call(s32[1]{0:T(128)} %bitcast.refs_0_, f32[1,128,256]{2,1,0:T(8,128)S(1)} %copy-done.1, f32[1,128,256]{2,1,0:T(8,128)S(1)} %copy-done.3, ...), custom_call_target="tpu_custom_call" | custom-call | flops 8053063680 | bytes 6119428 | tf_op jit(solution)/shard_map/pallas_call | solution.py:375
  82.1 2.3 %collective-permute-start.6 = (bf16[2,8,128,128]{3,2,1,0:T(8,128)(2,1)S(1)}, bf16[2,8,128,128]{3,2,1,0:T(8,128)(2,1)S(1)}, u32[]{:S(2)}, u32[]{:S(2)}) collective-permute-start(bf16[2,8,128,128]{3,2,1,0:T(8,128)(2,1)S(1)} %get-tuple-element.48), channel_id=1, source_target_pairs={{0,2},{2,0},{1,3},{3,1},{4,6},{6,4},{5,7},{7,5},{8,10},{10,8},{9,1... | collective-permute-start | bytes 1572872 | tf_op jit(solution)/shard_map/ppermute | solution.py:30
  84.4 1.5 collective-permute-done.6
  85.9 0.9 shard_map.134
  86.8 6.2 %all-to-all-start.2 = ((bf16[16,128,128]{2,1,0:T(8,128)(2,1)}), bf16[16,128,128]{2,1,0:T(8,128)(2,1)S(1)}, u32[]{:S(2)}, u32[]{:S(2)}) async-start(bf16[16,128,128]{2,1,0:T(8,128)(2,1)} %shard_map.134), calls=%async_computation.2 | async-start | bytes 1048576 | tf_op jit(solution)/shard_map/all_to_all | solution.py:435
  93.0 2.0 %collective-permute-start.7 = (f32[128,256]{1,0:T(8,128)S(1)}, f32[128,256]{1,0:T(8,128)S(1)}, u32[]{:S(2)}, u32[]{:S(2)}) collective-permute-start(f32[128,256]{1,0:T(8,128)S(1)} %get-tuple-element.49), channel_id=1, source_target_pairs={{2,4},{4,2},{6,8},{8,6},{10,12},{12,10},{14,16},{16,14},{18,20},{2... | collective-permute-start | bytes 393224 | tf_op jit(solution)/shard_map/ppermute | solution.py:37
  95.0 1.9 %collective-permute-start.8 = (f32[128,256]{1,0:T(8,128)S(1)}, f32[128,256]{1,0:T(8,128)S(1)}, u32[]{:S(2)}, u32[]{:S(2)}) collective-permute-start(f32[128,256]{1,0:T(8,128)S(1)} %get-tuple-element.49), channel_id=1, source_target_pairs={{0,2},{2,0},{1,3},{3,1},{4,6},{6,4},{5,7},{7,5},{8,10},{10,8},{9,1... | collective-permute-start | bytes 393224 | tf_op jit(solution)/shard_map/ppermute | solution.py:30
  97.0 0.0 copy-start.8
  97.0 0.0 copy-start.9
  97.0 5.0 %collective-permute-start.9 = (f32[8,256]{1,0:T(8,128)S(1)}, f32[8,256]{1,0:T(8,128)S(1)}, u32[]{:S(2)}, u32[]{:S(2)}) collective-permute-start(f32[8,256]{1,0:T(8,128)S(1)} %get-tuple-element.50), channel_id=1, source_target_pairs={{0,1},{1,0},{2,3},{3,2},{4,5},{5,4},{6,7},{7,6},{8,9},{9,8},{10,11... | collective-permute-start | bytes 24584 | tf_op jit(solution)/shard_map/ppermute | solution.py:30
  102.0 1.3 collective-permute-done.9
  103.4 0.0 collective-permute-done.7
  103.4 0.0 collective-permute-done.8
  103.4 0.4 all-to-all-done.2.parts
  103.7 0.7 shard_map.135
  104.5 3.3 %all-to-all-start.3 = ((bf16[4,128,128]{2,1,0:T(8,128)(2,1)}), bf16[4,128,128]{2,1,0:T(8,128)(2,1)S(1)}, u32[]{:S(2)}, u32[]{:S(2)}) async-start(bf16[4,128,128]{2,1,0:T(8,128)(2,1)} %shard_map.135), calls=%async_computation.3 | async-start | bytes 262144 | tf_op jit(solution)/shard_map/all_to_all | solution.py:445
  107.8 0.1 pad_add_fusion.place
  107.9 4.6 %all-to-all-done.3.parts = bf16[4,128,128]{2,1,0:T(8,128)(2,1)S(1)} async-done(((bf16[4,128,128]{2,1,0:T(8,128)(2,1)}), bf16[4,128,128]{2,1,0:T(8,128)(2,1)S(1)}, u32[]{:S(2)}, u32[]{:S(2)}) %all-to-all-start.3) | async-done | bytes 131104 | tf_op jit(solution)/shard_map/all_to_all | solution.py:445
  112.5 0.7 shard_map.136
  113.2 6.7 %all-to-all-start.4 = ((bf16[4,128,128]{2,1,0:T(8,128)(2,1)}), bf16[4,128,128]{2,1,0:T(8,128)(2,1)S(1)}, u32[]{:S(2)}, u32[]{:S(2)}) async-start(bf16[4,128,128]{2,1,0:T(8,128)(2,1)} %shard_map.136), calls=%async_computation.4 | async-start | bytes 262144 | tf_op jit(solution)/shard_map/all_to_all | solution.py:445
  120.0 12.1 %all-to-all-done.4.parts = bf16[4,128,128]{2,1,0:T(8,128)(2,1)S(1)} async-done(((bf16[4,128,128]{2,1,0:T(8,128)(2,1)}), bf16[4,128,128]{2,1,0:T(8,128)(2,1)S(1)}, u32[]{:S(2)}, u32[]{:S(2)}) %all-to-all-start.4) | async-done | bytes 131104 | tf_op jit(solution)/shard_map/all_to_all | solution.py:445
  132.1 0.7 shard_map.137
  132.8 11.5 %all-to-all-start.5 = ((bf16[32,16,128]{2,1,0:T(8,128)(2,1)}), bf16[32,16,128]{2,1,0:T(8,128)(2,1)S(1)}, u32[]{:S(2)}, u32[]{:S(2)}) async-start(bf16[32,16,128]{2,1,0:T(8,128)(2,1)} %shard_map.137), calls=%async_computation.5 | async-start | bytes 262144 | tf_op jit(solution)/shard_map/all_to_all | solution.py:456
  144.3 0.7 fusion.2
  145.0 7.0 %all-to-all-done.5.parts_ref = bf16[32,16,128]{2,1,0:T(8,128)(2,1)S(1)} async-done(((bf16[32,16,128]{2,1,0:T(8,128)(2,1)}), bf16[32,16,128]{2,1,0:T(8,128)(2,1)S(1)}, u32[]{:S(2)}, u32[]{:S(2)}) %all-to-all-start.5) | async-done | bytes 131104 | tf_op jit(solution)/shard_map/all_to_all | solution.py:456
  152.0 0.0 copy-done.8
  152.0 0.0 copy-done.9
  152.0 1.3 shard_map.138
  (9 shorter events, 0.1 us)
Async XLA Ops:
  11.7 22.5 %all-to-all-start = ((bf16[16,8,768]{2,1,0:T(8,128)(2,1)}), bf16[16,8,768]{2,1,0:T(8,128)(2,1)S(1)}, u32[]{:S(2)}, u32[]{:S(2)}) async-start(bf16[16,8,768]{2,1,0:T(8,128)(2,1)} %broadcast_in_dim.38), calls=%async_computation | async-start | bytes 393216 | tf_op jit(solution)/shard_map/all_to_all | solution.py:26
  21.3 7.9 %collective-permute-start = (f32[24,256]{1,0:T(8,128)}, f32[24,256]{1,0:T(8,128)S(1)}, u32[]{:S(2)}, u32[]{:S(2)}) collective-permute-start(f32[24,256]{1,0:T(8,128)} %get-tuple-element.33.mine.refs_4_), channel_id=1, source_target_pairs={{0,1},{1,0},{2,3},{3,2},{4,5},{5,4},{6,7},{7,6},{8,9},{9,8},{10,11... | collective-permute-start | bytes 73736 | tf_op jit(solution)/shard_map/ppermute | solution.py:30
  25.9 0.9 copy-start
  26.9 0.9 copy-start.2
  27.8 0.9 copy-start.4
  29.2 0.7 copy-start.6
  30.0 3.9 %collective-permute-start.1 = (bf16[448,256]{1,0:T(8,128)(2,1)S(1)}, bf16[448,256]{1,0:T(8,128)(2,1)S(1)}, u32[]{:S(2)}, u32[]{:S(2)}) collective-permute-start(bf16[448,256]{1,0:T(8,128)(2,1)S(1)} %shard_map.132), channel_id=1, source_target_pairs={{0,2},{2,0},{1,3},{3,1},{4,6},{6,4},{5,7},{7,5},{8,10},{10,8},{9,1... | collective-permute-start | bytes 688136 | tf_op jit(solution)/shard_map/ppermute | solution.py:30
  35.5 13.0 %copy-start.10 = (bf16[128,256]{1,0:T(8,128)(2,1)S(1)}, bf16[128,256]{1,0:T(8,128)(2,1)}, u32[]{:S(2)}) copy-start(bf16[128,256]{1,0:T(8,128)(2,1)} %get-tuple-element.40) | copy-start | bytes 196612
  35.5 35.4 %copy-start.1 = (f32[1,128,256]{2,1,0:T(8,128)S(1)}, f32[1,128,256]{2,1,0:T(8,128)}, u32[]{:S(2)}) copy-start(f32[1,128,256]{2,1,0:T(8,128)} %refs_1_.4) | copy-start | bytes 393220
  35.5 35.4 %copy-start.3 = (f32[1,128,256]{2,1,0:T(8,128)S(1)}, f32[1,128,256]{2,1,0:T(8,128)}, u32[]{:S(2)}) copy-start(f32[1,128,256]{2,1,0:T(8,128)} %refs_2_.4) | copy-start | bytes 393220
  35.5 35.4 %copy-start.5 = (f32[1,128,256]{2,1,0:T(8,128)S(1)}, f32[1,128,256]{2,1,0:T(8,128)}, u32[]{:S(2)}) copy-start(f32[1,128,256]{2,1,0:T(8,128)} %refs_3_.3) | copy-start | bytes 393220
  35.5 35.4 %copy-start.7 = (f32[24,256]{1,0:T(8,128)S(1)}, f32[24,256]{1,0:T(8,128)}, u32[]{:S(2)}) copy-start(f32[24,256]{1,0:T(8,128)} %get-tuple-element.33.mine.refs_4_) | copy-start | bytes 73732
  35.5 25.3 %all-to-all-start.1 = ((bf16[8,128,768]{2,1,0:T(8,128)(2,1)}), bf16[8,128,768]{2,1,0:T(8,128)(2,1)S(1)}, u32[]{:S(2)}, u32[]{:S(2)}) async-start(bf16[8,128,768]{2,1,0:T(8,128)(2,1)} %broadcast_in_dim.39), calls=%async_computation.1 | async-start | bytes 3145728 | tf_op jit(solution)/shard_map/all_to_all | solution.py:26
  40.8 16.3 %collective-permute-start.2 = (bf16[896,256]{1,0:T(8,128)(2,1)S(1)}, bf16[896,256]{1,0:T(8,128)(2,1)S(1)}, u32[]{:S(2)}, u32[]{:S(2)}) collective-permute-start(bf16[896,256]{1,0:T(8,128)(2,1)S(1)} %pad_maximum_fusion), channel_id=1, source_target_pairs={{2,4},{4,2},{6,8},{8,6},{10,12},{12,10},{14,16},{16,14},{18,20},{2... | collective-permute-start | bytes 1376264 | tf_op jit(solution)/shard_map/ppermute | solution.py:37
  48.5 8.7 %collective-permute-start.3 = (bf16[128,256]{1,0:T(8,128)(2,1)S(1)}, bf16[128,256]{1,0:T(8,128)(2,1)S(1)}, u32[]{:S(2)}, u32[]{:S(2)}) collective-permute-start(bf16[128,256]{1,0:T(8,128)(2,1)S(1)} %copy-done.10), channel_id=1, source_target_pairs={{2,8},{6,12},{10,16},{14,20},{18,24},{22,28},{26,32},{30,36},{34,4... | collective-permute-start | bytes 196616 | tf_op jit(solution)/shard_map/ppermute | solution.py:43
  57.2 3.7 %collective-permute-start.4 = (bf16[896,256]{1,0:T(8,128)(2,1)S(1)}, bf16[896,256]{1,0:T(8,128)(2,1)S(1)}, u32[]{:S(2)}, u32[]{:S(2)}) collective-permute-start(bf16[896,256]{1,0:T(8,128)(2,1)S(1)} %collective-permute-done.2.refs_7_), channel_id=1, source_target_pairs={{0,2},{2,0},{1,3},{3,1},{4,6},{6,4},{5,7},{7,5},{8,10},{10,8},{9,1... | collective-permute-start | bytes 1376264 | tf_op jit(solution)/shard_map/ppermute | solution.py:30
  60.9 10.1 %collective-permute-start.5 = (bf16[1024,768]{1,0:T(8,128)(2,1)S(1)}, bf16[1024,768]{1,0:T(8,128)(2,1)S(1)}, u32[]{:S(2)}, u32[]{:S(2)}) collective-permute-start(bf16[1024,768]{1,0:T(8,128)(2,1)S(1)} %bitcast.14), channel_id=1, source_target_pairs={{0,2},{2,0},{1,3},{3,1},{4,6},{6,4},{5,7},{7,5},{8,10},{10,8},{9,1... | collective-permute-start | bytes 4718600 | tf_op jit(solution)/shard_map/ppermute | solution.py:30
  82.1 3.8 %collective-permute-start.6 = (bf16[2,8,128,128]{3,2,1,0:T(8,128)(2,1)S(1)}, bf16[2,8,128,128]{3,2,1,0:T(8,128)(2,1)S(1)}, u32[]{:S(2)}, u32[]{:S(2)}) collective-permute-start(bf16[2,8,128,128]{3,2,1,0:T(8,128)(2,1)S(1)} %get-tuple-element.48), channel_id=1, source_target_pairs={{0,2},{2,0},{1,3},{3,1},{4,6},{6,4},{5,7},{7,5},{8,10},{10,8},{9,1... | collective-permute-start | bytes 1572872 | tf_op jit(solution)/shard_map/ppermute | solution.py:30
  86.8 16.9 %all-to-all-start.2 = ((bf16[16,128,128]{2,1,0:T(8,128)(2,1)}), bf16[16,128,128]{2,1,0:T(8,128)(2,1)S(1)}, u32[]{:S(2)}, u32[]{:S(2)}) async-start(bf16[16,128,128]{2,1,0:T(8,128)(2,1)} %shard_map.134), calls=%async_computation.2 | async-start | bytes 1048576 | tf_op jit(solution)/shard_map/all_to_all | solution.py:435
  93.0 10.4 %collective-permute-start.7 = (f32[128,256]{1,0:T(8,128)S(1)}, f32[128,256]{1,0:T(8,128)S(1)}, u32[]{:S(2)}, u32[]{:S(2)}) collective-permute-start(f32[128,256]{1,0:T(8,128)S(1)} %get-tuple-element.49), channel_id=1, source_target_pairs={{2,4},{4,2},{6,8},{8,6},{10,12},{12,10},{14,16},{16,14},{18,20},{2... | collective-permute-start | bytes 393224 | tf_op jit(solution)/shard_map/ppermute | solution.py:37
  95.0 8.3 %collective-permute-start.8 = (f32[128,256]{1,0:T(8,128)S(1)}, f32[128,256]{1,0:T(8,128)S(1)}, u32[]{:S(2)}, u32[]{:S(2)}) collective-permute-start(f32[128,256]{1,0:T(8,128)S(1)} %get-tuple-element.49), channel_id=1, source_target_pairs={{0,2},{2,0},{1,3},{3,1},{4,6},{6,4},{5,7},{7,5},{8,10},{10,8},{9,1... | collective-permute-start | bytes 393224 | tf_op jit(solution)/shard_map/ppermute | solution.py:30
  97.0 55.0 %copy-start.8 = (f32[4,256]{1,0:T(4,128)S(1)}, f32[4,256]{1,0:T(4,128)}, u32[]{:S(2)}) copy-start(f32[4,256]{1,0:T(4,128)} %w_in.1) | copy-start | bytes 12292
  97.0 55.0 %copy-start.9 = (f32[4,256]{1,0:T(4,128)S(1)}, f32[4,256]{1,0:T(4,128)}, u32[]{:S(2)}) copy-start(f32[4,256]{1,0:T(4,128)} %w_out.1) | copy-start | bytes 12292
  97.0 6.4 %collective-permute-start.9 = (f32[8,256]{1,0:T(8,128)S(1)}, f32[8,256]{1,0:T(8,128)S(1)}, u32[]{:S(2)}, u32[]{:S(2)}) collective-permute-start(f32[8,256]{1,0:T(8,128)S(1)} %get-tuple-element.50), channel_id=1, source_target_pairs={{0,1},{1,0},{2,3},{3,2},{4,5},{5,4},{6,7},{7,6},{8,9},{9,8},{10,11... | collective-permute-start | bytes 24584 | tf_op jit(solution)/shard_map/ppermute | solution.py:30
  104.5 8.1 %all-to-all-start.3 = ((bf16[4,128,128]{2,1,0:T(8,128)(2,1)}), bf16[4,128,128]{2,1,0:T(8,128)(2,1)S(1)}, u32[]{:S(2)}, u32[]{:S(2)}) async-start(bf16[4,128,128]{2,1,0:T(8,128)(2,1)} %shard_map.135), calls=%async_computation.3 | async-start | bytes 262144 | tf_op jit(solution)/shard_map/all_to_all | solution.py:445
  113.2 18.9 %all-to-all-start.4 = ((bf16[4,128,128]{2,1,0:T(8,128)(2,1)}), bf16[4,128,128]{2,1,0:T(8,128)(2,1)S(1)}, u32[]{:S(2)}, u32[]{:S(2)}) async-start(bf16[4,128,128]{2,1,0:T(8,128)(2,1)} %shard_map.136), calls=%async_computation.4 | async-start | bytes 262144 | tf_op jit(solution)/shard_map/all_to_all | solution.py:445
  132.8 19.2 %all-to-all-start.5 = ((bf16[32,16,128]{2,1,0:T(8,128)(2,1)}), bf16[32,16,128]{2,1,0:T(8,128)(2,1)S(1)}, u32[]{:S(2)}, u32[]{:S(2)}) async-start(bf16[32,16,128]{2,1,0:T(8,128)(2,1)} %shard_map.137), calls=%async_computation.5 | async-start | bytes 262144 | tf_op jit(solution)/shard_map/all_to_all | solution.py:456

commit v10 on v9

--- a/solution.py
+++ b/solution.py
@@ -423,7 +423,7 @@
     )
 
 
-def updated(kept, given, w_in, w_out, arriving):
+def updated(kept, given, w_in, w_out, arriving, later):
     halves, blocks, rows, columns = kept.shape
     peers = halves * blocks
     (grads,) = on_chip(
@@ -443,6 +443,8 @@
             grads.size,
         )
         grads = lax.all_to_all(copies, axis, 0, 0)
+        if axis == "z_lo":
+            grads, later = lax.optimization_barrier((grads, later))
     peers *= lax.axis_size("core")
     depth = rows // lax.axis_size(Z)
     (copies,) = on_chip(
@@ -463,7 +465,7 @@
         parts.size,
         scalars=1,
     )
-    return new_in, new_out, arriving
+    return new_in, new_out, arriving, later
 
 
 def local(
@@ -533,12 +535,11 @@
             rest[0].at[1 - numbers[0][0]],
         ],
     )
-    arriving = (
-        swapped_between_chips(spreading),
-        swapped(spreading, "core"),
-        swapped(ends, "x_hi"),
-    )
-    w_in_new, w_out_new, (far, near, ends) = updated(kept, given, w_in, w_out, arriving)
+    w_in_new, w_out_new, ends, spreading = updated(
+        kept, given, w_in, w_out, swapped(ends, "x_hi"), spreading
+    )
+    far = swapped_between_chips(spreading)
+    near = swapped(spreading, "core")
     east = jnp.concatenate([spreading[1:], ends[:1]])
     west = jnp.concatenate([ends[-1:], spreading[:-1]])
     adjoint = settled + (far + near + east + west)

time: 154 us -> 151 us (0.981)
  waiting for transfers between devices: 39.1 us -> 34.4 us
    all_to_all x2, waiting for transfers between devices: 16.8 us -> 8.2 us  [updated(): grads = lax.all_to_all(copies, axis, 0, 0)]
    ppermute x2, starting transfers between devices: 9.68 us -> 14.3 us  [swapped_between_chips(): return lax.ppermute(array, TILE, pairs)]
    ppermute x7, waiting for transfers between devices: 8.73 us -> 11.6 us  [swapped(): return lax.ppermute(array, axis, [(0, 1), (1, 0)])]
    all_to_all x1, starting transfers between devices: 11.5 us -> 8.67 us  [updated(): parts = lax.all_to_all(copies, AROUND, 0, 0)]
  transfers between devices with their start and end apart: 16 -> 16, of which waited for: 11 -> 11; matrix products, arithmetic and copies ran while one was open for 1% -> 1% of each run, Pallas kernels for 0% -> 1%
where the time goes in v10:
time: 151 us; the launch traced here: 150 us
  starting transfers between devices  82 us (54%)
  waiting for transfers between devices  34.4 us (23%)
  Pallas kernels  17.8 us (12%)
  blocking collectives  8.58 us (6%)
  local copies, waits for them, and re-layouts  5.49 us (4%)
    ppermute x7, starting transfers between devices, swapped(): return lax.ppermute(array, axis, [(0, 1), (1, 0)])  25.4 us
    pallas_call x9, Pallas kernels, on_chip(): pl.pallas_call(body, out_shape=outs, in_specs=[pl.BlockSpec(memory_space=...  17.8 us
    all_to_all x2, starting transfers between devices, spread(): lax.all_to_all(jnp.broadcast_to(block[None], (count,) + block.shape), axi...  14.8 us
    ppermute x2, starting transfers between devices, swapped_between_chips(): return lax.ppermute(array, TILE, pairs)  14.3 us
    ppermute x7, waiting for transfers between devices, swapped(): return lax.ppermute(array, axis, [(0, 1), (1, 0)])  11.6 us
    all_to_all x2, starting transfers between devices, updated(): grads = lax.all_to_all(copies, axis, 0, 0)  9.91 us
    all_to_all x1, starting transfers between devices, updated(): parts = lax.all_to_all(copies, AROUND, 0, 0)  8.67 us
    all_gather x1, blocking collectives, local(): rows = lax.all_gather(rows, 'core', axis=0, tiled=True)  8.58 us
  transfers between devices with their start and end apart: 16, of which 11 were waited for; matrix products, arithmetic and copies ran while one was open for 1% of the time, Pallas kernels for 1%

profile of v10, /device:TPU:1, one launch (start us, length us, event | category | flops | bytes accessed | tf_op | source)
XLA Modules:
  0.0 150.1 jit_solution(1245448257207069384)
XLA Ops:
  0.6 1.8 %shard_map.130 = (bf16[4,1536]{1,0:T(4,128)(2,1)}, f32[24,256]{1,0:T(8,128)}, bf16[128,256]{1,0:T(8,128)(2,1)}) custom-call(f32[1,128,256]{2,1,0:T(8,128)} %refs_1_.4, f32[1,128,256]{2,1,0:T(8,128)} %refs_2_.4, f32[1,128,256]{2,1,0:T(8,128)} %refs_3_.3, s32[1,128]{1,0:T(1,128)} %refs_3_.2, s32[1,64]{1,0:T(1,128)} %bitcast.20, s32[1,64]{1,0:T(1,128)} %bitcast.21, ...), custom_call_target="tpu_custom_call" | custom-call | bytes 513536 | tf_op jit(solution)/shard_map/pallas_call | solution.py:375
  2.4 8.6 %all-gather = bf16[2,4,1536]{2,1,0:T(4,128)(2,1)S(1)} all-gather(bf16[1,4,1536]{2,1,0:T(4,128)(2,1)} %bitcast.19), channel_id=1, replica_groups=mesh['x_lo'=2,'y'=4,'z_hi'=4,'z_lo'=4,'core'=2,'x_hi'=2] {'core'}, dimensions={0}, use_global_device_ids=true | all-gather | bytes 36864 | tf_op jit(solution)/shard_map/all_gather | solution.py:495
  11.1 0.7 broadcast_in_dim.38
  11.7 9.5 %all-to-all-start = ((bf16[16,8,768]{2,1,0:T(8,128)(2,1)}), bf16[16,8,768]{2,1,0:T(8,128)(2,1)S(1)}, u32[]{:S(2)}, u32[]{:S(2)}) async-start(bf16[16,8,768]{2,1,0:T(8,128)(2,1)} %broadcast_in_dim.38), calls=%async_computation | async-start | bytes 393216 | tf_op jit(solution)/shard_map/all_to_all | solution.py:26
  21.3 4.7 %collective-permute-start = (f32[24,256]{1,0:T(8,128)}, f32[24,256]{1,0:T(8,128)S(1)}, u32[]{:S(2)}, u32[]{:S(2)}) collective-permute-start(f32[24,256]{1,0:T(8,128)} %get-tuple-element.33.mine.refs_4_), channel_id=1, source_target_pairs={{0,1},{1,0},{2,3},{3,2},{4,5},{5,4},{6,7},{7,6},{8,9},{9,8},{10,11... | collective-permute-start | bytes 73736 | tf_op jit(solution)/shard_map/ppermute | solution.py:30
  25.9 0.0 copy-start
  26.0 0.9 copy-done
  26.9 0.0 copy-start.2
  26.9 0.9 copy-done.2
  27.8 0.0 copy-start.4
  27.8 0.9 copy-done.4
  28.7 0.5 shard_map.131.fields
  29.2 0.0 collective-permute-done.other.refs_5_
  29.2 0.0 copy-start.6
  29.2 0.7 copy-done.6
  29.9 0.1 shard_map.132
  30.0 2.8 %collective-permute-start.1 = (bf16[448,256]{1,0:T(8,128)(2,1)S(1)}, bf16[448,256]{1,0:T(8,128)(2,1)S(1)}, u32[]{:S(2)}, u32[]{:S(2)}) collective-permute-start(bf16[448,256]{1,0:T(8,128)(2,1)S(1)} %shard_map.132), channel_id=1, source_target_pairs={{0,2},{2,0},{1,3},{3,1},{4,6},{6,4},{5,7},{7,5},{8,10},{10,8},{9,1... | collective-permute-start | bytes 688136 | tf_op jit(solution)/shard_map/ppermute | solution.py:30
  32.8 1.1 collective-permute-done.1.refs_6_
  33.9 0.3 all-to-all-done
  34.2 1.3 broadcast_in_dim.39
  35.5 0.0 copy-start.7
  35.5 5.3 %all-to-all-start.1 = ((bf16[8,128,768]{2,1,0:T(8,128)(2,1)}), bf16[8,128,768]{2,1,0:T(8,128)(2,1)S(1)}, u32[]{:S(2)}, u32[]{:S(2)}) async-start(bf16[8,128,768]{2,1,0:T(8,128)(2,1)} %broadcast_in_dim.39), calls=%async_computation.1 | async-start | bytes 3145728 | tf_op jit(solution)/shard_map/all_to_all | solution.py:26
  40.8 7.6 %collective-permute-start.2 = (bf16[896,256]{1,0:T(8,128)(2,1)S(1)}, bf16[896,256]{1,0:T(8,128)(2,1)S(1)}, u32[]{:S(2)}, u32[]{:S(2)}) collective-permute-start(bf16[896,256]{1,0:T(8,128)(2,1)S(1)} %pad_maximum_fusion), channel_id=1, source_target_pairs={{2,4},{4,2},{6,8},{8,6},{10,12},{12,10},{14,16},{16,14},{18,20},{2... | collective-permute-start | bytes 1376264 | tf_op jit(solution)/shard_map/ppermute | solution.py:37
  48.5 0.0 copy-done.10
  48.5 2.8 %collective-permute-start.3 = (bf16[128,256]{1,0:T(8,128)(2,1)S(1)}, bf16[128,256]{1,0:T(8,128)(2,1)S(1)}, u32[]{:S(2)}, u32[]{:S(2)}) collective-permute-start(bf16[128,256]{1,0:T(8,128)(2,1)S(1)} %copy-done.10), channel_id=1, source_target_pairs={{2,8},{6,12},{10,16},{14,20},{18,24},{22,28},{26,32},{30,36},{34,4... | collective-permute-start | bytes 196616 | tf_op jit(solution)/shard_map/ppermute | solution.py:43
  51.3 5.9 %collective-permute-done.3.refs_9_ = bf16[128,256]{1,0:T(8,128)(2,1)S(1)} collective-permute-done((bf16[128,256]{1,0:T(8,128)(2,1)S(1)}, bf16[128,256]{1,0:T(8,128)(2,1)S(1)}, u32[]{:S(2)}, u32[]{:S(2)}) %collective-permute-start.3) | collective-permute-done | bytes 65568 | tf_op jit(solution)/shard_map/ppermute | solution.py:43
  57.2 0.0 collective-permute-done.2.refs_7_
  57.2 1.9 %collective-permute-start.4 = (bf16[896,256]{1,0:T(8,128)(2,1)S(1)}, bf16[896,256]{1,0:T(8,128)(2,1)S(1)}, u32[]{:S(2)}, u32[]{:S(2)}) collective-permute-start(bf16[896,256]{1,0:T(8,128)(2,1)S(1)} %collective-permute-done.2.refs_7_), channel_id=1, source_target_pairs={{0,2},{2,0},{1,3},{3,1},{4,6},{6,4},{5,7},{7,5},{8,10},{10,8},{9,1... | collective-permute-start | bytes 1376264 | tf_op jit(solution)/shard_map/ppermute | solution.py:30
  59.1 1.8 %collective-permute-done.4.refs_8_ = bf16[896,256]{1,0:T(8,128)(2,1)S(1)} collective-permute-done((bf16[896,256]{1,0:T(8,128)(2,1)S(1)}, bf16[896,256]{1,0:T(8,128)(2,1)S(1)}, u32[]{:S(2)}, u32[]{:S(2)}) %collective-permute-start.4) | collective-permute-done | bytes 458784 | tf_op jit(solution)/shard_map/ppermute | solution.py:30
  60.9 0.0 all-to-all-done.1
  60.9 7.0 %collective-permute-start.5 = (bf16[1024,768]{1,0:T(8,128)(2,1)S(1)}, bf16[1024,768]{1,0:T(8,128)(2,1)S(1)}, u32[]{:S(2)}, u32[]{:S(2)}) collective-permute-start(bf16[1024,768]{1,0:T(8,128)(2,1)S(1)} %bitcast.14), channel_id=1, source_target_pairs={{0,2},{2,0},{1,3},{3,1},{4,6},{6,4},{5,7},{7,5},{8,10},{10,8},{9,1... | collective-permute-start | bytes 4718600 | tf_op jit(solution)/shard_map/ppermute | solution.py:30
  67.9 3.0 %collective-permute-done.5.refs_11_ = bf16[1024,768]{1,0:T(8,128)(2,1)S(1)} collective-permute-done((bf16[1024,768]{1,0:T(8,128)(2,1)S(1)}, bf16[1024,768]{1,0:T(8,128)(2,1)S(1)}, u32[]{:S(2)}, u32[]{:S(2)}) %collective-permute-start.5) | collective-permute-done | bytes 1572896 | tf_op jit(solution)/shard_map/ppermute | solution.py:30
  71.0 0.0 copy-done.1
  71.0 0.0 copy-done.3
  71.0 0.0 copy-done.5
  71.0 0.0 copy-done.7
  71.0 11.1 %shard_map.133 = (f32[128,256]{1,0:T(8,128)S(1)}, f32[128,256]{1,0:T(8,128)S(1)}, f32[8,256]{1,0:T(8,128)S(1)}, bf16[2,8,128,128]{3,2,1,0:T(8,128)(2,1)S(1)}, bf16[2,8,128,128]{3,2,1,0:T(8,128)(2,1)S(1)}) custom-call(s32[1]{0:T(128)} %bitcast.refs_0_, f32[1,128,256]{2,1,0:T(8,128)S(1)} %copy-done.1, f32[1,128,256]{2,1,0:T(8,128)S(1)} %copy-done.3, ...), custom_call_target="tpu_custom_call" | custom-call | flops 8053063680 | bytes 6119428 | tf_op jit(solution)/shard_map/pallas_call | solution.py:375
  82.1 2.3 %collective-permute-start.6 = (bf16[2,8,128,128]{3,2,1,0:T(8,128)(2,1)S(1)}, bf16[2,8,128,128]{3,2,1,0:T(8,128)(2,1)S(1)}, u32[]{:S(2)}, u32[]{:S(2)}) collective-permute-start(bf16[2,8,128,128]{3,2,1,0:T(8,128)(2,1)S(1)} %get-tuple-element.48), channel_id=1, source_target_pairs={{0,2},{2,0},{1,3},{3,1},{4,6},{6,4},{5,7},{7,5},{8,10},{10,8},{9,1... | collective-permute-start | bytes 1572872 | tf_op jit(solution)/shard_map/ppermute | solution.py:30
  84.4 1.5 %collective-permute-done.6 = bf16[2,8,128,128]{3,2,1,0:T(8,128)(2,1)S(1)} collective-permute-done((bf16[2,8,128,128]{3,2,1,0:T(8,128)(2,1)S(1)}, bf16[2,8,128,128]{3,2,1,0:T(8,128)(2,1)S(1)}, u32[]{:S(2)}, u32[]{:S(2)}) %collective-permute-start.6) | collective-permute-done | bytes 524320 | tf_op jit(solution)/shard_map/ppermute | solution.py:30
  85.9 0.9 shard_map.134
  86.8 6.2 %all-to-all-start.2 = ((bf16[16,128,128]{2,1,0:T(8,128)(2,1)}), bf16[16,128,128]{2,1,0:T(8,128)(2,1)S(1)}, u32[]{:S(2)}, u32[]{:S(2)}) async-start(bf16[16,128,128]{2,1,0:T(8,128)(2,1)} %shard_map.134), calls=%async_computation.2 | async-start | bytes 1048576 | tf_op jit(solution)/shard_map/all_to_all | solution.py:435
  93.0 0.0 copy-start.8
  93.0 0.0 copy-start.9
  93.0 4.8 %collective-permute-start.7 = (f32[8,256]{1,0:T(8,128)S(1)}, f32[8,256]{1,0:T(8,128)S(1)}, u32[]{:S(2)}, u32[]{:S(2)}) collective-permute-start(f32[8,256]{1,0:T(8,128)S(1)} %get-tuple-element.49), channel_id=1, source_target_pairs={{0,1},{1,0},{2,3},{3,2},{4,5},{5,4},{6,7},{7,6},{8,9},{9,8},{10,11... | collective-permute-start | bytes 24584 | tf_op jit(solution)/shard_map/ppermute | solution.py:30
  97.8 4.2 %collective-permute-done.7 = f32[8,256]{1,0:T(8,128)S(1)} collective-permute-done((f32[8,256]{1,0:T(8,128)S(1)}, f32[8,256]{1,0:T(8,128)S(1)}, u32[]{:S(2)}, u32[]{:S(2)}) %collective-permute-start.7) | collective-permute-done | bytes 8224 | tf_op jit(solution)/shard_map/ppermute | solution.py:30
  102.0 1.3 all-to-all-done.2.parts
  103.3 0.7 shard_map.135
  104.1 3.3 %all-to-all-start.3 = ((bf16[4,128,128]{2,1,0:T(8,128)(2,1)}), bf16[4,128,128]{2,1,0:T(8,128)(2,1)S(1)}, u32[]{:S(2)}, u32[]{:S(2)}) async-start(bf16[4,128,128]{2,1,0:T(8,128)(2,1)} %shard_map.135), calls=%async_computation.3 | async-start | bytes 262144 | tf_op jit(solution)/shard_map/all_to_all | solution.py:445
  107.4 0.1 pad_add_fusion.place
  107.5 4.6 %all-to-all-done.3.parts = bf16[4,128,128]{2,1,0:T(8,128)(2,1)S(1)} async-done(((bf16[4,128,128]{2,1,0:T(8,128)(2,1)}), bf16[4,128,128]{2,1,0:T(8,128)(2,1)S(1)}, u32[]{:S(2)}, u32[]{:S(2)}) %all-to-all-start.3) | async-done | bytes 131104 | tf_op jit(solution)/shard_map/all_to_all | solution.py:445
  112.2 0.7 shard_map.136
  112.8 6.6 %all-to-all-start.4 = ((bf16[4,128,128]{2,1,0:T(8,128)(2,1)}), bf16[4,128,128]{2,1,0:T(8,128)(2,1)S(1)}, u32[]{:S(2)}, u32[]{:S(2)}) async-start(bf16[4,128,128]{2,1,0:T(8,128)(2,1)} %shard_map.136), calls=%async_computation.4 | async-start | bytes 262144 | tf_op jit(solution)/shard_map/all_to_all | solution.py:445
  119.4 6.7 %collective-permute-start.8 = (f32[128,256]{1,0:T(8,128)S(1)}, f32[128,256]{1,0:T(8,128)S(1)}, u32[]{:S(2)}, u32[]{:S(2)}) collective-permute-start(f32[128,256]{1,0:T(8,128)S(1)} %get-tuple-element.52), channel_id=1, source_target_pairs={{2,4},{4,2},{6,8},{8,6},{10,12},{12,10},{14,16},{16,14},{18,20},{2... | collective-permute-start | bytes 393224 | tf_op jit(solution)/shard_map/ppermute | solution.py:37
  126.1 1.9 %collective-permute-start.9 = (f32[128,256]{1,0:T(8,128)S(1)}, f32[128,256]{1,0:T(8,128)S(1)}, u32[]{:S(2)}, u32[]{:S(2)}) collective-permute-start(f32[128,256]{1,0:T(8,128)S(1)} %get-tuple-element.52), channel_id=1, source_target_pairs={{0,2},{2,0},{1,3},{3,1},{4,6},{6,4},{5,7},{7,5},{8,10},{10,8},{9,1... | collective-permute-start | bytes 393224 | tf_op jit(solution)/shard_map/ppermute | solution.py:30
  128.1 3.5 %all-to-all-done.4.parts = bf16[4,128,128]{2,1,0:T(8,128)(2,1)S(1)} async-done(((bf16[4,128,128]{2,1,0:T(8,128)(2,1)}), bf16[4,128,128]{2,1,0:T(8,128)(2,1)S(1)}, u32[]{:S(2)}, u32[]{:S(2)}) %all-to-all-start.4) | async-done | bytes 131104 | tf_op jit(solution)/shard_map/all_to_all | solution.py:445
  131.6 0.7 shard_map.137
  132.3 8.7 %all-to-all-start.5 = ((bf16[32,16,128]{2,1,0:T(8,128)(2,1)}), bf16[32,16,128]{2,1,0:T(8,128)(2,1)S(1)}, u32[]{:S(2)}, u32[]{:S(2)}) async-start(bf16[32,16,128]{2,1,0:T(8,128)(2,1)} %shard_map.137), calls=%async_computation.5 | async-start | bytes 262144 | tf_op jit(solution)/shard_map/all_to_all | solution.py:458
  141.0 0.0 collective-permute-done.8
  141.0 0.0 collective-permute-done.9
  141.0 0.7 fusion.2
  141.7 7.1 %all-to-all-done.5.parts_ref = bf16[32,16,128]{2,1,0:T(8,128)(2,1)S(1)} async-done(((bf16[32,16,128]{2,1,0:T(8,128)(2,1)}), bf16[32,16,128]{2,1,0:T(8,128)(2,1)S(1)}, u32[]{:S(2)}, u32[]{:S(2)}) %all-to-all-start.5) | async-done | bytes 131104 | tf_op jit(solution)/shard_map/all_to_all | solution.py:458
  148.8 0.0 copy-done.8
  148.8 0.0 copy-done.9
  148.8 1.3 shard_map.138
  (9 shorter events, 0.1 us)
Async XLA Ops:
  11.7 22.5 %all-to-all-start = ((bf16[16,8,768]{2,1,0:T(8,128)(2,1)}), bf16[16,8,768]{2,1,0:T(8,128)(2,1)S(1)}, u32[]{:S(2)}, u32[]{:S(2)}) async-start(bf16[16,8,768]{2,1,0:T(8,128)(2,1)} %broadcast_in_dim.38), calls=%async_computation | async-start | bytes 393216 | tf_op jit(solution)/shard_map/all_to_all | solution.py:26
  21.3 7.9 %collective-permute-start = (f32[24,256]{1,0:T(8,128)}, f32[24,256]{1,0:T(8,128)S(1)}, u32[]{:S(2)}, u32[]{:S(2)}) collective-permute-start(f32[24,256]{1,0:T(8,128)} %get-tuple-element.33.mine.refs_4_), channel_id=1, source_target_pairs={{0,1},{1,0},{2,3},{3,2},{4,5},{5,4},{6,7},{7,6},{8,9},{9,8},{10,11... | collective-permute-start | bytes 73736 | tf_op jit(solution)/shard_map/ppermute | solution.py:30
  25.9 0.9 copy-start
  26.9 0.9 copy-start.2
  27.8 0.9 copy-start.4
  29.2 0.7 copy-start.6
  30.0 3.9 %collective-permute-start.1 = (bf16[448,256]{1,0:T(8,128)(2,1)S(1)}, bf16[448,256]{1,0:T(8,128)(2,1)S(1)}, u32[]{:S(2)}, u32[]{:S(2)}) collective-permute-start(bf16[448,256]{1,0:T(8,128)(2,1)S(1)} %shard_map.132), channel_id=1, source_target_pairs={{0,2},{2,0},{1,3},{3,1},{4,6},{6,4},{5,7},{7,5},{8,10},{10,8},{9,1... | collective-permute-start | bytes 688136 | tf_op jit(solution)/shard_map/ppermute | solution.py:30
  35.5 13.0 %copy-start.10 = (bf16[128,256]{1,0:T(8,128)(2,1)S(1)}, bf16[128,256]{1,0:T(8,128)(2,1)}, u32[]{:S(2)}) copy-start(bf16[128,256]{1,0:T(8,128)(2,1)} %get-tuple-element.40) | copy-start | bytes 196612
  35.5 35.4 %copy-start.1 = (f32[1,128,256]{2,1,0:T(8,128)S(1)}, f32[1,128,256]{2,1,0:T(8,128)}, u32[]{:S(2)}) copy-start(f32[1,128,256]{2,1,0:T(8,128)} %refs_1_.4) | copy-start | bytes 393220
  35.5 35.4 %copy-start.3 = (f32[1,128,256]{2,1,0:T(8,128)S(1)}, f32[1,128,256]{2,1,0:T(8,128)}, u32[]{:S(2)}) copy-start(f32[1,128,256]{2,1,0:T(8,128)} %refs_2_.4) | copy-start | bytes 393220
  35.5 35.4 %copy-start.5 = (f32[1,128,256]{2,1,0:T(8,128)S(1)}, f32[1,128,256]{2,1,0:T(8,128)}, u32[]{:S(2)}) copy-start(f32[1,128,256]{2,1,0:T(8,128)} %refs_3_.3) | copy-start | bytes 393220
  35.5 35.4 %copy-start.7 = (f32[24,256]{1,0:T(8,128)S(1)}, f32[24,256]{1,0:T(8,128)}, u32[]{:S(2)}) copy-start(f32[24,256]{1,0:T(8,128)} %get-tuple-element.33.mine.refs_4_) | copy-start | bytes 73732
  35.5 25.3 %all-to-all-start.1 = ((bf16[8,128,768]{2,1,0:T(8,128)(2,1)}), bf16[8,128,768]{2,1,0:T(8,128)(2,1)S(1)}, u32[]{:S(2)}, u32[]{:S(2)}) async-start(bf16[8,128,768]{2,1,0:T(8,128)(2,1)} %broadcast_in_dim.39), calls=%async_computation.1 | async-start | bytes 3145728 | tf_op jit(solution)/shard_map/all_to_all | solution.py:26
  40.8 16.3 %collective-permute-start.2 = (bf16[896,256]{1,0:T(8,128)(2,1)S(1)}, bf16[896,256]{1,0:T(8,128)(2,1)S(1)}, u32[]{:S(2)}, u32[]{:S(2)}) collective-permute-start(bf16[896,256]{1,0:T(8,128)(2,1)S(1)} %pad_maximum_fusion), channel_id=1, source_target_pairs={{2,4},{4,2},{6,8},{8,6},{10,12},{12,10},{14,16},{16,14},{18,20},{2... | collective-permute-start | bytes 1376264 | tf_op jit(solution)/shard_map/ppermute | solution.py:37
  48.5 8.7 %collective-permute-start.3 = (bf16[128,256]{1,0:T(8,128)(2,1)S(1)}, bf16[128,256]{1,0:T(8,128)(2,1)S(1)}, u32[]{:S(2)}, u32[]{:S(2)}) collective-permute-start(bf16[128,256]{1,0:T(8,128)(2,1)S(1)} %copy-done.10), channel_id=1, source_target_pairs={{2,8},{6,12},{10,16},{14,20},{18,24},{22,28},{26,32},{30,36},{34,4... | collective-permute-start | bytes 196616 | tf_op jit(solution)/shard_map/ppermute | solution.py:43
  57.2 3.7 %collective-permute-start.4 = (bf16[896,256]{1,0:T(8,128)(2,1)S(1)}, bf16[896,256]{1,0:T(8,128)(2,1)S(1)}, u32[]{:S(2)}, u32[]{:S(2)}) collective-permute-start(bf16[896,256]{1,0:T(8,128)(2,1)S(1)} %collective-permute-done.2.refs_7_), channel_id=1, source_target_pairs={{0,2},{2,0},{1,3},{3,1},{4,6},{6,4},{5,7},{7,5},{8,10},{10,8},{9,1... | collective-permute-start | bytes 1376264 | tf_op jit(solution)/shard_map/ppermute | solution.py:30
  60.9 10.1 %collective-permute-start.5 = (bf16[1024,768]{1,0:T(8,128)(2,1)S(1)}, bf16[1024,768]{1,0:T(8,128)(2,1)S(1)}, u32[]{:S(2)}, u32[]{:S(2)}) collective-permute-start(bf16[1024,768]{1,0:T(8,128)(2,1)S(1)} %bitcast.14), channel_id=1, source_target_pairs={{0,2},{2,0},{1,3},{3,1},{4,6},{6,4},{5,7},{7,5},{8,10},{10,8},{9,1... | collective-permute-start | bytes 4718600 | tf_op jit(solution)/shard_map/ppermute | solution.py:30
  82.1 3.8 %collective-permute-start.6 = (bf16[2,8,128,128]{3,2,1,0:T(8,128)(2,1)S(1)}, bf16[2,8,128,128]{3,2,1,0:T(8,128)(2,1)S(1)}, u32[]{:S(2)}, u32[]{:S(2)}) collective-permute-start(bf16[2,8,128,128]{3,2,1,0:T(8,128)(2,1)S(1)} %get-tuple-element.48), channel_id=1, source_target_pairs={{0,2},{2,0},{1,3},{3,1},{4,6},{6,4},{5,7},{7,5},{8,10},{10,8},{9,1... | collective-permute-start | bytes 1572872 | tf_op jit(solution)/shard_map/ppermute | solution.py:30
  86.8 16.5 %all-to-all-start.2 = ((bf16[16,128,128]{2,1,0:T(8,128)(2,1)}), bf16[16,128,128]{2,1,0:T(8,128)(2,1)S(1)}, u32[]{:S(2)}, u32[]{:S(2)}) async-start(bf16[16,128,128]{2,1,0:T(8,128)(2,1)} %shard_map.134), calls=%async_computation.2 | async-start | bytes 1048576 | tf_op jit(solution)/shard_map/all_to_all | solution.py:435
  93.0 55.8 %copy-start.8 = (f32[4,256]{1,0:T(4,128)S(1)}, f32[4,256]{1,0:T(4,128)}, u32[]{:S(2)}) copy-start(f32[4,256]{1,0:T(4,128)} %w_in.1) | copy-start | bytes 12292
  93.0 55.8 %copy-start.9 = (f32[4,256]{1,0:T(4,128)S(1)}, f32[4,256]{1,0:T(4,128)}, u32[]{:S(2)}) copy-start(f32[4,256]{1,0:T(4,128)} %w_out.1) | copy-start | bytes 12292
  93.0 9.0 %collective-permute-start.7 = (f32[8,256]{1,0:T(8,128)S(1)}, f32[8,256]{1,0:T(8,128)S(1)}, u32[]{:S(2)}, u32[]{:S(2)}) collective-permute-start(f32[8,256]{1,0:T(8,128)S(1)} %get-tuple-element.49), channel_id=1, source_target_pairs={{0,1},{1,0},{2,3},{3,2},{4,5},{5,4},{6,7},{7,6},{8,9},{9,8},{10,11... | collective-permute-start | bytes 24584 | tf_op jit(solution)/shard_map/ppermute | solution.py:30
  104.1 8.1 %all-to-all-start.3 = ((bf16[4,128,128]{2,1,0:T(8,128)(2,1)}), bf16[4,128,128]{2,1,0:T(8,128)(2,1)S(1)}, u32[]{:S(2)}, u32[]{:S(2)}) async-start(bf16[4,128,128]{2,1,0:T(8,128)(2,1)} %shard_map.135), calls=%async_computation.3 | async-start | bytes 262144 | tf_op jit(solution)/shard_map/all_to_all | solution.py:445
  112.8 18.8 %all-to-all-start.4 = ((bf16[4,128,128]{2,1,0:T(8,128)(2,1)}), bf16[4,128,128]{2,1,0:T(8,128)(2,1)S(1)}, u32[]{:S(2)}, u32[]{:S(2)}) async-start(bf16[4,128,128]{2,1,0:T(8,128)(2,1)} %shard_map.136), calls=%async_computation.4 | async-start | bytes 262144 | tf_op jit(solution)/shard_map/all_to_all | solution.py:445
  119.4 21.6 %collective-permute-start.8 = (f32[128,256]{1,0:T(8,128)S(1)}, f32[128,256]{1,0:T(8,128)S(1)}, u32[]{:S(2)}, u32[]{:S(2)}) collective-permute-start(f32[128,256]{1,0:T(8,128)S(1)} %get-tuple-element.52), channel_id=1, source_target_pairs={{2,4},{4,2},{6,8},{8,6},{10,12},{12,10},{14,16},{16,14},{18,20},{2... | collective-permute-start | bytes 393224 | tf_op jit(solution)/shard_map/ppermute | solution.py:37
  126.1 14.9 %collective-permute-start.9 = (f32[128,256]{1,0:T(8,128)S(1)}, f32[128,256]{1,0:T(8,128)S(1)}, u32[]{:S(2)}, u32[]{:S(2)}) collective-permute-start(f32[128,256]{1,0:T(8,128)S(1)} %get-tuple-element.52), channel_id=1, source_target_pairs={{0,2},{2,0},{1,3},{3,1},{4,6},{6,4},{5,7},{7,5},{8,10},{10,8},{9,1... | collective-permute-start | bytes 393224 | tf_op jit(solution)/shard_map/ppermute | solution.py:30
  132.3 16.5 %all-to-all-start.5 = ((bf16[32,16,128]{2,1,0:T(8,128)(2,1)}), bf16[32,16,128]{2,1,0:T(8,128)(2,1)S(1)}, u32[]{:S(2)}, u32[]{:S(2)}) async-start(bf16[32,16,128]{2,1,0:T(8,128)(2,1)} %shard_map.137), calls=%async_computation.5 | async-start | bytes 262144 | tf_op jit(solution)/shard_map/all_to_all | solution.py:458

commit v11 on v10

--- a/solution.py
+++ b/solution.py
@@ -146,6 +146,14 @@
     pack[3 * BLOCK :] = jnp.concatenate(rest).astype(jnp.bfloat16)
 
 
+def behind_kernel(far, behind):
+    pack = 3 * BLOCK + 16
+    behind[:pack] = far[:pack]
+    total = far[pack : pack + BLOCK].astype(jnp.float32)
+    total = total + far[pack + BLOCK : pack + 2 * BLOCK].astype(jnp.float32)
+    behind[pack:] = total.astype(jnp.bfloat16)
+
+
 def whole_kernel(
     observations,
     core,
@@ -237,9 +245,8 @@
     own.append(gate)
     beside, beside_rest = zip(unpack(near, 0), unpack(far, 0))
     second = [unpack(beyond, 0)[0], unpack(far, pack)[0]]
-    third = [unpack(beyond, pack)[0]]
     third = [
-        third[0][0] + third[0][1],
+        beyond[pack : pack + BLOCK].astype(jnp.float32)[:length],
         jnp.concatenate(
             [outer[...].astype(jnp.float32), jnp.zeros((length - cells, features), jnp.float32)]
         ),
@@ -503,11 +510,15 @@
     (packs,) = on_chip(pack_fields_kernel, packed, fields, 0, fetched=3)
     (own,) = on_chip(pack_edges_kernel, packed, (packs, mine, other), 0)
     near = swapped(own, "core")
+    far = swapped_between_chips(jnp.concatenate([own, near]))
     half, near = lax.optimization_barrier((half, near))
     half = spread(half, ("x_lo", "y")).reshape(-1, width)
-    far = swapped_between_chips(jnp.concatenate([own, near]))
     far, outer = lax.optimization_barrier((far, outer))
-    beyond = swapped(far, "core")
+    pack = 3 * BLOCK + 16
+    (beyond,) = on_chip(
+        behind_kernel, outs(((pack + BLOCK, features), jnp.bfloat16)), (far,), 10**10
+    )
+    beyond = swapped(beyond, "core")
     half, far, beyond = lax.optimization_barrier((half, far, beyond))
     hidden_units = half.shape[0]
     blocks = lax.axis_size(("x_lo", "y"))

time: 151 us -> 153 us (1.013)
  waiting for transfers between devices: 34.4 us -> 39 us
  starting transfers between devices: 82 us -> 78.8 us
    all_to_all x2, waiting for transfers between devices: 0.32 us -> 7.85 us  [spread(): lax.all_to_all(jnp.broadcast_to(block[None], (count,) + block.shape), axi...]
    ppermute x2, starting transfers between devices: 14.3 us -> 10.2 us  [swapped_between_chips(): return lax.ppermute(array, TILE, pairs)]
    ppermute x7, starting transfers between devices: 25.4 us -> 21.4 us  [swapped(): return lax.ppermute(array, axis, [(0, 1), (1, 0)])]
    all_to_all x2, starting transfers between devices: 9.91 us -> 13 us  [updated(): grads = lax.all_to_all(copies, axis, 0, 0)]
    ppermute x1, starting transfers between devices: 2.76 us -> 5.83 us  [swapped_three_apart(): lax.ppermute(array, TILE, pairs + [(after, row) for row, after in pairs])]
    ppermute x1, waiting for transfers between devices: 5.91 us -> 2.93 us  [swapped_three_apart(): lax.ppermute(array, TILE, pairs + [(after, row) for row, after in pairs])]
    pallas_call x9 -> x10, Pallas kernels: 17.8 us -> 17.9 us  [on_chip(): pl.pallas_call(body, out_shape=outs, in_specs=[pl.BlockSpec(memory_space=...]
where the time goes in v11:
time: 153 us; the launch traced here: 151 us
  starting transfers between devices  78.8 us (52%)
  waiting for transfers between devices  39 us (25%)
  Pallas kernels  17.9 us (12%)
  blocking collectives  8.58 us (6%)
  local copies, waits for them, and re-layouts  5.49 us (4%)
    ppermute x7, starting transfers between devices, swapped(): return lax.ppermute(array, axis, [(0, 1), (1, 0)])  21.4 us
    pallas_call x10, Pallas kernels, on_chip(): pl.pallas_call(body, out_shape=outs, in_specs=[pl.BlockSpec(memory_space=...  17.9 us
    all_to_all x2, starting transfers between devices, spread(): lax.all_to_all(jnp.broadcast_to(block[None], (count,) + block.shape), axi...  14 us
    all_to_all x2, starting transfers between devices, updated(): grads = lax.all_to_all(copies, axis, 0, 0)  13 us
    ppermute x7, waiting for transfers between devices, swapped(): return lax.ppermute(array, axis, [(0, 1), (1, 0)])  11.4 us
    ppermute x2, starting transfers between devices, swapped_between_chips(): return lax.ppermute(array, TILE, pairs)  10.2 us
    all_to_all x1, starting transfers between devices, updated(): parts = lax.all_to_all(copies, AROUND, 0, 0)  8.59 us
    all_gather x1, blocking collectives, local(): rows = lax.all_gather(rows, 'core', axis=0, tiled=True)  8.58 us
  transfers between devices with their start and end apart: 16, of which 11 were waited for; matrix products, arithmetic and copies ran while one was open for 1% of the time, Pallas kernels for 1%

profile of v11, /device:TPU:1, one launch (start us, length us, event | category | flops | bytes accessed | tf_op | source)
XLA Modules:
  0.0 151.4 jit_solution(1651782038511599939)
XLA Ops:
  0.6 1.8 %shard_map.130 = (bf16[4,1536]{1,0:T(4,128)(2,1)}, f32[24,256]{1,0:T(8,128)}, bf16[128,256]{1,0:T(8,128)(2,1)}) custom-call(f32[1,128,256]{2,1,0:T(8,128)} %refs_1_.4, f32[1,128,256]{2,1,0:T(8,128)} %refs_2_.4, f32[1,128,256]{2,1,0:T(8,128)} %refs_3_.3, s32[1,128]{1,0:T(1,128)} %refs_3_.2, s32[1,64]{1,0:T(1,128)} %bitcast.20, s32[1,64]{1,0:T(1,128)} %bitcast.21, ...), custom_call_target="tpu_custom_call" | custom-call | bytes 513536 | tf_op jit(solution)/shard_map/pallas_call | solution.py:382
  2.4 8.6 %all-gather = bf16[2,4,1536]{2,1,0:T(4,128)(2,1)S(1)} all-gather(bf16[1,4,1536]{2,1,0:T(4,128)(2,1)} %bitcast.19), channel_id=1, replica_groups=mesh['x_lo'=2,'y'=4,'z_hi'=4,'z_lo'=4,'core'=2,'x_hi'=2] {'core'}, dimensions={0}, use_global_device_ids=true | all-gather | bytes 36864 | tf_op jit(solution)/shard_map/all_gather | solution.py:502
  11.1 0.7 broadcast_in_dim.38
  11.7 9.5 %all-to-all-start = ((bf16[16,8,768]{2,1,0:T(8,128)(2,1)}), bf16[16,8,768]{2,1,0:T(8,128)(2,1)S(1)}, u32[]{:S(2)}, u32[]{:S(2)}) async-start(bf16[16,8,768]{2,1,0:T(8,128)(2,1)} %broadcast_in_dim.38), calls=%async_computation | async-start | bytes 393216 | tf_op jit(solution)/shard_map/all_to_all | solution.py:26
  21.3 4.7 %collective-permute-start = (f32[24,256]{1,0:T(8,128)}, f32[24,256]{1,0:T(8,128)S(1)}, u32[]{:S(2)}, u32[]{:S(2)}) collective-permute-start(f32[24,256]{1,0:T(8,128)} %get-tuple-element.33.mine.refs_4_), channel_id=1, source_target_pairs={{0,1},{1,0},{2,3},{3,2},{4,5},{5,4},{6,7},{7,6},{8,9},{9,8},{10,11... | collective-permute-start | bytes 73736 | tf_op jit(solution)/shard_map/ppermute | solution.py:30
  25.9 0.0 copy-start
  26.0 0.9 copy-done
  26.9 0.9 copy-done.2
  27.8 0.9 copy-done.4
  28.7 0.5 shard_map.131.fields
  29.2 0.0 collective-permute-done.other.refs_5_
  29.2 0.0 copy-start.6
  29.2 0.7 copy-done.6
  29.9 0.1 shard_map.132
  30.0 2.8 %collective-permute-start.1 = (bf16[448,256]{1,0:T(8,128)(2,1)S(1)}, bf16[448,256]{1,0:T(8,128)(2,1)S(1)}, u32[]{:S(2)}, u32[]{:S(2)}) collective-permute-start(bf16[448,256]{1,0:T(8,128)(2,1)S(1)} %shard_map.132), channel_id=1, source_target_pairs={{0,2},{2,0},{1,3},{3,1},{4,6},{6,4},{5,7},{7,5},{8,10},{10,8},{9,1... | collective-permute-start | bytes 688136 | tf_op jit(solution)/shard_map/ppermute | solution.py:30
  32.8 1.1 collective-permute-done.1.refs_6_
  34.0 3.8 %collective-permute-start.2 = (bf16[896,256]{1,0:T(8,128)(2,1)S(1)}, bf16[896,256]{1,0:T(8,128)(2,1)S(1)}, u32[]{:S(2)}, u32[]{:S(2)}) collective-permute-start(bf16[896,256]{1,0:T(8,128)(2,1)S(1)} %pad_maximum_fusion), channel_id=1, source_target_pairs={{2,4},{4,2},{6,8},{8,6},{10,12},{12,10},{14,16},{16,14},{18,20},{2... | collective-permute-start | bytes 1376264 | tf_op jit(solution)/shard_map/ppermute | solution.py:37
  37.8 0.0 all-to-all-done
  37.8 1.3 broadcast_in_dim.39
  39.1 4.5 %all-to-all-start.1 = ((bf16[8,128,768]{2,1,0:T(8,128)(2,1)}), bf16[8,128,768]{2,1,0:T(8,128)(2,1)S(1)}, u32[]{:S(2)}, u32[]{:S(2)}) async-start(bf16[8,128,768]{2,1,0:T(8,128)(2,1)} %broadcast_in_dim.39), calls=%async_computation.1 | async-start | bytes 3145728 | tf_op jit(solution)/shard_map/all_to_all | solution.py:26
  43.6 0.0 copy-done.10
  43.6 0.0 copy-start.1
  43.6 0.0 copy-start.3
  43.6 0.0 copy-start.5
  43.6 0.0 copy-start.7
  43.6 5.8 %collective-permute-start.3 = (bf16[128,256]{1,0:T(8,128)(2,1)S(1)}, bf16[128,256]{1,0:T(8,128)(2,1)S(1)}, u32[]{:S(2)}, u32[]{:S(2)}) collective-permute-start(bf16[128,256]{1,0:T(8,128)(2,1)S(1)} %copy-done.10), channel_id=1, source_target_pairs={{2,8},{6,12},{10,16},{14,20},{18,24},{22,28},{26,32},{30,36},{34,4... | collective-permute-start | bytes 196616 | tf_op jit(solution)/shard_map/ppermute | solution.py:43
  49.5 2.9 %collective-permute-done.3.refs_9_ = bf16[128,256]{1,0:T(8,128)(2,1)S(1)} collective-permute-done((bf16[128,256]{1,0:T(8,128)(2,1)S(1)}, bf16[128,256]{1,0:T(8,128)(2,1)S(1)}, u32[]{:S(2)}, u32[]{:S(2)}) %collective-permute-start.3) | collective-permute-done | bytes 65568 | tf_op jit(solution)/shard_map/ppermute | solution.py:43
  52.4 0.0 collective-permute-done.2.far.refs_7_
  52.4 1.9 %collective-permute-start.4 = (bf16[592,256]{1,0:T(8,128)(2,1)S(1)}, bf16[592,256]{1,0:T(8,128)(2,1)S(1)}, u32[]{:S(2)}, u32[]{:S(2)}) collective-permute-start(bf16[592,256]{1,0:T(8,128)(2,1)S(1)} %shard_map.133), channel_id=1, source_target_pairs={{0,2},{2,0},{1,3},{3,1},{4,6},{6,4},{5,7},{7,5},{8,10},{10,8},{9,1... | collective-permute-start | bytes 909320 | tf_op jit(solution)/shard_map/ppermute | solution.py:30
  54.4 1.6 %collective-permute-done.4.refs_8_ = bf16[592,256]{1,0:T(8,128)(2,1)S(1)} collective-permute-done((bf16[592,256]{1,0:T(8,128)(2,1)S(1)}, bf16[592,256]{1,0:T(8,128)(2,1)S(1)}, u32[]{:S(2)}, u32[]{:S(2)}) %collective-permute-start.4) | collective-permute-done | bytes 303136 | tf_op jit(solution)/shard_map/ppermute | solution.py:30
  55.9 7.8 %all-to-all-done.1 = bf16[8,128,768]{2,1,0:T(8,128)(2,1)S(1)} async-done(((bf16[8,128,768]{2,1,0:T(8,128)(2,1)}), bf16[8,128,768]{2,1,0:T(8,128)(2,1)S(1)}, u32[]{:S(2)}, u32[]{:S(2)}) %all-to-all-start.1) | async-done | bytes 1572896 | tf_op jit(solution)/shard_map/all_to_all | solution.py:26
  63.8 3.1 %collective-permute-start.5 = (bf16[1024,768]{1,0:T(8,128)(2,1)S(1)}, bf16[1024,768]{1,0:T(8,128)(2,1)S(1)}, u32[]{:S(2)}, u32[]{:S(2)}) collective-permute-start(bf16[1024,768]{1,0:T(8,128)(2,1)S(1)} %bitcast.14), channel_id=1, source_target_pairs={{0,2},{2,0},{1,3},{3,1},{4,6},{6,4},{5,7},{7,5},{8,10},{10,8},{9,1... | collective-permute-start | bytes 4718600 | tf_op jit(solution)/shard_map/ppermute | solution.py:30
  66.8 3.0 %collective-permute-done.5.refs_11_ = bf16[1024,768]{1,0:T(8,128)(2,1)S(1)} collective-permute-done((bf16[1024,768]{1,0:T(8,128)(2,1)S(1)}, bf16[1024,768]{1,0:T(8,128)(2,1)S(1)}, u32[]{:S(2)}, u32[]{:S(2)}) %collective-permute-start.5) | collective-permute-done | bytes 1572896 | tf_op jit(solution)/shard_map/ppermute | solution.py:30
  69.8 0.0 copy-done.1
  69.9 0.0 copy-done.3
  69.9 0.0 copy-done.5
  69.9 0.0 copy-done.7
  69.9 11.1 %shard_map.134 = (f32[128,256]{1,0:T(8,128)S(1)}, f32[128,256]{1,0:T(8,128)S(1)}, f32[8,256]{1,0:T(8,128)S(1)}, bf16[2,8,128,128]{3,2,1,0:T(8,128)(2,1)S(1)}, bf16[2,8,128,128]{3,2,1,0:T(8,128)(2,1)S(1)}) custom-call(s32[1]{0:T(128)} %bitcast.refs_0_, f32[1,128,256]{2,1,0:T(8,128)S(1)} %copy-done.1, f32[1,128,256]{2,1,0:T(8,128)S(1)} %copy-done.3, ...), custom_call_target="tpu_custom_call" | custom-call | flops 8053063680 | bytes 5963780 | tf_op jit(solution)/shard_map/pallas_call | solution.py:382
  81.0 2.3 %collective-permute-start.6 = (bf16[2,8,128,128]{3,2,1,0:T(8,128)(2,1)S(1)}, bf16[2,8,128,128]{3,2,1,0:T(8,128)(2,1)S(1)}, u32[]{:S(2)}, u32[]{:S(2)}) collective-permute-start(bf16[2,8,128,128]{3,2,1,0:T(8,128)(2,1)S(1)} %get-tuple-element.48), channel_id=1, source_target_pairs={{0,2},{2,0},{1,3},{3,1},{4,6},{6,4},{5,7},{7,5},{8,10},{10,8},{9,1... | collective-permute-start | bytes 1572872 | tf_op jit(solution)/shard_map/ppermute | solution.py:30
  83.3 1.5 %collective-permute-done.6 = bf16[2,8,128,128]{3,2,1,0:T(8,128)(2,1)S(1)} collective-permute-done((bf16[2,8,128,128]{3,2,1,0:T(8,128)(2,1)S(1)}, bf16[2,8,128,128]{3,2,1,0:T(8,128)(2,1)S(1)}, u32[]{:S(2)}, u32[]{:S(2)}) %collective-permute-start.6) | collective-permute-done | bytes 524320 | tf_op jit(solution)/shard_map/ppermute | solution.py:30
  84.8 0.9 shard_map.135
  85.7 5.7 %all-to-all-start.2 = ((bf16[16,128,128]{2,1,0:T(8,128)(2,1)}), bf16[16,128,128]{2,1,0:T(8,128)(2,1)S(1)}, u32[]{:S(2)}, u32[]{:S(2)}) async-start(bf16[16,128,128]{2,1,0:T(8,128)(2,1)} %shard_map.135), calls=%async_computation.2 | async-start | bytes 1048576 | tf_op jit(solution)/shard_map/all_to_all | solution.py:442
  91.4 0.0 copy-start.8
  91.5 0.0 copy-start.9
  91.5 4.8 %collective-permute-start.7 = (f32[8,256]{1,0:T(8,128)S(1)}, f32[8,256]{1,0:T(8,128)S(1)}, u32[]{:S(2)}, u32[]{:S(2)}) collective-permute-start(f32[8,256]{1,0:T(8,128)S(1)} %get-tuple-element.49), channel_id=1, source_target_pairs={{0,1},{1,0},{2,3},{3,2},{4,5},{5,4},{6,7},{7,6},{8,9},{9,8},{10,11... | collective-permute-start | bytes 24584 | tf_op jit(solution)/shard_map/ppermute | solution.py:30
  96.3 4.2 %collective-permute-done.7 = f32[8,256]{1,0:T(8,128)S(1)} collective-permute-done((f32[8,256]{1,0:T(8,128)S(1)}, f32[8,256]{1,0:T(8,128)S(1)}, u32[]{:S(2)}, u32[]{:S(2)}) %collective-permute-start.7) | collective-permute-done | bytes 8224 | tf_op jit(solution)/shard_map/ppermute | solution.py:30
  100.4 1.3 all-to-all-done.2.parts
  101.8 0.7 shard_map.136
  102.5 4.9 %all-to-all-start.3 = ((bf16[4,128,128]{2,1,0:T(8,128)(2,1)}), bf16[4,128,128]{2,1,0:T(8,128)(2,1)S(1)}, u32[]{:S(2)}, u32[]{:S(2)}) async-start(bf16[4,128,128]{2,1,0:T(8,128)(2,1)} %shard_map.136), calls=%async_computation.3 | async-start | bytes 262144 | tf_op jit(solution)/shard_map/all_to_all | solution.py:452
  107.4 0.1 pad_add_fusion.place
  107.5 4.7 %all-to-all-done.3.parts = bf16[4,128,128]{2,1,0:T(8,128)(2,1)S(1)} async-done(((bf16[4,128,128]{2,1,0:T(8,128)(2,1)}), bf16[4,128,128]{2,1,0:T(8,128)(2,1)S(1)}, u32[]{:S(2)}, u32[]{:S(2)}) %all-to-all-start.3) | async-done | bytes 131104 | tf_op jit(solution)/shard_map/all_to_all | solution.py:452
  112.2 0.7 shard_map.137
  112.9 8.1 %all-to-all-start.4 = ((bf16[4,128,128]{2,1,0:T(8,128)(2,1)}), bf16[4,128,128]{2,1,0:T(8,128)(2,1)S(1)}, u32[]{:S(2)}, u32[]{:S(2)}) async-start(bf16[4,128,128]{2,1,0:T(8,128)(2,1)} %shard_map.137), calls=%async_computation.4 | async-start | bytes 262144 | tf_op jit(solution)/shard_map/all_to_all | solution.py:452
  121.0 6.4 %collective-permute-start.8 = (f32[128,256]{1,0:T(8,128)S(1)}, f32[128,256]{1,0:T(8,128)S(1)}, u32[]{:S(2)}, u32[]{:S(2)}) collective-permute-start(f32[128,256]{1,0:T(8,128)S(1)} %get-tuple-element.52), channel_id=1, source_target_pairs={{2,4},{4,2},{6,8},{8,6},{10,12},{12,10},{14,16},{16,14},{18,20},{2... | collective-permute-start | bytes 393224 | tf_op jit(solution)/shard_map/ppermute | solution.py:37
  127.4 1.9 %collective-permute-start.9 = (f32[128,256]{1,0:T(8,128)S(1)}, f32[128,256]{1,0:T(8,128)S(1)}, u32[]{:S(2)}, u32[]{:S(2)}) collective-permute-start(f32[128,256]{1,0:T(8,128)S(1)} %get-tuple-element.52), channel_id=1, source_target_pairs={{0,2},{2,0},{1,3},{3,1},{4,6},{6,4},{5,7},{7,5},{8,10},{10,8},{9,1... | collective-permute-start | bytes 393224 | tf_op jit(solution)/shard_map/ppermute | solution.py:30
  129.3 3.8 %all-to-all-done.4.parts = bf16[4,128,128]{2,1,0:T(8,128)(2,1)S(1)} async-done(((bf16[4,128,128]{2,1,0:T(8,128)(2,1)}), bf16[4,128,128]{2,1,0:T(8,128)(2,1)S(1)}, u32[]{:S(2)}, u32[]{:S(2)}) %all-to-all-start.4) | async-done | bytes 131104 | tf_op jit(solution)/shard_map/all_to_all | solution.py:452
  133.2 0.7 shard_map.138
  133.9 8.6 %all-to-all-start.5 = ((bf16[32,16,128]{2,1,0:T(8,128)(2,1)}), bf16[32,16,128]{2,1,0:T(8,128)(2,1)S(1)}, u32[]{:S(2)}, u32[]{:S(2)}) async-start(bf16[32,16,128]{2,1,0:T(8,128)(2,1)} %shard_map.138), calls=%async_computation.5 | async-start | bytes 262144 | tf_op jit(solution)/shard_map/all_to_all | solution.py:465
  142.5 0.0 collective-permute-done.8
  142.5 0.0 collective-permute-done.9
  142.5 0.7 fusion.2
  143.2 7.0 %all-to-all-done.5.parts_ref = bf16[32,16,128]{2,1,0:T(8,128)(2,1)S(1)} async-done(((bf16[32,16,128]{2,1,0:T(8,128)(2,1)}), bf16[32,16,128]{2,1,0:T(8,128)(2,1)S(1)}, u32[]{:S(2)}, u32[]{:S(2)}) %all-to-all-start.5) | async-done | bytes 131104 | tf_op jit(solution)/shard_map/all_to_all | solution.py:465
  150.2 0.0 copy-done.9
  150.2 1.3 shard_map.139
  (10 shorter events, 0.1 us)
Async XLA Ops:
  11.7 26.0 %all-to-all-start = ((bf16[16,8,768]{2,1,0:T(8,128)(2,1)}), bf16[16,8,768]{2,1,0:T(8,128)(2,1)S(1)}, u32[]{:S(2)}, u32[]{:S(2)}) async-start(bf16[16,8,768]{2,1,0:T(8,128)(2,1)} %broadcast_in_dim.38), calls=%async_computation | async-start | bytes 393216 | tf_op jit(solution)/shard_map/all_to_all | solution.py:26
  21.3 7.9 %collective-permute-start = (f32[24,256]{1,0:T(8,128)}, f32[24,256]{1,0:T(8,128)S(1)}, u32[]{:S(2)}, u32[]{:S(2)}) collective-permute-start(f32[24,256]{1,0:T(8,128)} %get-tuple-element.33.mine.refs_4_), channel_id=1, source_target_pairs={{0,1},{1,0},{2,3},{3,2},{4,5},{5,4},{6,7},{7,6},{8,9},{9,8},{10,11... | collective-permute-start | bytes 73736 | tf_op jit(solution)/shard_map/ppermute | solution.py:30
  25.9 0.9 copy-start
  26.9 0.9 copy-start.2
  27.8 0.9 copy-start.4
  29.2 0.7 copy-start.6
  30.0 3.9 %collective-permute-start.1 = (bf16[448,256]{1,0:T(8,128)(2,1)S(1)}, bf16[448,256]{1,0:T(8,128)(2,1)S(1)}, u32[]{:S(2)}, u32[]{:S(2)}) collective-permute-start(bf16[448,256]{1,0:T(8,128)(2,1)S(1)} %shard_map.132), channel_id=1, source_target_pairs={{0,2},{2,0},{1,3},{3,1},{4,6},{6,4},{5,7},{7,5},{8,10},{10,8},{9,1... | collective-permute-start | bytes 688136 | tf_op jit(solution)/shard_map/ppermute | solution.py:30
  34.0 18.4 %collective-permute-start.2 = (bf16[896,256]{1,0:T(8,128)(2,1)S(1)}, bf16[896,256]{1,0:T(8,128)(2,1)S(1)}, u32[]{:S(2)}, u32[]{:S(2)}) collective-permute-start(bf16[896,256]{1,0:T(8,128)(2,1)S(1)} %pad_maximum_fusion), channel_id=1, source_target_pairs={{2,4},{4,2},{6,8},{8,6},{10,12},{12,10},{14,16},{16,14},{18,20},{2... | collective-permute-start | bytes 1376264 | tf_op jit(solution)/shard_map/ppermute | solution.py:37
  39.1 4.5 %copy-start.10 = (bf16[128,256]{1,0:T(8,128)(2,1)S(1)}, bf16[128,256]{1,0:T(8,128)(2,1)}, u32[]{:S(2)}) copy-start(bf16[128,256]{1,0:T(8,128)(2,1)} %get-tuple-element.40) | copy-start | bytes 196612
  39.1 24.7 %all-to-all-start.1 = ((bf16[8,128,768]{2,1,0:T(8,128)(2,1)}), bf16[8,128,768]{2,1,0:T(8,128)(2,1)S(1)}, u32[]{:S(2)}, u32[]{:S(2)}) async-start(bf16[8,128,768]{2,1,0:T(8,128)(2,1)} %broadcast_in_dim.39), calls=%async_computation.1 | async-start | bytes 3145728 | tf_op jit(solution)/shard_map/all_to_all | solution.py:26
  43.6 26.3 %copy-start.1 = (f32[1,128,256]{2,1,0:T(8,128)S(1)}, f32[1,128,256]{2,1,0:T(8,128)}, u32[]{:S(2)}) copy-start(f32[1,128,256]{2,1,0:T(8,128)} %refs_1_.4) | copy-start | bytes 393220
  43.6 26.3 %copy-start.3 = (f32[1,128,256]{2,1,0:T(8,128)S(1)}, f32[1,128,256]{2,1,0:T(8,128)}, u32[]{:S(2)}) copy-start(f32[1,128,256]{2,1,0:T(8,128)} %refs_2_.4) | copy-start | bytes 393220
  43.6 26.3 %copy-start.5 = (f32[1,128,256]{2,1,0:T(8,128)S(1)}, f32[1,128,256]{2,1,0:T(8,128)}, u32[]{:S(2)}) copy-start(f32[1,128,256]{2,1,0:T(8,128)} %refs_3_.3) | copy-start | bytes 393220
  43.6 26.3 %copy-start.7 = (f32[24,256]{1,0:T(8,128)S(1)}, f32[24,256]{1,0:T(8,128)}, u32[]{:S(2)}) copy-start(f32[24,256]{1,0:T(8,128)} %get-tuple-element.33.mine.refs_4_) | copy-start | bytes 73732
  43.6 8.8 %collective-permute-start.3 = (bf16[128,256]{1,0:T(8,128)(2,1)S(1)}, bf16[128,256]{1,0:T(8,128)(2,1)S(1)}, u32[]{:S(2)}, u32[]{:S(2)}) collective-permute-start(bf16[128,256]{1,0:T(8,128)(2,1)S(1)} %copy-done.10), channel_id=1, source_target_pairs={{2,8},{6,12},{10,16},{14,20},{18,24},{22,28},{26,32},{30,36},{34,4... | collective-permute-start | bytes 196616 | tf_op jit(solution)/shard_map/ppermute | solution.py:43
  52.4 3.5 %collective-permute-start.4 = (bf16[592,256]{1,0:T(8,128)(2,1)S(1)}, bf16[592,256]{1,0:T(8,128)(2,1)S(1)}, u32[]{:S(2)}, u32[]{:S(2)}) collective-permute-start(bf16[592,256]{1,0:T(8,128)(2,1)S(1)} %shard_map.133), channel_id=1, source_target_pairs={{0,2},{2,0},{1,3},{3,1},{4,6},{6,4},{5,7},{7,5},{8,10},{10,8},{9,1... | collective-permute-start | bytes 909320 | tf_op jit(solution)/shard_map/ppermute | solution.py:30
  63.8 6.1 %collective-permute-start.5 = (bf16[1024,768]{1,0:T(8,128)(2,1)S(1)}, bf16[1024,768]{1,0:T(8,128)(2,1)S(1)}, u32[]{:S(2)}, u32[]{:S(2)}) collective-permute-start(bf16[1024,768]{1,0:T(8,128)(2,1)S(1)} %bitcast.14), channel_id=1, source_target_pairs={{0,2},{2,0},{1,3},{3,1},{4,6},{6,4},{5,7},{7,5},{8,10},{10,8},{9,1... | collective-permute-start | bytes 4718600 | tf_op jit(solution)/shard_map/ppermute | solution.py:30
  81.0 3.8 %collective-permute-start.6 = (bf16[2,8,128,128]{3,2,1,0:T(8,128)(2,1)S(1)}, bf16[2,8,128,128]{3,2,1,0:T(8,128)(2,1)S(1)}, u32[]{:S(2)}, u32[]{:S(2)}) collective-permute-start(bf16[2,8,128,128]{3,2,1,0:T(8,128)(2,1)S(1)} %get-tuple-element.48), channel_id=1, source_target_pairs={{0,2},{2,0},{1,3},{3,1},{4,6},{6,4},{5,7},{7,5},{8,10},{10,8},{9,1... | collective-permute-start | bytes 1572872 | tf_op jit(solution)/shard_map/ppermute | solution.py:30
  85.7 16.1 %all-to-all-start.2 = ((bf16[16,128,128]{2,1,0:T(8,128)(2,1)}), bf16[16,128,128]{2,1,0:T(8,128)(2,1)S(1)}, u32[]{:S(2)}, u32[]{:S(2)}) async-start(bf16[16,128,128]{2,1,0:T(8,128)(2,1)} %shard_map.135), calls=%async_computation.2 | async-start | bytes 1048576 | tf_op jit(solution)/shard_map/all_to_all | solution.py:442
  91.4 58.7 %copy-start.8 = (f32[4,256]{1,0:T(4,128)S(1)}, f32[4,256]{1,0:T(4,128)}, u32[]{:S(2)}) copy-start(f32[4,256]{1,0:T(4,128)} %w_in.1) | copy-start | bytes 12292
  91.5 58.7 %copy-start.9 = (f32[4,256]{1,0:T(4,128)S(1)}, f32[4,256]{1,0:T(4,128)}, u32[]{:S(2)}) copy-start(f32[4,256]{1,0:T(4,128)} %w_out.1) | copy-start | bytes 12292
  91.5 9.0 %collective-permute-start.7 = (f32[8,256]{1,0:T(8,128)S(1)}, f32[8,256]{1,0:T(8,128)S(1)}, u32[]{:S(2)}, u32[]{:S(2)}) collective-permute-start(f32[8,256]{1,0:T(8,128)S(1)} %get-tuple-element.49), channel_id=1, source_target_pairs={{0,1},{1,0},{2,3},{3,2},{4,5},{5,4},{6,7},{7,6},{8,9},{9,8},{10,11... | collective-permute-start | bytes 24584 | tf_op jit(solution)/shard_map/ppermute | solution.py:30
  102.5 9.7 %all-to-all-start.3 = ((bf16[4,128,128]{2,1,0:T(8,128)(2,1)}), bf16[4,128,128]{2,1,0:T(8,128)(2,1)S(1)}, u32[]{:S(2)}, u32[]{:S(2)}) async-start(bf16[4,128,128]{2,1,0:T(8,128)(2,1)} %shard_map.136), calls=%async_computation.3 | async-start | bytes 262144 | tf_op jit(solution)/shard_map/all_to_all | solution.py:452
  112.9 20.3 %all-to-all-start.4 = ((bf16[4,128,128]{2,1,0:T(8,128)(2,1)}), bf16[4,128,128]{2,1,0:T(8,128)(2,1)S(1)}, u32[]{:S(2)}, u32[]{:S(2)}) async-start(bf16[4,128,128]{2,1,0:T(8,128)(2,1)} %shard_map.137), calls=%async_computation.4 | async-start | bytes 262144 | tf_op jit(solution)/shard_map/all_to_all | solution.py:452
  121.0 21.5 %collective-permute-start.8 = (f32[128,256]{1,0:T(8,128)S(1)}, f32[128,256]{1,0:T(8,128)S(1)}, u32[]{:S(2)}, u32[]{:S(2)}) collective-permute-start(f32[128,256]{1,0:T(8,128)S(1)} %get-tuple-element.52), channel_id=1, source_target_pairs={{2,4},{4,2},{6,8},{8,6},{10,12},{12,10},{14,16},{16,14},{18,20},{2... | collective-permute-start | bytes 393224 | tf_op jit(solution)/shard_map/ppermute | solution.py:37
  127.4 15.1 %collective-permute-start.9 = (f32[128,256]{1,0:T(8,128)S(1)}, f32[128,256]{1,0:T(8,128)S(1)}, u32[]{:S(2)}, u32[]{:S(2)}) collective-permute-start(f32[128,256]{1,0:T(8,128)S(1)} %get-tuple-element.52), channel_id=1, source_target_pairs={{0,2},{2,0},{1,3},{3,1},{4,6},{6,4},{5,7},{7,5},{8,10},{10,8},{9,1... | collective-permute-start | bytes 393224 | tf_op jit(solution)/shard_map/ppermute | solution.py:30
  133.9 16.3 %all-to-all-start.5 = ((bf16[32,16,128]{2,1,0:T(8,128)(2,1)}), bf16[32,16,128]{2,1,0:T(8,128)(2,1)S(1)}, u32[]{:S(2)}, u32[]{:S(2)}) async-start(bf16[32,16,128]{2,1,0:T(8,128)(2,1)} %shard_map.138), calls=%async_computation.5 | async-start | bytes 262144 | tf_op jit(solution)/shard_map/all_to_all | solution.py:465

commit v12 on v11

--- a/solution.py
+++ b/solution.py
@@ -16,6 +16,7 @@
 FINE_SIZES = (2, 4, 4, 4, 2, 2)
 Z = ("z_hi", "z_lo")
 TILE = ("x_lo", "y", "z_hi", "z_lo", "core")
+X = ("x_lo", "x_hi")
 AROUND = ("x_hi", "x_lo", "y", "core")
 REACH = 3
 BLOCK = 144
@@ -35,6 +36,13 @@
     for row in range(1, lax.axis_size(TILE) - 1, 2):
         pairs += [(row, row + 1), (row + 1, row)]
     return lax.ppermute(array, TILE, pairs)
+
+
+def next_along_x(array, step):
+    high = lax.axis_size("x_hi")
+    places = [low * high + part for part in range(high) for low in range(lax.axis_size("x_lo"))]
+    pairs = [(place, places[(x + step) % len(places)]) for x, place in enumerate(places)]
+    return lax.ppermute(array, X, pairs)
 
 
 def swapped_three_apart(array):
@@ -508,19 +516,22 @@
     outer = swapped_three_apart(outer)
     packed = outs(((3 * BLOCK + 16, features), jnp.bfloat16))
     (packs,) = on_chip(pack_fields_kernel, packed, fields, 0, fetched=3)
+    other, outer = lax.optimization_barrier((other, outer))
     (own,) = on_chip(pack_edges_kernel, packed, (packs, mine, other), 0)
     near = swapped(own, "core")
     far = swapped_between_chips(jnp.concatenate([own, near]))
     half, near = lax.optimization_barrier((half, near))
-    half = spread(half, ("x_lo", "y")).reshape(-1, width)
-    far, outer = lax.optimization_barrier((far, outer))
+    half = spread(half, "y").reshape(-1, width)
+    middle = half.shape[0] // 2
+    parts = [half, next_along_x(half[:middle], 1), next_along_x(half[middle:], -1)]
     pack = 3 * BLOCK + 16
     (beyond,) = on_chip(
-        behind_kernel, outs(((pack + BLOCK, features), jnp.bfloat16)), (far,), 10**10
+        behind_kernel, outs(((pack + BLOCK, features), jnp.bfloat16)), (far,), far.size
     )
     beyond = swapped(beyond, "core")
-    half, far, beyond = lax.optimization_barrier((half, far, beyond))
-    hidden_units = half.shape[0]
+    parts[1], far, beyond = lax.optimization_barrier((parts[1], far, beyond))
+    hidden_units = 4 * middle
+    parts += [swapped(part, "core") for part in parts]
     blocks = lax.axis_size(("x_lo", "y"))
     halves = lax.axis_size("x_hi")
     part = ((halves, blocks, hidden_units // blocks, features // halves), jnp.bfloat16)
@@ -534,16 +545,21 @@
             part,
             part,
         ),
-        (lax.axis_index("core")[None], state, increment, diffusivity, mine, other, near, far, beyond, outer)
-        + (half, swapped(half, "core")),
+        (jnp.stack([lax.axis_index("core"), lax.axis_index("x_lo")]), state, increment, diffusivity, mine, other, near, far, beyond, outer)
+        + tuple(parts),
         40 * cells * hidden_units * (2 * features + hidden_units),
         scratch=(pltpu.VMEM((2, hidden_units, width), jnp.bfloat16),),
         scalars=1,
         direct=9,
         fetched=0,
         place=lambda numbers, rest: [
-            rest[0].at[numbers[0][0]],
-            rest[0].at[1 - numbers[0][0]],
+            rest[0].at[side, pl.ds(pl.multiple_of(start, middle), size)]
+            for side in (numbers[0][0], 1 - numbers[0][0])
+            for start, size in (
+                (numbers[0][1] * 2 * middle, 2 * middle),
+                ((1 - numbers[0][1]) * 2 * middle, middle),
+                ((1 - numbers[0][1]) * 2 * middle + middle, middle),
+            )
         ],
     )
     w_in_new, w_out_new, ends, spreading = updated(

time: 153 us -> 160 us (1.046)
  starting transfers between devices: 78.8 us -> 91.2 us
  waiting for transfers between devices: 39 us -> 33.2 us
  local copies, waits for them, and re-layouts: 5.49 us -> 3.44 us
  Pallas kernels: 17.9 us -> 19.7 us
    ppermute x0 -> x2, starting transfers between devices: none -> 15.4 us  [next_along_x(): return lax.ppermute(array, X, pairs)]
    ppermute x7 -> x9, starting transfers between devices: 21.4 us -> 28.8 us  [swapped(): return lax.ppermute(array, axis, [(0, 1), (1, 0)])]
    all_to_all x2, starting transfers between devices: 13 us -> 7.11 us  [updated(): grads = lax.all_to_all(copies, axis, 0, 0)]
    all_to_all x2, waiting for transfers between devices: 7.85 us -> 3.23 us  [spread(): lax.all_to_all(jnp.broadcast_to(block[None], (count,) + block.shape), axi...]
    pallas_call x10, Pallas kernels: 17.9 us -> 19.7 us  [on_chip(): pl.pallas_call(body, out_shape=outs, in_specs=[pl.BlockSpec(memory_space=...]
    all_to_all x1, starting transfers between devices: 5.72 us -> 3.87 us  [updated(): grads = lax.all_to_all(grads, AROUND[:-1], 0, 0)]
    unnamed x23 -> x19, local copies, waits for them, and re-layouts: 3.49 us -> 1.72 us
    ppermute x2, starting transfers between devices: 10.2 us -> 8.5 us  [swapped_between_chips(): return lax.ppermute(array, TILE, pairs)]
  transfers between devices with their start and end apart: 16 -> 20, of which waited for: 11 -> 12; matrix products, arithmetic and copies ran while one was open for 1% -> 1% of each run, Pallas kernels for 1% -> 1%
where the time goes in v12:
time: 160 us; the launch traced here: 159 us
  starting transfers between devices  91.2 us (57%)
  waiting for transfers between devices  33.2 us (21%)
  Pallas kernels  19.7 us (12%)
  blocking collectives  8.58 us (5%)
  local copies, waits for them, and re-layouts  3.44 us (2%)
  other arithmetic  1.67 us (1%)
    ppermute x9, starting transfers between devices, swapped(): return lax.ppermute(array, axis, [(0, 1), (1, 0)])  28.8 us
    pallas_call x10, Pallas kernels, on_chip(): pl.pallas_call(body, out_shape=outs, in_specs=[pl.BlockSpec(memory_space=...  19.7 us
    ppermute x2, starting transfers between devices, next_along_x(): return lax.ppermute(array, X, pairs)  15.4 us
    all_to_all x2, starting transfers between devices, spread(): lax.all_to_all(jnp.broadcast_to(block[None], (count,) + block.shape), axi...  13.9 us
    ppermute x9, waiting for transfers between devices, swapped(): return lax.ppermute(array, axis, [(0, 1), (1, 0)])  11.8 us
    all_to_all x1, starting transfers between devices, updated(): parts = lax.all_to_all(copies, AROUND, 0, 0)  8.73 us
    all_gather x1, blocking collectives, local(): rows = lax.all_gather(rows, 'core', axis=0, tiled=True)  8.58 us
    ppermute x2, starting transfers between devices, swapped_between_chips(): return lax.ppermute(array, TILE, pairs)  8.5 us
  transfers between devices with their start and end apart: 20, of which 12 were waited for; matrix products, arithmetic and copies ran while one was open for 1% of the time, Pallas kernels for 1%

profile of v12, /device:TPU:1, one launch (start us, length us, event | category | flops | bytes accessed | tf_op | source)
XLA Modules:
  0.0 158.8 jit_solution(9511465371113069071)
XLA Ops:
  0.6 1.8 %shard_map.130 = (bf16[4,1536]{1,0:T(4,128)(2,1)}, f32[24,256]{1,0:T(8,128)}, bf16[128,256]{1,0:T(8,128)(2,1)}) custom-call(f32[1,128,256]{2,1,0:T(8,128)} %refs_1_.4, f32[1,128,256]{2,1,0:T(8,128)} %refs_2_.4, f32[1,128,256]{2,1,0:T(8,128)} %refs_3_.3, s32[1,128]{1,0:T(1,128)} %refs_3_.2, s32[1,64]{1,0:T(1,128)} %bitcast.25, s32[1,64]{1,0:T(1,128)} %bitcast.26, ...), custom_call_target="tpu_custom_call" | custom-call | bytes 513536 | tf_op jit(solution)/shard_map/pallas_call | solution.py:390
  2.4 8.6 %all-gather = bf16[2,4,1536]{2,1,0:T(4,128)(2,1)S(1)} all-gather(bf16[1,4,1536]{2,1,0:T(4,128)(2,1)} %bitcast.24), channel_id=1, replica_groups=mesh['x_lo'=2,'y'=4,'z_hi'=4,'z_lo'=4,'core'=2,'x_hi'=2] {'core'}, dimensions={0}, use_global_device_ids=true | all-gather | bytes 36864 | tf_op jit(solution)/shard_map/all_gather | solution.py:510
  11.1 0.0 copy-start.8
  11.1 0.7 broadcast_in_dim.34
  11.8 9.7 %all-to-all-start = ((bf16[16,8,768]{2,1,0:T(8,128)(2,1)}), bf16[16,8,768]{2,1,0:T(8,128)(2,1)S(1)}, u32[]{:S(2)}, u32[]{:S(2)}) async-start(bf16[16,8,768]{2,1,0:T(8,128)(2,1)} %broadcast_in_dim.34), calls=%async_computation | async-start | bytes 393216 | tf_op jit(solution)/shard_map/all_to_all | solution.py:27
  21.5 0.0 copy-done.8
  21.5 4.9 %collective-permute-start.1 = (bf16[128,256]{1,0:T(8,128)(2,1)S(1)}, bf16[128,256]{1,0:T(8,128)(2,1)S(1)}, u32[]{:S(2)}, u32[]{:S(2)}) collective-permute-start(bf16[128,256]{1,0:T(8,128)(2,1)S(1)} %copy-done.8), channel_id=1, source_target_pairs={{2,8},{6,12},{10,16},{14,20},{18,24},{22,28},{26,32},{30,36},{34,4... | collective-permute-start | bytes 196616 | tf_op jit(solution)/shard_map/ppermute | solution.py:51
  26.4 4.7 %collective-permute-start = (f32[24,256]{1,0:T(8,128)S(1)}, f32[24,256]{1,0:T(8,128)S(1)}, u32[]{:S(2)}, u32[]{:S(2)}) collective-permute-start(f32[24,256]{1,0:T(8,128)S(1)} %copy-done.3), channel_id=1, source_target_pairs={{0,1},{1,0},{2,3},{3,2},{4,5},{5,4},{6,7},{7,6},{8,9},{9,8},{10,11... | collective-permute-start | bytes 73736 | tf_op jit(solution)/shard_map/ppermute | solution.py:31
  31.1 0.6 shard_map.131.fields
  31.7 0.9 collective-permute-done.other.refs_5_
  32.6 1.6 %collective-permute-done.1.refs_9_ = bf16[128,256]{1,0:T(8,128)(2,1)S(1)} collective-permute-done((bf16[128,256]{1,0:T(8,128)(2,1)S(1)}, bf16[128,256]{1,0:T(8,128)(2,1)S(1)}, u32[]{:S(2)}, u32[]{:S(2)}) %collective-permute-start.1) | collective-permute-done | bytes 65568 | tf_op jit(solution)/shard_map/ppermute | solution.py:51
  34.2 0.1 shard_map.132
  34.3 1.9 %collective-permute-start.2 = (bf16[448,256]{1,0:T(8,128)(2,1)S(1)}, bf16[448,256]{1,0:T(8,128)(2,1)S(1)}, u32[]{:S(2)}, u32[]{:S(2)}) collective-permute-start(bf16[448,256]{1,0:T(8,128)(2,1)S(1)} %shard_map.132), channel_id=1, source_target_pairs={{0,2},{2,0},{1,3},{3,1},{4,6},{6,4},{5,7},{7,5},{8,10},{10,8},{9,1... | collective-permute-start | bytes 688136 | tf_op jit(solution)/shard_map/ppermute | solution.py:31
  36.2 1.5 collective-permute-done.2.refs_6_
  37.7 0.0 all-to-all-done
  37.7 0.9 broadcast_in_dim.35
  38.6 4.2 %all-to-all-start.1 = ((bf16[4,128,768]{2,1,0:T(8,128)(2,1)}), bf16[4,128,768]{2,1,0:T(8,128)(2,1)S(1)}, u32[]{:S(2)}, u32[]{:S(2)}) async-start(bf16[4,128,768]{2,1,0:T(8,128)(2,1)} %broadcast_in_dim.35), calls=%async_computation.1 | async-start | bytes 1572864 | tf_op jit(solution)/shard_map/all_to_all | solution.py:27
  42.8 0.8 pad_maximum_fusion
  43.6 5.7 %collective-permute-start.4 = (bf16[896,256]{1,0:T(8,128)(2,1)}, bf16[896,256]{1,0:T(8,128)(2,1)S(1)}, u32[]{:S(2)}, u32[]{:S(2)}) collective-permute-start(bf16[896,256]{1,0:T(8,128)(2,1)} %pad_maximum_fusion), channel_id=1, source_target_pairs={{2,4},{4,2},{6,8},{8,6},{10,12},{12,10},{14,16},{16,14},{18,20},{2... | collective-permute-start | bytes 1376264 | tf_op jit(solution)/shard_map/ppermute | solution.py:38
  49.3 3.2 %all-to-all-done.1 = bf16[4,128,768]{2,1,0:T(8,128)(2,1)S(1)} async-done(((bf16[4,128,768]{2,1,0:T(8,128)(2,1)}), bf16[4,128,768]{2,1,0:T(8,128)(2,1)S(1)}, u32[]{:S(2)}, u32[]{:S(2)}) %all-to-all-start.1) | async-done | bytes 786464 | tf_op jit(solution)/shard_map/all_to_all | solution.py:27
  52.6 0.1 fusion.3
  52.6 11.6 %collective-permute-start.3 = (bf16[256,768]{1,0:T(8,128)(2,1)S(1)}, bf16[256,768]{1,0:T(8,128)(2,1)S(1)}, u32[]{:S(2)}, u32[]{:S(2)}) collective-permute-start(bf16[256,768]{1,0:T(8,128)(2,1)S(1)} %bitcast.23), channel_id=1, source_target_pairs={{0,256},{256,1},{1,257},{257,0},{2,258},{258,3},{3,259},{259,2},{4... | collective-permute-start | bytes 1179656 | tf_op jit(solution)/shard_map/ppermute | solution.py:45
  64.2 3.8 %collective-permute-start.6 = (bf16[256,768]{1,0:T(8,128)(2,1)S(1)}, bf16[256,768]{1,0:T(8,128)(2,1)}, u32[]{:S(2)}, u32[]{:S(2)}) collective-permute-start(bf16[256,768]{1,0:T(8,128)(2,1)S(1)} %bitcast.22), channel_id=1, source_target_pairs={{0,257},{256,0},{1,256},{257,1},{2,259},{258,2},{3,258},{259,3},{4... | collective-permute-start | bytes 1179656 | tf_op jit(solution)/shard_map/ppermute | solution.py:45
  68.0 3.4 %collective-permute-start.7 = (bf16[512,768]{1,0:T(8,128)(2,1)S(1)}, bf16[512,768]{1,0:T(8,128)(2,1)S(1)}, u32[]{:S(2)}, u32[]{:S(2)}) collective-permute-start(bf16[512,768]{1,0:T(8,128)(2,1)S(1)} %bitcast.17), channel_id=1, source_target_pairs={{0,2},{2,0},{1,3},{3,1},{4,6},{6,4},{5,7},{7,5},{8,10},{10,8},{9,1... | collective-permute-start | bytes 2359304 | tf_op jit(solution)/shard_map/ppermute | solution.py:31
  71.4 0.0 collective-permute-done.4.far.refs_7_
  71.5 1.9 %collective-permute-start.5 = (bf16[592,256]{1,0:T(8,128)(2,1)S(1)}, bf16[592,256]{1,0:T(8,128)(2,1)S(1)}, u32[]{:S(2)}, u32[]{:S(2)}) collective-permute-start(bf16[592,256]{1,0:T(8,128)(2,1)S(1)} %shard_map.133), channel_id=1, source_target_pairs={{0,2},{2,0},{1,3},{3,1},{4,6},{6,4},{5,7},{7,5},{8,10},{10,8},{9,1... | collective-permute-start | bytes 909320 | tf_op jit(solution)/shard_map/ppermute | solution.py:31
  73.4 1.6 collective-permute-done.5.refs_8_
  75.0 0.7 copy-done.6
  75.7 0.0 collective-permute-done.3.refs_11_
  75.7 2.4 %collective-permute-start.8 = (bf16[256,768]{1,0:T(8,128)(2,1)S(1)}, bf16[256,768]{1,0:T(8,128)(2,1)}, u32[]{:S(2)}, u32[]{:S(2)}) collective-permute-start(bf16[256,768]{1,0:T(8,128)(2,1)S(1)} %collective-permute-done.3.refs_11_), channel_id=1, source_target_pairs={{0,2},{2,0},{1,3},{3,1},{4,6},{6,4},{5,7},{7,5},{8,10},{10,8},{9,1... | collective-permute-start | bytes 1179656 | tf_op jit(solution)/shard_map/ppermute | solution.py:31
  78.1 0.0 collective-permute-done.6.refs_12_
  78.1 1.9 %collective-permute-start.9 = (bf16[256,768]{1,0:T(8,128)(2,1)}, bf16[256,768]{1,0:T(8,128)(2,1)}, u32[]{:S(2)}, u32[]{:S(2)}) collective-permute-start(bf16[256,768]{1,0:T(8,128)(2,1)} %collective-permute-done.6.refs_12_), channel_id=1, source_target_pairs={{0,2},{2,0},{1,3},{3,1},{4,6},{6,4},{5,7},{7,5},{8,10},{10,8},{9,1... | collective-permute-start | bytes 1179656 | tf_op jit(solution)/shard_map/ppermute | solution.py:31
  80.0 0.1 pad_add_fusion.refs_0_
  80.1 0.0 collective-permute-done.8.refs_14_
  80.1 1.9 %collective-permute-done.9.refs_15_ = bf16[256,768]{1,0:T(8,128)(2,1)} collective-permute-done((bf16[256,768]{1,0:T(8,128)(2,1)}, bf16[256,768]{1,0:T(8,128)(2,1)}, u32[]{:S(2)}, u32[]{:S(2)}) %collective-permute-start.9) | collective-permute-done | bytes 393248 | tf_op jit(solution)/shard_map/ppermute | solution.py:31
  82.0 0.0 collective-permute-done.7.refs_13_
  82.1 1.0 copy-done.7
  83.0 12.9 %shard_map.134 = (f32[128,256]{1,0:T(8,128)S(1)}, f32[128,256]{1,0:T(8,128)S(1)}, f32[8,256]{1,0:T(8,128)S(1)}, bf16[2,8,128,128]{3,2,1,0:T(8,128)(2,1)S(1)}, bf16[2,8,128,128]{3,2,1,0:T(8,128)(2,1)S(1)}) custom-call(s32[2]{0:T(128)S(1)} %pad_add_fusion.refs_0_, f32[1,128,256]{2,1,0:T(8,128)S(1)} %copy-done, f32[1,128,256]{2,1,0:T(8,128)S(1)} %copy-done.1, ...), custom_call_target="tpu_custom_call" | custom-call | flops 8053063680 | bytes 5963784 | tf_op jit(solution)/shard_map/pallas_call | solution.py:390
  96.0 2.0 %collective-permute-start.10 = (bf16[2,8,128,128]{3,2,1,0:T(8,128)(2,1)S(1)}, bf16[2,8,128,128]{3,2,1,0:T(8,128)(2,1)S(1)}, u32[]{:S(2)}, u32[]{:S(2)}) collective-permute-start(bf16[2,8,128,128]{3,2,1,0:T(8,128)(2,1)S(1)} %get-tuple-element.48), channel_id=1, source_target_pairs={{0,2},{2,0},{1,3},{3,1},{4,6},{6,4},{5,7},{7,5},{8,10},{10,8},{9,1... | collective-permute-start | bytes 1572872 | tf_op jit(solution)/shard_map/ppermute | solution.py:31
  98.0 1.8 %collective-permute-done.10 = bf16[2,8,128,128]{3,2,1,0:T(8,128)(2,1)S(1)} collective-permute-done((bf16[2,8,128,128]{3,2,1,0:T(8,128)(2,1)S(1)}, bf16[2,8,128,128]{3,2,1,0:T(8,128)(2,1)S(1)}, u32[]{:S(2)}, u32[]{:S(2)}) %collective-permute-start.10) | collective-permute-done | bytes 524320 | tf_op jit(solution)/shard_map/ppermute | solution.py:31
  99.8 0.9 shard_map.135
  100.7 3.9 %all-to-all-start.2 = ((bf16[16,128,128]{2,1,0:T(8,128)(2,1)}), bf16[16,128,128]{2,1,0:T(8,128)(2,1)S(1)}, u32[]{:S(2)}, u32[]{:S(2)}) async-start(bf16[16,128,128]{2,1,0:T(8,128)(2,1)} %shard_map.135), calls=%async_computation.2 | async-start | bytes 1048576 | tf_op jit(solution)/shard_map/all_to_all | solution.py:450
  104.6 4.8 %collective-permute-start.11 = (f32[8,256]{1,0:T(8,128)S(1)}, f32[8,256]{1,0:T(8,128)S(1)}, u32[]{:S(2)}, u32[]{:S(2)}) collective-permute-start(f32[8,256]{1,0:T(8,128)S(1)} %get-tuple-element.49), channel_id=1, source_target_pairs={{0,1},{1,0},{2,3},{3,2},{4,5},{5,4},{6,7},{7,6},{8,9},{9,8},{10,11... | collective-permute-start | bytes 24584 | tf_op jit(solution)/shard_map/ppermute | solution.py:31
  109.3 4.2 %collective-permute-done.11 = f32[8,256]{1,0:T(8,128)S(1)} collective-permute-done((f32[8,256]{1,0:T(8,128)S(1)}, f32[8,256]{1,0:T(8,128)S(1)}, u32[]{:S(2)}, u32[]{:S(2)}) %collective-permute-start.11) | collective-permute-done | bytes 8224 | tf_op jit(solution)/shard_map/ppermute | solution.py:31
  113.5 1.3 all-to-all-done.2.parts
  114.9 0.7 shard_map.136
  115.6 3.3 %all-to-all-start.3 = ((bf16[4,128,128]{2,1,0:T(8,128)(2,1)}), bf16[4,128,128]{2,1,0:T(8,128)(2,1)S(1)}, u32[]{:S(2)}, u32[]{:S(2)}) async-start(bf16[4,128,128]{2,1,0:T(8,128)(2,1)} %shard_map.136), calls=%async_computation.3 | async-start | bytes 262144 | tf_op jit(solution)/shard_map/all_to_all | solution.py:460
  119.0 0.1 pad_add_fusion.1.place
  119.0 4.6 %all-to-all-done.3.parts = bf16[4,128,128]{2,1,0:T(8,128)(2,1)S(1)} async-done(((bf16[4,128,128]{2,1,0:T(8,128)(2,1)}), bf16[4,128,128]{2,1,0:T(8,128)(2,1)S(1)}, u32[]{:S(2)}, u32[]{:S(2)}) %all-to-all-start.3) | async-done | bytes 131104 | tf_op jit(solution)/shard_map/all_to_all | solution.py:460
  123.7 0.7 shard_map.137
  124.4 3.8 %all-to-all-start.4 = ((bf16[4,128,128]{2,1,0:T(8,128)(2,1)}), bf16[4,128,128]{2,1,0:T(8,128)(2,1)S(1)}, u32[]{:S(2)}, u32[]{:S(2)}) async-start(bf16[4,128,128]{2,1,0:T(8,128)(2,1)} %shard_map.137), calls=%async_computation.4 | async-start | bytes 262144 | tf_op jit(solution)/shard_map/all_to_all | solution.py:460
  128.1 5.8 %collective-permute-start.13 = (f32[128,256]{1,0:T(8,128)S(1)}, f32[128,256]{1,0:T(8,128)S(1)}, u32[]{:S(2)}, u32[]{:S(2)}) collective-permute-start(f32[128,256]{1,0:T(8,128)S(1)} %get-tuple-element.52), channel_id=1, source_target_pairs={{0,2},{2,0},{1,3},{3,1},{4,6},{6,4},{5,7},{7,5},{8,10},{10,8},{9,1... | collective-permute-start | bytes 393224 | tf_op jit(solution)/shard_map/ppermute | solution.py:31
  134.0 2.8 %collective-permute-start.12 = (f32[128,256]{1,0:T(8,128)S(1)}, f32[128,256]{1,0:T(8,128)S(1)}, u32[]{:S(2)}, u32[]{:S(2)}) collective-permute-start(f32[128,256]{1,0:T(8,128)S(1)} %get-tuple-element.52), channel_id=1, source_target_pairs={{2,4},{4,2},{6,8},{8,6},{10,12},{12,10},{14,16},{16,14},{18,20},{2... | collective-permute-start | bytes 393224 | tf_op jit(solution)/shard_map/ppermute | solution.py:38
  136.8 3.5 %all-to-all-done.4.parts = bf16[4,128,128]{2,1,0:T(8,128)(2,1)S(1)} async-done(((bf16[4,128,128]{2,1,0:T(8,128)(2,1)}), bf16[4,128,128]{2,1,0:T(8,128)(2,1)S(1)}, u32[]{:S(2)}, u32[]{:S(2)}) %all-to-all-start.4) | async-done | bytes 131104 | tf_op jit(solution)/shard_map/all_to_all | solution.py:460
  140.3 0.7 shard_map.138
  141.0 8.7 %all-to-all-start.5 = ((bf16[32,16,128]{2,1,0:T(8,128)(2,1)}), bf16[32,16,128]{2,1,0:T(8,128)(2,1)S(1)}, u32[]{:S(2)}, u32[]{:S(2)}) async-start(bf16[32,16,128]{2,1,0:T(8,128)(2,1)} %shard_map.138), calls=%async_computation.5 | async-start | bytes 262144 | tf_op jit(solution)/shard_map/all_to_all | solution.py:473
  149.7 0.0 collective-permute-done.13
  149.7 0.0 collective-permute-done.12
  149.8 0.0 copy-start.4
  149.8 0.0 copy-start.5
  149.8 0.7 fusion.2
  150.5 7.1 %all-to-all-done.5.parts_ref = bf16[32,16,128]{2,1,0:T(8,128)(2,1)S(1)} async-done(((bf16[32,16,128]{2,1,0:T(8,128)(2,1)}), bf16[32,16,128]{2,1,0:T(8,128)(2,1)S(1)}, u32[]{:S(2)}, u32[]{:S(2)}) %all-to-all-start.5) | async-done | bytes 131104 | tf_op jit(solution)/shard_map/all_to_all | solution.py:473
  157.5 0.0 copy-done.5
  157.6 1.3 shard_map.139
  (16 shorter events, 0.1 us)
Async XLA Ops:
  11.1 10.4 %copy-start.8 = (bf16[128,256]{1,0:T(8,128)(2,1)S(1)}, bf16[128,256]{1,0:T(8,128)(2,1)}, u32[]{:S(2)}) copy-start(bf16[128,256]{1,0:T(8,128)(2,1)} %get-tuple-element.34) | copy-start | bytes 196612
  11.1 15.4 %copy-start.3 = (f32[24,256]{1,0:T(8,128)S(1)}, f32[24,256]{1,0:T(8,128)}, u32[]{:S(2)}) copy-start(f32[24,256]{1,0:T(8,128)} %get-tuple-element.33.mine.refs_4_) | copy-start | bytes 73732
  11.8 19.3 %copy-start = (f32[1,128,256]{2,1,0:T(8,128)S(1)}, f32[1,128,256]{2,1,0:T(8,128)}, u32[]{:S(2)}) copy-start(f32[1,128,256]{2,1,0:T(8,128)} %refs_1_.4) | copy-start | bytes 393220
  11.8 19.3 %copy-start.1 = (f32[1,128,256]{2,1,0:T(8,128)S(1)}, f32[1,128,256]{2,1,0:T(8,128)}, u32[]{:S(2)}) copy-start(f32[1,128,256]{2,1,0:T(8,128)} %refs_2_.4) | copy-start | bytes 393220
  11.8 19.3 %copy-start.2 = (f32[1,128,256]{2,1,0:T(8,128)S(1)}, f32[1,128,256]{2,1,0:T(8,128)}, u32[]{:S(2)}) copy-start(f32[1,128,256]{2,1,0:T(8,128)} %refs_3_.3) | copy-start | bytes 393220
  11.8 25.9 %all-to-all-start = ((bf16[16,8,768]{2,1,0:T(8,128)(2,1)}), bf16[16,8,768]{2,1,0:T(8,128)(2,1)S(1)}, u32[]{:S(2)}, u32[]{:S(2)}) async-start(bf16[16,8,768]{2,1,0:T(8,128)(2,1)} %broadcast_in_dim.34), calls=%async_computation | async-start | bytes 393216 | tf_op jit(solution)/shard_map/all_to_all | solution.py:27
  21.5 12.7 %collective-permute-start.1 = (bf16[128,256]{1,0:T(8,128)(2,1)S(1)}, bf16[128,256]{1,0:T(8,128)(2,1)S(1)}, u32[]{:S(2)}, u32[]{:S(2)}) collective-permute-start(bf16[128,256]{1,0:T(8,128)(2,1)S(1)} %copy-done.8), channel_id=1, source_target_pairs={{2,8},{6,12},{10,16},{14,20},{18,24},{22,28},{26,32},{30,36},{34,4... | collective-permute-start | bytes 196616 | tf_op jit(solution)/shard_map/ppermute | solution.py:51
  26.4 6.2 %collective-permute-start = (f32[24,256]{1,0:T(8,128)S(1)}, f32[24,256]{1,0:T(8,128)S(1)}, u32[]{:S(2)}, u32[]{:S(2)}) collective-permute-start(f32[24,256]{1,0:T(8,128)S(1)} %copy-done.3), channel_id=1, source_target_pairs={{0,1},{1,0},{2,3},{3,2},{4,5},{5,4},{6,7},{7,6},{8,9},{9,8},{10,11... | collective-permute-start | bytes 73736 | tf_op jit(solution)/shard_map/ppermute | solution.py:31
  34.3 3.4 %collective-permute-start.2 = (bf16[448,256]{1,0:T(8,128)(2,1)S(1)}, bf16[448,256]{1,0:T(8,128)(2,1)S(1)}, u32[]{:S(2)}, u32[]{:S(2)}) collective-permute-start(bf16[448,256]{1,0:T(8,128)(2,1)S(1)} %shard_map.132), channel_id=1, source_target_pairs={{0,2},{2,0},{1,3},{3,1},{4,6},{6,4},{5,7},{7,5},{8,10},{10,8},{9,1... | collective-permute-start | bytes 688136 | tf_op jit(solution)/shard_map/ppermute | solution.py:31
  38.6 13.9 %all-to-all-start.1 = ((bf16[4,128,768]{2,1,0:T(8,128)(2,1)}), bf16[4,128,768]{2,1,0:T(8,128)(2,1)S(1)}, u32[]{:S(2)}, u32[]{:S(2)}) async-start(bf16[4,128,768]{2,1,0:T(8,128)(2,1)} %broadcast_in_dim.35), calls=%async_computation.1 | async-start | bytes 1572864 | tf_op jit(solution)/shard_map/all_to_all | solution.py:27
  43.6 27.8 %collective-permute-start.4 = (bf16[896,256]{1,0:T(8,128)(2,1)}, bf16[896,256]{1,0:T(8,128)(2,1)S(1)}, u32[]{:S(2)}, u32[]{:S(2)}) collective-permute-start(bf16[896,256]{1,0:T(8,128)(2,1)} %pad_maximum_fusion), channel_id=1, source_target_pairs={{2,4},{4,2},{6,8},{8,6},{10,12},{12,10},{14,16},{16,14},{18,20},{2... | collective-permute-start | bytes 1376264 | tf_op jit(solution)/shard_map/ppermute | solution.py:38
  52.6 23.1 %collective-permute-start.3 = (bf16[256,768]{1,0:T(8,128)(2,1)S(1)}, bf16[256,768]{1,0:T(8,128)(2,1)S(1)}, u32[]{:S(2)}, u32[]{:S(2)}) collective-permute-start(bf16[256,768]{1,0:T(8,128)(2,1)S(1)} %bitcast.23), channel_id=1, source_target_pairs={{0,256},{256,1},{1,257},{257,0},{2,258},{258,3},{3,259},{259,2},{4... | collective-permute-start | bytes 1179656 | tf_op jit(solution)/shard_map/ppermute | solution.py:45
  64.2 13.8 %collective-permute-start.6 = (bf16[256,768]{1,0:T(8,128)(2,1)S(1)}, bf16[256,768]{1,0:T(8,128)(2,1)}, u32[]{:S(2)}, u32[]{:S(2)}) collective-permute-start(bf16[256,768]{1,0:T(8,128)(2,1)S(1)} %bitcast.22), channel_id=1, source_target_pairs={{0,257},{256,0},{1,256},{257,1},{2,259},{258,2},{3,258},{259,3},{4... | collective-permute-start | bytes 1179656 | tf_op jit(solution)/shard_map/ppermute | solution.py:45
  68.0 14.0 %collective-permute-start.7 = (bf16[512,768]{1,0:T(8,128)(2,1)S(1)}, bf16[512,768]{1,0:T(8,128)(2,1)S(1)}, u32[]{:S(2)}, u32[]{:S(2)}) collective-permute-start(bf16[512,768]{1,0:T(8,128)(2,1)S(1)} %bitcast.17), channel_id=1, source_target_pairs={{0,2},{2,0},{1,3},{3,1},{4,6},{6,4},{5,7},{7,5},{8,10},{10,8},{9,1... | collective-permute-start | bytes 2359304 | tf_op jit(solution)/shard_map/ppermute | solution.py:31
  71.5 3.5 %collective-permute-start.5 = (bf16[592,256]{1,0:T(8,128)(2,1)S(1)}, bf16[592,256]{1,0:T(8,128)(2,1)S(1)}, u32[]{:S(2)}, u32[]{:S(2)}) collective-permute-start(bf16[592,256]{1,0:T(8,128)(2,1)S(1)} %shard_map.133), channel_id=1, source_target_pairs={{0,2},{2,0},{1,3},{3,1},{4,6},{6,4},{5,7},{7,5},{8,10},{10,8},{9,1... | collective-permute-start | bytes 909320 | tf_op jit(solution)/shard_map/ppermute | solution.py:31
  75.0 0.7 copy-start.6
  75.7 4.4 %collective-permute-start.8 = (bf16[256,768]{1,0:T(8,128)(2,1)S(1)}, bf16[256,768]{1,0:T(8,128)(2,1)}, u32[]{:S(2)}, u32[]{:S(2)}) collective-permute-start(bf16[256,768]{1,0:T(8,128)(2,1)S(1)} %collective-permute-done.3.refs_11_), channel_id=1, source_target_pairs={{0,2},{2,0},{1,3},{3,1},{4,6},{6,4},{5,7},{7,5},{8,10},{10,8},{9,1... | collective-permute-start | bytes 1179656 | tf_op jit(solution)/shard_map/ppermute | solution.py:31
  78.1 4.0 %collective-permute-start.9 = (bf16[256,768]{1,0:T(8,128)(2,1)}, bf16[256,768]{1,0:T(8,128)(2,1)}, u32[]{:S(2)}, u32[]{:S(2)}) collective-permute-start(bf16[256,768]{1,0:T(8,128)(2,1)} %collective-permute-done.6.refs_12_), channel_id=1, source_target_pairs={{0,2},{2,0},{1,3},{3,1},{4,6},{6,4},{5,7},{7,5},{8,10},{10,8},{9,1... | collective-permute-start | bytes 1179656 | tf_op jit(solution)/shard_map/ppermute | solution.py:31
  82.1 1.0 copy-start.7
  96.0 3.8 %collective-permute-start.10 = (bf16[2,8,128,128]{3,2,1,0:T(8,128)(2,1)S(1)}, bf16[2,8,128,128]{3,2,1,0:T(8,128)(2,1)S(1)}, u32[]{:S(2)}, u32[]{:S(2)}) collective-permute-start(bf16[2,8,128,128]{3,2,1,0:T(8,128)(2,1)S(1)} %get-tuple-element.48), channel_id=1, source_target_pairs={{0,2},{2,0},{1,3},{3,1},{4,6},{6,4},{5,7},{7,5},{8,10},{10,8},{9,1... | collective-permute-start | bytes 1572872 | tf_op jit(solution)/shard_map/ppermute | solution.py:31
  100.7 14.2 %all-to-all-start.2 = ((bf16[16,128,128]{2,1,0:T(8,128)(2,1)}), bf16[16,128,128]{2,1,0:T(8,128)(2,1)S(1)}, u32[]{:S(2)}, u32[]{:S(2)}) async-start(bf16[16,128,128]{2,1,0:T(8,128)(2,1)} %shard_map.135), calls=%async_computation.2 | async-start | bytes 1048576 | tf_op jit(solution)/shard_map/all_to_all | solution.py:450
  104.6 9.0 %collective-permute-start.11 = (f32[8,256]{1,0:T(8,128)S(1)}, f32[8,256]{1,0:T(8,128)S(1)}, u32[]{:S(2)}, u32[]{:S(2)}) collective-permute-start(f32[8,256]{1,0:T(8,128)S(1)} %get-tuple-element.49), channel_id=1, source_target_pairs={{0,1},{1,0},{2,3},{3,2},{4,5},{5,4},{6,7},{7,6},{8,9},{9,8},{10,11... | collective-permute-start | bytes 24584 | tf_op jit(solution)/shard_map/ppermute | solution.py:31
  115.6 8.1 %all-to-all-start.3 = ((bf16[4,128,128]{2,1,0:T(8,128)(2,1)}), bf16[4,128,128]{2,1,0:T(8,128)(2,1)S(1)}, u32[]{:S(2)}, u32[]{:S(2)}) async-start(bf16[4,128,128]{2,1,0:T(8,128)(2,1)} %shard_map.136), calls=%async_computation.3 | async-start | bytes 262144 | tf_op jit(solution)/shard_map/all_to_all | solution.py:460
  124.4 15.9 %all-to-all-start.4 = ((bf16[4,128,128]{2,1,0:T(8,128)(2,1)}), bf16[4,128,128]{2,1,0:T(8,128)(2,1)S(1)}, u32[]{:S(2)}, u32[]{:S(2)}) async-start(bf16[4,128,128]{2,1,0:T(8,128)(2,1)} %shard_map.137), calls=%async_computation.4 | async-start | bytes 262144 | tf_op jit(solution)/shard_map/all_to_all | solution.py:460
  128.1 21.6 %collective-permute-start.13 = (f32[128,256]{1,0:T(8,128)S(1)}, f32[128,256]{1,0:T(8,128)S(1)}, u32[]{:S(2)}, u32[]{:S(2)}) collective-permute-start(f32[128,256]{1,0:T(8,128)S(1)} %get-tuple-element.52), channel_id=1, source_target_pairs={{0,2},{2,0},{1,3},{3,1},{4,6},{6,4},{5,7},{7,5},{8,10},{10,8},{9,1... | collective-permute-start | bytes 393224 | tf_op jit(solution)/shard_map/ppermute | solution.py:31
  134.0 15.8 %collective-permute-start.12 = (f32[128,256]{1,0:T(8,128)S(1)}, f32[128,256]{1,0:T(8,128)S(1)}, u32[]{:S(2)}, u32[]{:S(2)}) collective-permute-start(f32[128,256]{1,0:T(8,128)S(1)} %get-tuple-element.52), channel_id=1, source_target_pairs={{2,4},{4,2},{6,8},{8,6},{10,12},{12,10},{14,16},{16,14},{18,20},{2... | collective-permute-start | bytes 393224 | tf_op jit(solution)/shard_map/ppermute | solution.py:38
  141.0 16.6 %all-to-all-start.5 = ((bf16[32,16,128]{2,1,0:T(8,128)(2,1)}), bf16[32,16,128]{2,1,0:T(8,128)(2,1)S(1)}, u32[]{:S(2)}, u32[]{:S(2)}) async-start(bf16[32,16,128]{2,1,0:T(8,128)(2,1)} %shard_map.138), calls=%async_computation.5 | async-start | bytes 262144 | tf_op jit(solution)/shard_map/all_to_all | solution.py:473
  149.8 7.8 %copy-start.4 = (f32[4,256]{1,0:T(4,128)S(1)}, f32[4,256]{1,0:T(4,128)}, u32[]{:S(2)}) copy-start(f32[4,256]{1,0:T(4,128)} %w_in.1) | copy-start | bytes 12292
  149.8 7.8 %copy-start.5 = (f32[4,256]{1,0:T(4,128)S(1)}, f32[4,256]{1,0:T(4,128)}, u32[]{:S(2)}) copy-start(f32[4,256]{1,0:T(4,128)} %w_out.1) | copy-start | bytes 12292

commit v13 on v10

--- a/solution.py
+++ b/solution.py
@@ -214,23 +214,25 @@
         outs = [out[i * length : (i + 1) * length] for i in range(2 * len(rows))]
         return list(zip(outs[: len(rows)], outs[len(rows) :])), saved
 
+    def exactly(left, ones, contract):
+        total, ones = 0.0, ones.astype(jnp.bfloat16)
+        for _ in range(3):
+            term = left.astype(jnp.bfloat16)
+            total = total + lax.dot_general(
+                term, ones, contract, preferred_element_type=jnp.float32
+            )
+            left = left - term.astype(jnp.float32)
+        return total
+
     def observed(final, columns, levels, values, precisions):
         count = columns.shape[1]
         cell_ids = lax.broadcasted_iota(jnp.int32, (length, count), 0).astype(jnp.float32)
         level_ids = lax.broadcasted_iota(jnp.int32, (features, count), 0).astype(jnp.float32)
         pick_cell = (cell_ids == columns).astype(jnp.float32)
         pick_level = (level_ids == levels).astype(jnp.float32)
-        at_level = jnp.dot(
-            final, pick_level, precision=lax.Precision.HIGHEST, preferred_element_type=jnp.float32
-        )
+        at_level = exactly(final, pick_level, (((1,), (0,)), ((), ())))
         modelled = jnp.sum(pick_cell * at_level, axis=0, keepdims=True)
-        return lax.dot_general(
-            pick_cell * (precisions * (modelled - values)),
-            pick_level,
-            CONTRACT_LAST,
-            precision=lax.Precision.HIGHEST,
-            preferred_element_type=jnp.float32,
-        )
+        return exactly(pick_cell * (precisions * (modelled - values)), pick_level, CONTRACT_LAST)
 
     own = [ring_field(ref[0], other, i) for i, ref in enumerate((state, increment, diffusivity))]
     gate = column(ring_gating(mine[18:19, :cells], other[18:19, :cells])[:1])
@@ -423,7 +425,7 @@
     )
 
 
-def updated(kept, given, w_in, w_out, arriving, later):
+def updated(kept, given, w_in, w_out, soon, later):
     halves, blocks, rows, columns = kept.shape
     peers = halves * blocks
     (grads,) = on_chip(
@@ -433,7 +435,7 @@
         kept.size,
     )
     grads = lax.all_to_all(grads, AROUND[:-1], 0, 0)
-    grads, arriving = lax.optimization_barrier((grads, arriving))
+    grads, soon = lax.optimization_barrier((grads, soon))
     for axis in ("z_lo", "z_hi"):
         count = lax.axis_size(axis)
         (copies,) = on_chip(
@@ -465,7 +467,7 @@
         parts.size,
         scalars=1,
     )
-    return new_in, new_out, arriving, later
+    return new_in, new_out, soon, later
 
 
 def local(
@@ -536,8 +538,9 @@
         ],
     )
     w_in_new, w_out_new, ends, spreading = updated(
-        kept, given, w_in, w_out, swapped(ends, "x_hi"), spreading
-    )
+        kept, given, w_in, w_out, ends, spreading
+    )
+    ends = swapped(ends, "x_hi")
     far = swapped_between_chips(spreading)
     near = swapped(spreading, "core")
     east = jnp.concatenate([spreading[1:], ends[:1]])

time: 151 us -> 150 us (level)
  blocking collectives: 8.58 us -> 24.9 us
  waiting for transfers between devices: 34.4 us -> 26 us
  starting transfers between devices: 82 us -> 74.3 us
    all_to_all x0 -> x1, blocking collectives: none -> 16.3 us  [updated(): grads = lax.all_to_all(grads, AROUND[:-1], 0, 0)]
    all_to_all x1 -> x0, starting transfers between devices: 6.17 us -> none  [updated(): grads = lax.all_to_all(grads, AROUND[:-1], 0, 0)]
    ppermute x7, waiting for transfers between devices: 11.6 us -> 7.41 us  [swapped(): return lax.ppermute(array, axis, [(0, 1), (1, 0)])]
    all_to_all x2, waiting for transfers between devices: 8.2 us -> 5.28 us  [updated(): grads = lax.all_to_all(copies, axis, 0, 0)]
    ppermute x7, starting transfers between devices: 25.4 us -> 23.6 us  [swapped(): return lax.ppermute(array, axis, [(0, 1), (1, 0)])]
  transfers between devices with their start and end apart: 16 -> 15, of which waited for: 11 -> 9; matrix products, arithmetic and copies ran while one was open for 1% -> 1% of each run, Pallas kernels for 1% -> 1%
where the time goes in v13:
time: 150 us; the launch traced here: 149 us
  starting transfers between devices  74.3 us (50%)
  waiting for transfers between devices  26 us (17%)
  blocking collectives  24.9 us (17%)
  Pallas kernels  16.8 us (11%)
  local copies, waits for them, and re-layouts  5.48 us (4%)
    ppermute x7, starting transfers between devices, swapped(): return lax.ppermute(array, axis, [(0, 1), (1, 0)])  23.6 us
    pallas_call x9, Pallas kernels, on_chip(): pl.pallas_call(body, out_shape=outs, in_specs=[pl.BlockSpec(memory_space=...  16.8 us
    all_to_all x1, blocking collectives, updated(): grads = lax.all_to_all(grads, AROUND[:-1], 0, 0)  16.3 us
    all_to_all x2, starting transfers between devices, spread(): lax.all_to_all(jnp.broadcast_to(block[None], (count,) + block.shape), axi...  14.8 us
    ppermute x2, starting transfers between devices, swapped_between_chips(): return lax.ppermute(array, TILE, pairs)  14.2 us
    all_to_all x2, starting transfers between devices, updated(): grads = lax.all_to_all(copies, axis, 0, 0)  9.91 us
    all_to_all x1, starting transfers between devices, updated(): parts = lax.all_to_all(copies, AROUND, 0, 0)  8.96 us
    all_gather x1, blocking collectives, local(): rows = lax.all_gather(rows, 'core', axis=0, tiled=True)  8.58 us
  transfers between devices with their start and end apart: 15, of which 9 were waited for; matrix products, arithmetic and copies ran while one was open for 1% of the time, Pallas kernels for 1%

profile of v13, /device:TPU:1, one launch (start us, length us, event | category | flops | bytes accessed | tf_op | source)
XLA Modules:
  0.0 149.2 jit_solution(1902803611728076102)
XLA Ops:
  0.6 1.8 %shard_map.130 = (bf16[4,1536]{1,0:T(4,128)(2,1)}, f32[24,256]{1,0:T(8,128)}, bf16[128,256]{1,0:T(8,128)(2,1)}) custom-call(f32[1,128,256]{2,1,0:T(8,128)} %refs_1_.4, f32[1,128,256]{2,1,0:T(8,128)} %refs_2_.4, f32[1,128,256]{2,1,0:T(8,128)} %refs_3_.3, s32[1,128]{1,0:T(1,128)} %refs_3_.2, s32[1,64]{1,0:T(1,128)} %bitcast.20, s32[1,64]{1,0:T(1,128)} %bitcast.21, ...), custom_call_target="tpu_custom_call" | custom-call | bytes 513536 | tf_op jit(solution)/shard_map/pallas_call | solution.py:377
  2.4 8.6 %all-gather = bf16[2,4,1536]{2,1,0:T(4,128)(2,1)S(1)} all-gather(bf16[1,4,1536]{2,1,0:T(4,128)(2,1)} %bitcast.19), channel_id=1, replica_groups=mesh['x_lo'=2,'y'=4,'z_hi'=4,'z_lo'=4,'core'=2,'x_hi'=2] {'core'}, dimensions={0}, use_global_device_ids=true | all-gather | bytes 36864 | tf_op jit(solution)/shard_map/all_gather | solution.py:497
  11.1 0.7 broadcast_in_dim.38
  11.7 9.5 %all-to-all-start = ((bf16[16,8,768]{2,1,0:T(8,128)(2,1)}), bf16[16,8,768]{2,1,0:T(8,128)(2,1)S(1)}, u32[]{:S(2)}, u32[]{:S(2)}) async-start(bf16[16,8,768]{2,1,0:T(8,128)(2,1)} %broadcast_in_dim.38), calls=%async_computation | async-start | bytes 393216 | tf_op jit(solution)/shard_map/all_to_all | solution.py:26
  21.3 4.7 %collective-permute-start = (f32[24,256]{1,0:T(8,128)}, f32[24,256]{1,0:T(8,128)S(1)}, u32[]{:S(2)}, u32[]{:S(2)}) collective-permute-start(f32[24,256]{1,0:T(8,128)} %get-tuple-element.33.mine.refs_4_), channel_id=1, source_target_pairs={{0,1},{1,0},{2,3},{3,2},{4,5},{5,4},{6,7},{7,6},{8,9},{9,8},{10,11... | collective-permute-start | bytes 73736 | tf_op jit(solution)/shard_map/ppermute | solution.py:30
  26.0 0.0 copy-start
  26.0 0.9 copy-done
  26.9 0.0 copy-start.2
  26.9 0.9 copy-done.2
  27.8 0.0 copy-start.4
  27.8 0.9 copy-done.4
  28.7 0.5 shard_map.131.fields
  29.2 0.0 collective-permute-done.other.refs_5_
  29.2 0.0 copy-start.6
  29.2 0.7 copy-done.6
  29.9 0.1 shard_map.132
  30.0 2.8 %collective-permute-start.1 = (bf16[448,256]{1,0:T(8,128)(2,1)S(1)}, bf16[448,256]{1,0:T(8,128)(2,1)S(1)}, u32[]{:S(2)}, u32[]{:S(2)}) collective-permute-start(bf16[448,256]{1,0:T(8,128)(2,1)S(1)} %shard_map.132), channel_id=1, source_target_pairs={{0,2},{2,0},{1,3},{3,1},{4,6},{6,4},{5,7},{7,5},{8,10},{10,8},{9,1... | collective-permute-start | bytes 688136 | tf_op jit(solution)/shard_map/ppermute | solution.py:30
  32.8 1.1 collective-permute-done.1.refs_6_
  33.9 0.3 all-to-all-done
  34.2 1.3 broadcast_in_dim.39
  35.5 0.0 copy-start.10
  35.5 0.0 copy-start.1
  35.5 0.0 copy-start.3
  35.5 0.0 copy-start.7
  35.5 5.3 %all-to-all-start.1 = ((bf16[8,128,768]{2,1,0:T(8,128)(2,1)}), bf16[8,128,768]{2,1,0:T(8,128)(2,1)S(1)}, u32[]{:S(2)}, u32[]{:S(2)}) async-start(bf16[8,128,768]{2,1,0:T(8,128)(2,1)} %broadcast_in_dim.39), calls=%async_computation.1 | async-start | bytes 3145728 | tf_op jit(solution)/shard_map/all_to_all | solution.py:26
  40.8 7.6 %collective-permute-start.2 = (bf16[896,256]{1,0:T(8,128)(2,1)S(1)}, bf16[896,256]{1,0:T(8,128)(2,1)S(1)}, u32[]{:S(2)}, u32[]{:S(2)}) collective-permute-start(bf16[896,256]{1,0:T(8,128)(2,1)S(1)} %pad_maximum_fusion), channel_id=1, source_target_pairs={{2,4},{4,2},{6,8},{8,6},{10,12},{12,10},{14,16},{16,14},{18,20},{2... | collective-permute-start | bytes 1376264 | tf_op jit(solution)/shard_map/ppermute | solution.py:37
  48.5 0.0 copy-done.10
  48.5 2.8 %collective-permute-start.3 = (bf16[128,256]{1,0:T(8,128)(2,1)S(1)}, bf16[128,256]{1,0:T(8,128)(2,1)S(1)}, u32[]{:S(2)}, u32[]{:S(2)}) collective-permute-start(bf16[128,256]{1,0:T(8,128)(2,1)S(1)} %copy-done.10), channel_id=1, source_target_pairs={{2,8},{6,12},{10,16},{14,20},{18,24},{22,28},{26,32},{30,36},{34,4... | collective-permute-start | bytes 196616 | tf_op jit(solution)/shard_map/ppermute | solution.py:43
  51.3 5.9 %collective-permute-done.3.refs_9_ = bf16[128,256]{1,0:T(8,128)(2,1)S(1)} collective-permute-done((bf16[128,256]{1,0:T(8,128)(2,1)S(1)}, bf16[128,256]{1,0:T(8,128)(2,1)S(1)}, u32[]{:S(2)}, u32[]{:S(2)}) %collective-permute-start.3) | collective-permute-done | bytes 65568 | tf_op jit(solution)/shard_map/ppermute | solution.py:43
  57.2 0.0 collective-permute-done.2.refs_7_
  57.2 1.9 %collective-permute-start.4 = (bf16[896,256]{1,0:T(8,128)(2,1)S(1)}, bf16[896,256]{1,0:T(8,128)(2,1)S(1)}, u32[]{:S(2)}, u32[]{:S(2)}) collective-permute-start(bf16[896,256]{1,0:T(8,128)(2,1)S(1)} %collective-permute-done.2.refs_7_), channel_id=1, source_target_pairs={{0,2},{2,0},{1,3},{3,1},{4,6},{6,4},{5,7},{7,5},{8,10},{10,8},{9,1... | collective-permute-start | bytes 1376264 | tf_op jit(solution)/shard_map/ppermute | solution.py:30
  59.1 1.8 %collective-permute-done.4.refs_8_ = bf16[896,256]{1,0:T(8,128)(2,1)S(1)} collective-permute-done((bf16[896,256]{1,0:T(8,128)(2,1)S(1)}, bf16[896,256]{1,0:T(8,128)(2,1)S(1)}, u32[]{:S(2)}, u32[]{:S(2)}) %collective-permute-start.4) | collective-permute-done | bytes 458784 | tf_op jit(solution)/shard_map/ppermute | solution.py:30
  60.9 0.0 all-to-all-done.1
  60.9 7.0 %collective-permute-start.5 = (bf16[1024,768]{1,0:T(8,128)(2,1)S(1)}, bf16[1024,768]{1,0:T(8,128)(2,1)S(1)}, u32[]{:S(2)}, u32[]{:S(2)}) collective-permute-start(bf16[1024,768]{1,0:T(8,128)(2,1)S(1)} %bitcast.14), channel_id=1, source_target_pairs={{0,2},{2,0},{1,3},{3,1},{4,6},{6,4},{5,7},{7,5},{8,10},{10,8},{9,1... | collective-permute-start | bytes 4718600 | tf_op jit(solution)/shard_map/ppermute | solution.py:30
  67.9 3.0 %collective-permute-done.5.refs_11_ = bf16[1024,768]{1,0:T(8,128)(2,1)S(1)} collective-permute-done((bf16[1024,768]{1,0:T(8,128)(2,1)S(1)}, bf16[1024,768]{1,0:T(8,128)(2,1)S(1)}, u32[]{:S(2)}, u32[]{:S(2)}) %collective-permute-start.5) | collective-permute-done | bytes 1572896 | tf_op jit(solution)/shard_map/ppermute | solution.py:30
  71.0 0.0 copy-done.1
  71.0 0.0 copy-done.3
  71.0 0.0 copy-done.5
  71.0 0.0 copy-done.7
  71.0 10.9 %shard_map.133 = (f32[128,256]{1,0:T(8,128)S(1)}, f32[128,256]{1,0:T(8,128)S(1)}, f32[8,256]{1,0:T(8,128)S(1)}, bf16[2,8,128,128]{3,2,1,0:T(8,128)(2,1)S(1)}, bf16[2,8,128,128]{3,2,1,0:T(8,128)(2,1)S(1)}) custom-call(s32[1]{0:T(128)} %bitcast.refs_0_, f32[1,128,256]{2,1,0:T(8,128)S(1)} %copy-done.1, f32[1,128,256]{2,1,0:T(8,128)S(1)} %copy-done.3, ...), custom_call_target="tpu_custom_call" | custom-call | flops 8053063680 | bytes 6119428 | tf_op jit(solution)/shard_map/pallas_call | solution.py:377
  81.9 2.3 %collective-permute-start.6 = (bf16[2,8,128,128]{3,2,1,0:T(8,128)(2,1)S(1)}, bf16[2,8,128,128]{3,2,1,0:T(8,128)(2,1)S(1)}, u32[]{:S(2)}, u32[]{:S(2)}) collective-permute-start(bf16[2,8,128,128]{3,2,1,0:T(8,128)(2,1)S(1)} %get-tuple-element.48), channel_id=1, source_target_pairs={{0,2},{2,0},{1,3},{3,1},{4,6},{6,4},{5,7},{7,5},{8,10},{10,8},{9,1... | collective-permute-start | bytes 1572872 | tf_op jit(solution)/shard_map/ppermute | solution.py:30
  84.2 1.5 %collective-permute-done.6 = bf16[2,8,128,128]{3,2,1,0:T(8,128)(2,1)S(1)} collective-permute-done((bf16[2,8,128,128]{3,2,1,0:T(8,128)(2,1)S(1)}, bf16[2,8,128,128]{3,2,1,0:T(8,128)(2,1)S(1)}, u32[]{:S(2)}, u32[]{:S(2)}) %collective-permute-start.6) | collective-permute-done | bytes 524320 | tf_op jit(solution)/shard_map/ppermute | solution.py:30
  85.7 0.1 shard_map.134
  85.8 16.3 %all_to_all.30.parts = bf16[16,128,128]{2,1,0:T(8,128)(2,1)S(1)} all-to-all(bf16[16,128,128]{2,1,0:T(8,128)(2,1)S(1)} %shard_map.134), channel_id=1, replica_groups=mesh['x_lo'=2,'y'=4,'z_hi'=4,'z_lo'=4,'core'=2,'x_hi'=2] {'x_hi','x_lo',..., dimensions={0} | all-to-all | bytes 1048576 | tf_op jit(solution)/shard_map/all_to_all | solution.py:437
  102.2 0.7 shard_map.135
  102.9 3.3 %all-to-all-start.3 = ((bf16[4,128,128]{2,1,0:T(8,128)(2,1)}), bf16[4,128,128]{2,1,0:T(8,128)(2,1)S(1)}, u32[]{:S(2)}, u32[]{:S(2)}) async-start(bf16[4,128,128]{2,1,0:T(8,128)(2,1)} %shard_map.135), calls=%async_computation.3 | async-start | bytes 262144 | tf_op jit(solution)/shard_map/all_to_all | solution.py:447
  106.2 3.0 %collective-permute-start.9 = (f32[8,256]{1,0:T(8,128)S(1)}, f32[8,256]{1,0:T(8,128)S(1)}, u32[]{:S(2)}, u32[]{:S(2)}) collective-permute-start(f32[8,256]{1,0:T(8,128)S(1)} %get-tuple-element.53), channel_id=1, source_target_pairs={{0,1},{1,0},{2,3},{3,2},{4,5},{5,4},{6,7},{7,6},{8,9},{9,8},{10,11... | collective-permute-start | bytes 24584 | tf_op jit(solution)/shard_map/ppermute | solution.py:30
  109.2 0.1 pad_add_fusion.place
  109.3 1.6 %all-to-all-done.3.parts = bf16[4,128,128]{2,1,0:T(8,128)(2,1)S(1)} async-done(((bf16[4,128,128]{2,1,0:T(8,128)(2,1)}), bf16[4,128,128]{2,1,0:T(8,128)(2,1)S(1)}, u32[]{:S(2)}, u32[]{:S(2)}) %all-to-all-start.3) | async-done | bytes 131104 | tf_op jit(solution)/shard_map/all_to_all | solution.py:447
  111.0 0.7 shard_map.136
  111.6 6.6 %all-to-all-start.4 = ((bf16[4,128,128]{2,1,0:T(8,128)(2,1)}), bf16[4,128,128]{2,1,0:T(8,128)(2,1)S(1)}, u32[]{:S(2)}, u32[]{:S(2)}) async-start(bf16[4,128,128]{2,1,0:T(8,128)(2,1)} %shard_map.136), calls=%async_computation.4 | async-start | bytes 262144 | tf_op jit(solution)/shard_map/all_to_all | solution.py:447
  118.2 0.0 collective-permute-done.9
  118.2 6.6 %collective-permute-start.7 = (f32[128,256]{1,0:T(8,128)S(1)}, f32[128,256]{1,0:T(8,128)S(1)}, u32[]{:S(2)}, u32[]{:S(2)}) collective-permute-start(f32[128,256]{1,0:T(8,128)S(1)} %get-tuple-element.52), channel_id=1, source_target_pairs={{2,4},{4,2},{6,8},{8,6},{10,12},{12,10},{14,16},{16,14},{18,20},{2... | collective-permute-start | bytes 393224 | tf_op jit(solution)/shard_map/ppermute | solution.py:37
  124.8 1.9 %collective-permute-start.8 = (f32[128,256]{1,0:T(8,128)S(1)}, f32[128,256]{1,0:T(8,128)S(1)}, u32[]{:S(2)}, u32[]{:S(2)}) collective-permute-start(f32[128,256]{1,0:T(8,128)S(1)} %get-tuple-element.52), channel_id=1, source_target_pairs={{0,2},{2,0},{1,3},{3,1},{4,6},{6,4},{5,7},{7,5},{8,10},{10,8},{9,1... | collective-permute-start | bytes 393224 | tf_op jit(solution)/shard_map/ppermute | solution.py:30
  126.8 3.6 %all-to-all-done.4.parts = bf16[4,128,128]{2,1,0:T(8,128)(2,1)S(1)} async-done(((bf16[4,128,128]{2,1,0:T(8,128)(2,1)}), bf16[4,128,128]{2,1,0:T(8,128)(2,1)S(1)}, u32[]{:S(2)}, u32[]{:S(2)}) %all-to-all-start.4) | async-done | bytes 131104 | tf_op jit(solution)/shard_map/all_to_all | solution.py:447
  130.4 0.7 shard_map.137
  131.1 9.0 %all-to-all-start.5 = ((bf16[32,16,128]{2,1,0:T(8,128)(2,1)}), bf16[32,16,128]{2,1,0:T(8,128)(2,1)S(1)}, u32[]{:S(2)}, u32[]{:S(2)}) async-start(bf16[32,16,128]{2,1,0:T(8,128)(2,1)} %shard_map.137), calls=%async_computation.5 | async-start | bytes 262144 | tf_op jit(solution)/shard_map/all_to_all | solution.py:460
  140.1 0.0 collective-permute-done.7
  140.1 0.0 collective-permute-done.8
  140.1 0.7 fusion.2
  140.8 7.1 %all-to-all-done.5.parts_ref = bf16[32,16,128]{2,1,0:T(8,128)(2,1)S(1)} async-done(((bf16[32,16,128]{2,1,0:T(8,128)(2,1)}), bf16[32,16,128]{2,1,0:T(8,128)(2,1)S(1)}, u32[]{:S(2)}, u32[]{:S(2)}) %all-to-all-start.5) | async-done | bytes 131104 | tf_op jit(solution)/shard_map/all_to_all | solution.py:460
  147.9 0.0 copy-done.8
  147.9 0.0 copy-done.9
  147.9 1.3 shard_map.138
  (8 shorter events, 0.1 us)
Async XLA Ops:
  11.7 22.5 %all-to-all-start = ((bf16[16,8,768]{2,1,0:T(8,128)(2,1)}), bf16[16,8,768]{2,1,0:T(8,128)(2,1)S(1)}, u32[]{:S(2)}, u32[]{:S(2)}) async-start(bf16[16,8,768]{2,1,0:T(8,128)(2,1)} %broadcast_in_dim.38), calls=%async_computation | async-start | bytes 393216 | tf_op jit(solution)/shard_map/all_to_all | solution.py:26
  21.3 7.9 %collective-permute-start = (f32[24,256]{1,0:T(8,128)}, f32[24,256]{1,0:T(8,128)S(1)}, u32[]{:S(2)}, u32[]{:S(2)}) collective-permute-start(f32[24,256]{1,0:T(8,128)} %get-tuple-element.33.mine.refs_4_), channel_id=1, source_target_pairs={{0,1},{1,0},{2,3},{3,2},{4,5},{5,4},{6,7},{7,6},{8,9},{9,8},{10,11... | collective-permute-start | bytes 73736 | tf_op jit(solution)/shard_map/ppermute | solution.py:30
  26.0 0.9 copy-start
  26.9 0.9 copy-start.2
  27.8 0.9 copy-start.4
  29.2 0.7 copy-start.6
  30.0 3.9 %collective-permute-start.1 = (bf16[448,256]{1,0:T(8,128)(2,1)S(1)}, bf16[448,256]{1,0:T(8,128)(2,1)S(1)}, u32[]{:S(2)}, u32[]{:S(2)}) collective-permute-start(bf16[448,256]{1,0:T(8,128)(2,1)S(1)} %shard_map.132), channel_id=1, source_target_pairs={{0,2},{2,0},{1,3},{3,1},{4,6},{6,4},{5,7},{7,5},{8,10},{10,8},{9,1... | collective-permute-start | bytes 688136 | tf_op jit(solution)/shard_map/ppermute | solution.py:30
  35.5 13.0 %copy-start.10 = (bf16[128,256]{1,0:T(8,128)(2,1)S(1)}, bf16[128,256]{1,0:T(8,128)(2,1)}, u32[]{:S(2)}) copy-start(bf16[128,256]{1,0:T(8,128)(2,1)} %get-tuple-element.40) | copy-start | bytes 196612
  35.5 35.4 %copy-start.1 = (f32[1,128,256]{2,1,0:T(8,128)S(1)}, f32[1,128,256]{2,1,0:T(8,128)}, u32[]{:S(2)}) copy-start(f32[1,128,256]{2,1,0:T(8,128)} %refs_1_.4) | copy-start | bytes 393220
  35.5 35.4 %copy-start.3 = (f32[1,128,256]{2,1,0:T(8,128)S(1)}, f32[1,128,256]{2,1,0:T(8,128)}, u32[]{:S(2)}) copy-start(f32[1,128,256]{2,1,0:T(8,128)} %refs_2_.4) | copy-start | bytes 393220
  35.5 35.4 %copy-start.5 = (f32[1,128,256]{2,1,0:T(8,128)S(1)}, f32[1,128,256]{2,1,0:T(8,128)}, u32[]{:S(2)}) copy-start(f32[1,128,256]{2,1,0:T(8,128)} %refs_3_.3) | copy-start | bytes 393220
  35.5 35.4 %copy-start.7 = (f32[24,256]{1,0:T(8,128)S(1)}, f32[24,256]{1,0:T(8,128)}, u32[]{:S(2)}) copy-start(f32[24,256]{1,0:T(8,128)} %get-tuple-element.33.mine.refs_4_) | copy-start | bytes 73732
  35.5 25.3 %all-to-all-start.1 = ((bf16[8,128,768]{2,1,0:T(8,128)(2,1)}), bf16[8,128,768]{2,1,0:T(8,128)(2,1)S(1)}, u32[]{:S(2)}, u32[]{:S(2)}) async-start(bf16[8,128,768]{2,1,0:T(8,128)(2,1)} %broadcast_in_dim.39), calls=%async_computation.1 | async-start | bytes 3145728 | tf_op jit(solution)/shard_map/all_to_all | solution.py:26
  40.8 16.3 %collective-permute-start.2 = (bf16[896,256]{1,0:T(8,128)(2,1)S(1)}, bf16[896,256]{1,0:T(8,128)(2,1)S(1)}, u32[]{:S(2)}, u32[]{:S(2)}) collective-permute-start(bf16[896,256]{1,0:T(8,128)(2,1)S(1)} %pad_maximum_fusion), channel_id=1, source_target_pairs={{2,4},{4,2},{6,8},{8,6},{10,12},{12,10},{14,16},{16,14},{18,20},{2... | collective-permute-start | bytes 1376264 | tf_op jit(solution)/shard_map/ppermute | solution.py:37
  48.5 8.7 %collective-permute-start.3 = (bf16[128,256]{1,0:T(8,128)(2,1)S(1)}, bf16[128,256]{1,0:T(8,128)(2,1)S(1)}, u32[]{:S(2)}, u32[]{:S(2)}) collective-permute-start(bf16[128,256]{1,0:T(8,128)(2,1)S(1)} %copy-done.10), channel_id=1, source_target_pairs={{2,8},{6,12},{10,16},{14,20},{18,24},{22,28},{26,32},{30,36},{34,4... | collective-permute-start | bytes 196616 | tf_op jit(solution)/shard_map/ppermute | solution.py:43
  57.2 3.7 %collective-permute-start.4 = (bf16[896,256]{1,0:T(8,128)(2,1)S(1)}, bf16[896,256]{1,0:T(8,128)(2,1)S(1)}, u32[]{:S(2)}, u32[]{:S(2)}) collective-permute-start(bf16[896,256]{1,0:T(8,128)(2,1)S(1)} %collective-permute-done.2.refs_7_), channel_id=1, source_target_pairs={{0,2},{2,0},{1,3},{3,1},{4,6},{6,4},{5,7},{7,5},{8,10},{10,8},{9,1... | collective-permute-start | bytes 1376264 | tf_op jit(solution)/shard_map/ppermute | solution.py:30
  60.9 10.1 %collective-permute-start.5 = (bf16[1024,768]{1,0:T(8,128)(2,1)S(1)}, bf16[1024,768]{1,0:T(8,128)(2,1)S(1)}, u32[]{:S(2)}, u32[]{:S(2)}) collective-permute-start(bf16[1024,768]{1,0:T(8,128)(2,1)S(1)} %bitcast.14), channel_id=1, source_target_pairs={{0,2},{2,0},{1,3},{3,1},{4,6},{6,4},{5,7},{7,5},{8,10},{10,8},{9,1... | collective-permute-start | bytes 4718600 | tf_op jit(solution)/shard_map/ppermute | solution.py:30
  81.9 3.8 %collective-permute-start.6 = (bf16[2,8,128,128]{3,2,1,0:T(8,128)(2,1)S(1)}, bf16[2,8,128,128]{3,2,1,0:T(8,128)(2,1)S(1)}, u32[]{:S(2)}, u32[]{:S(2)}) collective-permute-start(bf16[2,8,128,128]{3,2,1,0:T(8,128)(2,1)S(1)} %get-tuple-element.48), channel_id=1, source_target_pairs={{0,2},{2,0},{1,3},{3,1},{4,6},{6,4},{5,7},{7,5},{8,10},{10,8},{9,1... | collective-permute-start | bytes 1572872 | tf_op jit(solution)/shard_map/ppermute | solution.py:30
  102.2 45.7 %copy-start.8 = (f32[4,256]{1,0:T(4,128)S(1)}, f32[4,256]{1,0:T(4,128)}, u32[]{:S(2)}) copy-start(f32[4,256]{1,0:T(4,128)} %w_in.1) | copy-start | bytes 12292
  102.2 45.7 %copy-start.9 = (f32[4,256]{1,0:T(4,128)S(1)}, f32[4,256]{1,0:T(4,128)}, u32[]{:S(2)}) copy-start(f32[4,256]{1,0:T(4,128)} %w_out.1) | copy-start | bytes 12292
  102.9 8.1 %all-to-all-start.3 = ((bf16[4,128,128]{2,1,0:T(8,128)(2,1)}), bf16[4,128,128]{2,1,0:T(8,128)(2,1)S(1)}, u32[]{:S(2)}, u32[]{:S(2)}) async-start(bf16[4,128,128]{2,1,0:T(8,128)(2,1)} %shard_map.135), calls=%async_computation.3 | async-start | bytes 262144 | tf_op jit(solution)/shard_map/all_to_all | solution.py:447
  106.2 12.0 %collective-permute-start.9 = (f32[8,256]{1,0:T(8,128)S(1)}, f32[8,256]{1,0:T(8,128)S(1)}, u32[]{:S(2)}, u32[]{:S(2)}) collective-permute-start(f32[8,256]{1,0:T(8,128)S(1)} %get-tuple-element.53), channel_id=1, source_target_pairs={{0,1},{1,0},{2,3},{3,2},{4,5},{5,4},{6,7},{7,6},{8,9},{9,8},{10,11... | collective-permute-start | bytes 24584 | tf_op jit(solution)/shard_map/ppermute | solution.py:30
  111.6 18.8 %all-to-all-start.4 = ((bf16[4,128,128]{2,1,0:T(8,128)(2,1)}), bf16[4,128,128]{2,1,0:T(8,128)(2,1)S(1)}, u32[]{:S(2)}, u32[]{:S(2)}) async-start(bf16[4,128,128]{2,1,0:T(8,128)(2,1)} %shard_map.136), calls=%async_computation.4 | async-start | bytes 262144 | tf_op jit(solution)/shard_map/all_to_all | solution.py:447
  118.2 21.9 %collective-permute-start.7 = (f32[128,256]{1,0:T(8,128)S(1)}, f32[128,256]{1,0:T(8,128)S(1)}, u32[]{:S(2)}, u32[]{:S(2)}) collective-permute-start(f32[128,256]{1,0:T(8,128)S(1)} %get-tuple-element.52), channel_id=1, source_target_pairs={{2,4},{4,2},{6,8},{8,6},{10,12},{12,10},{14,16},{16,14},{18,20},{2... | collective-permute-start | bytes 393224 | tf_op jit(solution)/shard_map/ppermute | solution.py:37
  124.8 15.3 %collective-permute-start.8 = (f32[128,256]{1,0:T(8,128)S(1)}, f32[128,256]{1,0:T(8,128)S(1)}, u32[]{:S(2)}, u32[]{:S(2)}) collective-permute-start(f32[128,256]{1,0:T(8,128)S(1)} %get-tuple-element.52), channel_id=1, source_target_pairs={{0,2},{2,0},{1,3},{3,1},{4,6},{6,4},{5,7},{7,5},{8,10},{10,8},{9,1... | collective-permute-start | bytes 393224 | tf_op jit(solution)/shard_map/ppermute | solution.py:30
  131.1 16.8 %all-to-all-start.5 = ((bf16[32,16,128]{2,1,0:T(8,128)(2,1)}), bf16[32,16,128]{2,1,0:T(8,128)(2,1)S(1)}, u32[]{:S(2)}, u32[]{:S(2)}) async-start(bf16[32,16,128]{2,1,0:T(8,128)(2,1)} %shard_map.137), calls=%async_computation.5 | async-start | bytes 262144 | tf_op jit(solution)/shard_map/all_to_all | solution.py:460

commit v14 on v13

--- a/solution.py
+++ b/solution.py
@@ -17,6 +17,7 @@
 Z = ("z_hi", "z_lo")
 TILE = ("x_lo", "y", "z_hi", "z_lo", "core")
 AROUND = ("x_hi", "x_lo", "y", "core")
+ACROSS = ("x_lo", "y", "core", "x_hi")
 REACH = 3
 BLOCK = 144
 
@@ -24,6 +25,28 @@
 def spread(block, axis):
     count = lax.axis_size(axis)
     return lax.all_to_all(jnp.broadcast_to(block[None], (count,) + block.shape), axis, 0, 0)
+
+
+def spread_across_x(block):
+    sizes = [lax.axis_size(axis) for axis in ACROSS]
+    lows, highs, cores = sizes[0], sizes[3], sizes[2]
+    groups = []
+    for core in range(cores):
+        for high in range(highs):
+            group = []
+            for low in range(lows):
+                side = (high + 1) % highs if core == 1 and low == 0 else high
+                for y in range(sizes[1]):
+                    group.append(((low * sizes[1] + y) * cores + core) * highs + side)
+            groups.append(group)
+    count = len(groups[0])
+    return lax.all_to_all(
+        jnp.broadcast_to(block[None], (count,) + block.shape),
+        ACROSS,
+        0,
+        0,
+        axis_index_groups=groups,
+    )
 
 
 def swapped(array, axis):
@@ -506,7 +529,7 @@
     (own,) = on_chip(pack_edges_kernel, packed, (packs, mine, other), 0)
     near = swapped(own, "core")
     half, near = lax.optimization_barrier((half, near))
-    half = spread(half, ("x_lo", "y")).reshape(-1, width)
+    half = spread_across_x(half).reshape(-1, width)
     far = swapped_between_chips(jnp.concatenate([own, near]))
     far, outer = lax.optimization_barrier((far, outer))
     beyond = swapped(far, "core")

time: 150 us -> 151 us (level)
    all_to_all x0 -> x1, starting transfers between devices: none -> 6.53 us  [spread_across_x(): lax.all_to_all(jnp.broadcast_to(block[None], (count,) + block.shape), ACR...]
    all_to_all x2 -> x1, starting transfers between devices: 14.8 us -> 9.54 us  [spread(): lax.all_to_all(jnp.broadcast_to(block[None], (count,) + block.shape), axi...]
  transfers between devices with their start and end apart: 15 -> 15, of which waited for: 9 -> 10; matrix products, arithmetic and copies ran while one was open for 1% -> 1% of each run, Pallas kernels for 1% -> 1%
where the time goes in v14:
time: 151 us; the launch traced here: 150 us
  starting transfers between devices  74.4 us (49%)
  waiting for transfers between devices  27.4 us (18%)
  blocking collectives  24.6 us (16%)
  Pallas kernels  16.8 us (11%)
  local copies, waits for them, and re-layouts  5.48 us (4%)
    ppermute x7, starting transfers between devices, swapped(): return lax.ppermute(array, axis, [(0, 1), (1, 0)])  22.8 us
    pallas_call x9, Pallas kernels, on_chip(): pl.pallas_call(body, out_shape=outs, in_specs=[pl.BlockSpec(memory_space=...  16.8 us
    all_to_all x1, blocking collectives, updated(): grads = lax.all_to_all(grads, AROUND[:-1], 0, 0)  16 us
    ppermute x2, starting transfers between devices, swapped_between_chips(): return lax.ppermute(array, TILE, pairs)  13 us
    all_to_all x2, starting transfers between devices, updated(): grads = lax.all_to_all(copies, axis, 0, 0)  10.1 us
    all_to_all x1, starting transfers between devices, spread(): lax.all_to_all(jnp.broadcast_to(block[None], (count,) + block.shape), axi...  9.54 us
    all_to_all x1, starting transfers between devices, updated(): parts = lax.all_to_all(copies, AROUND, 0, 0)  8.96 us
    all_gather x1, blocking collectives, local(): rows = lax.all_gather(rows, 'core', axis=0, tiled=True)  8.58 us
  transfers between devices with their start and end apart: 15, of which 10 were waited for; matrix products, arithmetic and copies ran while one was open for 1% of the time, Pallas kernels for 1%

profile of v14, /device:TPU:1, one launch (start us, length us, event | category | flops | bytes accessed | tf_op | source)
XLA Modules:
  0.0 150.4 jit_solution(14172297618960571282)
XLA Ops:
  0.6 1.8 %shard_map.130 = (bf16[4,1536]{1,0:T(4,128)(2,1)}, f32[24,256]{1,0:T(8,128)}, bf16[128,256]{1,0:T(8,128)(2,1)}) custom-call(f32[1,128,256]{2,1,0:T(8,128)} %refs_1_.4, f32[1,128,256]{2,1,0:T(8,128)} %refs_2_.4, f32[1,128,256]{2,1,0:T(8,128)} %refs_3_.3, s32[1,128]{1,0:T(1,128)} %refs_3_.2, s32[1,64]{1,0:T(1,128)} %bitcast.20, s32[1,64]{1,0:T(1,128)} %bitcast.21, ...), custom_call_target="tpu_custom_call" | custom-call | bytes 513536 | tf_op jit(solution)/shard_map/pallas_call | solution.py:400
  2.4 8.6 %all-gather = bf16[2,4,1536]{2,1,0:T(4,128)(2,1)S(1)} all-gather(bf16[1,4,1536]{2,1,0:T(4,128)(2,1)} %bitcast.19), channel_id=1, replica_groups=mesh['x_lo'=2,'y'=4,'z_hi'=4,'z_lo'=4,'core'=2,'x_hi'=2] {'core'}, dimensions={0}, use_global_device_ids=true | all-gather | bytes 36864 | tf_op jit(solution)/shard_map/all_gather | solution.py:520
  11.1 0.7 broadcast_in_dim.38
  11.7 9.5 %all-to-all-start = ((bf16[16,8,768]{2,1,0:T(8,128)(2,1)}), bf16[16,8,768]{2,1,0:T(8,128)(2,1)S(1)}, u32[]{:S(2)}, u32[]{:S(2)}) async-start(bf16[16,8,768]{2,1,0:T(8,128)(2,1)} %broadcast_in_dim.38), calls=%async_computation | async-start | bytes 393216 | tf_op jit(solution)/shard_map/all_to_all | solution.py:27
  21.3 4.7 %collective-permute-start = (f32[24,256]{1,0:T(8,128)}, f32[24,256]{1,0:T(8,128)S(1)}, u32[]{:S(2)}, u32[]{:S(2)}) collective-permute-start(f32[24,256]{1,0:T(8,128)} %get-tuple-element.33.mine.refs_4_), channel_id=1, source_target_pairs={{0,1},{1,0},{2,3},{3,2},{4,5},{5,4},{6,7},{7,6},{8,9},{9,8},{10,11... | collective-permute-start | bytes 73736 | tf_op jit(solution)/shard_map/ppermute | solution.py:53
  26.0 0.0 copy-start
  26.0 0.9 copy-done
  26.9 0.0 copy-start.2
  26.9 0.9 copy-done.2
  27.8 0.0 copy-start.4
  27.8 0.9 copy-done.4
  28.7 0.5 shard_map.131.fields
  29.2 0.0 collective-permute-done.other.refs_5_
  29.2 0.0 copy-start.6
  29.2 0.7 copy-done.6
  29.9 0.1 shard_map.132
  30.0 2.8 %collective-permute-start.1 = (bf16[448,256]{1,0:T(8,128)(2,1)S(1)}, bf16[448,256]{1,0:T(8,128)(2,1)S(1)}, u32[]{:S(2)}, u32[]{:S(2)}) collective-permute-start(bf16[448,256]{1,0:T(8,128)(2,1)S(1)} %shard_map.132), channel_id=1, source_target_pairs={{0,2},{2,0},{1,3},{3,1},{4,6},{6,4},{5,7},{7,5},{8,10},{10,8},{9,1... | collective-permute-start | bytes 688136 | tf_op jit(solution)/shard_map/ppermute | solution.py:53
  32.8 1.1 collective-permute-done.1.refs_6_
  33.9 0.3 all-to-all-done
  34.2 1.3 broadcast_in_dim.39
  35.5 0.0 copy-start.10
  35.5 0.0 copy-start.1
  35.5 0.0 copy-start.3
  35.5 0.0 copy-start.7
  35.5 6.5 %all-to-all-start.1 = ((bf16[8,128,768]{2,1,0:T(8,128)(2,1)}), bf16[8,128,768]{2,1,0:T(8,128)(2,1)S(1)}, u32[]{:S(2)}, u32[]{:S(2)}) async-start(bf16[8,128,768]{2,1,0:T(8,128)(2,1)} %broadcast_in_dim.39), calls=%async_computation.1 | async-start | bytes 3145728 | tf_op jit(solution)/shard_map/all_to_all | solution.py:43
  42.1 6.4 %collective-permute-start.2 = (bf16[896,256]{1,0:T(8,128)(2,1)S(1)}, bf16[896,256]{1,0:T(8,128)(2,1)S(1)}, u32[]{:S(2)}, u32[]{:S(2)}) collective-permute-start(bf16[896,256]{1,0:T(8,128)(2,1)S(1)} %pad_maximum_fusion), channel_id=1, source_target_pairs={{2,4},{4,2},{6,8},{8,6},{10,12},{12,10},{14,16},{16,14},{18,20},{2... | collective-permute-start | bytes 1376264 | tf_op jit(solution)/shard_map/ppermute | solution.py:60
  48.5 0.0 copy-done.10
  48.5 3.4 %collective-permute-start.3 = (bf16[128,256]{1,0:T(8,128)(2,1)S(1)}, bf16[128,256]{1,0:T(8,128)(2,1)S(1)}, u32[]{:S(2)}, u32[]{:S(2)}) collective-permute-start(bf16[128,256]{1,0:T(8,128)(2,1)S(1)} %copy-done.10), channel_id=1, source_target_pairs={{2,8},{6,12},{10,16},{14,20},{18,24},{22,28},{26,32},{30,36},{34,4... | collective-permute-start | bytes 196616 | tf_op jit(solution)/shard_map/ppermute | solution.py:66
  51.9 5.9 %collective-permute-done.3.refs_9_ = bf16[128,256]{1,0:T(8,128)(2,1)S(1)} collective-permute-done((bf16[128,256]{1,0:T(8,128)(2,1)S(1)}, bf16[128,256]{1,0:T(8,128)(2,1)S(1)}, u32[]{:S(2)}, u32[]{:S(2)}) %collective-permute-start.3) | collective-permute-done | bytes 65568 | tf_op jit(solution)/shard_map/ppermute | solution.py:66
  57.8 0.0 collective-permute-done.2.refs_7_
  57.8 1.9 %collective-permute-start.4 = (bf16[896,256]{1,0:T(8,128)(2,1)S(1)}, bf16[896,256]{1,0:T(8,128)(2,1)S(1)}, u32[]{:S(2)}, u32[]{:S(2)}) collective-permute-start(bf16[896,256]{1,0:T(8,128)(2,1)S(1)} %collective-permute-done.2.refs_7_), channel_id=1, source_target_pairs={{0,2},{2,0},{1,3},{3,1},{4,6},{6,4},{5,7},{7,5},{8,10},{10,8},{9,1... | collective-permute-start | bytes 1376264 | tf_op jit(solution)/shard_map/ppermute | solution.py:53
  59.7 1.8 %collective-permute-done.4.refs_8_ = bf16[896,256]{1,0:T(8,128)(2,1)S(1)} collective-permute-done((bf16[896,256]{1,0:T(8,128)(2,1)S(1)}, bf16[896,256]{1,0:T(8,128)(2,1)S(1)}, u32[]{:S(2)}, u32[]{:S(2)}) %collective-permute-start.4) | collective-permute-done | bytes 458784 | tf_op jit(solution)/shard_map/ppermute | solution.py:53
  61.5 1.4 all-to-all-done.1
  62.9 6.3 %collective-permute-start.5 = (bf16[1024,768]{1,0:T(8,128)(2,1)S(1)}, bf16[1024,768]{1,0:T(8,128)(2,1)S(1)}, u32[]{:S(2)}, u32[]{:S(2)}) collective-permute-start(bf16[1024,768]{1,0:T(8,128)(2,1)S(1)} %bitcast.14), channel_id=1, source_target_pairs={{0,2},{2,0},{1,3},{3,1},{4,6},{6,4},{5,7},{7,5},{8,10},{10,8},{9,1... | collective-permute-start | bytes 4718600 | tf_op jit(solution)/shard_map/ppermute | solution.py:53
  69.2 3.0 %collective-permute-done.5.refs_11_ = bf16[1024,768]{1,0:T(8,128)(2,1)S(1)} collective-permute-done((bf16[1024,768]{1,0:T(8,128)(2,1)S(1)}, bf16[1024,768]{1,0:T(8,128)(2,1)S(1)}, u32[]{:S(2)}, u32[]{:S(2)}) %collective-permute-start.5) | collective-permute-done | bytes 1572896 | tf_op jit(solution)/shard_map/ppermute | solution.py:53
  72.2 0.0 copy-done.1
  72.2 0.0 copy-done.3
  72.2 0.0 copy-done.5
  72.2 0.0 copy-done.7
  72.2 10.9 %shard_map.133 = (f32[128,256]{1,0:T(8,128)S(1)}, f32[128,256]{1,0:T(8,128)S(1)}, f32[8,256]{1,0:T(8,128)S(1)}, bf16[2,8,128,128]{3,2,1,0:T(8,128)(2,1)S(1)}, bf16[2,8,128,128]{3,2,1,0:T(8,128)(2,1)S(1)}) custom-call(s32[1]{0:T(128)} %bitcast.refs_0_, f32[1,128,256]{2,1,0:T(8,128)S(1)} %copy-done.1, f32[1,128,256]{2,1,0:T(8,128)S(1)} %copy-done.3, ...), custom_call_target="tpu_custom_call" | custom-call | flops 8053063680 | bytes 6119428 | tf_op jit(solution)/shard_map/pallas_call | solution.py:400
  83.1 2.3 %collective-permute-start.6 = (bf16[2,8,128,128]{3,2,1,0:T(8,128)(2,1)S(1)}, bf16[2,8,128,128]{3,2,1,0:T(8,128)(2,1)S(1)}, u32[]{:S(2)}, u32[]{:S(2)}) collective-permute-start(bf16[2,8,128,128]{3,2,1,0:T(8,128)(2,1)S(1)} %get-tuple-element.48), channel_id=1, source_target_pairs={{0,2},{2,0},{1,3},{3,1},{4,6},{6,4},{5,7},{7,5},{8,10},{10,8},{9,1... | collective-permute-start | bytes 1572872 | tf_op jit(solution)/shard_map/ppermute | solution.py:53
  85.4 1.5 %collective-permute-done.6 = bf16[2,8,128,128]{3,2,1,0:T(8,128)(2,1)S(1)} collective-permute-done((bf16[2,8,128,128]{3,2,1,0:T(8,128)(2,1)S(1)}, bf16[2,8,128,128]{3,2,1,0:T(8,128)(2,1)S(1)}, u32[]{:S(2)}, u32[]{:S(2)}) %collective-permute-start.6) | collective-permute-done | bytes 524320 | tf_op jit(solution)/shard_map/ppermute | solution.py:53
  87.0 0.1 shard_map.134
  87.1 16.0 %all_to_all.30.parts = bf16[16,128,128]{2,1,0:T(8,128)(2,1)S(1)} all-to-all(bf16[16,128,128]{2,1,0:T(8,128)(2,1)S(1)} %shard_map.134), channel_id=1, replica_groups=mesh['x_lo'=2,'y'=4,'z_hi'=4,'z_lo'=4,'core'=2,'x_hi'=2] {'x_hi','x_lo',..., dimensions={0} | all-to-all | bytes 1048576 | tf_op jit(solution)/shard_map/all_to_all | solution.py:460
  103.1 0.7 shard_map.135
  103.9 3.3 %all-to-all-start.3 = ((bf16[4,128,128]{2,1,0:T(8,128)(2,1)}), bf16[4,128,128]{2,1,0:T(8,128)(2,1)S(1)}, u32[]{:S(2)}, u32[]{:S(2)}) async-start(bf16[4,128,128]{2,1,0:T(8,128)(2,1)} %shard_map.135), calls=%async_computation.3 | async-start | bytes 262144 | tf_op jit(solution)/shard_map/all_to_all | solution.py:470
  107.2 3.0 %collective-permute-start.9 = (f32[8,256]{1,0:T(8,128)S(1)}, f32[8,256]{1,0:T(8,128)S(1)}, u32[]{:S(2)}, u32[]{:S(2)}) collective-permute-start(f32[8,256]{1,0:T(8,128)S(1)} %get-tuple-element.53), channel_id=1, source_target_pairs={{0,1},{1,0},{2,3},{3,2},{4,5},{5,4},{6,7},{7,6},{8,9},{9,8},{10,11... | collective-permute-start | bytes 24584 | tf_op jit(solution)/shard_map/ppermute | solution.py:53
  110.2 0.1 pad_add_fusion.place
  110.3 1.6 %all-to-all-done.3.parts = bf16[4,128,128]{2,1,0:T(8,128)(2,1)S(1)} async-done(((bf16[4,128,128]{2,1,0:T(8,128)(2,1)}), bf16[4,128,128]{2,1,0:T(8,128)(2,1)S(1)}, u32[]{:S(2)}, u32[]{:S(2)}) %all-to-all-start.3) | async-done | bytes 131104 | tf_op jit(solution)/shard_map/all_to_all | solution.py:470
  111.9 0.7 shard_map.136
  112.6 6.8 %all-to-all-start.4 = ((bf16[4,128,128]{2,1,0:T(8,128)(2,1)}), bf16[4,128,128]{2,1,0:T(8,128)(2,1)S(1)}, u32[]{:S(2)}, u32[]{:S(2)}) async-start(bf16[4,128,128]{2,1,0:T(8,128)(2,1)} %shard_map.136), calls=%async_computation.4 | async-start | bytes 262144 | tf_op jit(solution)/shard_map/all_to_all | solution.py:470
  119.4 0.0 collective-permute-done.9
  119.4 6.6 %collective-permute-start.7 = (f32[128,256]{1,0:T(8,128)S(1)}, f32[128,256]{1,0:T(8,128)S(1)}, u32[]{:S(2)}, u32[]{:S(2)}) collective-permute-start(f32[128,256]{1,0:T(8,128)S(1)} %get-tuple-element.52), channel_id=1, source_target_pairs={{2,4},{4,2},{6,8},{8,6},{10,12},{12,10},{14,16},{16,14},{18,20},{2... | collective-permute-start | bytes 393224 | tf_op jit(solution)/shard_map/ppermute | solution.py:60
  126.0 1.9 %collective-permute-start.8 = (f32[128,256]{1,0:T(8,128)S(1)}, f32[128,256]{1,0:T(8,128)S(1)}, u32[]{:S(2)}, u32[]{:S(2)}) collective-permute-start(f32[128,256]{1,0:T(8,128)S(1)} %get-tuple-element.52), channel_id=1, source_target_pairs={{0,2},{2,0},{1,3},{3,1},{4,6},{6,4},{5,7},{7,5},{8,10},{10,8},{9,1... | collective-permute-start | bytes 393224 | tf_op jit(solution)/shard_map/ppermute | solution.py:53
  128.0 3.6 %all-to-all-done.4.parts = bf16[4,128,128]{2,1,0:T(8,128)(2,1)S(1)} async-done(((bf16[4,128,128]{2,1,0:T(8,128)(2,1)}), bf16[4,128,128]{2,1,0:T(8,128)(2,1)S(1)}, u32[]{:S(2)}, u32[]{:S(2)}) %all-to-all-start.4) | async-done | bytes 131104 | tf_op jit(solution)/shard_map/all_to_all | solution.py:470
  131.6 0.7 shard_map.137
  132.3 9.0 %all-to-all-start.5 = ((bf16[32,16,128]{2,1,0:T(8,128)(2,1)}), bf16[32,16,128]{2,1,0:T(8,128)(2,1)S(1)}, u32[]{:S(2)}, u32[]{:S(2)}) async-start(bf16[32,16,128]{2,1,0:T(8,128)(2,1)} %shard_map.137), calls=%async_computation.5 | async-start | bytes 262144 | tf_op jit(solution)/shard_map/all_to_all | solution.py:483
  141.3 0.0 collective-permute-done.7
  141.3 0.0 collective-permute-done.8
  141.3 0.7 fusion.2
  142.0 7.1 %all-to-all-done.5.parts_ref = bf16[32,16,128]{2,1,0:T(8,128)(2,1)S(1)} async-done(((bf16[32,16,128]{2,1,0:T(8,128)(2,1)}), bf16[32,16,128]{2,1,0:T(8,128)(2,1)S(1)}, u32[]{:S(2)}, u32[]{:S(2)}) %all-to-all-start.5) | async-done | bytes 131104 | tf_op jit(solution)/shard_map/all_to_all | solution.py:483
  149.1 0.0 copy-done.8
  149.1 0.0 copy-done.9
  149.1 1.3 shard_map.138
  (8 shorter events, 0.1 us)
Async XLA Ops:
  11.7 22.5 %all-to-all-start = ((bf16[16,8,768]{2,1,0:T(8,128)(2,1)}), bf16[16,8,768]{2,1,0:T(8,128)(2,1)S(1)}, u32[]{:S(2)}, u32[]{:S(2)}) async-start(bf16[16,8,768]{2,1,0:T(8,128)(2,1)} %broadcast_in_dim.38), calls=%async_computation | async-start | bytes 393216 | tf_op jit(solution)/shard_map/all_to_all | solution.py:27
  21.3 7.9 %collective-permute-start = (f32[24,256]{1,0:T(8,128)}, f32[24,256]{1,0:T(8,128)S(1)}, u32[]{:S(2)}, u32[]{:S(2)}) collective-permute-start(f32[24,256]{1,0:T(8,128)} %get-tuple-element.33.mine.refs_4_), channel_id=1, source_target_pairs={{0,1},{1,0},{2,3},{3,2},{4,5},{5,4},{6,7},{7,6},{8,9},{9,8},{10,11... | collective-permute-start | bytes 73736 | tf_op jit(solution)/shard_map/ppermute | solution.py:53
  26.0 0.9 copy-start
  26.9 0.9 copy-start.2
  27.8 0.9 copy-start.4
  29.2 0.7 copy-start.6
  30.0 3.9 %collective-permute-start.1 = (bf16[448,256]{1,0:T(8,128)(2,1)S(1)}, bf16[448,256]{1,0:T(8,128)(2,1)S(1)}, u32[]{:S(2)}, u32[]{:S(2)}) collective-permute-start(bf16[448,256]{1,0:T(8,128)(2,1)S(1)} %shard_map.132), channel_id=1, source_target_pairs={{0,2},{2,0},{1,3},{3,1},{4,6},{6,4},{5,7},{7,5},{8,10},{10,8},{9,1... | collective-permute-start | bytes 688136 | tf_op jit(solution)/shard_map/ppermute | solution.py:53
  35.5 13.0 %copy-start.10 = (bf16[128,256]{1,0:T(8,128)(2,1)S(1)}, bf16[128,256]{1,0:T(8,128)(2,1)}, u32[]{:S(2)}) copy-start(bf16[128,256]{1,0:T(8,128)(2,1)} %get-tuple-element.40) | copy-start | bytes 196612
  35.5 36.7 %copy-start.1 = (f32[1,128,256]{2,1,0:T(8,128)S(1)}, f32[1,128,256]{2,1,0:T(8,128)}, u32[]{:S(2)}) copy-start(f32[1,128,256]{2,1,0:T(8,128)} %refs_1_.4) | copy-start | bytes 393220
  35.5 36.7 %copy-start.3 = (f32[1,128,256]{2,1,0:T(8,128)S(1)}, f32[1,128,256]{2,1,0:T(8,128)}, u32[]{:S(2)}) copy-start(f32[1,128,256]{2,1,0:T(8,128)} %refs_2_.4) | copy-start | bytes 393220
  35.5 36.7 %copy-start.5 = (f32[1,128,256]{2,1,0:T(8,128)S(1)}, f32[1,128,256]{2,1,0:T(8,128)}, u32[]{:S(2)}) copy-start(f32[1,128,256]{2,1,0:T(8,128)} %refs_3_.3) | copy-start | bytes 393220
  35.5 36.7 %copy-start.7 = (f32[24,256]{1,0:T(8,128)S(1)}, f32[24,256]{1,0:T(8,128)}, u32[]{:S(2)}) copy-start(f32[24,256]{1,0:T(8,128)} %get-tuple-element.33.mine.refs_4_) | copy-start | bytes 73732
  35.5 27.4 %all-to-all-start.1 = ((bf16[8,128,768]{2,1,0:T(8,128)(2,1)}), bf16[8,128,768]{2,1,0:T(8,128)(2,1)S(1)}, u32[]{:S(2)}, u32[]{:S(2)}) async-start(bf16[8,128,768]{2,1,0:T(8,128)(2,1)} %broadcast_in_dim.39), calls=%async_computation.1 | async-start | bytes 3145728 | tf_op jit(solution)/shard_map/all_to_all | solution.py:43
  42.1 15.7 %collective-permute-start.2 = (bf16[896,256]{1,0:T(8,128)(2,1)S(1)}, bf16[896,256]{1,0:T(8,128)(2,1)S(1)}, u32[]{:S(2)}, u32[]{:S(2)}) collective-permute-start(bf16[896,256]{1,0:T(8,128)(2,1)S(1)} %pad_maximum_fusion), channel_id=1, source_target_pairs={{2,4},{4,2},{6,8},{8,6},{10,12},{12,10},{14,16},{16,14},{18,20},{2... | collective-permute-start | bytes 1376264 | tf_op jit(solution)/shard_map/ppermute | solution.py:60
  48.5 9.3 %collective-permute-start.3 = (bf16[128,256]{1,0:T(8,128)(2,1)S(1)}, bf16[128,256]{1,0:T(8,128)(2,1)S(1)}, u32[]{:S(2)}, u32[]{:S(2)}) collective-permute-start(bf16[128,256]{1,0:T(8,128)(2,1)S(1)} %copy-done.10), channel_id=1, source_target_pairs={{2,8},{6,12},{10,16},{14,20},{18,24},{22,28},{26,32},{30,36},{34,4... | collective-permute-start | bytes 196616 | tf_op jit(solution)/shard_map/ppermute | solution.py:66
  57.8 3.7 %collective-permute-start.4 = (bf16[896,256]{1,0:T(8,128)(2,1)S(1)}, bf16[896,256]{1,0:T(8,128)(2,1)S(1)}, u32[]{:S(2)}, u32[]{:S(2)}) collective-permute-start(bf16[896,256]{1,0:T(8,128)(2,1)S(1)} %collective-permute-done.2.refs_7_), channel_id=1, source_target_pairs={{0,2},{2,0},{1,3},{3,1},{4,6},{6,4},{5,7},{7,5},{8,10},{10,8},{9,1... | collective-permute-start | bytes 1376264 | tf_op jit(solution)/shard_map/ppermute | solution.py:53
  62.9 9.3 %collective-permute-start.5 = (bf16[1024,768]{1,0:T(8,128)(2,1)S(1)}, bf16[1024,768]{1,0:T(8,128)(2,1)S(1)}, u32[]{:S(2)}, u32[]{:S(2)}) collective-permute-start(bf16[1024,768]{1,0:T(8,128)(2,1)S(1)} %bitcast.14), channel_id=1, source_target_pairs={{0,2},{2,0},{1,3},{3,1},{4,6},{6,4},{5,7},{7,5},{8,10},{10,8},{9,1... | collective-permute-start | bytes 4718600 | tf_op jit(solution)/shard_map/ppermute | solution.py:53
  83.1 3.8 %collective-permute-start.6 = (bf16[2,8,128,128]{3,2,1,0:T(8,128)(2,1)S(1)}, bf16[2,8,128,128]{3,2,1,0:T(8,128)(2,1)S(1)}, u32[]{:S(2)}, u32[]{:S(2)}) collective-permute-start(bf16[2,8,128,128]{3,2,1,0:T(8,128)(2,1)S(1)} %get-tuple-element.48), channel_id=1, source_target_pairs={{0,2},{2,0},{1,3},{3,1},{4,6},{6,4},{5,7},{7,5},{8,10},{10,8},{9,1... | collective-permute-start | bytes 1572872 | tf_op jit(solution)/shard_map/ppermute | solution.py:53
  103.1 46.0 %copy-start.8 = (f32[4,256]{1,0:T(4,128)S(1)}, f32[4,256]{1,0:T(4,128)}, u32[]{:S(2)}) copy-start(f32[4,256]{1,0:T(4,128)} %w_in.1) | copy-start | bytes 12292
  103.1 46.0 %copy-start.9 = (f32[4,256]{1,0:T(4,128)S(1)}, f32[4,256]{1,0:T(4,128)}, u32[]{:S(2)}) copy-start(f32[4,256]{1,0:T(4,128)} %w_out.1) | copy-start | bytes 12292
  103.9 8.1 %all-to-all-start.3 = ((bf16[4,128,128]{2,1,0:T(8,128)(2,1)}), bf16[4,128,128]{2,1,0:T(8,128)(2,1)S(1)}, u32[]{:S(2)}, u32[]{:S(2)}) async-start(bf16[4,128,128]{2,1,0:T(8,128)(2,1)} %shard_map.135), calls=%async_computation.3 | async-start | bytes 262144 | tf_op jit(solution)/shard_map/all_to_all | solution.py:470
  107.2 12.2 %collective-permute-start.9 = (f32[8,256]{1,0:T(8,128)S(1)}, f32[8,256]{1,0:T(8,128)S(1)}, u32[]{:S(2)}, u32[]{:S(2)}) collective-permute-start(f32[8,256]{1,0:T(8,128)S(1)} %get-tuple-element.53), channel_id=1, source_target_pairs={{0,1},{1,0},{2,3},{3,2},{4,5},{5,4},{6,7},{7,6},{8,9},{9,8},{10,11... | collective-permute-start | bytes 24584 | tf_op jit(solution)/shard_map/ppermute | solution.py:53
  112.6 19.0 %all-to-all-start.4 = ((bf16[4,128,128]{2,1,0:T(8,128)(2,1)}), bf16[4,128,128]{2,1,0:T(8,128)(2,1)S(1)}, u32[]{:S(2)}, u32[]{:S(2)}) async-start(bf16[4,128,128]{2,1,0:T(8,128)(2,1)} %shard_map.136), calls=%async_computation.4 | async-start | bytes 262144 | tf_op jit(solution)/shard_map/all_to_all | solution.py:470
  119.4 21.9 %collective-permute-start.7 = (f32[128,256]{1,0:T(8,128)S(1)}, f32[128,256]{1,0:T(8,128)S(1)}, u32[]{:S(2)}, u32[]{:S(2)}) collective-permute-start(f32[128,256]{1,0:T(8,128)S(1)} %get-tuple-element.52), channel_id=1, source_target_pairs={{2,4},{4,2},{6,8},{8,6},{10,12},{12,10},{14,16},{16,14},{18,20},{2... | collective-permute-start | bytes 393224 | tf_op jit(solution)/shard_map/ppermute | solution.py:60
  126.0 15.3 %collective-permute-start.8 = (f32[128,256]{1,0:T(8,128)S(1)}, f32[128,256]{1,0:T(8,128)S(1)}, u32[]{:S(2)}, u32[]{:S(2)}) collective-permute-start(f32[128,256]{1,0:T(8,128)S(1)} %get-tuple-element.52), channel_id=1, source_target_pairs={{0,2},{2,0},{1,3},{3,1},{4,6},{6,4},{5,7},{7,5},{8,10},{10,8},{9,1... | collective-permute-start | bytes 393224 | tf_op jit(solution)/shard_map/ppermute | solution.py:53
  132.3 16.8 %all-to-all-start.5 = ((bf16[32,16,128]{2,1,0:T(8,128)(2,1)}), bf16[32,16,128]{2,1,0:T(8,128)(2,1)S(1)}, u32[]{:S(2)}, u32[]{:S(2)}) async-start(bf16[32,16,128]{2,1,0:T(8,128)(2,1)} %shard_map.137), calls=%async_computation.5 | async-start | bytes 262144 | tf_op jit(solution)/shard_map/all_to_all | solution.py:483

commit v15 on v14

--- a/solution.py
+++ b/solution.py
@@ -169,6 +169,14 @@
     pack[3 * BLOCK :] = jnp.concatenate(rest).astype(jnp.bfloat16)
 
 
+def behind_kernel(far, behind):
+    pack = 3 * BLOCK + 16
+    behind[:pack] = far[:pack]
+    total = far[pack : pack + BLOCK].astype(jnp.float32)
+    total = total + far[pack + BLOCK : pack + 2 * BLOCK].astype(jnp.float32)
+    behind[pack:] = total.astype(jnp.bfloat16)
+
+
 def whole_kernel(
     observations,
     core,
@@ -262,9 +270,8 @@
     own.append(gate)
     beside, beside_rest = zip(unpack(near, 0), unpack(far, 0))
     second = [unpack(beyond, 0)[0], unpack(far, pack)[0]]
-    third = [unpack(beyond, pack)[0]]
     third = [
-        third[0][0] + third[0][1],
+        beyond[pack : pack + BLOCK].astype(jnp.float32)[:length],
         jnp.concatenate(
             [outer[...].astype(jnp.float32), jnp.zeros((length - cells, features), jnp.float32)]
         ),
@@ -528,11 +535,15 @@
     (packs,) = on_chip(pack_fields_kernel, packed, fields, 0, fetched=3)
     (own,) = on_chip(pack_edges_kernel, packed, (packs, mine, other), 0)
     near = swapped(own, "core")
+    far = swapped_between_chips(jnp.concatenate([own, near]))
     half, near = lax.optimization_barrier((half, near))
     half = spread_across_x(half).reshape(-1, width)
-    far = swapped_between_chips(jnp.concatenate([own, near]))
     far, outer = lax.optimization_barrier((far, outer))
-    beyond = swapped(far, "core")
+    pack = 3 * BLOCK + 16
+    (beyond,) = on_chip(
+        behind_kernel, outs(((pack + BLOCK, features), jnp.bfloat16)), (far,), 10**10
+    )
+    beyond = swapped(beyond, "core")
     half, far, beyond = lax.optimization_barrier((half, far, beyond))
     hidden_units = half.shape[0]
     blocks = lax.axis_size(("x_lo", "y"))

time: 151 us -> 151 us (level)
  waiting for transfers between devices: 27.4 us -> 32.3 us
  starting transfers between devices: 74.4 us -> 70.5 us
    all_to_all x1, waiting for transfers between devices: 1.4 us -> 10 us  [spread_across_x(): lax.all_to_all(jnp.broadcast_to(block[None], (count,) + block.shape), ACR...]
    ppermute x1, waiting for transfers between devices: 5.91 us -> 2.34 us  [swapped_three_apart(): lax.ppermute(array, TILE, pairs + [(after, row) for row, after in pairs])]
    ppermute x7, starting transfers between devices: 22.8 us -> 19.3 us  [swapped(): return lax.ppermute(array, axis, [(0, 1), (1, 0)])]
    ppermute x2, starting transfers between devices: 13 us -> 10.1 us  [swapped_between_chips(): return lax.ppermute(array, TILE, pairs)]
    all_to_all x2, starting transfers between devices: 10.1 us -> 12.9 us  [updated(): grads = lax.all_to_all(copies, axis, 0, 0)]
    pallas_call x9 -> x10, Pallas kernels: 16.8 us -> 16.8 us  [on_chip(): pl.pallas_call(body, out_shape=outs, in_specs=[pl.BlockSpec(memory_space=...]
  transfers between devices with their start and end apart: 15 -> 15, of which waited for: 10 -> 9; matrix products, arithmetic and copies ran while one was open for 1% -> 1% of each run, Pallas kernels for 1% -> 1%
where the time goes in v15:
time: 151 us
  starting transfers between devices  70.5 us (47%)
  waiting for transfers between devices  32.3 us (21%)
  blocking collectives  23.7 us (16%)
  Pallas kernels  16.8 us (11%)
  local copies, waits for them, and re-layouts  5.49 us (4%)
    ppermute x7, starting transfers between devices, swapped(): return lax.ppermute(array, axis, [(0, 1), (1, 0)])  19.3 us
    pallas_call x10, Pallas kernels, on_chip(): pl.pallas_call(body, out_shape=outs, in_specs=[pl.BlockSpec(memory_space=...  16.8 us
    all_to_all x1, blocking collectives, updated(): grads = lax.all_to_all(grads, AROUND[:-1], 0, 0)  15.1 us
    all_to_all x2, starting transfers between devices, updated(): grads = lax.all_to_all(copies, axis, 0, 0)  12.9 us
    ppermute x2, starting transfers between devices, swapped_between_chips(): return lax.ppermute(array, TILE, pairs)  10.1 us
    all_to_all x1, waiting for transfers between devices, spread_across_x(): lax.all_to_all(jnp.broadcast_to(block[None], (count,) + block.shape), ACR...  10 us
    all_to_all x1, starting transfers between devices, spread(): lax.all_to_all(jnp.broadcast_to(block[None], (count,) + block.shape), axi...  9.54 us
    all_gather x1, blocking collectives, local(): rows = lax.all_gather(rows, 'core', axis=0, tiled=True)  8.58 us
  transfers between devices with their start and end apart: 15, of which 9 were waited for; matrix products, arithmetic and copies ran while one was open for 1% of the time, Pallas kernels for 1%

profile of v15, /device:TPU:1, one launch (start us, length us, event | category | flops | bytes accessed | tf_op | source)
XLA Modules:
  0.0 150.5 jit_solution(8528759262865319787)
XLA Ops:
  0.6 1.8 %shard_map.130 = (bf16[4,1536]{1,0:T(4,128)(2,1)}, f32[24,256]{1,0:T(8,128)}, bf16[128,256]{1,0:T(8,128)(2,1)}) custom-call(f32[1,128,256]{2,1,0:T(8,128)} %refs_1_.4, f32[1,128,256]{2,1,0:T(8,128)} %refs_2_.4, f32[1,128,256]{2,1,0:T(8,128)} %refs_3_.3, s32[1,128]{1,0:T(1,128)} %refs_3_.2, s32[1,64]{1,0:T(1,128)} %bitcast.20, s32[1,64]{1,0:T(1,128)} %bitcast.21, ...), custom_call_target="tpu_custom_call" | custom-call | bytes 513536 | tf_op jit(solution)/shard_map/pallas_call | solution.py:407
  2.4 8.6 %all-gather = bf16[2,4,1536]{2,1,0:T(4,128)(2,1)S(1)} all-gather(bf16[1,4,1536]{2,1,0:T(4,128)(2,1)} %bitcast.19), channel_id=1, replica_groups=mesh['x_lo'=2,'y'=4,'z_hi'=4,'z_lo'=4,'core'=2,'x_hi'=2] {'core'}, dimensions={0}, use_global_device_ids=true | all-gather | bytes 36864 | tf_op jit(solution)/shard_map/all_gather | solution.py:527
  11.1 0.7 broadcast_in_dim.38
  11.7 9.5 %all-to-all-start = ((bf16[16,8,768]{2,1,0:T(8,128)(2,1)}), bf16[16,8,768]{2,1,0:T(8,128)(2,1)S(1)}, u32[]{:S(2)}, u32[]{:S(2)}) async-start(bf16[16,8,768]{2,1,0:T(8,128)(2,1)} %broadcast_in_dim.38), calls=%async_computation | async-start | bytes 393216 | tf_op jit(solution)/shard_map/all_to_all | solution.py:27
  21.3 4.7 %collective-permute-start = (f32[24,256]{1,0:T(8,128)}, f32[24,256]{1,0:T(8,128)S(1)}, u32[]{:S(2)}, u32[]{:S(2)}) collective-permute-start(f32[24,256]{1,0:T(8,128)} %get-tuple-element.33.mine.refs_4_), channel_id=1, source_target_pairs={{0,1},{1,0},{2,3},{3,2},{4,5},{5,4},{6,7},{7,6},{8,9},{9,8},{10,11... | collective-permute-start | bytes 73736 | tf_op jit(solution)/shard_map/ppermute | solution.py:53
  26.0 0.0 copy-start
  26.0 0.9 copy-done
  26.9 0.0 copy-start.2
  26.9 0.9 copy-done.2
  27.8 0.0 copy-start.4
  27.8 0.9 copy-done.4
  28.7 0.5 shard_map.131.fields
  29.2 0.0 collective-permute-done.other.refs_5_
  29.2 0.0 copy-start.6
  29.2 0.7 copy-done.6
  29.9 0.1 shard_map.132
  30.0 2.8 %collective-permute-start.1 = (bf16[448,256]{1,0:T(8,128)(2,1)S(1)}, bf16[448,256]{1,0:T(8,128)(2,1)S(1)}, u32[]{:S(2)}, u32[]{:S(2)}) collective-permute-start(bf16[448,256]{1,0:T(8,128)(2,1)S(1)} %shard_map.132), channel_id=1, source_target_pairs={{0,2},{2,0},{1,3},{3,1},{4,6},{6,4},{5,7},{7,5},{8,10},{10,8},{9,1... | collective-permute-start | bytes 688136 | tf_op jit(solution)/shard_map/ppermute | solution.py:53
  32.8 1.1 collective-permute-done.1.refs_6_
  34.0 3.8 %collective-permute-start.2 = (bf16[896,256]{1,0:T(8,128)(2,1)S(1)}, bf16[896,256]{1,0:T(8,128)(2,1)S(1)}, u32[]{:S(2)}, u32[]{:S(2)}) collective-permute-start(bf16[896,256]{1,0:T(8,128)(2,1)S(1)} %pad_maximum_fusion), channel_id=1, source_target_pairs={{2,4},{4,2},{6,8},{8,6},{10,12},{12,10},{14,16},{16,14},{18,20},{2... | collective-permute-start | bytes 1376264 | tf_op jit(solution)/shard_map/ppermute | solution.py:60
  37.8 0.0 all-to-all-done
  37.8 1.3 broadcast_in_dim.39
  39.1 5.8 %all-to-all-start.1 = ((bf16[8,128,768]{2,1,0:T(8,128)(2,1)}), bf16[8,128,768]{2,1,0:T(8,128)(2,1)S(1)}, u32[]{:S(2)}, u32[]{:S(2)}) async-start(bf16[8,128,768]{2,1,0:T(8,128)(2,1)} %broadcast_in_dim.39), calls=%async_computation.1 | async-start | bytes 3145728 | tf_op jit(solution)/shard_map/all_to_all | solution.py:43
  44.8 0.0 copy-done.10
  44.8 0.0 copy-start.1
  44.8 0.0 copy-start.3
  44.9 0.0 copy-start.5
  44.9 0.0 copy-start.7
  44.9 4.6 %collective-permute-start.3 = (bf16[128,256]{1,0:T(8,128)(2,1)S(1)}, bf16[128,256]{1,0:T(8,128)(2,1)S(1)}, u32[]{:S(2)}, u32[]{:S(2)}) collective-permute-start(bf16[128,256]{1,0:T(8,128)(2,1)S(1)} %copy-done.10), channel_id=1, source_target_pairs={{2,8},{6,12},{10,16},{14,20},{18,24},{22,28},{26,32},{30,36},{34,4... | collective-permute-start | bytes 196616 | tf_op jit(solution)/shard_map/ppermute | solution.py:66
  49.5 2.3 %collective-permute-done.3.refs_9_ = bf16[128,256]{1,0:T(8,128)(2,1)S(1)} collective-permute-done((bf16[128,256]{1,0:T(8,128)(2,1)S(1)}, bf16[128,256]{1,0:T(8,128)(2,1)S(1)}, u32[]{:S(2)}, u32[]{:S(2)}) %collective-permute-start.3) | collective-permute-done | bytes 65568 | tf_op jit(solution)/shard_map/ppermute | solution.py:66
  51.8 0.0 collective-permute-done.2.far.refs_7_
  51.8 1.9 %collective-permute-start.4 = (bf16[592,256]{1,0:T(8,128)(2,1)S(1)}, bf16[592,256]{1,0:T(8,128)(2,1)S(1)}, u32[]{:S(2)}, u32[]{:S(2)}) collective-permute-start(bf16[592,256]{1,0:T(8,128)(2,1)S(1)} %shard_map.133), channel_id=1, source_target_pairs={{0,2},{2,0},{1,3},{3,1},{4,6},{6,4},{5,7},{7,5},{8,10},{10,8},{9,1... | collective-permute-start | bytes 909320 | tf_op jit(solution)/shard_map/ppermute | solution.py:53
  53.8 1.6 %collective-permute-done.4.refs_8_ = bf16[592,256]{1,0:T(8,128)(2,1)S(1)} collective-permute-done((bf16[592,256]{1,0:T(8,128)(2,1)S(1)}, bf16[592,256]{1,0:T(8,128)(2,1)S(1)}, u32[]{:S(2)}, u32[]{:S(2)}) %collective-permute-start.4) | collective-permute-done | bytes 303136 | tf_op jit(solution)/shard_map/ppermute | solution.py:53
  55.3 10.0 %all-to-all-done.1 = bf16[8,128,768]{2,1,0:T(8,128)(2,1)S(1)} async-done(((bf16[8,128,768]{2,1,0:T(8,128)(2,1)}), bf16[8,128,768]{2,1,0:T(8,128)(2,1)S(1)}, u32[]{:S(2)}, u32[]{:S(2)}) %all-to-all-start.1) | async-done | bytes 1572896 | tf_op jit(solution)/shard_map/all_to_all | solution.py:43
  65.4 2.7 %collective-permute-start.5 = (bf16[1024,768]{1,0:T(8,128)(2,1)S(1)}, bf16[1024,768]{1,0:T(8,128)(2,1)S(1)}, u32[]{:S(2)}, u32[]{:S(2)}) collective-permute-start(bf16[1024,768]{1,0:T(8,128)(2,1)S(1)} %bitcast.14), channel_id=1, source_target_pairs={{0,2},{2,0},{1,3},{3,1},{4,6},{6,4},{5,7},{7,5},{8,10},{10,8},{9,1... | collective-permute-start | bytes 4718600 | tf_op jit(solution)/shard_map/ppermute | solution.py:53
  68.1 3.0 %collective-permute-done.5.refs_11_ = bf16[1024,768]{1,0:T(8,128)(2,1)S(1)} collective-permute-done((bf16[1024,768]{1,0:T(8,128)(2,1)S(1)}, bf16[1024,768]{1,0:T(8,128)(2,1)S(1)}, u32[]{:S(2)}, u32[]{:S(2)}) %collective-permute-start.5) | collective-permute-done | bytes 1572896 | tf_op jit(solution)/shard_map/ppermute | solution.py:53
  71.1 0.0 copy-done.1
  71.1 0.0 copy-done.3
  71.1 0.0 copy-done.5
  71.1 0.0 copy-done.7
  71.1 10.9 %shard_map.134 = (f32[128,256]{1,0:T(8,128)S(1)}, f32[128,256]{1,0:T(8,128)S(1)}, f32[8,256]{1,0:T(8,128)S(1)}, bf16[2,8,128,128]{3,2,1,0:T(8,128)(2,1)S(1)}, bf16[2,8,128,128]{3,2,1,0:T(8,128)(2,1)S(1)}) custom-call(s32[1]{0:T(128)} %bitcast.refs_0_, f32[1,128,256]{2,1,0:T(8,128)S(1)} %copy-done.1, f32[1,128,256]{2,1,0:T(8,128)S(1)} %copy-done.3, ...), custom_call_target="tpu_custom_call" | custom-call | flops 8053063680 | bytes 5963780 | tf_op jit(solution)/shard_map/pallas_call | solution.py:407
  82.0 2.3 %collective-permute-start.6 = (bf16[2,8,128,128]{3,2,1,0:T(8,128)(2,1)S(1)}, bf16[2,8,128,128]{3,2,1,0:T(8,128)(2,1)S(1)}, u32[]{:S(2)}, u32[]{:S(2)}) collective-permute-start(bf16[2,8,128,128]{3,2,1,0:T(8,128)(2,1)S(1)} %get-tuple-element.48), channel_id=1, source_target_pairs={{0,2},{2,0},{1,3},{3,1},{4,6},{6,4},{5,7},{7,5},{8,10},{10,8},{9,1... | collective-permute-start | bytes 1572872 | tf_op jit(solution)/shard_map/ppermute | solution.py:53
  84.3 1.5 %collective-permute-done.6 = bf16[2,8,128,128]{3,2,1,0:T(8,128)(2,1)S(1)} collective-permute-done((bf16[2,8,128,128]{3,2,1,0:T(8,128)(2,1)S(1)}, bf16[2,8,128,128]{3,2,1,0:T(8,128)(2,1)S(1)}, u32[]{:S(2)}, u32[]{:S(2)}) %collective-permute-start.6) | collective-permute-done | bytes 524320 | tf_op jit(solution)/shard_map/ppermute | solution.py:53
  85.9 0.1 shard_map.135
  86.0 15.1 %all_to_all.30.parts = bf16[16,128,128]{2,1,0:T(8,128)(2,1)S(1)} all-to-all(bf16[16,128,128]{2,1,0:T(8,128)(2,1)S(1)} %shard_map.135), channel_id=1, replica_groups=mesh['x_lo'=2,'y'=4,'z_hi'=4,'z_lo'=4,'core'=2,'x_hi'=2] {'x_hi','x_lo',..., dimensions={0} | all-to-all | bytes 1048576 | tf_op jit(solution)/shard_map/all_to_all | solution.py:467
  101.1 0.7 shard_map.136
  101.8 4.5 %all-to-all-start.3 = ((bf16[4,128,128]{2,1,0:T(8,128)(2,1)}), bf16[4,128,128]{2,1,0:T(8,128)(2,1)S(1)}, u32[]{:S(2)}, u32[]{:S(2)}) async-start(bf16[4,128,128]{2,1,0:T(8,128)(2,1)} %shard_map.136), calls=%async_computation.3 | async-start | bytes 262144 | tf_op jit(solution)/shard_map/all_to_all | solution.py:477
  106.3 3.0 %collective-permute-start.9 = (f32[8,256]{1,0:T(8,128)S(1)}, f32[8,256]{1,0:T(8,128)S(1)}, u32[]{:S(2)}, u32[]{:S(2)}) collective-permute-start(f32[8,256]{1,0:T(8,128)S(1)} %get-tuple-element.53), channel_id=1, source_target_pairs={{0,1},{1,0},{2,3},{3,2},{4,5},{5,4},{6,7},{7,6},{8,9},{9,8},{10,11... | collective-permute-start | bytes 24584 | tf_op jit(solution)/shard_map/ppermute | solution.py:53
  109.3 0.1 pad_add_fusion.place
  109.4 1.7 %all-to-all-done.3.parts = bf16[4,128,128]{2,1,0:T(8,128)(2,1)S(1)} async-done(((bf16[4,128,128]{2,1,0:T(8,128)(2,1)}), bf16[4,128,128]{2,1,0:T(8,128)(2,1)S(1)}, u32[]{:S(2)}, u32[]{:S(2)}) %all-to-all-start.3) | async-done | bytes 131104 | tf_op jit(solution)/shard_map/all_to_all | solution.py:477
  111.1 0.7 shard_map.137
  111.8 8.4 %all-to-all-start.4 = ((bf16[4,128,128]{2,1,0:T(8,128)(2,1)}), bf16[4,128,128]{2,1,0:T(8,128)(2,1)S(1)}, u32[]{:S(2)}, u32[]{:S(2)}) async-start(bf16[4,128,128]{2,1,0:T(8,128)(2,1)} %shard_map.137), calls=%async_computation.4 | async-start | bytes 262144 | tf_op jit(solution)/shard_map/all_to_all | solution.py:477
  120.2 0.0 collective-permute-done.9
  120.2 6.3 %collective-permute-start.7 = (f32[128,256]{1,0:T(8,128)S(1)}, f32[128,256]{1,0:T(8,128)S(1)}, u32[]{:S(2)}, u32[]{:S(2)}) collective-permute-start(f32[128,256]{1,0:T(8,128)S(1)} %get-tuple-element.52), channel_id=1, source_target_pairs={{2,4},{4,2},{6,8},{8,6},{10,12},{12,10},{14,16},{16,14},{18,20},{2... | collective-permute-start | bytes 393224 | tf_op jit(solution)/shard_map/ppermute | solution.py:60
  126.5 1.9 %collective-permute-start.8 = (f32[128,256]{1,0:T(8,128)S(1)}, f32[128,256]{1,0:T(8,128)S(1)}, u32[]{:S(2)}, u32[]{:S(2)}) collective-permute-start(f32[128,256]{1,0:T(8,128)S(1)} %get-tuple-element.52), channel_id=1, source_target_pairs={{0,2},{2,0},{1,3},{3,1},{4,6},{6,4},{5,7},{7,5},{8,10},{10,8},{9,1... | collective-permute-start | bytes 393224 | tf_op jit(solution)/shard_map/ppermute | solution.py:53
  128.5 4.0 %all-to-all-done.4.parts = bf16[4,128,128]{2,1,0:T(8,128)(2,1)S(1)} async-done(((bf16[4,128,128]{2,1,0:T(8,128)(2,1)}), bf16[4,128,128]{2,1,0:T(8,128)(2,1)S(1)}, u32[]{:S(2)}, u32[]{:S(2)}) %all-to-all-start.4) | async-done | bytes 131104 | tf_op jit(solution)/shard_map/all_to_all | solution.py:477
  132.4 0.7 shard_map.138
  133.1 8.3 %all-to-all-start.5 = ((bf16[32,16,128]{2,1,0:T(8,128)(2,1)}), bf16[32,16,128]{2,1,0:T(8,128)(2,1)S(1)}, u32[]{:S(2)}, u32[]{:S(2)}) async-start(bf16[32,16,128]{2,1,0:T(8,128)(2,1)} %shard_map.138), calls=%async_computation.5 | async-start | bytes 262144 | tf_op jit(solution)/shard_map/all_to_all | solution.py:490
  141.4 0.0 collective-permute-done.7
  141.4 0.0 collective-permute-done.8
  141.4 0.7 fusion.2
  142.1 7.1 %all-to-all-done.5.parts_ref = bf16[32,16,128]{2,1,0:T(8,128)(2,1)S(1)} async-done(((bf16[32,16,128]{2,1,0:T(8,128)(2,1)}), bf16[32,16,128]{2,1,0:T(8,128)(2,1)S(1)}, u32[]{:S(2)}, u32[]{:S(2)}) %all-to-all-start.5) | async-done | bytes 131104 | tf_op jit(solution)/shard_map/all_to_all | solution.py:490
  149.2 0.0 copy-done.8
  149.2 0.0 copy-done.9
  149.2 1.3 shard_map.139
  (9 shorter events, 0.1 us)
Async XLA Ops:
  11.7 26.0 %all-to-all-start = ((bf16[16,8,768]{2,1,0:T(8,128)(2,1)}), bf16[16,8,768]{2,1,0:T(8,128)(2,1)S(1)}, u32[]{:S(2)}, u32[]{:S(2)}) async-start(bf16[16,8,768]{2,1,0:T(8,128)(2,1)} %broadcast_in_dim.38), calls=%async_computation | async-start | bytes 393216 | tf_op jit(solution)/shard_map/all_to_all | solution.py:27
  21.3 7.9 %collective-permute-start = (f32[24,256]{1,0:T(8,128)}, f32[24,256]{1,0:T(8,128)S(1)}, u32[]{:S(2)}, u32[]{:S(2)}) collective-permute-start(f32[24,256]{1,0:T(8,128)} %get-tuple-element.33.mine.refs_4_), channel_id=1, source_target_pairs={{0,1},{1,0},{2,3},{3,2},{4,5},{5,4},{6,7},{7,6},{8,9},{9,8},{10,11... | collective-permute-start | bytes 73736 | tf_op jit(solution)/shard_map/ppermute | solution.py:53
  26.0 0.9 copy-start
  26.9 0.9 copy-start.2
  27.8 0.9 copy-start.4
  29.2 0.7 copy-start.6
  30.0 3.9 %collective-permute-start.1 = (bf16[448,256]{1,0:T(8,128)(2,1)S(1)}, bf16[448,256]{1,0:T(8,128)(2,1)S(1)}, u32[]{:S(2)}, u32[]{:S(2)}) collective-permute-start(bf16[448,256]{1,0:T(8,128)(2,1)S(1)} %shard_map.132), channel_id=1, source_target_pairs={{0,2},{2,0},{1,3},{3,1},{4,6},{6,4},{5,7},{7,5},{8,10},{10,8},{9,1... | collective-permute-start | bytes 688136 | tf_op jit(solution)/shard_map/ppermute | solution.py:53
  34.0 17.8 %collective-permute-start.2 = (bf16[896,256]{1,0:T(8,128)(2,1)S(1)}, bf16[896,256]{1,0:T(8,128)(2,1)S(1)}, u32[]{:S(2)}, u32[]{:S(2)}) collective-permute-start(bf16[896,256]{1,0:T(8,128)(2,1)S(1)} %pad_maximum_fusion), channel_id=1, source_target_pairs={{2,4},{4,2},{6,8},{8,6},{10,12},{12,10},{14,16},{16,14},{18,20},{2... | collective-permute-start | bytes 1376264 | tf_op jit(solution)/shard_map/ppermute | solution.py:60
  39.1 5.8 %copy-start.10 = (bf16[128,256]{1,0:T(8,128)(2,1)S(1)}, bf16[128,256]{1,0:T(8,128)(2,1)}, u32[]{:S(2)}) copy-start(bf16[128,256]{1,0:T(8,128)(2,1)} %get-tuple-element.40) | copy-start | bytes 196612
  39.1 26.3 %all-to-all-start.1 = ((bf16[8,128,768]{2,1,0:T(8,128)(2,1)}), bf16[8,128,768]{2,1,0:T(8,128)(2,1)S(1)}, u32[]{:S(2)}, u32[]{:S(2)}) async-start(bf16[8,128,768]{2,1,0:T(8,128)(2,1)} %broadcast_in_dim.39), calls=%async_computation.1 | async-start | bytes 3145728 | tf_op jit(solution)/shard_map/all_to_all | solution.py:43
  44.8 26.3 %copy-start.1 = (f32[1,128,256]{2,1,0:T(8,128)S(1)}, f32[1,128,256]{2,1,0:T(8,128)}, u32[]{:S(2)}) copy-start(f32[1,128,256]{2,1,0:T(8,128)} %refs_1_.4) | copy-start | bytes 393220
  44.8 26.3 %copy-start.3 = (f32[1,128,256]{2,1,0:T(8,128)S(1)}, f32[1,128,256]{2,1,0:T(8,128)}, u32[]{:S(2)}) copy-start(f32[1,128,256]{2,1,0:T(8,128)} %refs_2_.4) | copy-start | bytes 393220
  44.9 26.3 %copy-start.5 = (f32[1,128,256]{2,1,0:T(8,128)S(1)}, f32[1,128,256]{2,1,0:T(8,128)}, u32[]{:S(2)}) copy-start(f32[1,128,256]{2,1,0:T(8,128)} %refs_3_.3) | copy-start | bytes 393220
  44.9 26.3 %copy-start.7 = (f32[24,256]{1,0:T(8,128)S(1)}, f32[24,256]{1,0:T(8,128)}, u32[]{:S(2)}) copy-start(f32[24,256]{1,0:T(8,128)} %get-tuple-element.33.mine.refs_4_) | copy-start | bytes 73732
  44.9 6.9 %collective-permute-start.3 = (bf16[128,256]{1,0:T(8,128)(2,1)S(1)}, bf16[128,256]{1,0:T(8,128)(2,1)S(1)}, u32[]{:S(2)}, u32[]{:S(2)}) collective-permute-start(bf16[128,256]{1,0:T(8,128)(2,1)S(1)} %copy-done.10), channel_id=1, source_target_pairs={{2,8},{6,12},{10,16},{14,20},{18,24},{22,28},{26,32},{30,36},{34,4... | collective-permute-start | bytes 196616 | tf_op jit(solution)/shard_map/ppermute | solution.py:66
  51.8 3.5 %collective-permute-start.4 = (bf16[592,256]{1,0:T(8,128)(2,1)S(1)}, bf16[592,256]{1,0:T(8,128)(2,1)S(1)}, u32[]{:S(2)}, u32[]{:S(2)}) collective-permute-start(bf16[592,256]{1,0:T(8,128)(2,1)S(1)} %shard_map.133), channel_id=1, source_target_pairs={{0,2},{2,0},{1,3},{3,1},{4,6},{6,4},{5,7},{7,5},{8,10},{10,8},{9,1... | collective-permute-start | bytes 909320 | tf_op jit(solution)/shard_map/ppermute | solution.py:53
  65.4 5.8 %collective-permute-start.5 = (bf16[1024,768]{1,0:T(8,128)(2,1)S(1)}, bf16[1024,768]{1,0:T(8,128)(2,1)S(1)}, u32[]{:S(2)}, u32[]{:S(2)}) collective-permute-start(bf16[1024,768]{1,0:T(8,128)(2,1)S(1)} %bitcast.14), channel_id=1, source_target_pairs={{0,2},{2,0},{1,3},{3,1},{4,6},{6,4},{5,7},{7,5},{8,10},{10,8},{9,1... | collective-permute-start | bytes 4718600 | tf_op jit(solution)/shard_map/ppermute | solution.py:53
  82.0 3.8 %collective-permute-start.6 = (bf16[2,8,128,128]{3,2,1,0:T(8,128)(2,1)S(1)}, bf16[2,8,128,128]{3,2,1,0:T(8,128)(2,1)S(1)}, u32[]{:S(2)}, u32[]{:S(2)}) collective-permute-start(bf16[2,8,128,128]{3,2,1,0:T(8,128)(2,1)S(1)} %get-tuple-element.48), channel_id=1, source_target_pairs={{0,2},{2,0},{1,3},{3,1},{4,6},{6,4},{5,7},{7,5},{8,10},{10,8},{9,1... | collective-permute-start | bytes 1572872 | tf_op jit(solution)/shard_map/ppermute | solution.py:53
  101.1 48.1 %copy-start.8 = (f32[4,256]{1,0:T(4,128)S(1)}, f32[4,256]{1,0:T(4,128)}, u32[]{:S(2)}) copy-start(f32[4,256]{1,0:T(4,128)} %w_in.1) | copy-start | bytes 12292
  101.1 48.1 %copy-start.9 = (f32[4,256]{1,0:T(4,128)S(1)}, f32[4,256]{1,0:T(4,128)}, u32[]{:S(2)}) copy-start(f32[4,256]{1,0:T(4,128)} %w_out.1) | copy-start | bytes 12292
  101.8 9.3 %all-to-all-start.3 = ((bf16[4,128,128]{2,1,0:T(8,128)(2,1)}), bf16[4,128,128]{2,1,0:T(8,128)(2,1)S(1)}, u32[]{:S(2)}, u32[]{:S(2)}) async-start(bf16[4,128,128]{2,1,0:T(8,128)(2,1)} %shard_map.136), calls=%async_computation.3 | async-start | bytes 262144 | tf_op jit(solution)/shard_map/all_to_all | solution.py:477
  106.3 13.9 %collective-permute-start.9 = (f32[8,256]{1,0:T(8,128)S(1)}, f32[8,256]{1,0:T(8,128)S(1)}, u32[]{:S(2)}, u32[]{:S(2)}) collective-permute-start(f32[8,256]{1,0:T(8,128)S(1)} %get-tuple-element.53), channel_id=1, source_target_pairs={{0,1},{1,0},{2,3},{3,2},{4,5},{5,4},{6,7},{7,6},{8,9},{9,8},{10,11... | collective-permute-start | bytes 24584 | tf_op jit(solution)/shard_map/ppermute | solution.py:53
  111.8 20.7 %all-to-all-start.4 = ((bf16[4,128,128]{2,1,0:T(8,128)(2,1)}), bf16[4,128,128]{2,1,0:T(8,128)(2,1)S(1)}, u32[]{:S(2)}, u32[]{:S(2)}) async-start(bf16[4,128,128]{2,1,0:T(8,128)(2,1)} %shard_map.137), calls=%async_computation.4 | async-start | bytes 262144 | tf_op jit(solution)/shard_map/all_to_all | solution.py:477
  120.2 21.2 %collective-permute-start.7 = (f32[128,256]{1,0:T(8,128)S(1)}, f32[128,256]{1,0:T(8,128)S(1)}, u32[]{:S(2)}, u32[]{:S(2)}) collective-permute-start(f32[128,256]{1,0:T(8,128)S(1)} %get-tuple-element.52), channel_id=1, source_target_pairs={{2,4},{4,2},{6,8},{8,6},{10,12},{12,10},{14,16},{16,14},{18,20},{2... | collective-permute-start | bytes 393224 | tf_op jit(solution)/shard_map/ppermute | solution.py:60
  126.5 14.9 %collective-permute-start.8 = (f32[128,256]{1,0:T(8,128)S(1)}, f32[128,256]{1,0:T(8,128)S(1)}, u32[]{:S(2)}, u32[]{:S(2)}) collective-permute-start(f32[128,256]{1,0:T(8,128)S(1)} %get-tuple-element.52), channel_id=1, source_target_pairs={{0,2},{2,0},{1,3},{3,1},{4,6},{6,4},{5,7},{7,5},{8,10},{10,8},{9,1... | collective-permute-start | bytes 393224 | tf_op jit(solution)/shard_map/ppermute | solution.py:53
  133.1 16.1 %all-to-all-start.5 = ((bf16[32,16,128]{2,1,0:T(8,128)(2,1)}), bf16[32,16,128]{2,1,0:T(8,128)(2,1)S(1)}, u32[]{:S(2)}, u32[]{:S(2)}) async-start(bf16[32,16,128]{2,1,0:T(8,128)(2,1)} %shard_map.138), calls=%async_computation.5 | async-start | bytes 262144 | tf_op jit(solution)/shard_map/all_to_all | solution.py:490
